TPU v7x, 256 devices: a whole 4x4x8 slice. The times are simulated.
256 devices in a mesh: section: 4 (over z_hi, core), dp: 64 (over x, y, z_lo).
Axes of the slice: x: 4, y: 4, z: 8 (z_hi: 2, z_lo: 4; z = z_hi * 4 + z_lo), core: 2. Of those that a mesh axis runs over, the one named last changes fastest.
Arguments:
- qkv_a: bfloat16 [4, 8192, 5120], P('section', 'dp'), may hold values from -4 to 4
- qkv_b: bfloat16 [4, 8192, 5120], P('section', 'dp'), may hold values from -4 to 4
- slot_grad_b: bfloat16 [4, 24576, 4096], P('section', 'dp'), may hold values from -16 to 16
- adapter_down: bfloat16 [4, 4096, 64], P('section'), may hold values from -0.09375 to 0.09375
- adapter_up: bfloat16 [4, 64, 4096], P('section'), may hold values from -0.75 to 0.75
- lang_scale: float32 [102], replicated, may hold values from 0.25 to 1
- languages: int32 [2, 64], replicated, may hold values from 0 to 101
- lengths: int32 [2, 64, 8], replicated, may hold values from 1 to 64, 128 in all within a row
- destination: int32 [2, 64], replicated, may hold values from 0 to 63, as said below
Outputs:
- handed_forward: bfloat16 [4, 24576, 4096], P('section', 'dp')
- handed_back: bfloat16 [4, 8192, 5120], P('section', 'dp')
- adapter_grad: float32 [4, 4096, 128], P('section', 'dp')
Inputs may be any that keep to these rules, and one draw needn't show every extreme that they name: `destination`: of each micro-batch, a data rank's first tile goes to that rank or the rank before it, its last tile to that rank or the rank after it, its other tiles stay; at most one tile of a rank leaves.
All inputs are finite; a program needn't handle non-finite values.
Results may differ from a plain program's by a relative error of at most 0.014.
Values may be sent and summed in bfloat16 or wider, within the bound.
No kernel may reach another device: no remote copies, remote signals or barrier semaphores. Data moves between devices by JAX's collectives and lax.ppermute only.
A program may use at most 128 MiB of HBM per device.

v0:
```python
import math

import jax
import jax.numpy as jnp
from jax import lax
from jax.sharding import PartitionSpec as P

HEADS = 32
KV = 4
HEAD_DIM = 128
TILE = 128
LANGS = 102


def extended_2(x, sides, width):
    for axis, dim in sides:
        size, length = (lax.axis_size(axis), x.shape[dim])
        up = [(i, (i + 1) % size) for i in range(size - 1)]
        down = [(j, i) for i, j in up]
        last = lax.slice_in_dim(x, length - width, length, axis=dim)
        first = lax.slice_in_dim(x, 0, width, axis=dim)
        before = lax.ppermute(last, axis, up)
        after = lax.ppermute(first, axis, down)
        x = jnp.concatenate([before, x, after], axis=dim)
    return x


def from_behind(block, axis, distance):
    devices = range(lax.axis_size(axis))
    route = [(i - distance, i) for i in devices if i - distance in devices]
    return lax.ppermute(block, axis, route)


def mix(form, left, right):
    return jnp.einsum(form, left, right, preferred_element_type=jnp.float32)


def segment_mask(lens):
    ends = jnp.cumsum(lens, axis=-1)
    place = jnp.arange(TILE, dtype=jnp.int32)
    segment = jnp.sum((place[None, :, None] >= ends[:, None, :]).astype(jnp.int32), axis=-1)
    causal = place[:, None] >= place[None, :]
    return (segment[:, :, None] == segment[:, None, :]) & causal[None]


def split_heads(joined):
    count = joined.shape[0]
    group = HEADS // KV
    queries = joined[:, :, : HEADS * HEAD_DIM].reshape(count, TILE, KV, group, HEAD_DIM)
    keys = joined[:, :, HEADS * HEAD_DIM : (HEADS + KV) * HEAD_DIM].reshape(
        count, TILE, KV, HEAD_DIM
    )
    values = joined[:, :, (HEADS + KV) * HEAD_DIM :].reshape(count, TILE, KV, HEAD_DIM)
    return (queries, keys, values)


def attend(joined, mask):
    count = joined.shape[0]
    queries, keys, values = split_heads(joined)
    scale = 1.0 / math.sqrt(HEAD_DIM)
    scores = mix("nqhgd,nkhd->nhgqk", queries, keys) * scale
    allowed = mask[:, None, None]
    masked = jnp.where(allowed, scores, -1e30)
    top = jnp.max(masked, axis=-1, keepdims=True)
    weights = jnp.where(allowed, jnp.exp(masked - top), 0.0)
    probs = weights / jnp.sum(weights, axis=-1, keepdims=True)
    probs_low = probs.astype(jnp.bfloat16)
    attn = mix("nhgqk,nkhd->nqhgd", probs_low, values).astype(jnp.bfloat16)
    return (attn.reshape(count, TILE, HEADS * HEAD_DIM), probs, probs_low)


def adapt(attn, rate, down, up):
    width = HEADS * HEAD_DIM
    rows = attn.reshape(-1, width)
    low = jnp.dot(rows, down, preferred_element_type=jnp.float32).astype(jnp.bfloat16)
    lift = jnp.dot(low, up, preferred_element_type=jnp.float32).reshape(attn.shape)
    return (attn.astype(jnp.float32) + rate[:, None, None] * lift).astype(jnp.bfloat16)


def backward(joined, mask, grad_in, rate, down, up):
    count = joined.shape[0]
    group = HEADS // KV
    width = HEADS * HEAD_DIM
    scale = 1.0 / math.sqrt(HEAD_DIM)
    queries, keys, values = split_heads(joined)
    attn, probs, probs_low = attend(joined, mask)
    rows = attn.reshape(-1, width)
    low = jnp.dot(rows, down, preferred_element_type=jnp.float32).astype(jnp.bfloat16)
    scaled = (
        (rate[:, None, None] * grad_in.astype(jnp.float32)).astype(jnp.bfloat16).reshape(-1, width)
    )
    back_low = jnp.dot(scaled, up.T, preferred_element_type=jnp.float32).astype(jnp.bfloat16)
    grad_attn = (
        grad_in.reshape(-1, width).astype(jnp.float32)
        + jnp.dot(back_low, down.T, preferred_element_type=jnp.float32)
    ).astype(jnp.bfloat16)
    grad_heads = grad_attn.reshape(count, TILE, KV, group, HEAD_DIM)
    attn_heads = attn.reshape(count, TILE, KV, group, HEAD_DIM)
    grad_probs = mix("nqhgd,nkhd->nhgqk", grad_heads, values)
    delta = jnp.sum(grad_heads.astype(jnp.float32) * attn_heads.astype(jnp.float32), axis=-1)
    delta = jnp.transpose(delta, (0, 2, 3, 1))[..., None]
    grad_scores = (probs * (grad_probs - delta) * scale).astype(jnp.bfloat16)
    grad_queries = mix("nhgqk,nkhd->nqhgd", grad_scores, keys).astype(jnp.bfloat16)
    grad_keys = mix("nhgqk,nqhgd->nkhd", grad_scores, queries).astype(jnp.bfloat16)
    grad_values = mix("nhgqk,nqhgd->nkhd", probs_low, grad_heads).astype(jnp.bfloat16)
    grad_qkv = jnp.concatenate(
        [
            grad_queries.reshape(count, TILE, -1),
            grad_keys.reshape(count, TILE, -1),
            grad_values.reshape(count, TILE, -1),
        ],
        axis=-1,
    )
    return (grad_qkv, rows, back_low, scaled, low)


def shards(
    qkv_a, qkv_b, slot_grad_b, adapter_down, adapter_up, lang_scale, languages, lengths, destination
):
    groups = lax.axis_size("dp")
    rank = lax.axis_index("dp")
    joined_width = qkv_a.shape[-1]
    width = HEADS * HEAD_DIM
    tiles = qkv_a.shape[1] // TILE
    total_tiles = groups * tiles
    down = adapter_down[0]
    up = adapter_up[0]
    table = jnp.arange(LANGS, dtype=jnp.int32)
    rates = jnp.sum(
        jnp.where(languages[:, :, None] == table[None, None, :], lang_scale[None, None, :], 0.0),
        axis=-1,
    )
    offsets = jnp.arange(-1, tiles + 1, dtype=jnp.int32)
    source = rank * tiles + offsets
    clipped = jnp.clip(source, 0, total_tiles - 1)
    inside = (source >= 0) & (source < total_tiles)
    home = rank * tiles + jnp.arange(tiles, dtype=jnp.int32)
    live_a = inside & (destination[0][clipped] == rank)
    tiles_a = qkv_a[0].reshape(tiles, TILE, joined_width)
    slots_a = extended_2(tiles_a, (("dp", 0),), 1)
    attn, probs, probs_low = attend(slots_a, segment_mask(lengths[0][clipped]))
    section_out = adapt(attn, rates[0][clipped], down, up)
    section_out = jnp.where(live_a[:, None, None], section_out, jnp.zeros((), section_out.dtype))
    handed_forward = from_behind(section_out.reshape(1, -1, width), "section", 1)
    home_dest = destination[1][home]
    went_left = home_dest < rank
    went_right = home_dest > rank
    grad_slots = slot_grad_b[0].reshape(tiles + 2, TILE, width)
    tiles_b = qkv_b[0].reshape(tiles, TILE, joined_width)
    slots_b = extended_2(tiles_b, (("dp", 0),), 1)
    live_b = inside & (destination[1][clipped] == rank)
    rate_b = jnp.where(live_b, rates[1][clipped], 0.0)
    grad_qkv, rows, back_low, scaled, low = backward(
        slots_b, segment_mask(lengths[1][clipped]), grad_slots, rate_b, down, up
    )
    returned = extended_2(grad_qkv, (("dp", 0),), 1)
    own = returned[2 : tiles + 2]
    grad_qkv_home = jnp.where(
        went_left[:, None, None],
        returned[0][None],
        jnp.where(went_right[:, None, None], returned[tiles + 3][None], own),
    )
    local = jnp.concatenate(
        [mix("rq,rk->qk", rows, back_low), mix("rq,rk->qk", scaled, low)], axis=1
    )
    adapter_grad = lax.psum_scatter(local, "dp", scatter_dimension=0, tiled=True)
    handed_back = from_behind(grad_qkv_home, "section", -1)
    return (handed_forward, handed_back, adapter_grad[None])


def solution(mesh):
    return jax.shard_map(
        shards,
        mesh=mesh,
        in_specs=(
            P("section", "dp", None),
            P("section", "dp", None),
            P("section", "dp", None),
            P("section", None, None),
            P("section", None, None),
            P(),
            P(),
            P(),
            P(),
        ),
        out_specs=(P("section", "dp", None), P("section", "dp", None), P("section", "dp", None)),
        check_vma=False,
    )
```

profile of v0, /device:TPU:0, one launch (start us, length us, event | category | flops | bytes accessed | tf_op | source)
XLA Modules:
  0.0 652.7 jit_solution(1493815369048295265)
XLA Ops:
  7.3 1.8 copy.90
  10.4 5.6 collective-permute-start
  16.0 1.8 copy.100
  19.1 5.6 collective-permute-start.3
  30.3 3.3 fusion.40
  35.2 2.6 copy.144
  37.8 4.9 copy.108
  44.1 52.1 %collective-permute-done.4 = bf16[1,128,5120]{1,2,0:T(8,128)(2,1)} collective-permute-done((bf16[1,128,5120]{1,2,0:T(8,128)(2,1)S(1)}, bf16[1,128,5120]{1,2,0:T(8,128)(2,1)}, u32[]{:S(2)}, u32[]{:S(2)}) %collective-permute-start.4) | collective-permute-done | bytes 1310752 | tf_op jit(solution)/shard_map/ppermute | solution.py:23
  96.2 1.9 pad_maximum_fusion
  98.2 1.9 slice.81
  100.0 1.9 pad_maximum_fusion.5
  101.9 7.1 %fusion.65 = (f32[3,4,8,128]{3,2,1,0:T(8,128)S(1)}, f32[3,4,8,128,128]{3,4,2,1,0:T(8,128)}) fusion(pred[3,128,128]{1,2,0:T(8,128)(4,1)} %get-tuple-element.32, bf16[3,128,4,128,1]{1,3,4,2,0:T(8,128)(2,1)} %bitcast.185, bf16[3,128,4,8,128]{1,4,3,2,0:T(8,128)(2,1)} %bitcast.177), kind=kOutput, calls=%fused_computation.107 | convolution fusion | flops 410517632 | bytes 9928704 | tf_op jit(solution)/shard_map/sub | solution.py:65
  109.0 5.5 fusion.29
  114.5 4.8 copy.113
  119.3 5.7 multiply_reduce_fusion
  126.1 1.7 fusion.9
  128.9 2.6 convolution_convert_fusion
  131.6 5.0 copy.117
  136.6 5.8 reshape_reshape.7
  142.4 5.0 fusion.16
  147.4 3.7 fusion.66
  151.1 3.7 fusion.36
  154.8 1.9 copy.116
  157.7 4.7 copy.114
  162.4 2.7 pad_maximum_fusion.4
  165.1 3.0 copy.139
  168.2 2.1 pad_maximum_fusion.1
  170.3 1.4 fusion.61
  171.8 2.2 pad_maximum_fusion.7
  174.0 3.4 pad_maximum_fusion.2
  177.4 7.1 %fusion.64 = (f32[3,4,8,128]{3,2,1,0:T(8,128)S(1)}, f32[3,4,8,128,128]{3,4,2,1,0:T(8,128)}) fusion(pred[3,128,128]{1,2,0:T(8,128)(4,1)} %get-tuple-element.33, bf16[3,128,4,128,1]{1,3,4,2,0:T(8,128)(2,1)} %bitcast.189, bf16[3,128,4,8,128]{1,4,3,2,0:T(8,128)(2,1)} %bitcast.182), kind=kOutput, calls=%fused_computation.106 | convolution fusion | flops 410517632 | bytes 9928704 | tf_op jit(solution)/shard_map/sub | solution.py:65
  184.5 3.8 fusion.30
  188.3 1.7 copy-done.6
  190.0 3.3 bitcast_convert_fusion
  193.2 6.5 %copy.99 = f32[3,128,4096]{2,1,0:T(8,128)} copy(f32[3,128,4096]{1,2,0:T(8,128)} %bitcast_convert_fusion) | data formatting | bytes 12582912 | tf_op jit(solution)/shard_map/convert_element_type | solution.py:77
  199.8 5.0 copy.97
  204.8 5.9 reshape_reshape.6
  210.7 4.0 collective-permute-start.5
  214.7 1.3 collective-permute-start.6
  216.0 3.0 fusion.43
  219.0 3.8 fusion.12
  222.8 2.9 collective-permute-start.2
  227.7 20.4 %collective-permute-done.5 = bf16[1,128,5120]{2,1,0:T(8,128)(2,1)S(1)} collective-permute-done((bf16[1,128,5120]{2,1,0:T(8,128)(2,1)S(1)}, bf16[1,128,5120]{2,1,0:T(8,128)(2,1)S(1)}, u32[]{:S(2)}, u32[]{:S(2)}) %collective-permute-start.5) | collective-permute-done | bytes 1310752 | tf_op jit(solution)/shard_map/ppermute | solution.py:22
  248.1 34.4 %collective-permute-done.6 = bf16[1,128,5120]{2,1,0:T(8,128)(2,1)S(1)} collective-permute-done((bf16[1,128,5120]{2,1,0:T(8,128)(2,1)S(1)}, bf16[1,128,5120]{2,1,0:T(8,128)(2,1)S(1)}, u32[]{:S(2)}, u32[]{:S(2)}) %collective-permute-start.6) | collective-permute-done | bytes 1310752 | tf_op jit(solution)/shard_map/ppermute | solution.py:23
  282.5 1.5 fusion.32
  285.3 3.6 collective-permute-done.7
  288.9 350.4 %reduce-scatter.4.cloned.1.call-done = f32[64,128]{1,0:T(8,128)} async-done(((f32[4096,128]{1,0:T(8,128)}), f32[64,128]{1,0:T(8,128)}) %reduce-scatter.4.cloned.1.call-update) | async-done | bytes 32784
  640.8 3.9 copy.157
  (81 shorter events, 18.9 us)
Async XLA Ops:
  7.2 27.1 %copy-start = (bf16[1,4096,64]{1,2,0:T(8,128)(2,1)S(1)}, bf16[1,4096,64]{1,2,0:T(8,128)(2,1)}, u32[]{:S(2)}) copy-start(bf16[1,4096,64]{1,2,0:T(8,128)(2,1)} %param.12) | copy-start | bytes 1572868
  7.2 17.5 %copy-start.15 = (s32[2,64,8]{1,2,0:T(8,128)S(1)}, s32[2,64,8]{1,2,0:T(8,128)}, u32[]{:S(2)}) copy-start(s32[2,64,8]{1,2,0:T(8,128)} %param.16) | copy-start | bytes 12292
  7.2 17.5 %copy-start.20 = (f32[102]{0:T(128)S(1)}, f32[102]{0:T(128)}, u32[]{:S(2)}) copy-start(f32[102]{0:T(128)} %param.14) | copy-start | bytes 1228
  7.2 17.5 %copy-start.17 = (s32[2,64]{1,0:T(2,128)S(1)}, s32[2,64]{1,0:T(2,128)}, u32[]{:S(2)}) copy-start(s32[2,64]{1,0:T(2,128)} %param.15) | copy-start | bytes 1540
  7.2 17.7 %copy-start.18 = (s32[2,64]{1,0:T(2,128)S(1)}, s32[2,64]{1,0:T(2,128)}, u32[]{:S(2)}) copy-start(s32[2,64]{1,0:T(2,128)} %param.17) | copy-start | bytes 1540
  7.2 632.1 %reduce-scatter.4.cloned.1.call-start = ((), (), s32[]{:S(2)}) async-start(), calls=%async_computation.1 | async-start | bytes 2129920
  9.1 162.7 %collective-permute-start.1 = (bf16[1,128,5120]{1,2,0:T(8,128)(2,1)S(1)}, bf16[1,128,5120]{1,2,0:T(8,128)(2,1)}, u32[]{:S(2)}, u32[]{:S(2)}) collective-permute-start(bf16[1,128,5120]{1,2,0:T(8,128)(2,1)S(1)} %copy.90), channel_id=1, source_target_pairs={{1,0},{2,1},{3,2},{4,3},{5,4},{6,5},{7,6},{8,7},{9,8},{10,9},{11,1... | collective-permute-start | bytes 3932168 | tf_op jit(solution)/shard_map/ppermute | solution.py:23
  10.4 161.4 %collective-permute-start = (bf16[1,128,5120]{1,2,0:T(8,128)(2,1)S(1)}, bf16[1,128,5120]{1,2,0:T(8,128)(2,1)}, u32[]{:S(2)}, u32[]{:S(2)}) collective-permute-start(bf16[1,128,5120]{1,2,0:T(8,128)(2,1)S(1)} %copy.90), channel_id=1, source_target_pairs={{0,1},{1,2},{2,3},{3,4},{4,5},{5,6},{6,7},{7,8},{8,9},{9,10},{10,1... | collective-permute-start | bytes 3932168 | tf_op jit(solution)/shard_map/ppermute | solution.py:22
  17.8 78.5 %collective-permute-start.4 = (bf16[1,128,5120]{1,2,0:T(8,128)(2,1)S(1)}, bf16[1,128,5120]{1,2,0:T(8,128)(2,1)}, u32[]{:S(2)}, u32[]{:S(2)}) collective-permute-start(bf16[1,128,5120]{1,2,0:T(8,128)(2,1)S(1)} %copy.100), channel_id=1, source_target_pairs={{1,0},{2,1},{3,2},{4,3},{5,4},{6,5},{7,6},{8,7},{9,8},{10,9},{11,1... | collective-permute-start | bytes 3932168 | tf_op jit(solution)/shard_map/ppermute | solution.py:23
  19.1 77.2 %collective-permute-start.3 = (bf16[1,128,5120]{1,2,0:T(8,128)(2,1)S(1)}, bf16[1,128,5120]{1,2,0:T(8,128)(2,1)}, u32[]{:S(2)}, u32[]{:S(2)}) collective-permute-start(bf16[1,128,5120]{1,2,0:T(8,128)(2,1)S(1)} %copy.100), channel_id=1, source_target_pairs={{0,1},{1,2},{2,3},{3,4},{4,5},{5,6},{6,7},{7,8},{8,9},{9,10},{10,1... | collective-permute-start | bytes 3932168 | tf_op jit(solution)/shard_map/ppermute | solution.py:22
  30.3 3.9 copy-start.4
  33.6 0.6 copy-start.13
  119.3 5.7 copy-start.5
  119.3 6.7 %copy-start.7 = (f32[3,4,8,128,128]{3,4,2,1,0:T(8,128)S(1)}, f32[3,4,8,128,128]{3,4,2,1,0:T(8,128)}, u32[]{:S(2)}) copy-start(f32[3,4,8,128,128]{3,4,2,1,0:T(8,128)} %get-tuple-element.44) | copy-start | bytes 18874372
  126.1 1.9 copy-start.3
  127.9 1.0 copy-start.8
  142.4 5.0 copy-start.14
  147.4 3.7 copy-start.2
  165.1 3.0 copy-start.9
  165.1 3.0 copy-start.10
  170.3 3.7 copy-start.1
  188.3 1.7 copy-start.6
  204.8 5.9 copy-start.11
  210.7 8.3 %copy-start.12 = (bf16[1,64,4096]{2,1,0:T(8,128)(2,1)S(1)}, bf16[1,64,4096]{2,1,0:T(8,128)(2,1)}, u32[]{:S(2)}) copy-start(bf16[1,64,4096]{2,1,0:T(8,128)(2,1)} %param.13) | copy-start | bytes 1572868
  210.7 8.3 %copy-start.16 = (f32[3]{0:T(128)S(1)}, f32[3]{0:T(128)}, u32[]{:S(2)}) copy-start(f32[3]{0:T(128)} %gather_fusion.2) | copy-start | bytes 40
  210.7 8.4 %copy-start.19 = (pred[3]{0:T(512)(128)(4,1)S(1)}, pred[3]{0:T(512)(128)(4,1)}, u32[]{:S(2)}) copy-start(pred[3]{0:T(512)(128)(4,1)} %compare_and_fusion.2) | copy-start | bytes 13
  210.7 37.4 %collective-permute-start.5 = (bf16[1,128,5120]{2,1,0:T(8,128)(2,1)S(1)}, bf16[1,128,5120]{2,1,0:T(8,128)(2,1)S(1)}, u32[]{:S(2)}, u32[]{:S(2)}) collective-permute-start(bf16[1,128,5120]{2,1,0:T(8,128)(2,1)S(1)} %copy-done.11), channel_id=1, source_target_pairs={{0,1},{1,2},{2,3},{3,4},{4,5},{5,6},{6,7},{7,8},{8,9},{9,10},{10,1... | collective-permute-start | bytes 3932168 | tf_op jit(solution)/shard_map/ppermute | solution.py:22
  214.7 67.8 %collective-permute-start.6 = (bf16[1,128,5120]{2,1,0:T(8,128)(2,1)S(1)}, bf16[1,128,5120]{2,1,0:T(8,128)(2,1)S(1)}, u32[]{:S(2)}, u32[]{:S(2)}) collective-permute-start(bf16[1,128,5120]{2,1,0:T(8,128)(2,1)S(1)} %get-tuple-element.26), channel_id=1, source_target_pairs={{1,0},{2,1},{3,2},{4,3},{5,4},{6,5},{7,6},{8,7},{9,8},{10,9},{11,1... | collective-permute-start | bytes 3932168 | tf_op jit(solution)/shard_map/ppermute | solution.py:23
  219.0 6.7 %copy-start.21 = (s32[1,64]{1,0:T(1,128)S(1)}, s32[1,64]{1,0:T(1,128)}, u32[]{:S(2)}) copy-start(s32[1,64]{1,0:T(1,128)} %get-tuple-element.36) | copy-start | bytes 772
  222.8 66.1 %collective-permute-start.2 = (bf16[1,384,4096]{2,1,0:T(8,128)(2,1)S(1)}, bf16[1,384,4096]{2,1,0:T(8,128)(2,1)}, u32[]{:S(2)}, u32[]{:S(2)}) collective-permute-start(bf16[1,384,4096]{2,1,0:T(8,128)(2,1)S(1)} %bitcast.181), channel_id=1, source_target_pairs={{0,64},{64,128},{128,192},{1,65},{65,129},{129,193},{2,66},{66,130... | collective-permute-start | bytes 9437192 | tf_op jit(solution)/shard_map/ppermute | solution.py:31
  284.0 4.9 collective-permute-start.7
Sparse Core Ops, SparseCore 0:
  168.3 470.9 reduce-scatter.3
where the time goes:
time: 654 us; the launch traced here: 653 us
  waiting for transfers between devices  461 us (70%)
  local copies, waits for them, and re-layouts  73.7 us (11%)
  matrix products  52.4 us (8%)
  other arithmetic  26.5 us (4%)
  starting transfers between devices  23.4 us (4%)
  between operations  15.7 us (2%)
    unnamed x2, waiting for transfers between devices  350 us
    ppermute x3, waiting for transfers between devices, extended_2(): after = lax.ppermute(first, axis, down)  86.5 us
    dot_general x8, matrix products, mix(): return jnp.einsum(form, left, right, preferred_element_type=jnp.float32)  27.1 us
    ppermute x3, waiting for transfers between devices, extended_2(): before = lax.ppermute(last, axis, up)  20.4 us
    unnamed x54, local copies, waits for them, and re-layouts  19.4 us
    ppermute x3, starting transfers between devices, extended_2(): before = lax.ppermute(last, axis, up)  15.3 us
    sub x2, matrix products, attend(): weights = jnp.where(allowed, jnp.exp(masked - top), 0.0)  14.2 us
  transfers between devices with their start and end apart: 9, of which 5 were waited for; matrix products, arithmetic and copies ran while one was open for 22% of the time, Pallas kernels for 0%

commit v1 on v0

v1 whole, which is shorter than its diff:
```python
import functools
import math

import jax
import jax.numpy as jnp
from jax import lax
from jax.experimental import pallas as pl
from jax.experimental.pallas import tpu as pltpu
from jax.sharding import PartitionSpec as P

HEADS = 32
KV = 4
GROUP = HEADS // KV
HEAD_DIM = 128
TILE = 128
SEGS = 8
RANK = 64
QW = HEADS * HEAD_DIM
KW = KV * HEAD_DIM
GW = GROUP * HEAD_DIM
SCALE = 1.0 / math.sqrt(HEAD_DIM)
AXES = ("section", "dp")
BF16 = jnp.bfloat16
F32 = jnp.float32


def dot(a, b, dims):
    return lax.dot_general(a, b, (dims, ((), ())), preferred_element_type=F32)


NN = ((1,), (0,))
NT = ((1,), (1,))
TN = ((0,), (0,))


def mask_bias(lens_ref, m, rank):
    shape = (TILE, TILE)
    row = lax.broadcasted_iota(jnp.int32, shape, 0)
    col = lax.broadcasted_iota(jnp.int32, shape, 1)
    seg_row = jnp.zeros(shape, jnp.int32)
    seg_col = jnp.zeros(shape, jnp.int32)
    end = jnp.int32(0)
    for k in range(SEGS):
        end = end + lens_ref[m, rank, k]
        seg_row = seg_row + (row >= end).astype(jnp.int32)
        seg_col = seg_col + (col >= end).astype(jnp.int32)
    allowed = (seg_row == seg_col) & (row >= col)
    return jnp.where(allowed, 0.0, -1e30).astype(F32)


def stacked(ref, base):
    return jnp.concatenate(
        [ref[:, base + h * HEAD_DIM : base + (h + 1) * HEAD_DIM] for h in range(GROUP)], axis=0
    )


def softmax(scores, bias):
    masked = scores + bias
    top = jnp.max(masked, axis=-1, keepdims=True)
    weights = jnp.exp2((masked - top) * (SCALE * math.log2(math.e)))
    return weights * (1.0 / jnp.sum(weights, axis=-1, keepdims=True))


def attend_group(j, qkv_ref, bias, probs_ref):
    keys = qkv_ref[:, QW + j * HEAD_DIM : QW + (j + 1) * HEAD_DIM]
    values = qkv_ref[:, QW + KW + j * HEAD_DIM : QW + KW + (j + 1) * HEAD_DIM]
    queries = stacked(qkv_ref, j * GW)
    probs_ref[...] = dot(queries, keys, NT)
    lows = []
    for h in range(GROUP):
        rows = slice(h * TILE, (h + 1) * TILE)
        probs = softmax(probs_ref[rows, :], bias)
        probs_ref[rows, :] = probs
        lows.append(probs.astype(BF16))
    probs_low = jnp.concatenate(lows, axis=0)
    attn = dot(probs_low, values, NN).astype(BF16)
    return queries, keys, values, probs_low, attn


def forward_kernel(rank_ref, lens_ref, langs_ref, table_ref, qkv_ref, down_ref, up_ref, out_ref, probs_ref):
    rank = rank_ref[0]
    rate = table_ref[langs_ref[0, rank]]
    bias = mask_bias(lens_ref, 0, rank)
    low = jnp.zeros((TILE, RANK), F32)
    for j in range(KV):
        attn = attend_group(j, qkv_ref, bias, probs_ref)[-1]
        for h in range(GROUP):
            cols = slice(j * GW + h * HEAD_DIM, j * GW + (h + 1) * HEAD_DIM)
            out_ref[:, cols] = attn[h * TILE : (h + 1) * TILE]
        low = low + dot(out_ref[:, j * GW : (j + 1) * GW], down_ref[j * GW : (j + 1) * GW, :], NN)
    low = low.astype(BF16)
    for c in range(0, QW, 512):
        lift = dot(low, up_ref[:, c : c + 512], NN)
        out_ref[:, c : c + 512] = (out_ref[:, c : c + 512].astype(F32) + rate * lift).astype(BF16)


def backward_kernel(
    rank_ref, lens_ref, langs_ref, dest_ref, table_ref, qkv_ref, left_ref, mid_ref, right_ref,
    down_ref, up_ref, grad_ref, terms_ref, probs_ref, attn_ref, scaled_ref, gattn_ref,
):
    rank = rank_ref[0]
    rate = table_ref[langs_ref[1, rank]]
    went = dest_ref[1, rank] - rank
    bias = mask_bias(lens_ref, 1, rank)
    back = jnp.zeros((TILE, RANK), F32)
    for c in range(0, QW, 512):
        cols = slice(c, c + 512)
        grad = jnp.where(
            went < 0, left_ref[:, cols], jnp.where(went > 0, right_ref[:, cols], mid_ref[:, cols])
        )
        gattn_ref[:, cols] = grad
        scaled = (rate * grad.astype(F32)).astype(BF16)
        scaled_ref[:, cols] = scaled
        back = back + dot(scaled, up_ref[:, cols], NT)
    back = back.astype(BF16)
    low = jnp.zeros((TILE, RANK), F32)
    for j in range(KV):
        block = slice(j * GW, (j + 1) * GW)
        gattn = gattn_ref[:, block].astype(F32) + dot(back, down_ref[block, :], NT)
        gattn_ref[:, block] = gattn.astype(BF16)
        queries, keys, values, probs_low, attn = attend_group(j, qkv_ref, bias, probs_ref)
        for h in range(GROUP):
            cols = slice(j * GW + h * HEAD_DIM, j * GW + (h + 1) * HEAD_DIM)
            attn_ref[:, cols] = attn[h * TILE : (h + 1) * TILE]
        low = low + dot(attn_ref[:, block], down_ref[block, :], NN)
        grads = stacked(gattn_ref, j * GW)
        grad_probs = dot(grads, values, NT)
        scores = []
        for h in range(GROUP):
            rows = slice(h * TILE, (h + 1) * TILE)
            probs = probs_ref[rows, :]
            weighed = probs * grad_probs[rows]
            delta = jnp.sum(weighed, axis=-1, keepdims=True)
            scores.append(((weighed - probs * delta) * SCALE).astype(BF16))
        grad_scores = jnp.concatenate(scores, axis=0)
        grad_queries = dot(grad_scores, keys, NN).astype(BF16)
        for h in range(GROUP):
            cols = slice(j * GW + h * HEAD_DIM, j * GW + (h + 1) * HEAD_DIM)
            grad_ref[:, cols] = grad_queries[h * TILE : (h + 1) * TILE]
        cols = slice(QW + j * HEAD_DIM, QW + (j + 1) * HEAD_DIM)
        grad_ref[:, cols] = dot(grad_scores, queries, TN).astype(BF16)
        cols = slice(QW + KW + j * HEAD_DIM, QW + KW + (j + 1) * HEAD_DIM)
        grad_ref[:, cols] = dot(probs_low, grads, TN).astype(BF16)
    low = low.astype(BF16)
    for c in range(0, QW, 512):
        cols = slice(c, c + 512)
        one = dot(attn_ref[:, cols], back, TN)
        two = dot(scaled_ref[:, cols], low, TN)
        terms_ref[cols, :] = jnp.concatenate([one, two], axis=1).astype(terms_ref.dtype)


SMEM = pl.BlockSpec(memory_space=pltpu.SMEM)
VMEM = pl.BlockSpec(memory_space=pltpu.VMEM)


def run_forward(rank, lengths, languages, table, qkv, down, up):
    return pl.pallas_call(
        forward_kernel,
        out_shape=jax.ShapeDtypeStruct((TILE, QW), BF16),
        in_specs=[SMEM] * 4 + [VMEM] * 3,
        out_specs=VMEM,
        scratch_shapes=[pltpu.VMEM((GROUP * TILE, TILE), F32)],
        compiler_params=pltpu.CompilerParams(vmem_limit_bytes=24 * 2**20),
        name="forward_tile",
    )(rank, lengths, languages, table, qkv, down, up)


def run_backward(rank, lengths, languages, dest, table, qkv, left, mid, right, down, up):
    return pl.pallas_call(
        backward_kernel,
        out_shape=(
            jax.ShapeDtypeStruct((TILE, QW + 2 * KW), BF16),
            jax.ShapeDtypeStruct((QW, 2 * RANK), BF16),
        ),
        in_specs=[SMEM] * 5 + [VMEM] * 6,
        out_specs=(VMEM, VMEM),
        scratch_shapes=[
            pltpu.VMEM((GROUP * TILE, TILE), F32),
            pltpu.VMEM((TILE, QW), BF16),
            pltpu.VMEM((TILE, QW), BF16),
            pltpu.VMEM((TILE, QW), BF16),
        ],
        compiler_params=pltpu.CompilerParams(vmem_limit_bytes=40 * 2**20),
        name="backward_tile",
    )(rank, lengths, languages, dest, table, qkv, left, mid, right, down, up)


def shift_dp(x, step):
    size = lax.axis_size("dp")
    return lax.ppermute(x, "dp", [(t, t + step) for t in range(size) if 0 <= t + step < size])


def shift_section(x, step):
    size = lax.axis_size("section")
    return lax.ppermute(
        x, "section", [(s, s + step) for s in range(size) if 0 <= s + step < size]
    )


def exchange(x, stride, count):
    size = lax.axis_size("dp")
    place = (lax.axis_index("dp") // stride) % count
    total = lax.dynamic_index_in_dim(x, place, 0, keepdims=False).astype(F32)
    for step in range(1, count):
        piece = lax.dynamic_index_in_dim(x, (place + step) % count, 0, keepdims=False)
        route = []
        for t in range(size):
            at = (t // stride) % count
            route.append((t, t + ((at + step) % count - at) * stride))
        total = total + lax.ppermute(piece, "dp", route).astype(F32)
    return total


def shards(
    qkv_a, qkv_b, slot_grad_b, adapter_down, adapter_up, lang_scale, languages, lengths, destination
):
    rank = lax.axis_index("dp")
    rank_word = jnp.reshape(rank.astype(jnp.int32), (1,))
    down, up = adapter_down[0], adapter_up[0]
    slots = slot_grad_b[0]
    from_left = shift_dp(slots[2 * TILE :], 1)
    from_right = shift_dp(slots[:TILE], -1)
    out = run_forward(rank_word, lengths, languages, lang_scale, qkv_a[0], down, up)
    hop = shift_section(out, 1)
    to_right = shift_dp(hop, 1)
    to_left = shift_dp(hop, -1)
    dest = destination[0]
    size = lax.axis_size("dp")
    zero = jnp.zeros((), BF16)
    slot0 = jnp.where(dest[jnp.maximum(rank - 1, 0)] == rank, to_right, zero)
    slot1 = jnp.where(dest[rank] == rank, hop, zero)
    slot2 = jnp.where(dest[jnp.minimum(rank + 1, size - 1)] == rank, to_left, zero)
    first, last = rank == 0, rank == size - 1
    slot0 = jnp.where(first, zero, slot0)
    slot2 = jnp.where(last, zero, slot2)
    handed_forward = jnp.concatenate([slot0, slot1, slot2], axis=0)[None]
    grad_qkv, terms = run_backward(
        rank_word, lengths, languages, destination, lang_scale, qkv_b[0],
        from_left, slots[TILE : 2 * TILE], from_right, down, up,
    )
    handed_back = shift_section(grad_qkv, -1)[None]
    terms = exchange(terms.reshape(4, 1024, 128), 16, 4).astype(BF16)
    terms = exchange(terms.reshape(4, 256, 128), 4, 4).astype(BF16)
    terms = exchange(terms.reshape(4, 64, 128), 1, 4)
    return (handed_forward, handed_back, terms[None])


def solution(mesh):
    return jax.shard_map(
        shards,
        mesh=mesh,
        in_specs=(
            P("section", "dp", None),
            P("section", "dp", None),
            P("section", "dp", None),
            P("section", None, None),
            P("section", None, None),
            P(),
            P(),
            P(),
            P(),
        ),
        out_specs=(P("section", "dp", None), P("section", "dp", None), P("section", "dp", None)),
        check_vma=False,
    )
```

time: 654 us -> 192 us (0.29)
  the two profiles are of different devices: /device:TPU:0 before, /device:TPU:34 now
where the time goes in v1:
time: 192 us
  waiting for transfers between devices  130 us (68%)
  starting transfers between devices  31.3 us (16%)
  Pallas kernels  13.4 us (7%)
  local copies, waits for them, and re-layouts  9.91 us (5%)
  other arithmetic  3.83 us (2%)
  between operations  2.86 us (1%)
    ppermute x4, waiting for transfers between devices, shift_dp(): lax.ppermute(x, 'dp', [(t, t + step) for t in range(size) if 0 <= t + ste...  69.9 us
    ppermute x9, waiting for transfers between devices, exchange(): total = total + lax.ppermute(piece, 'dp', route).astype(F32)  60.6 us
    ppermute x9, starting transfers between devices, exchange(): total = total + lax.ppermute(piece, 'dp', route).astype(F32)  14.8 us
    ppermute x4, starting transfers between devices, shift_dp(): lax.ppermute(x, 'dp', [(t, t + step) for t in range(size) if 0 <= t + ste...  12.8 us
    pallas_call x1, Pallas kernels, run_backward(): pl.pallas_call(backward_kernel, out_shape=(jax.ShapeDtypeStruct((TILE, QW...  7.82 us
    pallas_call x1, Pallas kernels, run_forward(): pl.pallas_call(forward_kernel, out_shape=jax.ShapeDtypeStruct((TILE, QW),...  5.61 us
    unnamed x23, local copies, waits for them, and re-layouts  5.59 us
  transfers between devices with their start and end apart: 15, of which 6 were waited for; matrix products, arithmetic and copies ran while one was open for 3% of the time, Pallas kernels for 7%

profile of v1, /device:TPU:34, one launch (start us, length us, event | category | flops | bytes accessed | tf_op | source)
XLA Modules:
  0.0 191.8 jit_solution(11186248085503550342)
XLA Ops:
  0.7 3.6 %slice_bitcast_fusion = (bf16[128,4096]{1,0:T(8,128)(2,1)}, bf16[128,4096]{1,0:T(8,128)(2,1)}, bf16[128,4096]{1,0:T(8,128)(2,1)S(1)}) fusion(bf16[1,384,4096]{2,1,0:T(8,128)(2,1)} %param.11), kind=kLoop, calls=%fused_computation.1 | loop fusion | bytes 6291456 | tf_op jit(solution)/shard_map/slice | solution.py:222
  4.2 3.9 %collective-permute-start.3 = (bf16[128,4096]{1,0:T(8,128)(2,1)}, bf16[128,4096]{1,0:T(8,128)(2,1)}, u32[]{:S(2)}, u32[]{:S(2)}) collective-permute-start(bf16[128,4096]{1,0:T(8,128)(2,1)} %get-tuple-element.8), channel_id=1, source_target_pairs={{0,1},{1,2},{2,3},{3,4},{4,5},{5,6},{6,7},{7,8},{8,9},{9,10},{10,1... | collective-permute-start | bytes 3145736 | tf_op jit(solution)/shard_map/ppermute | solution.py:190
  8.2 2.0 %collective-permute-start.4 = (bf16[128,4096]{1,0:T(8,128)(2,1)}, bf16[128,4096]{1,0:T(8,128)(2,1)}, u32[]{:S(2)}, u32[]{:S(2)}) collective-permute-start(bf16[128,4096]{1,0:T(8,128)(2,1)} %get-tuple-element.7), channel_id=1, source_target_pairs={{1,0},{2,1},{3,2},{4,3},{5,4},{6,5},{7,6},{8,7},{9,8},{10,9},{11,1... | collective-permute-start | bytes 3145736 | tf_op jit(solution)/shard_map/ppermute | solution.py:190
  10.2 0.5 copy.12
  10.7 0.1 copy.13.lens_ref
  10.9 0.0 copy-start.1
  10.9 1.3 copy-done.1
  12.2 5.6 %forward_tile.1 = bf16[128,4096]{1,0:T(8,128)(2,1)} custom-call(s32[1]{0:T(128)} %bitcast.1.rank_ref, s32[2,64,8]{2,1,0:T(8,128)S(1)} %copy.13.lens_ref, s32[2,64]{1,0:T(2,128)S(1)} %copy-done.4, f32[102]{0:T(128)S(1)} %copy-done.5, bf16[128,5120]{1,0:T(8,128)(2,1)S(1)} %bitcast.53, bf16[4096,64]{1,0:T(8,128)(2,1)S(1)} %bitcast.49, bf16[64,4096]{1,0:T(8,128)(2,1)S(1)} %bitcast.51), custom_call_target="tpu_custom_call" | custom-call | tf_op jit(solution)/shard_map/forward_tile/pallas_call | solution.py:157
  17.8 2.3 %collective-permute-start = (bf16[128,4096]{1,0:T(8,128)(2,1)}, bf16[128,4096]{1,0:T(8,128)(2,1)}, u32[]{:S(2)}, u32[]{:S(2)}) collective-permute-start(bf16[128,4096]{1,0:T(8,128)(2,1)} %forward_tile.1), channel_id=1, source_target_pairs={{0,64},{64,128},{128,192},{1,65},{65,129},{129,193},{2,66},{66,130... | collective-permute-start | bytes 3145736 | tf_op jit(solution)/shard_map/ppermute | solution.py:195
  20.1 44.5 %collective-permute-done.3.left_ref = bf16[128,4096]{1,0:T(8,128)(2,1)} collective-permute-done((bf16[128,4096]{1,0:T(8,128)(2,1)}, bf16[128,4096]{1,0:T(8,128)(2,1)}, u32[]{:S(2)}, u32[]{:S(2)}) %collective-permute-start.3) | collective-permute-done | bytes 1048608 | tf_op jit(solution)/shard_map/ppermute | solution.py:190
  64.7 0.0 collective-permute-done.4.right_ref
  64.7 1.3 copy-done.2
  66.0 7.8 %backward_tile.1 = (bf16[128,5120]{1,0:T(8,128)(2,1)S(1)}, bf16[4096,128]{1,0:T(8,128)(2,1)S(1)}) custom-call(s32[1]{0:T(128)} %bitcast.1.rank_ref, s32[2,64,8]{2,1,0:T(8,128)S(1)} %copy.13.lens_ref, s32[2,64]{1,0:T(2,128)S(1)} %copy-done.4, s32[2,64]{1,0:T(2,128)S(1)} %copy-done.6, f32[102]{0:T(128)S(1)} %copy-done.5, bf16[128,5120]{1,0:T(8,128)(2,1)S(1)} %bitcast.54, ...), custom_call_target="tpu_custom_call" | custom-call | tf_op jit(solution)/shard_map/backward_tile/pallas_call | solution.py:169
  73.8 0.0 copy-start.7
  73.8 0.0 slice-start
  73.8 0.9 copy-done.3
  74.8 0.1 dynamic-slice_bitcast_fusion.2
  74.8 0.4 copy-done.7
  75.2 1.5 collective-permute-start.6
  76.7 0.6 collective-permute-start.7
  77.3 2.6 %collective-permute-start.8 = (bf16[1024,128]{1,0:T(8,128)(2,1)S(1)}, bf16[1024,128]{1,0:T(8,128)(2,1)S(1)}, u32[]{:S(2)}, u32[]{:S(2)}) collective-permute-start(bf16[1024,128]{1,0:T(8,128)(2,1)S(1)} %get-tuple-element.11), channel_id=1, source_target_pairs={{0,48},{1,49},{2,50},{3,51},{4,52},{5,53},{6,54},{7,55},{8,56},{9,... | collective-permute-start | bytes 786440 | tf_op jit(solution)/shard_map/ppermute | solution.py:210
  80.0 1.6 collective-permute-done.6
  81.6 3.1 %collective-permute-done.7 = bf16[1024,128]{1,0:T(8,128)(2,1)S(1)} collective-permute-done((bf16[1024,128]{1,0:T(8,128)(2,1)S(1)}, bf16[1024,128]{1,0:T(8,128)(2,1)S(1)}, u32[]{:S(2)}, u32[]{:S(2)}) %collective-permute-start.7) | collective-permute-done | bytes 262176 | tf_op jit(solution)/shard_map/ppermute | solution.py:210
  84.7 1.8 collective-permute-done.8
  86.5 1.1 fusion.2
  87.7 3.9 %collective-permute-start.10 = (bf16[256,128]{1,0:T(8,128)(2,1)S(1)}, bf16[256,128]{1,0:T(8,128)(2,1)S(1)}, u32[]{:S(2)}, u32[]{:S(2)}) collective-permute-start(bf16[256,128]{1,0:T(8,128)(2,1)S(1)} %get-tuple-element.15), channel_id=1, source_target_pairs={{0,8},{1,9},{2,10},{3,11},{4,12},{5,13},{6,14},{7,15},{8,0},{9,1},... | collective-permute-start | bytes 196616 | tf_op jit(solution)/shard_map/ppermute | solution.py:210
  91.6 1.1 collective-permute-start.11
  92.7 1.0 collective-permute-start.9
  93.6 0.7 constant_dynamic-slice_fusion.2
  96.2 1.3 collective-permute-start.5
  97.5 0.0 collective-permute-done
  97.5 4.9 %collective-permute-start.1 = (bf16[128,4096]{1,0:T(8,128)(2,1)}, bf16[128,4096]{1,0:T(8,128)(2,1)S(1)}, u32[]{:S(2)}, u32[]{:S(2)}) collective-permute-start(bf16[128,4096]{1,0:T(8,128)(2,1)} %collective-permute-done), channel_id=1, source_target_pairs={{0,1},{1,2},{2,3},{3,4},{4,5},{5,6},{6,7},{7,8},{8,9},{9,10},{10,1... | collective-permute-start | bytes 3145736 | tf_op jit(solution)/shard_map/ppermute | solution.py:190
  102.5 0.0 collective-permute-done.10
  102.5 0.0 collective-permute-done.11
  102.5 0.0 collective-permute-done.9
  102.6 2.6 %collective-permute-start.12 = (bf16[64,128]{1,0:T(8,128)(2,1)S(1)}, bf16[64,128]{1,0:T(8,128)(2,1)S(1)}, u32[]{:S(2)}, u32[]{:S(2)}) collective-permute-start(bf16[64,128]{1,0:T(8,128)(2,1)S(1)} %get-tuple-element.16), channel_id=1, source_target_pairs={{0,1},{1,2},{2,3},{3,0},{4,5},{5,6},{6,7},{7,4},{8,9},{9,10},{10,1... | collective-permute-start | bytes 49160 | tf_op jit(solution)/shard_map/ppermute | solution.py:210
  105.2 0.0 collective-permute-start.13
  105.2 1.6 collective-permute-start.14
  106.7 0.1 broadcast_select_fusion
  106.8 54.0 %collective-permute-done.12 = bf16[64,128]{1,0:T(8,128)(2,1)S(1)} collective-permute-done((bf16[64,128]{1,0:T(8,128)(2,1)S(1)}, bf16[64,128]{1,0:T(8,128)(2,1)S(1)}, u32[]{:S(2)}, u32[]{:S(2)}) %collective-permute-start.12) | collective-permute-done | bytes 16416 | tf_op jit(solution)/shard_map/ppermute | solution.py:210
  160.8 1.9 collective-permute-start.2
  162.7 0.0 collective-permute-done.13
  162.7 0.6 fusion.8
  163.4 0.1 select_select_fusion.1
  163.5 25.4 %collective-permute-done.2 = bf16[128,4096]{1,0:T(8,128)(2,1)S(1)} collective-permute-done((bf16[128,4096]{1,0:T(8,128)(2,1)}, bf16[128,4096]{1,0:T(8,128)(2,1)S(1)}, u32[]{:S(2)}, u32[]{:S(2)}) %collective-permute-start.2) | collective-permute-done | bytes 1048608 | tf_op jit(solution)/shard_map/ppermute | solution.py:190
  188.8 0.1 select_select_fusion
  188.9 1.8 maximum_bitcast_fusion
  190.7 1.1 copy.16
  (21 shorter events, 0.1 us)
Async XLA Ops:
  0.6 9.6 %copy-start.8 = (bf16[1,4096,64]{1,2,0:T(8,128)(2,1)S(1)}, bf16[1,4096,64]{1,2,0:T(8,128)(2,1)}, u32[]{:S(2)}) copy-start(bf16[1,4096,64]{1,2,0:T(8,128)(2,1)} %param.12) | copy-start | bytes 1572868
  0.6 10.1 %copy-start.9 = (s32[2,64,8]{1,2,0:T(8,128)S(1)}, s32[2,64,8]{1,2,0:T(8,128)}, u32[]{:S(2)}) copy-start(s32[2,64,8]{1,2,0:T(8,128)} %param.16) | copy-start | bytes 12292
  0.7 10.2 %copy-start = (bf16[1,64,4096]{2,1,0:T(8,128)(2,1)S(1)}, bf16[1,64,4096]{2,1,0:T(8,128)(2,1)}, u32[]{:S(2)}) copy-start(bf16[1,64,4096]{2,1,0:T(8,128)(2,1)} %param.13) | copy-start | bytes 1572868
  0.7 10.2 %copy-start.5 = (f32[102]{0:T(128)S(1)}, f32[102]{0:T(128)}, u32[]{:S(2)}) copy-start(f32[102]{0:T(128)} %table_ref.3) | copy-start | bytes 1228
  0.7 10.2 %copy-start.4 = (s32[2,64]{1,0:T(2,128)S(1)}, s32[2,64]{1,0:T(2,128)}, u32[]{:S(2)}) copy-start(s32[2,64]{1,0:T(2,128)} %langs_ref.3) | copy-start | bytes 1540
  4.2 60.4 %copy-start.6 = (s32[2,64]{1,0:T(2,128)S(1)}, s32[2,64]{1,0:T(2,128)}, u32[]{:S(2)}) copy-start(s32[2,64]{1,0:T(2,128)} %dest_ref.1) | copy-start | bytes 1540
  4.2 60.4 %collective-permute-start.3 = (bf16[128,4096]{1,0:T(8,128)(2,1)}, bf16[128,4096]{1,0:T(8,128)(2,1)}, u32[]{:S(2)}, u32[]{:S(2)}) collective-permute-start(bf16[128,4096]{1,0:T(8,128)(2,1)} %get-tuple-element.8), channel_id=1, source_target_pairs={{0,1},{1,2},{2,3},{3,4},{4,5},{5,6},{6,7},{7,8},{8,9},{9,10},{10,1... | collective-permute-start | bytes 3145736 | tf_op jit(solution)/shard_map/ppermute | solution.py:190
  8.2 56.5 %collective-permute-start.4 = (bf16[128,4096]{1,0:T(8,128)(2,1)}, bf16[128,4096]{1,0:T(8,128)(2,1)}, u32[]{:S(2)}, u32[]{:S(2)}) collective-permute-start(bf16[128,4096]{1,0:T(8,128)(2,1)} %get-tuple-element.7), channel_id=1, source_target_pairs={{1,0},{2,1},{3,2},{4,3},{5,4},{6,5},{7,6},{8,7},{9,8},{10,9},{11,1... | collective-permute-start | bytes 3145736 | tf_op jit(solution)/shard_map/ppermute | solution.py:190
  10.9 1.3 copy-start.1
  17.8 79.7 %collective-permute-start = (bf16[128,4096]{1,0:T(8,128)(2,1)}, bf16[128,4096]{1,0:T(8,128)(2,1)}, u32[]{:S(2)}, u32[]{:S(2)}) collective-permute-start(bf16[128,4096]{1,0:T(8,128)(2,1)} %forward_tile.1), channel_id=1, source_target_pairs={{0,64},{64,128},{128,192},{1,65},{65,129},{129,193},{2,66},{66,130... | collective-permute-start | bytes 3145736 | tf_op jit(solution)/shard_map/ppermute | solution.py:195
  64.7 1.3 copy-start.2
  73.8 1.0 copy-start.3
  73.8 1.4 copy-start.7
  73.8 19.8 %slice-start = ((s32[2,64]{1,0:T(2,128)}), s32[1,64]{1,0:T(1,128)S(1)}, s32[]{:S(2)}) async-start(s32[2,64]{1,0:T(2,128)} %dest_ref.1), calls=%async_computation | async-start | bytes 1024 | tf_op jit(solution)/shard_map/slice | solution.py:227
  75.2 6.4 %collective-permute-start.6 = (bf16[1024,128]{1,0:T(8,128)(2,1)S(1)}, bf16[1024,128]{1,0:T(8,128)(2,1)S(1)}, u32[]{:S(2)}, u32[]{:S(2)}) collective-permute-start(bf16[1024,128]{1,0:T(8,128)(2,1)S(1)} %get-tuple-element.10), channel_id=1, source_target_pairs={{0,16},{1,17},{2,18},{3,19},{4,20},{5,21},{6,22},{7,23},{8,24},{9,... | collective-permute-start | bytes 786440 | tf_op jit(solution)/shard_map/ppermute | solution.py:210
  76.7 8.0 %collective-permute-start.7 = (bf16[1024,128]{1,0:T(8,128)(2,1)S(1)}, bf16[1024,128]{1,0:T(8,128)(2,1)S(1)}, u32[]{:S(2)}, u32[]{:S(2)}) collective-permute-start(bf16[1024,128]{1,0:T(8,128)(2,1)S(1)} %get-tuple-element.12), channel_id=1, source_target_pairs={{0,32},{1,33},{2,34},{3,35},{4,36},{5,37},{6,38},{7,39},{8,40},{9,... | collective-permute-start | bytes 786440 | tf_op jit(solution)/shard_map/ppermute | solution.py:210
  77.3 9.2 %collective-permute-start.8 = (bf16[1024,128]{1,0:T(8,128)(2,1)S(1)}, bf16[1024,128]{1,0:T(8,128)(2,1)S(1)}, u32[]{:S(2)}, u32[]{:S(2)}) collective-permute-start(bf16[1024,128]{1,0:T(8,128)(2,1)S(1)} %get-tuple-element.11), channel_id=1, source_target_pairs={{0,48},{1,49},{2,50},{3,51},{4,52},{5,53},{6,54},{7,55},{8,56},{9,... | collective-permute-start | bytes 786440 | tf_op jit(solution)/shard_map/ppermute | solution.py:210
  87.7 14.8 %collective-permute-start.10 = (bf16[256,128]{1,0:T(8,128)(2,1)S(1)}, bf16[256,128]{1,0:T(8,128)(2,1)S(1)}, u32[]{:S(2)}, u32[]{:S(2)}) collective-permute-start(bf16[256,128]{1,0:T(8,128)(2,1)S(1)} %get-tuple-element.15), channel_id=1, source_target_pairs={{0,8},{1,9},{2,10},{3,11},{4,12},{5,13},{6,14},{7,15},{8,0},{9,1},... | collective-permute-start | bytes 196616 | tf_op jit(solution)/shard_map/ppermute | solution.py:210
  91.6 10.9 %collective-permute-start.11 = (bf16[256,128]{1,0:T(8,128)(2,1)S(1)}, bf16[256,128]{1,0:T(8,128)(2,1)S(1)}, u32[]{:S(2)}, u32[]{:S(2)}) collective-permute-start(bf16[256,128]{1,0:T(8,128)(2,1)S(1)} %get-tuple-element.14), channel_id=1, source_target_pairs={{0,12},{1,13},{2,14},{3,15},{4,0},{5,1},{6,2},{7,3},{8,4},{9,5},{1... | collective-permute-start | bytes 196616 | tf_op jit(solution)/shard_map/ppermute | solution.py:210
  92.7 9.9 %collective-permute-start.9 = (bf16[256,128]{1,0:T(8,128)(2,1)S(1)}, bf16[256,128]{1,0:T(8,128)(2,1)S(1)}, u32[]{:S(2)}, u32[]{:S(2)}) collective-permute-start(bf16[256,128]{1,0:T(8,128)(2,1)S(1)} %get-tuple-element.13), channel_id=1, source_target_pairs={{0,4},{1,5},{2,6},{3,7},{4,8},{5,9},{6,10},{7,11},{8,12},{9,13},{1... | collective-permute-start | bytes 196616 | tf_op jit(solution)/shard_map/ppermute | solution.py:210
  96.2 94.5 %collective-permute-start.5 = (bf16[128,5120]{1,0:T(8,128)(2,1)}, bf16[128,5120]{1,0:T(8,128)(2,1)S(1)}, u32[]{:S(2)}, u32[]{:S(2)}) collective-permute-start(bf16[128,5120]{1,0:T(8,128)(2,1)} %copy-done.7), channel_id=1, source_target_pairs={{64,0},{128,64},{192,128},{65,1},{129,65},{193,129},{66,2},{130,66... | collective-permute-start | bytes 3932168 | tf_op jit(solution)/shard_map/ppermute | solution.py:195
  97.5 65.8 %collective-permute-start.1 = (bf16[128,4096]{1,0:T(8,128)(2,1)}, bf16[128,4096]{1,0:T(8,128)(2,1)S(1)}, u32[]{:S(2)}, u32[]{:S(2)}) collective-permute-start(bf16[128,4096]{1,0:T(8,128)(2,1)} %collective-permute-done), channel_id=1, source_target_pairs={{0,1},{1,2},{2,3},{3,4},{4,5},{5,6},{6,7},{7,8},{8,9},{9,10},{10,1... | collective-permute-start | bytes 3145736 | tf_op jit(solution)/shard_map/ppermute | solution.py:190
  102.6 58.2 %collective-permute-start.12 = (bf16[64,128]{1,0:T(8,128)(2,1)S(1)}, bf16[64,128]{1,0:T(8,128)(2,1)S(1)}, u32[]{:S(2)}, u32[]{:S(2)}) collective-permute-start(bf16[64,128]{1,0:T(8,128)(2,1)S(1)} %get-tuple-element.16), channel_id=1, source_target_pairs={{0,1},{1,2},{2,3},{3,0},{4,5},{5,6},{6,7},{7,4},{8,9},{9,10},{10,1... | collective-permute-start | bytes 49160 | tf_op jit(solution)/shard_map/ppermute | solution.py:210
  105.2 57.6 %collective-permute-start.13 = (bf16[64,128]{1,0:T(8,128)(2,1)S(1)}, bf16[64,128]{1,0:T(8,128)(2,1)S(1)}, u32[]{:S(2)}, u32[]{:S(2)}) collective-permute-start(bf16[64,128]{1,0:T(8,128)(2,1)S(1)} %get-tuple-element.18), channel_id=1, source_target_pairs={{0,2},{1,3},{2,0},{3,1},{4,6},{5,7},{6,4},{7,5},{8,10},{9,11},{10,... | collective-permute-start | bytes 49160 | tf_op jit(solution)/shard_map/ppermute | solution.py:210
  105.2 57.6 %collective-permute-start.14 = (bf16[64,128]{1,0:T(8,128)(2,1)S(1)}, bf16[64,128]{1,0:T(8,128)(2,1)S(1)}, u32[]{:S(2)}, u32[]{:S(2)}) collective-permute-start(bf16[64,128]{1,0:T(8,128)(2,1)S(1)} %get-tuple-element.17), channel_id=1, source_target_pairs={{0,3},{1,0},{2,1},{3,2},{4,7},{5,4},{6,5},{7,6},{8,11},{9,8},{10,9... | collective-permute-start | bytes 49160 | tf_op jit(solution)/shard_map/ppermute | solution.py:210
  160.8 28.0 %collective-permute-start.2 = (bf16[128,4096]{1,0:T(8,128)(2,1)}, bf16[128,4096]{1,0:T(8,128)(2,1)S(1)}, u32[]{:S(2)}, u32[]{:S(2)}) collective-permute-start(bf16[128,4096]{1,0:T(8,128)(2,1)} %collective-permute-done), channel_id=1, source_target_pairs={{1,0},{2,1},{3,2},{4,3},{5,4},{6,5},{7,6},{8,7},{9,8},{10,9},{11,1... | collective-permute-start | bytes 3145736 | tf_op jit(solution)/shard_map/ppermute | solution.py:190

commit v2 on v1

--- a/solution.py
+++ b/solution.py
@@ -94,44 +94,79 @@
         out_ref[:, c : c + 512] = (out_ref[:, c : c + 512].astype(F32) + rate * lift).astype(BF16)
 
 
-def backward_kernel(
-    rank_ref, lens_ref, langs_ref, dest_ref, table_ref, qkv_ref, left_ref, mid_ref, right_ref,
-    down_ref, up_ref, grad_ref, terms_ref, probs_ref, attn_ref, scaled_ref, gattn_ref,
+def prepare_kernel(
+    rank_ref, lens_ref, langs_ref, dest_ref, table_ref, qkv_ref, slots_ref, down_ref, up_ref,
+    probs_ref, attn_ref, scaled_ref, left_ref, own_ref, right_ref,
 ):
     rank = rank_ref[0]
-    rate = table_ref[langs_ref[1, rank]]
-    went = dest_ref[1, rank] - rank
+    tiles = lens_ref.shape[1]
     bias = mask_bias(lens_ref, 1, rank)
-    back = jnp.zeros((TILE, RANK), F32)
-    for c in range(0, QW, 512):
-        cols = slice(c, c + 512)
-        grad = jnp.where(
-            went < 0, left_ref[:, cols], jnp.where(went > 0, right_ref[:, cols], mid_ref[:, cols])
-        )
-        gattn_ref[:, cols] = grad
-        scaled = (rate * grad.astype(F32)).astype(BF16)
-        scaled_ref[:, cols] = scaled
-        back = back + dot(scaled, up_ref[:, cols], NT)
-    back = back.astype(BF16)
     low = jnp.zeros((TILE, RANK), F32)
     for j in range(KV):
         block = slice(j * GW, (j + 1) * GW)
-        gattn = gattn_ref[:, block].astype(F32) + dot(back, down_ref[block, :], NT)
-        gattn_ref[:, block] = gattn.astype(BF16)
-        queries, keys, values, probs_low, attn = attend_group(j, qkv_ref, bias, probs_ref)
+        attn = attend_group(j, qkv_ref, bias, probs_ref.at[block, :])[-1]
         for h in range(GROUP):
             cols = slice(j * GW + h * HEAD_DIM, j * GW + (h + 1) * HEAD_DIM)
             attn_ref[:, cols] = attn[h * TILE : (h + 1) * TILE]
         low = low + dot(attn_ref[:, block], down_ref[block, :], NN)
+    for k, out_ref in enumerate((left_ref, own_ref, right_ref)):
+        tile = rank + (k - 1)
+        near = jnp.clip(tile, 0, tiles - 1)
+        live = (tile == near) & (dest_ref[1, near] == rank)
+        rate = jnp.where(live, table_ref[langs_ref[1, near]], 0.0)
+        rows = slice(k * TILE, (k + 1) * TILE)
+        back = jnp.zeros((TILE, RANK), F32)
+        for c in range(0, QW, 512):
+            cols = slice(c, c + 512)
+            scaled = (rate * slots_ref[rows, cols].astype(F32)).astype(BF16)
+            scaled_ref[rows, cols] = scaled
+            back = back + dot(scaled, up_ref[:, cols], NT)
+        out_ref[...] = jnp.concatenate([low, back], axis=1).astype(BF16)
+
+
+def terms_kernel(
+    rank_ref, dest_ref, attn_ref, scaled_ref, left_ref, own_ref, right_ref, terms_ref, back_ref
+):
+    rank = rank_ref[0]
+    went = dest_ref[1, rank] - rank
+    back = jnp.where(went < 0, left_ref[...], jnp.where(went > 0, right_ref[...], own_ref[...]))
+    back_ref[...] = back
+    lows = jnp.concatenate([left_ref[...], own_ref[...], right_ref[...]], axis=0)
+    for c in range(0, QW, 512):
+        cols = slice(c, c + 512)
+        one = dot(attn_ref[:, cols], back, TN)
+        two = dot(scaled_ref[:, cols], lows, TN)
+        terms = jnp.concatenate([one[:, RANK:], two[:, :RANK]], axis=1)
+        terms_ref[cols, :] = terms.astype(terms_ref.dtype)
+
+
+def backward_kernel(
+    rank_ref, dest_ref, qkv_ref, left_ref, mid_ref, right_ref, back_ref, probs_ref, down_ref,
+    grad_ref, gattn_ref,
+):
+    rank = rank_ref[0]
+    went = dest_ref[1, rank] - rank
+    back = back_ref[...][:, RANK:]
+    for j in range(KV):
+        block = slice(j * GW, (j + 1) * GW)
+        grad = jnp.where(
+            went < 0, left_ref[:, block], jnp.where(went > 0, right_ref[:, block], mid_ref[:, block])
+        )
+        gattn = grad.astype(F32) + dot(back, down_ref[block, :], NT)
+        gattn_ref[:, block] = gattn.astype(BF16)
+        queries = stacked(qkv_ref, j * GW)
+        keys = qkv_ref[:, QW + j * HEAD_DIM : QW + (j + 1) * HEAD_DIM]
+        values = qkv_ref[:, QW + KW + j * HEAD_DIM : QW + KW + (j + 1) * HEAD_DIM]
         grads = stacked(gattn_ref, j * GW)
         grad_probs = dot(grads, values, NT)
-        scores = []
+        lows, scores = [], []
         for h in range(GROUP):
-            rows = slice(h * TILE, (h + 1) * TILE)
-            probs = probs_ref[rows, :]
-            weighed = probs * grad_probs[rows]
+            probs = probs_ref[j * GW + h * TILE : j * GW + (h + 1) * TILE, :]
+            lows.append(probs.astype(BF16))
+            weighed = probs * grad_probs[h * TILE : (h + 1) * TILE]
             delta = jnp.sum(weighed, axis=-1, keepdims=True)
             scores.append(((weighed - probs * delta) * SCALE).astype(BF16))
+        probs_low = jnp.concatenate(lows, axis=0)
         grad_scores = jnp.concatenate(scores, axis=0)
         grad_queries = dot(grad_scores, keys, NN).astype(BF16)
         for h in range(GROUP):
@@ -141,12 +176,6 @@
         grad_ref[:, cols] = dot(grad_scores, queries, TN).astype(BF16)
         cols = slice(QW + KW + j * HEAD_DIM, QW + KW + (j + 1) * HEAD_DIM)
         grad_ref[:, cols] = dot(probs_low, grads, TN).astype(BF16)
-    low = low.astype(BF16)
-    for c in range(0, QW, 512):
-        cols = slice(c, c + 512)
-        one = dot(attn_ref[:, cols], back, TN)
-        two = dot(scaled_ref[:, cols], low, TN)
-        terms_ref[cols, :] = jnp.concatenate([one, two], axis=1).astype(terms_ref.dtype)
 
 
 SMEM = pl.BlockSpec(memory_space=pltpu.SMEM)
@@ -165,36 +194,68 @@
     )(rank, lengths, languages, table, qkv, down, up)
 
 
-def run_backward(rank, lengths, languages, dest, table, qkv, left, mid, right, down, up):
+def run_prepare(rank, lengths, languages, dest, table, qkv, slots, down, up):
+    message = jax.ShapeDtypeStruct((TILE, 2 * RANK), BF16)
+    return pl.pallas_call(
+        prepare_kernel,
+        out_shape=(
+            jax.ShapeDtypeStruct((QW, TILE), F32),
+            jax.ShapeDtypeStruct((TILE, QW), BF16),
+            jax.ShapeDtypeStruct((3 * TILE, QW), BF16),
+            message,
+            message,
+            message,
+        ),
+        in_specs=[SMEM] * 5 + [VMEM] * 4,
+        out_specs=(VMEM,) * 6,
+        compiler_params=pltpu.CompilerParams(vmem_limit_bytes=40 * 2**20),
+        name="prepare_tile",
+    )(rank, lengths, languages, dest, table, qkv, slots, down, up)
+
+
+def run_terms(rank, dest, attn, scaled, left, own, right):
+    return pl.pallas_call(
+        terms_kernel,
+        out_shape=(
+            jax.ShapeDtypeStruct((QW, 2 * RANK), BF16),
+            jax.ShapeDtypeStruct((TILE, 2 * RANK), BF16),
+        ),
+        in_specs=[SMEM] * 2 + [VMEM] * 5,
+        out_specs=(VMEM, VMEM),
+        compiler_params=pltpu.CompilerParams(vmem_limit_bytes=24 * 2**20),
+        name="adapter_terms",
+    )(rank, dest, attn, scaled, left, own, right)
+
+
+def run_backward(rank, dest, qkv, left, mid, right, back, probs, down):
     return pl.pallas_call(
         backward_kernel,
-        out_shape=(
-            jax.ShapeDtypeStruct((TILE, QW + 2 * KW), BF16),
-            jax.ShapeDtypeStruct((QW, 2 * RANK), BF16),
-        ),
-        in_specs=[SMEM] * 5 + [VMEM] * 6,
-        out_specs=(VMEM, VMEM),
-        scratch_shapes=[
-            pltpu.VMEM((GROUP * TILE, TILE), F32),
-            pltpu.VMEM((TILE, QW), BF16),
-            pltpu.VMEM((TILE, QW), BF16),
-            pltpu.VMEM((TILE, QW), BF16),
-        ],
+        out_shape=jax.ShapeDtypeStruct((TILE, QW + 2 * KW), BF16),
+        in_specs=[SMEM] * 2 + [VMEM] * 7,
+        out_specs=VMEM,
+        scratch_shapes=[pltpu.VMEM((TILE, QW), BF16)],
         compiler_params=pltpu.CompilerParams(vmem_limit_bytes=40 * 2**20),
         name="backward_tile",
-    )(rank, lengths, languages, dest, table, qkv, left, mid, right, down, up)
-
-
-def shift_dp(x, step):
+    )(rank, dest, qkv, left, mid, right, back, probs, down)
+
+
+def sections():
+    return lax.axis_size("section")
+
+
+def shift(x, moves):
     size = lax.axis_size("dp")
-    return lax.ppermute(x, "dp", [(t, t + step) for t in range(size) if 0 <= t + step < size])
-
-
-def shift_section(x, step):
-    size = lax.axis_size("section")
-    return lax.ppermute(
-        x, "section", [(s, s + step) for s in range(size) if 0 <= s + step < size]
-    )
+    route = []
+    for s_list, up, step, keep in moves:
+        for s in s_list:
+            for t in range(size):
+                if 0 <= s + up < sections() and 0 <= t + step < size and keep(t):
+                    route.append((s * size + t, (s + up) * size + t + step))
+    return lax.ppermute(x, AXES, route)
+
+
+def anywhere(t):
+    return True
 
 
 def exchange(x, stride, count):
@@ -215,33 +276,41 @@
     qkv_a, qkv_b, slot_grad_b, adapter_down, adapter_up, lang_scale, languages, lengths, destination
 ):
     rank = lax.axis_index("dp")
+    size = lax.axis_size("dp")
     rank_word = jnp.reshape(rank.astype(jnp.int32), (1,))
     down, up = adapter_down[0], adapter_up[0]
     slots = slot_grad_b[0]
-    from_left = shift_dp(slots[2 * TILE :], 1)
-    from_right = shift_dp(slots[:TILE], -1)
+    every = range(sections())
+    later = range(1, sections())
+    from_left = shift(slots[2 * TILE :], [(later, 0, 1, anywhere)])
+    from_right = shift(slots[:TILE], [(later, 0, -1, anywhere)])
     out = run_forward(rank_word, lengths, languages, lang_scale, qkv_a[0], down, up)
-    hop = shift_section(out, 1)
-    to_right = shift_dp(hop, 1)
-    to_left = shift_dp(hop, -1)
-    dest = destination[0]
-    size = lax.axis_size("dp")
-    zero = jnp.zeros((), BF16)
-    slot0 = jnp.where(dest[jnp.maximum(rank - 1, 0)] == rank, to_right, zero)
-    slot1 = jnp.where(dest[rank] == rank, hop, zero)
-    slot2 = jnp.where(dest[jnp.minimum(rank + 1, size - 1)] == rank, to_left, zero)
-    first, last = rank == 0, rank == size - 1
-    slot0 = jnp.where(first, zero, slot0)
-    slot2 = jnp.where(last, zero, slot2)
-    handed_forward = jnp.concatenate([slot0, slot1, slot2], axis=0)[None]
-    grad_qkv, terms = run_backward(
-        rank_word, lengths, languages, destination, lang_scale, qkv_b[0],
-        from_left, slots[TILE : 2 * TILE], from_right, down, up,
-    )
-    handed_back = shift_section(grad_qkv, -1)[None]
+    hop = shift(out, [(every, 1, 0, anywhere)])
+    probs, attn, scaled, to_left, own, to_right = run_prepare(
+        rank_word, lengths, languages, destination, lang_scale, qkv_b[0], slots, down, up
+    )
+    left = shift(to_right, [(every, 0, 1, anywhere)])
+    right = shift(to_left, [(every, 0, -1, anywhere)])
+    terms, back = run_terms(rank_word, destination, attn, scaled, left, own, right)
     terms = exchange(terms.reshape(4, 1024, 128), 16, 4).astype(BF16)
     terms = exchange(terms.reshape(4, 256, 128), 4, 4).astype(BF16)
     terms = exchange(terms.reshape(4, 64, 128), 1, 4)
+    terms, back, hop = lax.optimization_barrier((terms, back, hop))
+    grad_qkv = run_backward(
+        rank_word, destination, qkv_b[0], from_left, slots[TILE : 2 * TILE], from_right, back,
+        probs, down,
+    )
+    handed_back = shift(grad_qkv, [(every, -1, 0, anywhere)])[None]
+    before = shift(hop, [(later, 0, 1, anywhere)])
+    after = shift(hop, [(later, 0, -1, anywhere)])
+    dest = destination[0]
+    zero = jnp.zeros((), BF16)
+    slot0 = jnp.where((dest[jnp.maximum(rank - 1, 0)] == rank) & (rank > 0), before, zero)
+    slot1 = jnp.where(dest[rank] == rank, hop, zero)
+    slot2 = jnp.where(
+        (dest[jnp.minimum(rank + 1, size - 1)] == rank) & (rank < size - 1), after, zero
+    )
+    handed_forward = jnp.concatenate([slot0, slot1, slot2], axis=0)[None]
     return (handed_forward, handed_back, terms[None])
 
 

time: 192 us -> 199 us (1.036)
  the two profiles are of different devices: /device:TPU:34 before, /device:TPU:33 now
where the time goes in v2:
time: 199 us; the launch traced here: 198 us
  waiting for transfers between devices  96.2 us (48%)
  starting transfers between devices  49.9 us (25%)
  local copies, waits for them, and re-layouts  23 us (12%)
  Pallas kernels  18.6 us (9%)
  other arithmetic  7.01 us (4%)
  between operations  3.13 us (2%)
    ppermute x8, waiting for transfers between devices, shift(): return lax.ppermute(x, AXES, route)  83.5 us
    ppermute x8, starting transfers between devices, shift(): return lax.ppermute(x, AXES, route)  32.2 us
    unnamed x39, local copies, waits for them, and re-layouts  18.3 us
    ppermute x9, starting transfers between devices, exchange(): total = total + lax.ppermute(piece, 'dp', route).astype(F32)  17.7 us
    ppermute x9, waiting for transfers between devices, exchange(): total = total + lax.ppermute(piece, 'dp', route).astype(F32)  12.7 us
    pallas_call x1, Pallas kernels, run_prepare(): pl.pallas_call(prepare_kernel, out_shape=(jax.ShapeDtypeStruct((QW, TILE)...  6.03 us
    pallas_call x1, Pallas kernels, run_forward(): pl.pallas_call(forward_kernel, out_shape=jax.ShapeDtypeStruct((TILE, QW),...  5.61 us
    pallas_call x1, Pallas kernels, run_backward(): pl.pallas_call(backward_kernel, out_shape=jax.ShapeDtypeStruct((TILE, QW...  4.46 us
  transfers between devices with their start and end apart: 17, of which 6 were waited for; matrix products, arithmetic and copies ran while one was open for 6% of the time, Pallas kernels for 6%

profile of v2, /device:TPU:33, one launch (start us, length us, event | category | flops | bytes accessed | tf_op | source)
XLA Modules:
  0.0 197.8 jit_solution(243075533302567332)
XLA Ops:
  0.6 1.6 copy.12
  2.3 0.8 copy.13.lens_ref
  3.1 1.9 copy-done
  5.0 1.3 copy-done.2
  6.3 1.0 copy-done.8
  7.3 0.7 copy-done.11
  8.0 0.7 copy-done.13
  8.7 0.7 copy-done.14
  9.3 6.0 %prepare_tile.1 = (f32[4096,128]{1,0:T(8,128)S(1)}, bf16[128,4096]{1,0:T(8,128)(2,1)S(1)}, bf16[384,4096]{1,0:T(8,128)(2,1)S(1)}, bf16[128,128]{1,0:T(8,128)(2,1...) custom-call(s32[1]{0:T(128)} %bitcast.1.rank_ref, s32[2,64,8]{2,1,0:T(8,128)S(1)} %copy.13.lens_ref, ...), custom_call_target="tpu_custom_call" | custom-call | tf_op jit(solution)/shard_map/prepare_tile/pallas_call | solution.py:199
  15.4 1.7 copy-done.4
  17.0 1.4 copy-done.6
  18.4 3.7 %collective-permute-start = (bf16[128,128]{1,0:T(8,128)(2,1)}, bf16[128,128]{1,0:T(8,128)(2,1)S(1)}, u32[]{:S(2)}, u32[]{:S(2)}) collective-permute-start(bf16[128,128]{1,0:T(8,128)(2,1)} %get-tuple-element.16), channel_id=1, source_target_pairs={{0,1},{1,2},{2,3},{3,4},{4,5},{5,6},{6,7},{7,8},{8,9},{9,10},{10,1... | collective-permute-start | bytes 98312 | tf_op jit(solution)/shard_map/ppermute | solution.py:254
  22.1 1.9 collective-permute-start.1
  24.0 5.6 %forward_tile.1 = bf16[128,4096]{1,0:T(8,128)(2,1)} custom-call(s32[1]{0:T(128)} %bitcast.1.rank_ref, s32[2,64,8]{2,1,0:T(8,128)S(1)} %copy.13.lens_ref, s32[2,64]{1,0:T(2,128)S(1)} %copy-done.13, f32[102]{0:T(128)S(1)} %copy-done.14, bf16[128,5120]{1,0:T(8,128)(2,1)S(1)} %bitcast.57, bf16[4096,64]{1,0:T(8,128)(2,1)S(1)} %bitcast.50, ...), custom_call_target="tpu_custom_call" | custom-call | tf_op jit(solution)/shard_map/forward_tile/pallas_call | solution.py:186
  29.6 8.8 %collective-permute-start.11 = (bf16[128,4096]{1,0:T(8,128)(2,1)}, bf16[128,4096]{1,0:T(8,128)(2,1)}, u32[]{:S(2)}, u32[]{:S(2)}) collective-permute-start(bf16[128,4096]{1,0:T(8,128)(2,1)} %forward_tile.1), channel_id=1, source_target_pairs={{0,64},{1,65},{2,66},{3,67},{4,68},{5,69},{6,70},{7,71},{8,72},{9,... | collective-permute-start | bytes 3145736 | tf_op jit(solution)/shard_map/ppermute | solution.py:254
  38.6 2.0 %copy-done.5 = bf16[384,4096]{1,0:T(8,128)(2,1)S(1)} copy-done((bf16[384,4096]{1,0:T(8,128)(2,1)S(1)}, bf16[384,4096]{1,0:T(8,128)(2,1)}, u32[]{:S(2)}) %copy-start.5) | copy-done | bytes 3145752
  40.6 2.5 %adapter_terms.1 = (bf16[4096,128]{1,0:T(8,128)(2,1)S(1)}, bf16[128,128]{1,0:T(8,128)(2,1)S(1)}) custom-call(s32[1]{0:T(128)} %bitcast.1.rank_ref, s32[2,64]{1,0:T(2,128)S(1)} %copy-done.12, bf16[128,4096]{1,0:T(8,128)(2,1)S(1)} %get-tuple-element.14.attn_ref, bf16[384,4096]{1,0:T(8,128)(2,1)S(1)} %copy-done.5, ...), custom_call_target="tpu_custom_call" | custom-call | tf_op jit(solution)/shard_map/adapter_terms/pallas_call | solution.py:217
  43.1 1.1 dynamic-slice_bitcast_fusion.2
  44.2 1.2 collective-permute-start.2
  45.4 2.5 %collective-permute-start.3 = (bf16[1024,128]{1,0:T(8,128)(2,1)}, bf16[1024,128]{1,0:T(8,128)(2,1)}, u32[]{:S(2)}, u32[]{:S(2)}) collective-permute-start(bf16[1024,128]{1,0:T(8,128)(2,1)} %get-tuple-element.30), channel_id=1, source_target_pairs={{0,32},{1,33},{2,34},{3,35},{4,36},{5,37},{6,38},{7,39},{8,40},{9,... | collective-permute-start | bytes 786440 | tf_op jit(solution)/shard_map/ppermute | solution.py:271
  47.9 1.2 collective-permute-start.4
  49.0 1.7 slice_bitcast_fusion
  50.7 2.6 %collective-permute-start.14 = (bf16[128,4096]{1,0:T(8,128)(2,1)}, bf16[128,4096]{1,0:T(8,128)(2,1)}, u32[]{:S(2)}, u32[]{:S(2)}) collective-permute-start(bf16[128,4096]{1,0:T(8,128)(2,1)} %get-tuple-element.26), channel_id=1, source_target_pairs={{64,65},{65,66},{66,67},{67,68},{68,69},{69,70},{70,71},{71,72},{7... | collective-permute-start | bytes 3145736 | tf_op jit(solution)/shard_map/ppermute | solution.py:254
  53.5 7.0 %collective-permute-start.15 = (bf16[128,4096]{1,0:T(8,128)(2,1)}, bf16[128,4096]{1,0:T(8,128)(2,1)}, u32[]{:S(2)}, u32[]{:S(2)}) collective-permute-start(bf16[128,4096]{1,0:T(8,128)(2,1)} %get-tuple-element.25), channel_id=1, source_target_pairs={{65,64},{66,65},{67,66},{68,67},{69,68},{70,69},{71,70},{72,71},{7... | collective-permute-start | bytes 3145736 | tf_op jit(solution)/shard_map/ppermute | solution.py:254
  60.5 1.3 fusion.2
  61.8 0.7 copy-done.15
  62.5 0.7 dynamic-slice_bitcast_fusion.5
  63.2 1.5 collective-permute-start.6
  64.7 3.5 %collective-permute-done.5 = bf16[256,128]{1,0:T(8,128)(2,1)S(1)} collective-permute-done((bf16[256,128]{1,0:T(8,128)(2,1)S(1)}, bf16[256,128]{1,0:T(8,128)(2,1)S(1)}, u32[]{:S(2)}, u32[]{:S(2)}) %collective-permute-start.5) | collective-permute-done | bytes 65568 | tf_op jit(solution)/shard_map/ppermute | solution.py:271
  68.8 2.8 %collective-permute-done.7 = bf16[256,128]{1,0:T(8,128)(2,1)} collective-permute-done((bf16[256,128]{1,0:T(8,128)(2,1)}, bf16[256,128]{1,0:T(8,128)(2,1)}, u32[]{:S(2)}, u32[]{:S(2)}) %collective-permute-start.7) | collective-permute-done | bytes 65568 | tf_op jit(solution)/shard_map/ppermute | solution.py:271
  71.6 1.0 fusion.5
  72.6 0.6 dynamic-slice_bitcast_fusion.8
  73.2 6.4 %collective-permute-start.10 = (bf16[64,128]{1,0:T(8,128)(2,1)S(1)}, bf16[64,128]{1,0:T(8,128)(2,1)S(1)}, u32[]{:S(2)}, u32[]{:S(2)}) collective-permute-start(bf16[64,128]{1,0:T(8,128)(2,1)S(1)} %get-tuple-element.35), channel_id=1, source_target_pairs={{0,3},{1,0},{2,1},{3,2},{4,7},{5,4},{6,5},{7,6},{8,11},{9,8},{10,9... | collective-permute-start | bytes 49160 | tf_op jit(solution)/shard_map/ppermute | solution.py:271
  79.7 5.2 %collective-permute-done.10 = bf16[64,128]{1,0:T(8,128)(2,1)S(1)} collective-permute-done((bf16[64,128]{1,0:T(8,128)(2,1)S(1)}, bf16[64,128]{1,0:T(8,128)(2,1)S(1)}, u32[]{:S(2)}, u32[]{:S(2)}) %collective-permute-start.10) | collective-permute-done | bytes 16416 | tf_op jit(solution)/shard_map/ppermute | solution.py:271
  85.4 4.9 %collective-permute-start.9 = (bf16[64,128]{1,0:T(8,128)(2,1)S(1)}, bf16[64,128]{1,0:T(8,128)(2,1)}, u32[]{:S(2)}, u32[]{:S(2)}) collective-permute-start(bf16[64,128]{1,0:T(8,128)(2,1)S(1)} %get-tuple-element.36), channel_id=1, source_target_pairs={{0,2},{1,3},{2,0},{3,1},{4,6},{5,7},{6,4},{7,5},{8,10},{9,11},{10,... | collective-permute-start | bytes 49160 | tf_op jit(solution)/shard_map/ppermute | solution.py:271
  90.3 1.2 collective-permute-done.9
  91.5 1.4 fusion.7
  92.9 1.9 collective-permute-start.12
  94.9 0.7 constant_dynamic-slice_fusion.2
  97.6 4.3 %collective-permute-start.13 = (bf16[128,4096]{1,0:T(8,128)(2,1)}, bf16[128,4096]{1,0:T(8,128)(2,1)S(1)}, u32[]{:S(2)}, u32[]{:S(2)}) collective-permute-start(bf16[128,4096]{1,0:T(8,128)(2,1)} %collective-permute-done.11), channel_id=1, source_target_pairs={{65,64},{66,65},{67,66},{68,67},{69,68},{70,69},{71,70},{72,71},{7... | collective-permute-start | bytes 3145736 | tf_op jit(solution)/shard_map/ppermute | solution.py:254
  101.9 1.6 copy-done.7
  103.5 4.5 %backward_tile.1 = bf16[128,5120]{1,0:T(8,128)(2,1)S(1)} custom-call(s32[1]{0:T(128)} %bitcast.1.rank_ref, s32[2,64]{1,0:T(2,128)S(1)} %copy-done.12, bf16[128,5120]{1,0:T(8,128)(2,1)S(1)} %bitcast.54, bf16[128,4096]{1,0:T(8,128)(2,1)} %collective-permute-done.14.left_ref, bf16[128,4096]{1,0:T(8,128)(2,1)S(1)} %get-tuple-element.27.mid_ref, ...), custom_call_target="tpu_custom_call" | custom-call | tf_op jit(solution)/shard_map/backward_tile/pallas_call | solution.py:231
  108.0 1.9 collective-permute-start.16
  110.0 1.3 broadcast_select_fusion.2
  111.3 9.8 %collective-permute-done.13 = bf16[128,4096]{1,0:T(8,128)(2,1)S(1)} collective-permute-done((bf16[128,4096]{1,0:T(8,128)(2,1)}, bf16[128,4096]{1,0:T(8,128)(2,1)S(1)}, u32[]{:S(2)}, u32[]{:S(2)}) %collective-permute-start.13) | collective-permute-done | bytes 1048608 | tf_op jit(solution)/shard_map/ppermute | solution.py:254
  121.2 1.9 maximum_bitcast_fusion
  123.0 73.7 %collective-permute-done.16 = bf16[128,5120]{1,0:T(8,128)(2,1)S(1)} collective-permute-done((bf16[128,5120]{1,0:T(8,128)(2,1)S(1)}, bf16[128,5120]{1,0:T(8,128)(2,1)S(1)}, u32[]{:S(2)}, u32[]{:S(2)}) %collective-permute-start.16) | collective-permute-done | bytes 1310752 | tf_op jit(solution)/shard_map/ppermute | solution.py:254
  196.7 1.1 copy.16
  (43 shorter events, 1.4 us)
Async XLA Ops:
  0.6 23.4 %copy-start.9 = (bf16[1,128,5120]{2,1,0:T(8,128)(2,1)S(1)}, bf16[1,128,5120]{2,1,0:T(8,128)(2,1)}, u32[]{:S(2)}) copy-start(bf16[1,128,5120]{2,1,0:T(8,128)(2,1)} %param.9) | copy-start | bytes 3932164
  3.1 1.9 copy-start
  5.0 1.3 copy-start.2
  6.3 1.0 copy-start.8
  7.3 0.7 copy-start.11
  8.0 0.7 copy-start.13
  8.7 0.7 copy-start.14
  15.4 1.7 copy-start.4
  17.0 1.4 copy-start.6
  18.4 20.2 %copy-start.12 = (s32[2,64]{1,0:T(2,128)S(1)}, s32[2,64]{1,0:T(2,128)}, u32[]{:S(2)}) copy-start(s32[2,64]{1,0:T(2,128)} %dest_ref.5) | copy-start | bytes 1540
  18.4 20.2 %collective-permute-start = (bf16[128,128]{1,0:T(8,128)(2,1)}, bf16[128,128]{1,0:T(8,128)(2,1)S(1)}, u32[]{:S(2)}, u32[]{:S(2)}) collective-permute-start(bf16[128,128]{1,0:T(8,128)(2,1)} %get-tuple-element.16), channel_id=1, source_target_pairs={{0,1},{1,2},{2,3},{3,4},{4,5},{5,6},{6,7},{7,8},{8,9},{9,10},{10,1... | collective-permute-start | bytes 98312 | tf_op jit(solution)/shard_map/ppermute | solution.py:254
  22.1 16.5 %collective-permute-start.1 = (bf16[128,128]{1,0:T(8,128)(2,1)}, bf16[128,128]{1,0:T(8,128)(2,1)}, u32[]{:S(2)}, u32[]{:S(2)}) collective-permute-start(bf16[128,128]{1,0:T(8,128)(2,1)} %get-tuple-element.18), channel_id=1, source_target_pairs={{1,0},{2,1},{3,2},{4,3},{5,4},{6,5},{7,6},{8,7},{9,8},{10,9},{11,1... | collective-permute-start | bytes 98312 | tf_op jit(solution)/shard_map/ppermute | solution.py:254
  29.6 63.3 %collective-permute-start.11 = (bf16[128,4096]{1,0:T(8,128)(2,1)}, bf16[128,4096]{1,0:T(8,128)(2,1)}, u32[]{:S(2)}, u32[]{:S(2)}) collective-permute-start(bf16[128,4096]{1,0:T(8,128)(2,1)} %forward_tile.1), channel_id=1, source_target_pairs={{0,64},{1,65},{2,66},{3,67},{4,68},{5,69},{6,70},{7,71},{8,72},{9,... | collective-permute-start | bytes 3145736 | tf_op jit(solution)/shard_map/ppermute | solution.py:254
  38.5 10.5 %copy-start.1 = (bf16[1,384,4096]{2,1,0:T(8,128)(2,1)S(1)}, bf16[1,384,4096]{2,1,0:T(8,128)(2,1)}, u32[]{:S(2)}) copy-start(bf16[1,384,4096]{2,1,0:T(8,128)(2,1)} %param.11) | copy-start | bytes 9437188
  38.6 2.0 %copy-start.5 = (bf16[384,4096]{1,0:T(8,128)(2,1)S(1)}, bf16[384,4096]{1,0:T(8,128)(2,1)}, u32[]{:S(2)}) copy-start(bf16[384,4096]{1,0:T(8,128)(2,1)} %copy-done.4) | copy-start | bytes 9437188
  43.1 4.7 %copy-start.10 = (bf16[4096,128]{1,0:T(8,128)(2,1)}, bf16[4096,128]{1,0:T(8,128)(2,1)S(1)}, u32[]{:S(2)}) copy-start(bf16[4096,128]{1,0:T(8,128)(2,1)S(1)} %get-tuple-element.19) | copy-start | bytes 3145732
  44.2 9.3 %collective-permute-start.2 = (bf16[1024,128]{1,0:T(8,128)(2,1)}, bf16[1024,128]{1,0:T(8,128)(2,1)}, u32[]{:S(2)}, u32[]{:S(2)}) collective-permute-start(bf16[1024,128]{1,0:T(8,128)(2,1)} %get-tuple-element.28), channel_id=1, source_target_pairs={{0,16},{1,17},{2,18},{3,19},{4,20},{5,21},{6,22},{7,23},{8,24},{9,... | collective-permute-start | bytes 786440 | tf_op jit(solution)/shard_map/ppermute | solution.py:271
  45.4 15.0 %collective-permute-start.3 = (bf16[1024,128]{1,0:T(8,128)(2,1)}, bf16[1024,128]{1,0:T(8,128)(2,1)}, u32[]{:S(2)}, u32[]{:S(2)}) collective-permute-start(bf16[1024,128]{1,0:T(8,128)(2,1)} %get-tuple-element.30), channel_id=1, source_target_pairs={{0,32},{1,33},{2,34},{3,35},{4,36},{5,37},{6,38},{7,39},{8,40},{9,... | collective-permute-start | bytes 786440 | tf_op jit(solution)/shard_map/ppermute | solution.py:271
  47.9 47.0 %slice-start = ((s32[2,64]{1,0:T(2,128)}), s32[1,64]{1,0:T(1,128)S(1)}, s32[]{:S(2)}) async-start(s32[2,64]{1,0:T(2,128)} %dest_ref.5), calls=%async_computation | async-start | bytes 1024 | tf_op jit(solution)/shard_map/slice | solution.py:306
  47.9 54.0 %copy-start.3 = (bf16[1,128,5120]{2,1,0:T(8,128)(2,1)S(1)}, bf16[1,128,5120]{2,1,0:T(8,128)(2,1)}, u32[]{:S(2)}) copy-start(bf16[1,128,5120]{2,1,0:T(8,128)(2,1)} %param.10) | copy-start | bytes 3932164
  47.9 12.6 %collective-permute-start.4 = (bf16[1024,128]{1,0:T(8,128)(2,1)}, bf16[1024,128]{1,0:T(8,128)(2,1)}, u32[]{:S(2)}, u32[]{:S(2)}) collective-permute-start(bf16[1024,128]{1,0:T(8,128)(2,1)} %get-tuple-element.29), channel_id=1, source_target_pairs={{0,48},{1,49},{2,50},{3,51},{4,52},{5,53},{6,54},{7,55},{8,56},{9,... | collective-permute-start | bytes 786440 | tf_op jit(solution)/shard_map/ppermute | solution.py:271
  50.7 51.1 %collective-permute-start.14 = (bf16[128,4096]{1,0:T(8,128)(2,1)}, bf16[128,4096]{1,0:T(8,128)(2,1)}, u32[]{:S(2)}, u32[]{:S(2)}) collective-permute-start(bf16[128,4096]{1,0:T(8,128)(2,1)} %get-tuple-element.26), channel_id=1, source_target_pairs={{64,65},{65,66},{66,67},{67,68},{68,69},{69,70},{70,71},{71,72},{7... | collective-permute-start | bytes 3145736 | tf_op jit(solution)/shard_map/ppermute | solution.py:254
  53.5 48.4 %collective-permute-start.15 = (bf16[128,4096]{1,0:T(8,128)(2,1)}, bf16[128,4096]{1,0:T(8,128)(2,1)}, u32[]{:S(2)}, u32[]{:S(2)}) collective-permute-start(bf16[128,4096]{1,0:T(8,128)(2,1)} %get-tuple-element.25), channel_id=1, source_target_pairs={{65,64},{66,65},{67,66},{68,67},{69,68},{70,69},{71,70},{72,71},{7... | collective-permute-start | bytes 3145736 | tf_op jit(solution)/shard_map/ppermute | solution.py:254
  61.8 0.7 copy-start.15
  63.2 5.0 %collective-permute-start.5 = (bf16[256,128]{1,0:T(8,128)(2,1)S(1)}, bf16[256,128]{1,0:T(8,128)(2,1)S(1)}, u32[]{:S(2)}, u32[]{:S(2)}) collective-permute-start(bf16[256,128]{1,0:T(8,128)(2,1)S(1)} %get-tuple-element.31), channel_id=1, source_target_pairs={{0,4},{1,5},{2,6},{3,7},{4,8},{5,9},{6,10},{7,11},{8,12},{9,13},{1... | collective-permute-start | bytes 196616 | tf_op jit(solution)/shard_map/ppermute | solution.py:271
  63.2 5.0 %collective-permute-start.6 = (bf16[256,128]{1,0:T(8,128)(2,1)}, bf16[256,128]{1,0:T(8,128)(2,1)}, u32[]{:S(2)}, u32[]{:S(2)}) collective-permute-start(bf16[256,128]{1,0:T(8,128)(2,1)} %get-tuple-element.33), channel_id=1, source_target_pairs={{0,8},{1,9},{2,10},{3,11},{4,12},{5,13},{6,14},{7,15},{8,0},{9,1},... | collective-permute-start | bytes 196616 | tf_op jit(solution)/shard_map/ppermute | solution.py:271
  68.2 0.6 copy-start.16
  68.2 3.4 %collective-permute-start.7 = (bf16[256,128]{1,0:T(8,128)(2,1)}, bf16[256,128]{1,0:T(8,128)(2,1)}, u32[]{:S(2)}, u32[]{:S(2)}) collective-permute-start(bf16[256,128]{1,0:T(8,128)(2,1)} %get-tuple-element.32), channel_id=1, source_target_pairs={{0,12},{1,13},{2,14},{3,15},{4,0},{5,1},{6,2},{7,3},{8,4},{9,5},{1... | collective-permute-start | bytes 196616 | tf_op jit(solution)/shard_map/ppermute | solution.py:271
  73.2 11.6 %collective-permute-start.10 = (bf16[64,128]{1,0:T(8,128)(2,1)S(1)}, bf16[64,128]{1,0:T(8,128)(2,1)S(1)}, u32[]{:S(2)}, u32[]{:S(2)}) collective-permute-start(bf16[64,128]{1,0:T(8,128)(2,1)S(1)} %get-tuple-element.35), channel_id=1, source_target_pairs={{0,3},{1,0},{2,1},{3,2},{4,7},{5,4},{6,5},{7,6},{8,11},{9,8},{10,9... | collective-permute-start | bytes 49160 | tf_op jit(solution)/shard_map/ppermute | solution.py:271
  79.7 10.6 %collective-permute-start.8 = (bf16[64,128]{1,0:T(8,128)(2,1)}, bf16[64,128]{1,0:T(8,128)(2,1)}, u32[]{:S(2)}, u32[]{:S(2)}) collective-permute-start(bf16[64,128]{1,0:T(8,128)(2,1)} %get-tuple-element.34), channel_id=1, source_target_pairs={{0,1},{1,2},{2,3},{3,0},{4,5},{5,6},{6,7},{7,4},{8,9},{9,10},{10,1... | collective-permute-start | bytes 49160 | tf_op jit(solution)/shard_map/ppermute | solution.py:271
  84.8 0.6 copy-start.17
  85.4 6.1 %collective-permute-start.9 = (bf16[64,128]{1,0:T(8,128)(2,1)S(1)}, bf16[64,128]{1,0:T(8,128)(2,1)}, u32[]{:S(2)}, u32[]{:S(2)}) collective-permute-start(bf16[64,128]{1,0:T(8,128)(2,1)S(1)} %get-tuple-element.36), channel_id=1, source_target_pairs={{0,2},{1,3},{2,0},{3,1},{4,6},{5,7},{6,4},{7,5},{8,10},{9,11},{10,... | collective-permute-start | bytes 49160 | tf_op jit(solution)/shard_map/ppermute | solution.py:271
  92.9 17.1 %collective-permute-start.12 = (bf16[128,4096]{1,0:T(8,128)(2,1)}, bf16[128,4096]{1,0:T(8,128)(2,1)}, u32[]{:S(2)}, u32[]{:S(2)}) collective-permute-start(bf16[128,4096]{1,0:T(8,128)(2,1)} %collective-permute-done.11), channel_id=1, source_target_pairs={{64,65},{65,66},{66,67},{67,68},{68,69},{69,70},{70,71},{71,72},{7... | collective-permute-start | bytes 3145736 | tf_op jit(solution)/shard_map/ppermute | solution.py:254
  97.6 23.5 %collective-permute-start.13 = (bf16[128,4096]{1,0:T(8,128)(2,1)}, bf16[128,4096]{1,0:T(8,128)(2,1)S(1)}, u32[]{:S(2)}, u32[]{:S(2)}) collective-permute-start(bf16[128,4096]{1,0:T(8,128)(2,1)} %collective-permute-done.11), channel_id=1, source_target_pairs={{65,64},{66,65},{67,66},{68,67},{69,68},{70,69},{71,70},{72,71},{7... | collective-permute-start | bytes 3145736 | tf_op jit(solution)/shard_map/ppermute | solution.py:254
  101.9 1.6 copy-start.7
  108.0 88.8 %collective-permute-start.16 = (bf16[128,5120]{1,0:T(8,128)(2,1)S(1)}, bf16[128,5120]{1,0:T(8,128)(2,1)S(1)}, u32[]{:S(2)}, u32[]{:S(2)}) collective-permute-start(bf16[128,5120]{1,0:T(8,128)(2,1)S(1)} %backward_tile.1), channel_id=1, source_target_pairs={{64,0},{65,1},{66,2},{67,3},{68,4},{69,5},{70,6},{71,7},{72,8},{73... | collective-permute-start | bytes 3932168 | tf_op jit(solution)/shard_map/ppermute | solution.py:254

commit v3 on v2

--- a/solution.py
+++ b/solution.py
@@ -19,6 +19,7 @@
 KW = KV * HEAD_DIM
 GW = GROUP * HEAD_DIM
 SCALE = 1.0 / math.sqrt(HEAD_DIM)
+HALF = QW // 2
 AXES = ("section", "dp")
 BF16 = jnp.bfloat16
 F32 = jnp.float32
@@ -141,16 +142,18 @@
 
 
 def backward_kernel(
-    rank_ref, dest_ref, qkv_ref, left_ref, mid_ref, right_ref, back_ref, probs_ref, down_ref,
-    grad_ref, gattn_ref,
+    rank_ref, dest_ref, qkv_ref, left_a_ref, left_b_ref, mid_ref, right_a_ref, right_b_ref, back_ref,
+    probs_ref, down_ref, grad_ref, gattn_ref,
 ):
     rank = rank_ref[0]
     went = dest_ref[1, rank] - rank
     back = back_ref[...][:, RANK:]
     for j in range(KV):
         block = slice(j * GW, (j + 1) * GW)
+        left_ref, right_ref = ((left_a_ref, right_a_ref), (left_b_ref, right_b_ref))[2 * j // KV]
+        part = slice(j * GW % HALF, j * GW % HALF + GW)
         grad = jnp.where(
-            went < 0, left_ref[:, block], jnp.where(went > 0, right_ref[:, block], mid_ref[:, block])
+            went < 0, left_ref[:, part], jnp.where(went > 0, right_ref[:, part], mid_ref[:, block])
         )
         gattn = grad.astype(F32) + dot(back, down_ref[block, :], NT)
         gattn_ref[:, block] = gattn.astype(BF16)
@@ -178,6 +181,7 @@
         grad_ref[:, cols] = dot(probs_low, grads, TN).astype(BF16)
 
 
+COST = pl.CostEstimate(flops=2**20, bytes_accessed=2**20, transcendentals=0)
 SMEM = pl.BlockSpec(memory_space=pltpu.SMEM)
 VMEM = pl.BlockSpec(memory_space=pltpu.VMEM)
 
@@ -190,6 +194,7 @@
         out_specs=VMEM,
         scratch_shapes=[pltpu.VMEM((GROUP * TILE, TILE), F32)],
         compiler_params=pltpu.CompilerParams(vmem_limit_bytes=24 * 2**20),
+        cost_estimate=COST,
         name="forward_tile",
     )(rank, lengths, languages, table, qkv, down, up)
 
@@ -209,6 +214,7 @@
         in_specs=[SMEM] * 5 + [VMEM] * 4,
         out_specs=(VMEM,) * 6,
         compiler_params=pltpu.CompilerParams(vmem_limit_bytes=40 * 2**20),
+        cost_estimate=COST,
         name="prepare_tile",
     )(rank, lengths, languages, dest, table, qkv, slots, down, up)
 
@@ -223,6 +229,7 @@
         in_specs=[SMEM] * 2 + [VMEM] * 5,
         out_specs=(VMEM, VMEM),
         compiler_params=pltpu.CompilerParams(vmem_limit_bytes=24 * 2**20),
+        cost_estimate=COST,
         name="adapter_terms",
     )(rank, dest, attn, scaled, left, own, right)
 
@@ -231,12 +238,13 @@
     return pl.pallas_call(
         backward_kernel,
         out_shape=jax.ShapeDtypeStruct((TILE, QW + 2 * KW), BF16),
-        in_specs=[SMEM] * 2 + [VMEM] * 7,
+        in_specs=[SMEM] * 2 + [VMEM] * 9,
         out_specs=VMEM,
         scratch_shapes=[pltpu.VMEM((TILE, QW), BF16)],
         compiler_params=pltpu.CompilerParams(vmem_limit_bytes=40 * 2**20),
+        cost_estimate=COST,
         name="backward_tile",
-    )(rank, dest, qkv, left, mid, right, back, probs, down)
+    )(rank, dest, qkv, *left, mid, *right, back, probs, down)
 
 
 def sections():
@@ -261,14 +269,14 @@
 def exchange(x, stride, count):
     size = lax.axis_size("dp")
     place = (lax.axis_index("dp") // stride) % count
-    total = lax.dynamic_index_in_dim(x, place, 0, keepdims=False).astype(F32)
+    total = lax.dynamic_index_in_dim(x, place, 0, keepdims=False)
     for step in range(1, count):
         piece = lax.dynamic_index_in_dim(x, (place + step) % count, 0, keepdims=False)
         route = []
         for t in range(size):
             at = (t // stride) % count
             route.append((t, t + ((at + step) % count - at) * stride))
-        total = total + lax.ppermute(piece, "dp", route).astype(F32)
+        total = total + lax.ppermute(piece, "dp", route)
     return total
 
 
@@ -282,8 +290,12 @@
     slots = slot_grad_b[0]
     every = range(sections())
     later = range(1, sections())
-    from_left = shift(slots[2 * TILE :], [(later, 0, 1, anywhere)])
-    from_right = shift(slots[:TILE], [(later, 0, -1, anywhere)])
+    first, second = slice(0, HALF), slice(HALF, QW)
+    to_up, to_down = slots[2 * TILE :], slots[:TILE]
+    left_a = shift(to_up[:, first], [(later, 0, 1, anywhere)])
+    right_a = shift(to_down[:, first], [(later, 0, -1, anywhere)])
+    left_b = shift(to_up[:, second], [(later, 0, 1, anywhere)])
+    right_b = shift(to_down[:, second], [(later, 0, -1, anywhere)])
     out = run_forward(rank_word, lengths, languages, lang_scale, qkv_a[0], down, up)
     hop = shift(out, [(every, 1, 0, anywhere)])
     probs, attn, scaled, to_left, own, to_right = run_prepare(
@@ -292,14 +304,18 @@
     left = shift(to_right, [(every, 0, 1, anywhere)])
     right = shift(to_left, [(every, 0, -1, anywhere)])
     terms, back = run_terms(rank_word, destination, attn, scaled, left, own, right)
-    terms = exchange(terms.reshape(4, 1024, 128), 16, 4).astype(BF16)
-    terms = exchange(terms.reshape(4, 256, 128), 4, 4).astype(BF16)
-    terms = exchange(terms.reshape(4, 64, 128), 1, 4)
+    terms, left_a, right_a = lax.optimization_barrier((terms, left_a, right_a))
+    planes = [[4 * k + z for k in range(size // 4)] for z in range(4)]
+    terms = lax.all_to_all(
+        terms.reshape(size // 4, 256, 128), "dp", 0, 0, axis_index_groups=planes, tiled=True
+    )
+    terms = jnp.sum(terms.astype(F32), axis=0)
     terms, back, hop = lax.optimization_barrier((terms, back, hop))
     grad_qkv = run_backward(
-        rank_word, destination, qkv_b[0], from_left, slots[TILE : 2 * TILE], from_right, back,
-        probs, down,
-    )
+        rank_word, destination, qkv_b[0], (left_a, left_b), slots[TILE : 2 * TILE],
+        (right_a, right_b), back, probs, down,
+    )
+    terms = exchange(terms.reshape(4, 64, 128), 1, 4)
     handed_back = shift(grad_qkv, [(every, -1, 0, anywhere)])[None]
     before = shift(hop, [(later, 0, 1, anywhere)])
     after = shift(hop, [(later, 0, -1, anywhere)])

time: 199 us -> 179 us (0.90)
  the two profiles are of different devices: /device:TPU:33 before, /device:TPU:35 now
where the time goes in v3:
time: 179 us; the launch traced here: 178 us
  waiting for transfers between devices  86.2 us (48%)
  starting transfers between devices  52.8 us (29%)
  Pallas kernels  17.7 us (10%)
  local copies, waits for them, and re-layouts  14 us (8%)
  other arithmetic  4.22 us (2%)
  between operations  2.91 us (2%)
    ppermute x10, waiting for transfers between devices, shift(): return lax.ppermute(x, AXES, route)  86.2 us
    ppermute x10, starting transfers between devices, shift(): return lax.ppermute(x, AXES, route)  45 us
    unnamed x27, local copies, waits for them, and re-layouts  8.95 us
    all_to_all x1, starting transfers between devices, shards(): lax.all_to_all(terms.reshape(size // 4, 256, 128), 'dp', 0, 0, axis_index...  5.69 us
    pallas_call x1, Pallas kernels, run_forward(): pl.pallas_call(forward_kernel, out_shape=jax.ShapeDtypeStruct((TILE, QW),...  5.6 us
    pallas_call x1, Pallas kernels, run_prepare(): pl.pallas_call(prepare_kernel, out_shape=(jax.ShapeDtypeStruct((QW, TILE)...  5.42 us
    pallas_call x1, Pallas kernels, run_backward(): pl.pallas_call(backward_kernel, out_shape=jax.ShapeDtypeStruct((TILE, QW...  4.44 us
  transfers between devices with their start and end apart: 14, of which 4 were waited for; matrix products, arithmetic and copies ran while one was open for 4% of the time, Pallas kernels for 10%

profile of v3, /device:TPU:35, one launch (start us, length us, event | category | flops | bytes accessed | tf_op | source)
XLA Modules:
  0.0 177.8 jit_solution(17251712628754128063)
XLA Ops:
  0.6 2.2 %slice_bitcast_fusion = (bf16[128,4096]{1,0:T(8,128)(2,1)S(1)}, bf16[128,4096]{1,0:T(8,128)(2,1)S(1)}, bf16[128,4096]{1,0:T(8,128)(2,1)S(1)}) fusion(bf16[1,384,4096]{2,1,0:T(8,128)(2,1)} %param.11), kind=kLoop, calls=%fused_computation.2 | loop fusion | bytes 6291456 | tf_op jit(solution)/shard_map/slice | solution.py:315
  2.8 0.0 copy-start.11
  2.9 0.0 copy-start.1
  2.9 0.0 copy-start.8
  2.9 0.0 copy-start.9
  2.9 0.0 copy-start.10
  2.9 1.1 fusion.4
  4.0 3.5 %collective-permute-start.2 = (bf16[128,2048]{1,0:T(8,128)(2,1)}, bf16[128,2048]{1,0:T(8,128)(2,1)}, u32[]{:S(2)}, u32[]{:S(2)}) collective-permute-start(bf16[128,2048]{1,0:T(8,128)(2,1)} %get-tuple-element.37), channel_id=1, source_target_pairs={{64,65},{65,66},{66,67},{67,68},{68,69},{69,70},{70,71},{71,72},{7... | collective-permute-start | bytes 1572872 | tf_op jit(solution)/shard_map/ppermute | solution.py:262
  7.5 1.1 fusion.3
  8.6 1.9 %collective-permute-start.3 = (bf16[128,2048]{1,0:T(8,128)(2,1)}, bf16[128,2048]{1,0:T(8,128)(2,1)}, u32[]{:S(2)}, u32[]{:S(2)}) collective-permute-start(bf16[128,2048]{1,0:T(8,128)(2,1)} %get-tuple-element.35), channel_id=1, source_target_pairs={{65,64},{66,65},{67,66},{68,67},{69,68},{70,69},{71,70},{72,71},{7... | collective-permute-start | bytes 1572872 | tf_op jit(solution)/shard_map/ppermute | solution.py:262
  10.5 1.5 copy.12
  12.1 0.1 copy.13.lens_ref
  12.2 0.0 copy-start
  12.2 1.9 %copy-done = bf16[1,384,4096]{2,1,0:T(8,128)(2,1)S(1)} copy-done((bf16[1,384,4096]{2,1,0:T(8,128)(2,1)S(1)}, bf16[1,384,4096]{2,1,0:T(8,128)(2,1)}, u32[]{:S(2)}) %copy-start) | copy-done | bytes 3145752
  14.1 1.0 copy-done.4
  15.1 5.4 %prepare_tile.1 = (f32[4096,128]{1,0:T(8,128)S(1)}, bf16[128,4096]{1,0:T(8,128)(2,1)S(1)}, bf16[384,4096]{1,0:T(8,128)(2,1)S(1)}, bf16[128,128]{1,0:T(8,128)(2,1...) custom-call(s32[1]{0:T(128)} %bitcast.1.rank_ref, s32[2,64,8]{2,1,0:T(8,128)S(1)} %copy.13.lens_ref, ...), custom_call_target="tpu_custom_call" | custom-call | flops 1048576 | bytes 1048576 | tf_op jit(solution)/shard_map/prepare_tile/pallas_call | solution.py:204
  20.6 0.0 copy-start.2
  20.6 3.5 %collective-permute-start = (bf16[128,128]{1,0:T(8,128)(2,1)S(1)}, bf16[128,128]{1,0:T(8,128)(2,1)S(1)}, u32[]{:S(2)}, u32[]{:S(2)}) collective-permute-start(bf16[128,128]{1,0:T(8,128)(2,1)S(1)} %get-tuple-element.19), channel_id=1, source_target_pairs={{0,1},{1,2},{2,3},{3,4},{4,5},{5,6},{6,7},{7,8},{8,9},{9,10},{10,1... | collective-permute-start | bytes 98312 | tf_op jit(solution)/shard_map/ppermute | solution.py:262
  24.1 5.2 %collective-permute-start.1 = (bf16[128,128]{1,0:T(8,128)(2,1)S(1)}, bf16[128,128]{1,0:T(8,128)(2,1)S(1)}, u32[]{:S(2)}, u32[]{:S(2)}) collective-permute-start(bf16[128,128]{1,0:T(8,128)(2,1)S(1)} %get-tuple-element.21), channel_id=1, source_target_pairs={{1,0},{2,1},{3,2},{4,3},{5,4},{6,5},{7,6},{8,7},{9,8},{10,9},{11,1... | collective-permute-start | bytes 98312 | tf_op jit(solution)/shard_map/ppermute | solution.py:262
  29.4 1.0 collective-permute-done.1.right_ref
  30.4 2.3 %adapter_terms.1 = (bf16[4096,128]{1,0:T(8,128)(2,1)S(1)}, bf16[128,128]{1,0:T(8,128)(2,1)S(1)}) custom-call(s32[1]{0:T(128)} %bitcast.1.rank_ref, s32[2,64]{1,0:T(2,128)S(1)} %copy-done.8, bf16[128,4096]{1,0:T(8,128)(2,1)S(1)} %get-tuple-element.17.attn_ref, bf16[384,4096]{1,0:T(8,128)(2,1)S(1)} %get-tuple-element.18.scaled_ref, ...), custom_call_target="tpu_custom_call" | custom-call | flops 1048576 | bytes 1048576 | tf_op jit(solution)/shard_map/adapter_terms/pallas_call | solution.py:223
  32.7 1.0 copy-done.7
  33.7 5.7 %all-to-all-start = ((bf16[16,256,128]{2,1,0:T(8,128)(2,1)}), bf16[16,256,128]{2,1,0:T(8,128)(2,1)}, u32[]{:S(2)}, u32[]{:S(2)}) async-start(bf16[16,256,128]{2,1,0:T(8,128)(2,1)} %bitcast.45), calls=%async_computation | async-start | bytes 2097152 | tf_op jit(solution)/shard_map/all_to_all | solution.py:309
  39.3 1.0 copy-done.5
  40.4 1.3 copy-done.6
  41.7 5.6 %forward_tile.1 = bf16[128,4096]{1,0:T(8,128)(2,1)} custom-call(s32[1]{0:T(128)} %bitcast.1.rank_ref, s32[2,64,8]{2,1,0:T(8,128)S(1)} %copy.13.lens_ref, s32[2,64]{1,0:T(2,128)S(1)} %copy-done.9, f32[102]{0:T(128)S(1)} %copy-done.10, bf16[128,5120]{1,0:T(8,128)(2,1)S(1)} %bitcast.44, bf16[4096,64]{1,0:T(8,128)(2,1)S(1)} %bitcast.37, ...), custom_call_target="tpu_custom_call" | custom-call | flops 1048576 | bytes 1048576 | tf_op jit(solution)/shard_map/forward_tile/pallas_call | solution.py:190
  47.3 14.3 %collective-permute-start.4 = (bf16[128,4096]{1,0:T(8,128)(2,1)}, bf16[128,4096]{1,0:T(8,128)(2,1)}, u32[]{:S(2)}, u32[]{:S(2)}) collective-permute-start(bf16[128,4096]{1,0:T(8,128)(2,1)} %forward_tile.1), channel_id=1, source_target_pairs={{0,64},{1,65},{2,66},{3,67},{4,68},{5,69},{6,70},{7,71},{8,72},{9,... | collective-permute-start | bytes 3145736 | tf_op jit(solution)/shard_map/ppermute | solution.py:262
  61.6 2.7 %collective-permute-start.7 = (bf16[128,2048]{1,0:T(8,128)(2,1)}, bf16[128,2048]{1,0:T(8,128)(2,1)}, u32[]{:S(2)}, u32[]{:S(2)}) collective-permute-start(bf16[128,2048]{1,0:T(8,128)(2,1)} %get-tuple-element.36), channel_id=1, source_target_pairs={{64,65},{65,66},{66,67},{67,68},{68,69},{69,70},{70,71},{71,72},{7... | collective-permute-start | bytes 1572872 | tf_op jit(solution)/shard_map/ppermute | solution.py:262
  64.4 2.8 %collective-permute-start.8 = (bf16[128,2048]{1,0:T(8,128)(2,1)}, bf16[128,2048]{1,0:T(8,128)(2,1)}, u32[]{:S(2)}, u32[]{:S(2)}) collective-permute-start(bf16[128,2048]{1,0:T(8,128)(2,1)} %get-tuple-element.34), channel_id=1, source_target_pairs={{65,64},{66,65},{67,66},{68,67},{69,68},{70,69},{71,70},{72,71},{7... | collective-permute-start | bytes 1572872 | tf_op jit(solution)/shard_map/ppermute | solution.py:262
  67.2 0.7 constant_dynamic-slice_fusion.2
  69.7 0.0 all-to-all-done
  69.7 0.0 copy-start.3
  69.8 1.5 convert_reduce_fusion
  71.3 20.3 %collective-permute-done.4 = bf16[128,4096]{1,0:T(8,128)(2,1)} collective-permute-done((bf16[128,4096]{1,0:T(8,128)(2,1)}, bf16[128,4096]{1,0:T(8,128)(2,1)}, u32[]{:S(2)}, u32[]{:S(2)}) %collective-permute-start.4) | collective-permute-done | bytes 1048608 | tf_op jit(solution)/shard_map/ppermute | solution.py:262
  91.6 0.8 collective-permute-start.10
  92.4 1.3 collective-permute-start.12
  93.7 7.1 %collective-permute-start.5 = (bf16[128,4096]{1,0:T(8,128)(2,1)}, bf16[128,4096]{1,0:T(8,128)(2,1)S(1)}, u32[]{:S(2)}, u32[]{:S(2)}) collective-permute-start(bf16[128,4096]{1,0:T(8,128)(2,1)} %collective-permute-done.4), channel_id=1, source_target_pairs={{64,65},{65,66},{66,67},{67,68},{68,69},{69,70},{70,71},{71,72},{7... | collective-permute-start | bytes 3145736 | tf_op jit(solution)/shard_map/ppermute | solution.py:262
  100.8 0.1 broadcast_select_fusion.1
  100.9 1.9 %collective-permute-start.6 = (bf16[128,4096]{1,0:T(8,128)(2,1)}, bf16[128,4096]{1,0:T(8,128)(2,1)S(1)}, u32[]{:S(2)}, u32[]{:S(2)}) collective-permute-start(bf16[128,4096]{1,0:T(8,128)(2,1)} %collective-permute-done.4), channel_id=1, source_target_pairs={{65,64},{66,65},{67,66},{68,67},{69,68},{70,69},{71,70},{72,71},{7... | collective-permute-start | bytes 3145736 | tf_op jit(solution)/shard_map/ppermute | solution.py:262
  102.8 4.4 %backward_tile.1 = bf16[128,5120]{1,0:T(8,128)(2,1)S(1)} custom-call(s32[1]{0:T(128)} %bitcast.1.rank_ref, s32[2,64]{1,0:T(2,128)S(1)} %copy-done.8, bf16[128,5120]{1,0:T(8,128)(2,1)S(1)} %bitcast.41, bf16[128,2048]{1,0:T(8,128)(2,1)} %collective-permute-done.2.left_a_ref, bf16[128,2048]{1,0:T(8,128)(2,1)} %collective-permute-done.7.left_b_ref, ...), custom_call_target="tpu_custom_call" | custom-call | flops 1048576 | bytes 1048576 | tf_op jit(solution)/shard_map/backward_tile/pallas_call | solution.py:238
  107.3 1.9 %collective-permute-start.9 = (bf16[128,5120]{1,0:T(8,128)(2,1)S(1)}, bf16[128,5120]{1,0:T(8,128)(2,1)S(1)}, u32[]{:S(2)}, u32[]{:S(2)}) collective-permute-start(bf16[128,5120]{1,0:T(8,128)(2,1)S(1)} %backward_tile.1), channel_id=1, source_target_pairs={{64,0},{65,1},{66,2},{67,3},{68,4},{69,5},{70,6},{71,7},{72,8},{73... | collective-permute-start | bytes 3932168 | tf_op jit(solution)/shard_map/ppermute | solution.py:262
  109.2 0.6 fusion.2
  109.9 18.6 %collective-permute-done.5 = bf16[128,4096]{1,0:T(8,128)(2,1)S(1)} collective-permute-done((bf16[128,4096]{1,0:T(8,128)(2,1)}, bf16[128,4096]{1,0:T(8,128)(2,1)S(1)}, u32[]{:S(2)}, u32[]{:S(2)}) %collective-permute-start.5) | collective-permute-done | bytes 1048608 | tf_op jit(solution)/shard_map/ppermute | solution.py:262
  128.5 0.1 broadcast_select_fusion.2
  128.5 0.1 broadcast_select_fusion
  128.6 1.8 %maximum_bitcast_fusion = bf16[1,384,4096]{2,1,0:T(8,128)(2,1)} fusion(bf16[128,4096]{1,0:T(8,128)(2,1)S(1)} %broadcast_select_fusion, bf16[128,4096]{1,0:T(8,128)(2,1)S(1)} %broadcast_select_fusion.1, bf16[128,4096]{1,0:T(8,128)(2,1)S(1)} %broadcast_select_fusion.2), kind=kLoop, calls=%fused_computation | loop fusion | flops 9437184 | bytes 6291456 | tf_op jit(solution)/shard_map/broadcast_in_dim | solution.py:329
  130.5 46.3 %collective-permute-done.9 = bf16[128,5120]{1,0:T(8,128)(2,1)S(1)} collective-permute-done((bf16[128,5120]{1,0:T(8,128)(2,1)S(1)}, bf16[128,5120]{1,0:T(8,128)(2,1)S(1)}, u32[]{:S(2)}, u32[]{:S(2)}) %collective-permute-start.9) | collective-permute-done | bytes 1310752 | tf_op jit(solution)/shard_map/ppermute | solution.py:262
  176.7 1.1 copy.16
  (24 shorter events, 0.1 us)
Async XLA Ops:
  2.8 9.2 %copy-start.11 = (s32[2,64,8]{1,2,0:T(8,128)S(1)}, s32[2,64,8]{1,2,0:T(8,128)}, u32[]{:S(2)}) copy-start(s32[2,64,8]{1,2,0:T(8,128)} %param.16) | copy-start | bytes 12292
  2.9 9.3 %copy-start.1 = (bf16[1,128,5120]{2,1,0:T(8,128)(2,1)S(1)}, bf16[1,128,5120]{2,1,0:T(8,128)(2,1)}, u32[]{:S(2)}) copy-start(bf16[1,128,5120]{2,1,0:T(8,128)(2,1)} %param.10) | copy-start | bytes 3932164
  2.9 9.3 %copy-start.8 = (s32[2,64]{1,0:T(2,128)S(1)}, s32[2,64]{1,0:T(2,128)}, u32[]{:S(2)}) copy-start(s32[2,64]{1,0:T(2,128)} %dest_ref.5) | copy-start | bytes 1540
  2.9 9.3 %copy-start.9 = (s32[2,64]{1,0:T(2,128)S(1)}, s32[2,64]{1,0:T(2,128)}, u32[]{:S(2)}) copy-start(s32[2,64]{1,0:T(2,128)} %langs_ref.3) | copy-start | bytes 1540
  2.9 9.3 %copy-start.10 = (f32[102]{0:T(128)S(1)}, f32[102]{0:T(128)}, u32[]{:S(2)}) copy-start(f32[102]{0:T(128)} %table_ref.3) | copy-start | bytes 1228
  4.0 29.7 %collective-permute-start.2 = (bf16[128,2048]{1,0:T(8,128)(2,1)}, bf16[128,2048]{1,0:T(8,128)(2,1)}, u32[]{:S(2)}, u32[]{:S(2)}) collective-permute-start(bf16[128,2048]{1,0:T(8,128)(2,1)} %get-tuple-element.37), channel_id=1, source_target_pairs={{64,65},{65,66},{66,67},{67,68},{68,69},{69,70},{70,71},{71,72},{7... | collective-permute-start | bytes 1572872 | tf_op jit(solution)/shard_map/ppermute | solution.py:262
  8.6 25.0 %collective-permute-start.3 = (bf16[128,2048]{1,0:T(8,128)(2,1)}, bf16[128,2048]{1,0:T(8,128)(2,1)}, u32[]{:S(2)}, u32[]{:S(2)}) collective-permute-start(bf16[128,2048]{1,0:T(8,128)(2,1)} %get-tuple-element.35), channel_id=1, source_target_pairs={{65,64},{66,65},{67,66},{68,67},{69,68},{70,69},{71,70},{72,71},{7... | collective-permute-start | bytes 1572872 | tf_op jit(solution)/shard_map/ppermute | solution.py:262
  12.2 1.9 %copy-start = (bf16[1,384,4096]{2,1,0:T(8,128)(2,1)S(1)}, bf16[1,384,4096]{2,1,0:T(8,128)(2,1)}, u32[]{:S(2)}) copy-start(bf16[1,384,4096]{2,1,0:T(8,128)(2,1)} %param.11) | copy-start | bytes 9437188
  14.1 1.0 copy-start.4
  20.6 12.1 %copy-start.2 = (f32[4096,128]{1,0:T(8,128)}, f32[4096,128]{1,0:T(8,128)S(1)}, u32[]{:S(2)}) copy-start(f32[4096,128]{1,0:T(8,128)S(1)} %get-tuple-element.29.probs_ref) | copy-start | bytes 6291460
  20.6 8.8 %collective-permute-start = (bf16[128,128]{1,0:T(8,128)(2,1)S(1)}, bf16[128,128]{1,0:T(8,128)(2,1)S(1)}, u32[]{:S(2)}, u32[]{:S(2)}) collective-permute-start(bf16[128,128]{1,0:T(8,128)(2,1)S(1)} %get-tuple-element.19), channel_id=1, source_target_pairs={{0,1},{1,2},{2,3},{3,4},{4,5},{5,6},{6,7},{7,8},{8,9},{9,10},{10,1... | collective-permute-start | bytes 98312 | tf_op jit(solution)/shard_map/ppermute | solution.py:262
  24.1 6.3 %collective-permute-start.1 = (bf16[128,128]{1,0:T(8,128)(2,1)S(1)}, bf16[128,128]{1,0:T(8,128)(2,1)S(1)}, u32[]{:S(2)}, u32[]{:S(2)}) collective-permute-start(bf16[128,128]{1,0:T(8,128)(2,1)S(1)} %get-tuple-element.21), channel_id=1, source_target_pairs={{1,0},{2,1},{3,2},{4,3},{5,4},{6,5},{7,6},{8,7},{9,8},{10,9},{11,1... | collective-permute-start | bytes 98312 | tf_op jit(solution)/shard_map/ppermute | solution.py:262
  32.7 1.0 copy-start.7
  33.6 33.6 %slice-start = ((s32[2,64]{1,0:T(2,128)}), s32[1,64]{1,0:T(1,128)S(1)}, s32[]{:S(2)}) async-start(s32[2,64]{1,0:T(2,128)} %dest_ref.5), calls=%async_computation.1 | async-start | bytes 1024 | tf_op jit(solution)/shard_map/slice | solution.py:322
  33.7 36.1 %all-to-all-start = ((bf16[16,256,128]{2,1,0:T(8,128)(2,1)}), bf16[16,256,128]{2,1,0:T(8,128)(2,1)}, u32[]{:S(2)}, u32[]{:S(2)}) async-start(bf16[16,256,128]{2,1,0:T(8,128)(2,1)} %bitcast.45), calls=%async_computation | async-start | bytes 2097152 | tf_op jit(solution)/shard_map/all_to_all | solution.py:309
  39.3 1.0 copy-start.5
  40.4 1.3 copy-start.6
  47.3 44.3 %collective-permute-start.4 = (bf16[128,4096]{1,0:T(8,128)(2,1)}, bf16[128,4096]{1,0:T(8,128)(2,1)}, u32[]{:S(2)}, u32[]{:S(2)}) collective-permute-start(bf16[128,4096]{1,0:T(8,128)(2,1)} %forward_tile.1), channel_id=1, source_target_pairs={{0,64},{1,65},{2,66},{3,67},{4,68},{5,69},{6,70},{7,71},{8,72},{9,... | collective-permute-start | bytes 3145736 | tf_op jit(solution)/shard_map/ppermute | solution.py:262
  61.6 32.0 %collective-permute-start.7 = (bf16[128,2048]{1,0:T(8,128)(2,1)}, bf16[128,2048]{1,0:T(8,128)(2,1)}, u32[]{:S(2)}, u32[]{:S(2)}) collective-permute-start(bf16[128,2048]{1,0:T(8,128)(2,1)} %get-tuple-element.36), channel_id=1, source_target_pairs={{64,65},{65,66},{66,67},{67,68},{68,69},{69,70},{70,71},{71,72},{7... | collective-permute-start | bytes 1572872 | tf_op jit(solution)/shard_map/ppermute | solution.py:262
  64.4 36.5 %collective-permute-start.8 = (bf16[128,2048]{1,0:T(8,128)(2,1)}, bf16[128,2048]{1,0:T(8,128)(2,1)}, u32[]{:S(2)}, u32[]{:S(2)}) collective-permute-start(bf16[128,2048]{1,0:T(8,128)(2,1)} %get-tuple-element.34), channel_id=1, source_target_pairs={{65,64},{66,65},{67,66},{68,67},{69,68},{70,69},{71,70},{72,71},{7... | collective-permute-start | bytes 1572872 | tf_op jit(solution)/shard_map/ppermute | solution.py:262
  69.7 33.1 %copy-start.3 = (f32[4096,128]{1,0:T(8,128)S(1)}, f32[4096,128]{1,0:T(8,128)}, u32[]{:S(2)}) copy-start(f32[4096,128]{1,0:T(8,128)} %copy-done.2) | copy-start | bytes 6291460
  91.6 15.7 %collective-permute-start.10 = (f32[64,128]{1,0:T(8,128)S(1)}, f32[64,128]{1,0:T(8,128)S(1)}, u32[]{:S(2)}, u32[]{:S(2)}) collective-permute-start(f32[64,128]{1,0:T(8,128)S(1)} %get-tuple-element.38), channel_id=1, source_target_pairs={{0,1},{1,2},{2,3},{3,0},{4,5},{5,6},{6,7},{7,4},{8,9},{9,10},{10,1... | collective-permute-start | bytes 98312 | tf_op jit(solution)/shard_map/ppermute | solution.py:279
  92.4 16.8 %collective-permute-start.11 = (f32[64,128]{1,0:T(8,128)S(1)}, f32[64,128]{1,0:T(8,128)S(1)}, u32[]{:S(2)}, u32[]{:S(2)}) collective-permute-start(f32[64,128]{1,0:T(8,128)S(1)} %get-tuple-element.40), channel_id=1, source_target_pairs={{0,2},{1,3},{2,0},{3,1},{4,6},{5,7},{6,4},{7,5},{8,10},{9,11},{10,... | collective-permute-start | bytes 98312 | tf_op jit(solution)/shard_map/ppermute | solution.py:279
  92.4 16.8 %collective-permute-start.12 = (f32[64,128]{1,0:T(8,128)S(1)}, f32[64,128]{1,0:T(8,128)S(1)}, u32[]{:S(2)}, u32[]{:S(2)}) collective-permute-start(f32[64,128]{1,0:T(8,128)S(1)} %get-tuple-element.39), channel_id=1, source_target_pairs={{0,3},{1,0},{2,1},{3,2},{4,7},{5,4},{6,5},{7,6},{8,11},{9,8},{10,9... | collective-permute-start | bytes 98312 | tf_op jit(solution)/shard_map/ppermute | solution.py:279
  93.7 34.8 %collective-permute-start.5 = (bf16[128,4096]{1,0:T(8,128)(2,1)}, bf16[128,4096]{1,0:T(8,128)(2,1)S(1)}, u32[]{:S(2)}, u32[]{:S(2)}) collective-permute-start(bf16[128,4096]{1,0:T(8,128)(2,1)} %collective-permute-done.4), channel_id=1, source_target_pairs={{64,65},{65,66},{66,67},{67,68},{68,69},{69,70},{70,71},{71,72},{7... | collective-permute-start | bytes 3145736 | tf_op jit(solution)/shard_map/ppermute | solution.py:262
  100.9 27.6 %collective-permute-start.6 = (bf16[128,4096]{1,0:T(8,128)(2,1)}, bf16[128,4096]{1,0:T(8,128)(2,1)S(1)}, u32[]{:S(2)}, u32[]{:S(2)}) collective-permute-start(bf16[128,4096]{1,0:T(8,128)(2,1)} %collective-permute-done.4), channel_id=1, source_target_pairs={{65,64},{66,65},{67,66},{68,67},{69,68},{70,69},{71,70},{72,71},{7... | collective-permute-start | bytes 3145736 | tf_op jit(solution)/shard_map/ppermute | solution.py:262
  107.3 69.4 %collective-permute-start.9 = (bf16[128,5120]{1,0:T(8,128)(2,1)S(1)}, bf16[128,5120]{1,0:T(8,128)(2,1)S(1)}, u32[]{:S(2)}, u32[]{:S(2)}) collective-permute-start(bf16[128,5120]{1,0:T(8,128)(2,1)S(1)} %backward_tile.1), channel_id=1, source_target_pairs={{64,0},{65,1},{66,2},{67,3},{68,4},{69,5},{70,6},{71,7},{72,8},{73... | collective-permute-start | bytes 3932168 | tf_op jit(solution)/shard_map/ppermute | solution.py:262

commit v4 on v2

--- a/solution.py
+++ b/solution.py
@@ -178,6 +178,7 @@
         grad_ref[:, cols] = dot(probs_low, grads, TN).astype(BF16)
 
 
+COST = pl.CostEstimate(flops=2**20, bytes_accessed=2**20, transcendentals=0)
 SMEM = pl.BlockSpec(memory_space=pltpu.SMEM)
 VMEM = pl.BlockSpec(memory_space=pltpu.VMEM)
 
@@ -190,6 +191,7 @@
         out_specs=VMEM,
         scratch_shapes=[pltpu.VMEM((GROUP * TILE, TILE), F32)],
         compiler_params=pltpu.CompilerParams(vmem_limit_bytes=24 * 2**20),
+        cost_estimate=COST,
         name="forward_tile",
     )(rank, lengths, languages, table, qkv, down, up)
 
@@ -209,6 +211,7 @@
         in_specs=[SMEM] * 5 + [VMEM] * 4,
         out_specs=(VMEM,) * 6,
         compiler_params=pltpu.CompilerParams(vmem_limit_bytes=40 * 2**20),
+        cost_estimate=COST,
         name="prepare_tile",
     )(rank, lengths, languages, dest, table, qkv, slots, down, up)
 
@@ -223,6 +226,7 @@
         in_specs=[SMEM] * 2 + [VMEM] * 5,
         out_specs=(VMEM, VMEM),
         compiler_params=pltpu.CompilerParams(vmem_limit_bytes=24 * 2**20),
+        cost_estimate=COST,
         name="adapter_terms",
     )(rank, dest, attn, scaled, left, own, right)
 
@@ -235,6 +239,7 @@
         out_specs=VMEM,
         scratch_shapes=[pltpu.VMEM((TILE, QW), BF16)],
         compiler_params=pltpu.CompilerParams(vmem_limit_bytes=40 * 2**20),
+        cost_estimate=COST,
         name="backward_tile",
     )(rank, dest, qkv, left, mid, right, back, probs, down)
 
@@ -258,18 +263,9 @@
     return True
 
 
-def exchange(x, stride, count):
-    size = lax.axis_size("dp")
-    place = (lax.axis_index("dp") // stride) % count
-    total = lax.dynamic_index_in_dim(x, place, 0, keepdims=False).astype(F32)
-    for step in range(1, count):
-        piece = lax.dynamic_index_in_dim(x, (place + step) % count, 0, keepdims=False)
-        route = []
-        for t in range(size):
-            at = (t // stride) % count
-            route.append((t, t + ((at + step) % count - at) * stride))
-        total = total + lax.ppermute(piece, "dp", route).astype(F32)
-    return total
+def spread(x, groups):
+    pieces = lax.all_to_all(x, "dp", 0, 0, axis_index_groups=groups, tiled=True)
+    return jnp.sum(pieces.astype(F32), axis=0)
 
 
 def shards(
@@ -285,6 +281,7 @@
     from_left = shift(slots[2 * TILE :], [(later, 0, 1, anywhere)])
     from_right = shift(slots[:TILE], [(later, 0, -1, anywhere)])
     out = run_forward(rank_word, lengths, languages, lang_scale, qkv_a[0], down, up)
+    out, rank_word = lax.optimization_barrier((out, rank_word))
     hop = shift(out, [(every, 1, 0, anywhere)])
     probs, attn, scaled, to_left, own, to_right = run_prepare(
         rank_word, lengths, languages, destination, lang_scale, qkv_b[0], slots, down, up
@@ -292,10 +289,14 @@
     left = shift(to_right, [(every, 0, 1, anywhere)])
     right = shift(to_left, [(every, 0, -1, anywhere)])
     terms, back = run_terms(rank_word, destination, attn, scaled, left, own, right)
-    terms = exchange(terms.reshape(4, 1024, 128), 16, 4).astype(BF16)
-    terms = exchange(terms.reshape(4, 256, 128), 4, 4).astype(BF16)
-    terms = exchange(terms.reshape(4, 64, 128), 1, 4)
+    terms, back, from_left, from_right = lax.optimization_barrier(
+        (terms, back, from_left, from_right)
+    )
     terms, back, hop = lax.optimization_barrier((terms, back, hop))
+    planes = [[4 * k + z for k in range(size // 4)] for z in range(4)]
+    columns = [[4 * k + z for z in range(4)] for k in range(size // 4)]
+    terms = spread(terms.reshape(size // 4, 256, 128), planes)
+    terms = spread(terms.reshape(4, 64, 128), columns)
     grad_qkv = run_backward(
         rank_word, destination, qkv_b[0], from_left, slots[TILE : 2 * TILE], from_right, back,
         probs, down,

time: 199 us -> 172 us (0.86)
  starting transfers between devices: 49.9 us -> 40.8 us
  local copies, waits for them, and re-layouts: 23 us -> 14.4 us
  waiting for transfers between devices: 96.2 us -> 89.8 us
    ppermute x9 -> x0, starting transfers between devices: 17.7 us -> none  [exchange(): total = total + lax.ppermute(piece, 'dp', route).astype(F32)]
    ppermute x9 -> x0, waiting for transfers between devices: 12.7 us -> none  [exchange(): total = total + lax.ppermute(piece, 'dp', route).astype(F32)]
    all_to_all x0 -> x2, starting transfers between devices: none -> 11.9 us  [spread(): pieces = lax.all_to_all(x, 'dp', 0, 0, axis_index_groups=groups, tiled=True)]
    unnamed x39 -> x31, local copies, waits for them, and re-layouts: 18.3 us -> 10.2 us
    ppermute x8, waiting for transfers between devices: 83.5 us -> 89.8 us  [shift(): return lax.ppermute(x, AXES, route)]
    ppermute x8, starting transfers between devices: 32.2 us -> 29 us  [shift(): return lax.ppermute(x, AXES, route)]
    reduce_sum x0 -> x2, other arithmetic: none -> 2.65 us  [spread(): return jnp.sum(pieces.astype(F32), axis=0)]
    squeeze x3 -> x0, local copies, waits for them, and re-layouts: 2.34 us -> none  [exchange(): lax.dynamic_index_in_dim(x, (place + step) % count, 0, keepdims=False)]
  transfers between devices with their start and end apart: 17 -> 10, of which waited for: 6 -> 4; matrix products, arithmetic and copies ran while one was open for 6% -> 5% of each run, Pallas kernels for 6% -> 10%
where the time goes in v4:
time: 172 us
  waiting for transfers between devices  89.8 us (52%)
  starting transfers between devices  40.8 us (24%)
  Pallas kernels  17.9 us (10%)
  local copies, waits for them, and re-layouts  14.4 us (8%)
  other arithmetic  5.96 us (3%)
  between operations  2.81 us (2%)
    ppermute x8, waiting for transfers between devices, shift(): return lax.ppermute(x, AXES, route)  89.8 us
    ppermute x8, starting transfers between devices, shift(): return lax.ppermute(x, AXES, route)  29 us
    all_to_all x2, starting transfers between devices, spread(): pieces = lax.all_to_all(x, 'dp', 0, 0, axis_index_groups=groups, tiled=True)  11.9 us
    unnamed x31, local copies, waits for them, and re-layouts  10.2 us
    pallas_call x1, Pallas kernels, run_backward(): pl.pallas_call(backward_kernel, out_shape=jax.ShapeDtypeStruct((TILE, QW...  5.61 us
    pallas_call x1, Pallas kernels, run_prepare(): pl.pallas_call(prepare_kernel, out_shape=(jax.ShapeDtypeStruct((QW, TILE)...  5.42 us
    pallas_call x1, Pallas kernels, run_forward(): pl.pallas_call(forward_kernel, out_shape=jax.ShapeDtypeStruct((TILE, QW),...  4.64 us
    slice x1, local copies, waits for them, and re-layouts, shards(): slots[TILE:2 * TILE]  3.59 us
  transfers between devices with their start and end apart: 10, of which 4 were waited for; matrix products, arithmetic and copies ran while one was open for 5% of the time, Pallas kernels for 10%

profile of v4, /device:TPU:33, one launch (start us, length us, event | category | flops | bytes accessed | tf_op | source)
XLA Modules:
  0.0 171.7 jit_solution(2632258050283948468)
XLA Ops:
  0.7 3.6 %slice_bitcast_fusion = (bf16[128,4096]{1,0:T(8,128)(2,1)S(1)}, bf16[128,4096]{1,0:T(8,128)(2,1)}, bf16[128,4096]{1,0:T(8,128)(2,1)}) fusion(bf16[1,384,4096]{2,1,0:T(8,128)(2,1)} %param.11), kind=kLoop, calls=%fused_computation.2 | loop fusion | bytes 6291456 | tf_op jit(solution)/shard_map/slice | solution.py:301
  4.3 3.7 %collective-permute-start.2 = (bf16[128,4096]{1,0:T(8,128)(2,1)}, bf16[128,4096]{1,0:T(8,128)(2,1)}, u32[]{:S(2)}, u32[]{:S(2)}) collective-permute-start(bf16[128,4096]{1,0:T(8,128)(2,1)} %get-tuple-element.38), channel_id=1, source_target_pairs={{64,65},{65,66},{66,67},{67,68},{68,69},{69,70},{70,71},{71,72},{7... | collective-permute-start | bytes 3145736 | tf_op jit(solution)/shard_map/ppermute | solution.py:259
  7.9 2.7 %collective-permute-start.3 = (bf16[128,4096]{1,0:T(8,128)(2,1)}, bf16[128,4096]{1,0:T(8,128)(2,1)}, u32[]{:S(2)}, u32[]{:S(2)}) collective-permute-start(bf16[128,4096]{1,0:T(8,128)(2,1)} %get-tuple-element.39), channel_id=1, source_target_pairs={{65,64},{66,65},{67,66},{68,67},{69,68},{70,69},{71,70},{72,71},{7... | collective-permute-start | bytes 3145736 | tf_op jit(solution)/shard_map/ppermute | solution.py:259
  10.6 1.5 copy.15
  12.2 0.1 copy.16.lens_ref
  12.3 0.0 copy-start
  12.3 0.0 copy-done.10
  12.3 0.0 copy-done.9
  12.3 0.0 copy-start.4
  12.3 1.2 copy-done.4
  13.5 1.3 copy-done.6
  14.8 4.6 %forward_tile.1 = bf16[128,4096]{1,0:T(8,128)(2,1)S(1)} custom-call(s32[1]{0:T(128)} %bitcast.1.rank_ref, s32[2,64,8]{2,1,0:T(8,128)S(1)} %copy.16.lens_ref, s32[2,64]{1,0:T(2,128)S(1)} %copy-done.9, f32[102]{0:T(128)S(1)} %copy-done.10, bf16[128,5120]{1,0:T(8,128)(2,1)S(1)} %bitcast.29, bf16[4096,64]{1,0:T(8,128)(2,1)S(1)} %bitcast.21, ...), custom_call_target="tpu_custom_call" | custom-call | flops 1048576 | bytes 1048576 | tf_op jit(solution)/shard_map/forward_tile/pallas_call | solution.py:187
  19.4 9.0 %collective-permute-start.4 = (bf16[128,4096]{1,0:T(8,128)(2,1)S(1)}, bf16[128,4096]{1,0:T(8,128)(2,1)S(1)}, u32[]{:S(2)}, u32[]{:S(2)}) collective-permute-start(bf16[128,4096]{1,0:T(8,128)(2,1)S(1)} %forward_tile.1), channel_id=1, source_target_pairs={{0,64},{1,65},{2,66},{3,67},{4,68},{5,69},{6,70},{7,71},{8,72},{9,... | collective-permute-start | bytes 3145736 | tf_op jit(solution)/shard_map/ppermute | solution.py:259
  28.5 5.4 %prepare_tile.1 = (f32[4096,128]{1,0:T(8,128)S(1)}, bf16[128,4096]{1,0:T(8,128)(2,1)S(1)}, bf16[384,4096]{1,0:T(8,128)(2,1)S(1)}, bf16[128,128]{1,0:T(8,128)(2,1...) custom-call(s32[1]{0:T(128)} %bitcast.1.rank_ref, s32[2,64,8]{2,1,0:T(8,128)S(1)} %copy.16.lens_ref, ...), custom_call_target="tpu_custom_call" | custom-call | flops 1048576 | bytes 1048576 | tf_op jit(solution)/shard_map/prepare_tile/pallas_call | solution.py:201
  34.0 0.0 copy-start.2
  34.0 1.9 %collective-permute-start = (bf16[128,128]{1,0:T(8,128)(2,1)S(1)}, bf16[128,128]{1,0:T(8,128)(2,1)S(1)}, u32[]{:S(2)}, u32[]{:S(2)}) collective-permute-start(bf16[128,128]{1,0:T(8,128)(2,1)S(1)} %get-tuple-element.23), channel_id=1, source_target_pairs={{0,1},{1,2},{2,3},{3,4},{4,5},{5,6},{6,7},{7,8},{8,9},{9,10},{10,1... | collective-permute-start | bytes 98312 | tf_op jit(solution)/shard_map/ppermute | solution.py:259
  35.9 3.4 %collective-permute-start.1 = (bf16[128,128]{1,0:T(8,128)(2,1)S(1)}, bf16[128,128]{1,0:T(8,128)(2,1)S(1)}, u32[]{:S(2)}, u32[]{:S(2)}) collective-permute-start(bf16[128,128]{1,0:T(8,128)(2,1)S(1)} %get-tuple-element.25), channel_id=1, source_target_pairs={{1,0},{2,1},{3,2},{4,3},{5,4},{6,5},{7,6},{8,7},{9,8},{10,9},{11,1... | collective-permute-start | bytes 98312 | tf_op jit(solution)/shard_map/ppermute | solution.py:259
  39.3 1.2 collective-permute-done.left_ref
  40.5 15.6 %collective-permute-done.1.right_ref = bf16[128,128]{1,0:T(8,128)(2,1)S(1)} collective-permute-done((bf16[128,128]{1,0:T(8,128)(2,1)S(1)}, bf16[128,128]{1,0:T(8,128)(2,1)S(1)}, u32[]{:S(2)}, u32[]{:S(2)}) %collective-permute-start.1) | collective-permute-done | bytes 32800 | tf_op jit(solution)/shard_map/ppermute | solution.py:259
  56.1 2.3 %adapter_terms.1 = (bf16[4096,128]{1,0:T(8,128)(2,1)S(1)}, bf16[128,128]{1,0:T(8,128)(2,1)S(1)}) custom-call(s32[1]{0:T(128)} %bitcast.1.rank_ref, s32[2,64]{1,0:T(2,128)S(1)} %copy-done.8, bf16[128,4096]{1,0:T(8,128)(2,1)S(1)} %get-tuple-element.21.attn_ref, bf16[384,4096]{1,0:T(8,128)(2,1)S(1)} %get-tuple-element.22.scaled_ref, ...), custom_call_target="tpu_custom_call" | custom-call | flops 1048576 | bytes 1048576 | tf_op jit(solution)/shard_map/adapter_terms/pallas_call | solution.py:220
  58.3 0.0 copy-done.2
  58.3 0.0 copy-start.7
  58.3 1.0 copy-done.7
  59.3 0.0 collective-permute-done.2.left_ref
  59.3 0.0 collective-permute-done.3.right_ref
  59.3 0.0 collective-permute-done.4
  59.3 1.0 copy-done.11
  60.3 6.8 %all-to-all-start = ((bf16[16,256,128]{2,1,0:T(8,128)(2,1)}), bf16[16,256,128]{2,1,0:T(8,128)(2,1)}, u32[]{:S(2)}, u32[]{:S(2)}) async-start(bf16[16,256,128]{2,1,0:T(8,128)(2,1)} %bitcast.30), calls=%async_computation | async-start | bytes 2097152 | tf_op jit(solution)/shard_map/all_to_all | solution.py:267
  67.2 0.6 constant_dynamic-slice_fusion.2
  69.6 2.5 %collective-permute-start.5 = (bf16[128,4096]{1,0:T(8,128)(2,1)}, bf16[128,4096]{1,0:T(8,128)(2,1)}, u32[]{:S(2)}, u32[]{:S(2)}) collective-permute-start(bf16[128,4096]{1,0:T(8,128)(2,1)} %copy-done.11), channel_id=1, source_target_pairs={{64,65},{65,66},{66,67},{67,68},{68,69},{69,70},{70,71},{71,72},{7... | collective-permute-start | bytes 3145736 | tf_op jit(solution)/shard_map/ppermute | solution.py:259
  72.1 3.9 %collective-permute-start.6 = (bf16[128,4096]{1,0:T(8,128)(2,1)}, bf16[128,4096]{1,0:T(8,128)(2,1)}, u32[]{:S(2)}, u32[]{:S(2)}) collective-permute-start(bf16[128,4096]{1,0:T(8,128)(2,1)} %copy-done.11), channel_id=1, source_target_pairs={{65,64},{66,65},{67,66},{68,67},{69,68},{70,69},{71,70},{72,71},{7... | collective-permute-start | bytes 3145736 | tf_op jit(solution)/shard_map/ppermute | solution.py:259
  76.1 0.0 copy-start.3
  76.1 1.6 copy-done.3
  77.7 5.6 %backward_tile.1 = bf16[128,5120]{1,0:T(8,128)(2,1)} custom-call(s32[1]{0:T(128)} %bitcast.1.rank_ref, s32[2,64]{1,0:T(2,128)S(1)} %copy-done.8, bf16[128,5120]{1,0:T(8,128)(2,1)S(1)} %bitcast.26, bf16[128,4096]{1,0:T(8,128)(2,1)} %collective-permute-done.2.left_ref, bf16[128,4096]{1,0:T(8,128)(2,1)S(1)} %get-tuple-element.37.mid_ref, ...), custom_call_target="tpu_custom_call" | custom-call | flops 1048576 | bytes 1048576 | tf_op jit(solution)/shard_map/backward_tile/pallas_call | solution.py:235
  83.3 1.9 %collective-permute-start.7 = (bf16[128,5120]{1,0:T(8,128)(2,1)}, bf16[128,5120]{1,0:T(8,128)(2,1)}, u32[]{:S(2)}, u32[]{:S(2)}) collective-permute-start(bf16[128,5120]{1,0:T(8,128)(2,1)} %backward_tile.1), channel_id=1, source_target_pairs={{64,0},{65,1},{66,2},{67,3},{68,4},{69,5},{70,6},{71,7},{72,8},{73... | collective-permute-start | bytes 3932168 | tf_op jit(solution)/shard_map/ppermute | solution.py:259
  85.2 0.1 broadcast_select_fusion.1
  85.3 0.0 all-to-all-done
  85.3 2.0 %convert_reduce_fusion = f32[256,128]{1,0:T(8,128)} fusion(bf16[16,256,128]{2,1,0:T(8,128)(2,1)} %all-to-all-done), kind=kLoop, calls=%fused_computation.1 | loop fusion | flops 1015808 | bytes 1179648 | tf_op jit(solution)/shard_map/reduce_sum | solution.py:268
  87.3 5.1 %all-to-all-start.1 = ((f32[4,64,128]{2,1,0:T(8,128)}), f32[4,64,128]{2,1,0:T(8,128)S(1)}, u32[]{:S(2)}, u32[]{:S(2)}) async-start(f32[4,64,128]{2,1,0:T(8,128)} %bitcast.15), calls=%async_computation.1 | async-start | bytes 262144 | tf_op jit(solution)/shard_map/all_to_all | solution.py:267
  92.4 0.0 collective-permute-done.5
  92.4 1.3 broadcast_select_fusion.2
  93.7 7.4 %collective-permute-done.6 = bf16[128,4096]{1,0:T(8,128)(2,1)} collective-permute-done((bf16[128,4096]{1,0:T(8,128)(2,1)}, bf16[128,4096]{1,0:T(8,128)(2,1)}, u32[]{:S(2)}, u32[]{:S(2)}) %collective-permute-start.6) | collective-permute-done | bytes 1048608 | tf_op jit(solution)/shard_map/ppermute | solution.py:259
  101.1 0.1 broadcast_select_fusion
  101.1 1.9 %maximum_bitcast_fusion = bf16[1,384,4096]{2,1,0:T(8,128)(2,1)} fusion(bf16[128,4096]{1,0:T(8,128)(2,1)S(1)} %broadcast_select_fusion, bf16[128,4096]{1,0:T(8,128)(2,1)S(1)} %broadcast_select_fusion.1, bf16[128,4096]{1,0:T(8,128)(2,1)S(1)} %broadcast_select_fusion.2), kind=kLoop, calls=%fused_computation | loop fusion | flops 9437184 | bytes 6291456 | tf_op jit(solution)/shard_map/broadcast_in_dim | solution.py:314
  103.0 0.0 all-to-all-done.1
  103.0 0.6 reduce_sum.19
  103.6 65.6 %collective-permute-done.7 = bf16[128,5120]{1,0:T(8,128)(2,1)} collective-permute-done((bf16[128,5120]{1,0:T(8,128)(2,1)}, bf16[128,5120]{1,0:T(8,128)(2,1)}, u32[]{:S(2)}, u32[]{:S(2)}) %collective-permute-start.7) | collective-permute-done | bytes 1310752 | tf_op jit(solution)/shard_map/ppermute | solution.py:259
  169.2 2.5 %copy.19 = bf16[1,128,5120]{2,1,0:T(8,128)(2,1)} copy(bf16[1,128,5120]{2,1,0:T(8,128)(2,1)} %bitcast.13) | data formatting | bytes 2621440
  (17 shorter events, 0.0 us)
Async XLA Ops:
  0.6 11.5 %copy-start.13 = (s32[2,64,8]{1,2,0:T(8,128)S(1)}, s32[2,64,8]{1,2,0:T(8,128)}, u32[]{:S(2)}) copy-start(s32[2,64,8]{1,2,0:T(8,128)} %param.16) | copy-start | bytes 12292
  0.6 11.6 %copy-start.10 = (f32[102]{0:T(128)S(1)}, f32[102]{0:T(128)}, u32[]{:S(2)}) copy-start(f32[102]{0:T(128)} %table_ref.3) | copy-start | bytes 1228
  0.7 11.6 %copy-start.9 = (s32[2,64]{1,0:T(2,128)S(1)}, s32[2,64]{1,0:T(2,128)}, u32[]{:S(2)}) copy-start(s32[2,64]{1,0:T(2,128)} %langs_ref.3) | copy-start | bytes 1540
  4.2 24.2 %copy-start.1 = (bf16[1,128,5120]{2,1,0:T(8,128)(2,1)S(1)}, bf16[1,128,5120]{2,1,0:T(8,128)(2,1)}, u32[]{:S(2)}) copy-start(bf16[1,128,5120]{2,1,0:T(8,128)(2,1)} %param.10) | copy-start | bytes 3932164
  4.3 24.2 %copy-start.8 = (s32[2,64]{1,0:T(2,128)S(1)}, s32[2,64]{1,0:T(2,128)}, u32[]{:S(2)}) copy-start(s32[2,64]{1,0:T(2,128)} %dest_ref.5) | copy-start | bytes 1540
  4.3 55.1 %collective-permute-start.2 = (bf16[128,4096]{1,0:T(8,128)(2,1)}, bf16[128,4096]{1,0:T(8,128)(2,1)}, u32[]{:S(2)}, u32[]{:S(2)}) collective-permute-start(bf16[128,4096]{1,0:T(8,128)(2,1)} %get-tuple-element.38), channel_id=1, source_target_pairs={{64,65},{65,66},{66,67},{67,68},{68,69},{69,70},{70,71},{71,72},{7... | collective-permute-start | bytes 3145736 | tf_op jit(solution)/shard_map/ppermute | solution.py:259
  7.9 51.4 %collective-permute-start.3 = (bf16[128,4096]{1,0:T(8,128)(2,1)}, bf16[128,4096]{1,0:T(8,128)(2,1)}, u32[]{:S(2)}, u32[]{:S(2)}) collective-permute-start(bf16[128,4096]{1,0:T(8,128)(2,1)} %get-tuple-element.39), channel_id=1, source_target_pairs={{65,64},{66,65},{67,66},{68,67},{69,68},{70,69},{71,70},{72,71},{7... | collective-permute-start | bytes 3145736 | tf_op jit(solution)/shard_map/ppermute | solution.py:259
  12.3 16.3 %copy-start = (bf16[1,384,4096]{2,1,0:T(8,128)(2,1)S(1)}, bf16[1,384,4096]{2,1,0:T(8,128)(2,1)}, u32[]{:S(2)}) copy-start(bf16[1,384,4096]{2,1,0:T(8,128)(2,1)} %param.11) | copy-start | bytes 9437188
  12.3 1.2 copy-start.4
  13.5 1.3 copy-start.6
  14.8 13.7 %copy-start.5 = (bf16[1,64,4096]{2,1,0:T(8,128)(2,1)S(1)}, bf16[1,64,4096]{2,1,0:T(8,128)(2,1)}, u32[]{:S(2)}) copy-start(bf16[1,64,4096]{2,1,0:T(8,128)(2,1)} %param.13) | copy-start | bytes 1572868
  19.4 39.9 %collective-permute-start.4 = (bf16[128,4096]{1,0:T(8,128)(2,1)S(1)}, bf16[128,4096]{1,0:T(8,128)(2,1)S(1)}, u32[]{:S(2)}, u32[]{:S(2)}) collective-permute-start(bf16[128,4096]{1,0:T(8,128)(2,1)S(1)} %forward_tile.1), channel_id=1, source_target_pairs={{0,64},{1,65},{2,66},{3,67},{4,68},{5,69},{6,70},{7,71},{8,72},{9,... | collective-permute-start | bytes 3145736 | tf_op jit(solution)/shard_map/ppermute | solution.py:259
  34.0 24.4 %copy-start.2 = (f32[4096,128]{1,0:T(8,128)}, f32[4096,128]{1,0:T(8,128)S(1)}, u32[]{:S(2)}) copy-start(f32[4096,128]{1,0:T(8,128)S(1)} %get-tuple-element.35.probs_ref) | copy-start | bytes 6291460
  34.0 6.5 %collective-permute-start = (bf16[128,128]{1,0:T(8,128)(2,1)S(1)}, bf16[128,128]{1,0:T(8,128)(2,1)S(1)}, u32[]{:S(2)}, u32[]{:S(2)}) collective-permute-start(bf16[128,128]{1,0:T(8,128)(2,1)S(1)} %get-tuple-element.23), channel_id=1, source_target_pairs={{0,1},{1,2},{2,3},{3,4},{4,5},{5,6},{6,7},{7,8},{8,9},{9,10},{10,1... | collective-permute-start | bytes 98312 | tf_op jit(solution)/shard_map/ppermute | solution.py:259
  35.9 20.2 %collective-permute-start.1 = (bf16[128,128]{1,0:T(8,128)(2,1)S(1)}, bf16[128,128]{1,0:T(8,128)(2,1)S(1)}, u32[]{:S(2)}, u32[]{:S(2)}) collective-permute-start(bf16[128,128]{1,0:T(8,128)(2,1)S(1)} %get-tuple-element.25), channel_id=1, source_target_pairs={{1,0},{2,1},{3,2},{4,3},{5,4},{6,5},{7,6},{8,7},{9,8},{10,9},{11,1... | collective-permute-start | bytes 98312 | tf_op jit(solution)/shard_map/ppermute | solution.py:259
  56.1 11.1 %slice-start = ((s32[2,64]{1,0:T(2,128)}), s32[1,64]{1,0:T(1,128)S(1)}, s32[]{:S(2)}) async-start(s32[2,64]{1,0:T(2,128)} %dest_ref.5), calls=%async_computation.2 | async-start | bytes 1024 | tf_op jit(solution)/shard_map/slice | solution.py:307
  58.3 1.0 copy-start.7
  59.3 1.0 copy-start.11
  60.3 24.9 %all-to-all-start = ((bf16[16,256,128]{2,1,0:T(8,128)(2,1)}), bf16[16,256,128]{2,1,0:T(8,128)(2,1)}, u32[]{:S(2)}, u32[]{:S(2)}) async-start(bf16[16,256,128]{2,1,0:T(8,128)(2,1)} %bitcast.30), calls=%async_computation | async-start | bytes 2097152 | tf_op jit(solution)/shard_map/all_to_all | solution.py:267
  69.6 22.7 %collective-permute-start.5 = (bf16[128,4096]{1,0:T(8,128)(2,1)}, bf16[128,4096]{1,0:T(8,128)(2,1)}, u32[]{:S(2)}, u32[]{:S(2)}) collective-permute-start(bf16[128,4096]{1,0:T(8,128)(2,1)} %copy-done.11), channel_id=1, source_target_pairs={{64,65},{65,66},{66,67},{67,68},{68,69},{69,70},{70,71},{71,72},{7... | collective-permute-start | bytes 3145736 | tf_op jit(solution)/shard_map/ppermute | solution.py:259
  72.1 29.0 %collective-permute-start.6 = (bf16[128,4096]{1,0:T(8,128)(2,1)}, bf16[128,4096]{1,0:T(8,128)(2,1)}, u32[]{:S(2)}, u32[]{:S(2)}) collective-permute-start(bf16[128,4096]{1,0:T(8,128)(2,1)} %copy-done.11), channel_id=1, source_target_pairs={{65,64},{66,65},{67,66},{68,67},{69,68},{70,69},{71,70},{72,71},{7... | collective-permute-start | bytes 3145736 | tf_op jit(solution)/shard_map/ppermute | solution.py:259
  76.1 1.6 copy-start.3
  77.7 7.5 %copy-start.12 = (bf16[128,4096]{1,0:T(8,128)(2,1)S(1)}, bf16[128,4096]{1,0:T(8,128)(2,1)}, u32[]{:S(2)}) copy-start(bf16[128,4096]{1,0:T(8,128)(2,1)} %copy-done.11) | copy-start | bytes 3145732
  83.3 86.0 %collective-permute-start.7 = (bf16[128,5120]{1,0:T(8,128)(2,1)}, bf16[128,5120]{1,0:T(8,128)(2,1)}, u32[]{:S(2)}, u32[]{:S(2)}) collective-permute-start(bf16[128,5120]{1,0:T(8,128)(2,1)} %backward_tile.1), channel_id=1, source_target_pairs={{64,0},{65,1},{66,2},{67,3},{68,4},{69,5},{70,6},{71,7},{72,8},{73... | collective-permute-start | bytes 3932168 | tf_op jit(solution)/shard_map/ppermute | solution.py:259
  87.3 15.7 %all-to-all-start.1 = ((f32[4,64,128]{2,1,0:T(8,128)}), f32[4,64,128]{2,1,0:T(8,128)S(1)}, u32[]{:S(2)}, u32[]{:S(2)}) async-start(f32[4,64,128]{2,1,0:T(8,128)} %bitcast.15), calls=%async_computation.1 | async-start | bytes 262144 | tf_op jit(solution)/shard_map/all_to_all | solution.py:267

commit v5 on v4

v5 whole, which is shorter than its diff:
```python
import functools
import math

import jax
import jax.numpy as jnp
from jax import lax
from jax.experimental import pallas as pl
from jax.experimental.pallas import tpu as pltpu
from jax.sharding import PartitionSpec as P

HEADS = 32
KV = 4
GROUP = HEADS // KV
HEAD_DIM = 128
TILE = 128
SEGS = 8
RANK = 64
QW = HEADS * HEAD_DIM
KW = KV * HEAD_DIM
GW = GROUP * HEAD_DIM
SCALE = 1.0 / math.sqrt(HEAD_DIM)
RUN = 4
AXES = ("section", "dp")
BF16 = jnp.bfloat16
F32 = jnp.float32


def dot(a, b, dims):
    return lax.dot_general(a, b, (dims, ((), ())), preferred_element_type=F32)


NN = ((1,), (0,))
NT = ((1,), (1,))
TN = ((0,), (0,))


def mask_bias(lens_ref, m, rank):
    shape = (TILE, TILE)
    row = lax.broadcasted_iota(jnp.int32, shape, 0)
    col = lax.broadcasted_iota(jnp.int32, shape, 1)
    seg_row = jnp.zeros(shape, jnp.int32)
    seg_col = jnp.zeros(shape, jnp.int32)
    end = jnp.int32(0)
    for k in range(SEGS):
        end = end + lens_ref[m, rank, k]
        seg_row = seg_row + (row >= end).astype(jnp.int32)
        seg_col = seg_col + (col >= end).astype(jnp.int32)
    allowed = (seg_row == seg_col) & (row >= col)
    return jnp.where(allowed, 0.0, -1e30).astype(F32)


def stacked(ref, base):
    return jnp.concatenate(
        [ref[:, base + h * HEAD_DIM : base + (h + 1) * HEAD_DIM] for h in range(GROUP)], axis=0
    )


def softmax(scores, bias):
    masked = scores + bias
    top = jnp.max(masked, axis=-1, keepdims=True)
    weights = jnp.exp2((masked - top) * (SCALE * math.log2(math.e)))
    return weights * (1.0 / jnp.sum(weights, axis=-1, keepdims=True))


def attend_group(j, qkv_ref, bias, probs_ref):
    keys = qkv_ref[:, QW + j * HEAD_DIM : QW + (j + 1) * HEAD_DIM]
    values = qkv_ref[:, QW + KW + j * HEAD_DIM : QW + KW + (j + 1) * HEAD_DIM]
    queries = stacked(qkv_ref, j * GW)
    probs_ref[...] = dot(queries, keys, NT)
    lows = []
    for h in range(GROUP):
        rows = slice(h * TILE, (h + 1) * TILE)
        probs = softmax(probs_ref[rows, :], bias)
        probs_ref[rows, :] = probs
        lows.append(probs.astype(BF16))
    probs_low = jnp.concatenate(lows, axis=0)
    attn = dot(probs_low, values, NN).astype(BF16)
    return queries, keys, values, probs_low, attn


def forward_kernel(rank_ref, lens_ref, langs_ref, table_ref, qkv_ref, down_ref, up_ref, out_ref, probs_ref):
    rank = rank_ref[0]
    rate = table_ref[langs_ref[0, rank]]
    bias = mask_bias(lens_ref, 0, rank)
    low = jnp.zeros((TILE, RANK), F32)
    for j in range(KV):
        attn = attend_group(j, qkv_ref, bias, probs_ref)[-1]
        for h in range(GROUP):
            cols = slice(j * GW + h * HEAD_DIM, j * GW + (h + 1) * HEAD_DIM)
            out_ref[:, cols] = attn[h * TILE : (h + 1) * TILE]
        low = low + dot(out_ref[:, j * GW : (j + 1) * GW], down_ref[j * GW : (j + 1) * GW, :], NN)
    low = low.astype(BF16)
    for c in range(0, QW, 512):
        lift = dot(low, up_ref[:, c : c + 512], NN)
        out_ref[:, c : c + 512] = (out_ref[:, c : c + 512].astype(F32) + rate * lift).astype(BF16)


def slot_rate(k, rank, tiles, langs_ref, dest_ref, table_ref):
    tile = rank + (k - 1)
    near = jnp.clip(tile, 0, tiles - 1)
    live = (tile == near) & (dest_ref[1, near] == rank)
    return jnp.where(live, table_ref[langs_ref[1, near]], 0.0)


def prepare_kernel(
    place_ref, lens_ref, langs_ref, dest_ref, table_ref, qkv_ref, slots_ref, down_ref, up_ref,
    probs_ref, attn_ref, low_ref, left_ref, own_ref, right_ref,
):
    rank = place_ref[0]
    tiles = lens_ref.shape[1]
    bias = mask_bias(lens_ref, 1, rank)
    low = jnp.zeros((TILE, RANK), F32)
    for j in range(KV):
        block = slice(j * GW, (j + 1) * GW)
        attn = attend_group(j, qkv_ref, bias, probs_ref.at[block, :])[-1]
        for h in range(GROUP):
            cols = slice(j * GW + h * HEAD_DIM, j * GW + (h + 1) * HEAD_DIM)
            attn_ref[:, cols] = attn[h * TILE : (h + 1) * TILE]
        low = low + dot(attn_ref[:, block], down_ref[block, :], NN)
    low_ref[...] = low.astype(BF16)

    @pl.when(place_ref[1] == 0)
    def _():
        for k, out_ref in enumerate((left_ref, own_ref, right_ref)):
            rate = slot_rate(k, rank, tiles, langs_ref, dest_ref, table_ref)
            back = jnp.zeros((TILE, RANK), F32)
            for c in range(0, QW, 512):
                cols = slice(c, c + 512)
                grad = slots_ref[k * TILE : (k + 1) * TILE, cols]
                scaled = (rate * grad.astype(F32)).astype(BF16)
                back = back + dot(scaled, up_ref[:, cols], NT)
            out_ref[...] = jnp.concatenate([low, back], axis=1).astype(BF16)

    @pl.when(place_ref[1] != 0)
    def _():
        for out_ref in (left_ref, own_ref, right_ref):
            out_ref[...] = jnp.zeros(out_ref.shape, BF16)


def terms_kernel(
    place_ref, langs_ref, dest_ref, table_ref, attn_ref, slots_ref, left_ref, own_ref, right_ref,
    scaled_ref, back_ref, low_ref, terms_ref, slot_scaled_ref,
):
    rank = place_ref[0]
    tiles = dest_ref.shape[1]

    @pl.when(place_ref[1] == 0)
    def _():
        went = dest_ref[1, rank] - rank
        back = jnp.where(went < 0, left_ref[...], jnp.where(went > 0, right_ref[...], own_ref[...]))
        lows = jnp.concatenate([left_ref[...], own_ref[...], right_ref[...]], axis=0)
        for c in range(0, QW, 512):
            cols = slice(c, c + 512)
            for k in range(3):
                rows = slice(k * TILE, (k + 1) * TILE)
                rate = slot_rate(k, rank, tiles, langs_ref, dest_ref, table_ref)
                slot_scaled_ref[rows, :] = (rate * slots_ref[rows, cols].astype(F32)).astype(BF16)
            one = dot(attn_ref[:, cols], back, TN)
            two = dot(slot_scaled_ref[...], lows, TN)
            terms = jnp.concatenate([one[:, RANK:], two[:, :RANK]], axis=1)
            terms_ref[cols, :] = terms.astype(terms_ref.dtype)

    @pl.when(place_ref[1] != 0)
    def _():
        for c in range(0, QW, 512):
            cols = slice(c, c + 512)
            one = dot(attn_ref[:, cols], back_ref[...], TN)
            two = dot(scaled_ref[:, cols], low_ref[...], TN)
            terms_ref[cols, :] = jnp.concatenate([one, two], axis=1).astype(terms_ref.dtype)


def backward_kernel(
    place_ref, langs_ref, dest_ref, table_ref, qkv_ref, left_ref, right_ref, last_left_ref,
    last_right_ref, slots_ref, probs_ref, down_ref, up_ref, grad_ref, scaled_ref, back_ref,
    gattn_ref,
):
    rank = place_ref[0]
    rate = table_ref[langs_ref[1, rank]]
    went = dest_ref[1, rank] - rank
    last = place_ref[1] == place_ref[2] - 1

    def chosen():
        back = jnp.zeros((TILE, RANK), F32)
        for c in range(0, QW, 512):
            cols = slice(c, c + 512)
            left = jnp.where(last, last_left_ref[:, cols], left_ref[:, cols])
            right = jnp.where(last, last_right_ref[:, cols], right_ref[:, cols])
            mid = slots_ref[TILE : 2 * TILE, cols]
            grad = jnp.where(went < 0, left, jnp.where(went > 0, right, mid))
            gattn_ref[:, cols] = grad
            scaled = (rate * grad.astype(F32)).astype(BF16)
            scaled_ref[:, cols] = scaled
            back = back + dot(scaled, up_ref[:, cols], NT)
        return back.astype(BF16)

    @pl.when(place_ref[1] != 0)
    def _():
        back = chosen()
        back_ref[...] = back
        for j in range(KV):
            block = slice(j * GW, (j + 1) * GW)
            gattn = gattn_ref[:, block].astype(F32) + dot(back, down_ref[block, :], NT)
            gattn_ref[:, block] = gattn.astype(BF16)
            queries = stacked(qkv_ref, j * GW)
            keys = qkv_ref[:, QW + j * HEAD_DIM : QW + (j + 1) * HEAD_DIM]
            values = qkv_ref[:, QW + KW + j * HEAD_DIM : QW + KW + (j + 1) * HEAD_DIM]
            grads = stacked(gattn_ref, j * GW)
            grad_probs = dot(grads, values, NT)
            lows, scores = [], []
            for h in range(GROUP):
                probs = probs_ref[j * GW + h * TILE : j * GW + (h + 1) * TILE, :]
                lows.append(probs.astype(BF16))
                weighed = probs * grad_probs[h * TILE : (h + 1) * TILE]
                delta = jnp.sum(weighed, axis=-1, keepdims=True)
                scores.append(((weighed - probs * delta) * SCALE).astype(BF16))
            probs_low = jnp.concatenate(lows, axis=0)
            grad_scores = jnp.concatenate(scores, axis=0)
            grad_queries = dot(grad_scores, keys, NN).astype(BF16)
            for h in range(GROUP):
                cols = slice(j * GW + h * HEAD_DIM, j * GW + (h + 1) * HEAD_DIM)
                grad_ref[:, cols] = grad_queries[h * TILE : (h + 1) * TILE]
            cols = slice(QW + j * HEAD_DIM, QW + (j + 1) * HEAD_DIM)
            grad_ref[:, cols] = dot(grad_scores, queries, TN).astype(BF16)
            cols = slice(QW + KW + j * HEAD_DIM, QW + KW + (j + 1) * HEAD_DIM)
            grad_ref[:, cols] = dot(probs_low, grads, TN).astype(BF16)

    @pl.when(place_ref[1] == 0)
    def _():
        grad_ref[...] = jnp.zeros(grad_ref.shape, BF16)
        scaled_ref[...] = jnp.zeros(scaled_ref.shape, BF16)
        back_ref[...] = jnp.zeros(back_ref.shape, BF16)


COST = pl.CostEstimate(flops=2**20, bytes_accessed=2**20, transcendentals=0)
SMEM = pl.BlockSpec(memory_space=pltpu.SMEM)
VMEM = pl.BlockSpec(memory_space=pltpu.VMEM)


def run_forward(rank, lengths, languages, table, qkv, down, up):
    return pl.pallas_call(
        forward_kernel,
        out_shape=jax.ShapeDtypeStruct((TILE, QW), BF16),
        in_specs=[SMEM] * 4 + [VMEM] * 3,
        out_specs=VMEM,
        scratch_shapes=[pltpu.VMEM((GROUP * TILE, TILE), F32)],
        compiler_params=pltpu.CompilerParams(vmem_limit_bytes=24 * 2**20),
        cost_estimate=COST,
        name="forward_tile",
    )(rank, lengths, languages, table, qkv, down, up)


def run_prepare(place, lengths, languages, dest, table, qkv, slots, down, up):
    message = jax.ShapeDtypeStruct((TILE, 2 * RANK), BF16)
    return pl.pallas_call(
        prepare_kernel,
        out_shape=(
            jax.ShapeDtypeStruct((QW, TILE), F32),
            jax.ShapeDtypeStruct((TILE, QW), BF16),
            jax.ShapeDtypeStruct((TILE, RANK), BF16),
            message,
            message,
            message,
        ),
        in_specs=[SMEM] * 5 + [VMEM] * 4,
        out_specs=(VMEM,) * 6,
        compiler_params=pltpu.CompilerParams(vmem_limit_bytes=40 * 2**20),
        cost_estimate=COST,
        name="prepare_tile",
    )(place, lengths, languages, dest, table, qkv, slots, down, up)


def run_terms(place, languages, dest, table, attn, slots, left, own, right, scaled, back, low):
    return pl.pallas_call(
        terms_kernel,
        out_shape=jax.ShapeDtypeStruct((QW, 2 * RANK), BF16),
        in_specs=[SMEM] * 4 + [VMEM] * 8,
        out_specs=VMEM,
        scratch_shapes=[pltpu.VMEM((3 * TILE, 512), BF16)],
        compiler_params=pltpu.CompilerParams(vmem_limit_bytes=40 * 2**20),
        cost_estimate=COST,
        name="adapter_terms",
    )(place, languages, dest, table, attn, slots, left, own, right, scaled, back, low)


def run_backward(place, languages, dest, table, qkv, moved, slots, probs, down, up):
    return pl.pallas_call(
        backward_kernel,
        out_shape=(
            jax.ShapeDtypeStruct((TILE, QW + 2 * KW), BF16),
            jax.ShapeDtypeStruct((TILE, QW), BF16),
            jax.ShapeDtypeStruct((TILE, RANK), BF16),
        ),
        in_specs=[SMEM] * 4 + [VMEM] * 9,
        out_specs=(VMEM,) * 3,
        scratch_shapes=[pltpu.VMEM((TILE, QW), BF16)],
        compiler_params=pltpu.CompilerParams(vmem_limit_bytes=48 * 2**20),
        cost_estimate=COST,
        name="backward_tile",
    )(place, languages, dest, table, qkv, *moved, slots, probs, down, up)


def sections():
    return lax.axis_size("section")


def shift(x, moves):
    size = lax.axis_size("dp")
    route = []
    for s_list, up, step, keep in moves:
        for s in s_list:
            for t in range(size):
                if 0 <= s + up < sections() and 0 <= t + step < size and keep(t):
                    route.append((s * size + t, (s + up) * size + t + step))
    return lax.ppermute(x, AXES, route)


def anywhere(t):
    return True


def run_start(t):
    return t % RUN == 0


def run_end(t):
    return t % RUN == RUN - 1


def not_run_start(t):
    return t % RUN != 0


def not_run_end(t):
    return t % RUN != RUN - 1


def spread(x, groups):
    pieces = lax.all_to_all(x, "dp", 0, 0, axis_index_groups=groups, tiled=True)
    return jnp.sum(pieces.astype(F32), axis=0)


def shards(
    qkv_a, qkv_b, slot_grad_b, adapter_down, adapter_up, lang_scale, languages, lengths, destination
):
    rank, size = lax.axis_index("dp"), lax.axis_size("dp")
    section, last = lax.axis_index("section"), sections() - 1
    place = jnp.stack([rank, section, jnp.int32(sections())]).astype(jnp.int32)
    down, up = adapter_down[0], adapter_up[0]
    slots = slot_grad_b[0]
    every, early = range(sections()), range(1, last)
    to_up, to_down = slots[2 * TILE :], slots[:TILE]
    from_left = shift(to_up, [(early, 0, 1, anywhere)])
    from_right = shift(to_down, [(early, 0, -1, anywhere)])
    out = run_forward(place, lengths, languages, lang_scale, qkv_a[0], down, up)
    out, place = lax.optimization_barrier((out, place))
    near = shift(out, [([0, 2], 1, 0, anywhere)])
    far = shift(out, [([1], 1, 0, anywhere)])
    probs, attn, low, to_left, own, to_right = run_prepare(
        place, lengths, languages, destination, lang_scale, qkv_b[0], slots, down, up
    )
    from_left, from_right, low = lax.optimization_barrier((from_left, from_right, low))
    to_up, to_down, near, low = lax.optimization_barrier((to_up, to_down, near, low))
    last_left = shift(to_up, [([last], 0, 1, anywhere)])
    last_right = shift(to_down, [([last], 0, -1, anywhere)])
    grad_qkv, scaled, back = run_backward(
        place, languages, destination, lang_scale, qkv_b[0],
        (from_left, from_right, last_left, last_right), slots, probs, down, up,
    )
    grad_qkv, near, to_left, to_right = lax.optimization_barrier(
        (grad_qkv, near, to_left, to_right)
    )
    handed_back = shift(grad_qkv, [(every, -1, 0, anywhere)])[None]
    before = shift(near, [([1, 3], 0, 1, anywhere)])
    after = shift(near, [([1, 3], 0, -1, anywhere)])
    left = shift(to_right, [([0], 0, 1, anywhere)])
    right = shift(to_left, [([0], 0, -1, anywhere)])
    terms = run_terms(
        place, languages, destination, lang_scale, attn, slots, left, own, right, scaled, back, low
    )
    planes = [[RUN * k + z for k in range(size // RUN)] for z in range(RUN)]
    columns = [[RUN * k + z for z in range(RUN)] for k in range(size // RUN)]
    terms = spread(terms.reshape(size // RUN, -1, 2 * RANK), planes)
    far, terms = lax.optimization_barrier((far, terms))
    crossed = section == 2
    sent = jnp.where(crossed, far, out)
    far_before = shift(sent, [([1], 1, 1, run_end), ([2], 0, 1, not_run_end)])
    far_after = shift(sent, [([1], 1, -1, run_start), ([2], 0, -1, not_run_start)])
    terms, handed_back, before, after = lax.optimization_barrier(
        (terms, handed_back, before, after)
    )
    terms = spread(terms.reshape(RUN, -1, 2 * RANK), columns)
    hop = jnp.where(crossed, far, near)
    slot0 = jnp.where(crossed, far_before, before)
    slot2 = jnp.where(crossed, far_after, after)
    dest = destination[0]
    zero = jnp.zeros((), BF16)
    slot0 = jnp.where((dest[jnp.maximum(rank - 1, 0)] == rank) & (rank > 0), slot0, zero)
    slot1 = jnp.where(dest[rank] == rank, hop, zero)
    slot2 = jnp.where(
        (dest[jnp.minimum(rank + 1, size - 1)] == rank) & (rank < size - 1), slot2, zero
    )
    handed_forward = jnp.concatenate([slot0, slot1, slot2], axis=0)[None]
    return (handed_forward, handed_back, terms[None])


def solution(mesh):
    return jax.shard_map(
        shards,
        mesh=mesh,
        in_specs=(
            P("section", "dp", None),
            P("section", "dp", None),
            P("section", "dp", None),
            P("section", None, None),
            P("section", None, None),
            P(),
            P(),
            P(),
            P(),
        ),
        out_specs=(P("section", "dp", None), P("section", "dp", None), P("section", "dp", None)),
        check_vma=False,
    )
```

time: 172 us -> 167 us (0.971)
  the two profiles are of different devices: /device:TPU:33 before, /device:TPU:7 now
where the time goes in v5:
time: 167 us
  starting transfers between devices  77.7 us (47%)
  waiting for transfers between devices  43.9 us (26%)
  Pallas kernels  20.3 us (12%)
  local copies, waits for them, and re-layouts  13.3 us (8%)
  other arithmetic  8.65 us (5%)
  between operations  2.76 us (2%)
    ppermute x13, starting transfers between devices, shift(): return lax.ppermute(x, AXES, route)  57.2 us
    ppermute x13, waiting for transfers between devices, shift(): return lax.ppermute(x, AXES, route)  43.9 us
    all_to_all x2, starting transfers between devices, spread(): pieces = lax.all_to_all(x, 'dp', 0, 0, axis_index_groups=groups, tiled=True)  20.5 us
    unnamed x35, local copies, waits for them, and re-layouts  9.55 us
    pallas_call x1, Pallas kernels, run_backward(): pl.pallas_call(backward_kernel, out_shape=(jax.ShapeDtypeStruct((TILE, QW...  8.69 us
    pallas_call x1, Pallas kernels, run_forward(): pl.pallas_call(forward_kernel, out_shape=jax.ShapeDtypeStruct((TILE, QW),...  4.65 us
    pallas_call x1, Pallas kernels, run_prepare(): pl.pallas_call(prepare_kernel, out_shape=(jax.ShapeDtypeStruct((QW, TILE)...  4.28 us
  transfers between devices with their start and end apart: 15, of which 5 were waited for; matrix products, arithmetic and copies ran while one was open for 5% of the time, Pallas kernels for 5%

profile of v5, /device:TPU:7, one launch (start us, length us, event | category | flops | bytes accessed | tf_op | source)
XLA Modules:
  0.0 166.6 jit_solution(12522791904786004545)
XLA Ops:
  0.7 0.0 copy-start.13
  0.7 3.1 %slice_bitcast_fusion = (bf16[128,4096]{1,0:T(8,128)(2,1)}, bf16[128,4096]{1,0:T(8,128)(2,1)}) fusion(bf16[1,384,4096]{2,1,0:T(8,128)(2,1)} %param.11), kind=kLoop, calls=%fused_computation.5 | loop fusion | bytes 4194304 | tf_op jit(solution)/shard_map/slice | solution.py:351
  3.8 3.8 %collective-permute-start.1 = (bf16[128,4096]{1,0:T(8,128)(2,1)}, bf16[128,4096]{1,0:T(8,128)(2,1)}, u32[]{:S(2)}, u32[]{:S(2)}) collective-permute-start(bf16[128,4096]{1,0:T(8,128)(2,1)} %get-tuple-element.38), channel_id=1, source_target_pairs={{64,65},{65,66},{66,67},{67,68},{68,69},{69,70},{70,71},{71,72},{7... | collective-permute-start | bytes 3145736 | tf_op jit(solution)/shard_map/ppermute | solution.py:314
  7.6 7.3 %collective-permute-start.2 = (bf16[128,4096]{1,0:T(8,128)(2,1)}, bf16[128,4096]{1,0:T(8,128)(2,1)}, u32[]{:S(2)}, u32[]{:S(2)}) collective-permute-start(bf16[128,4096]{1,0:T(8,128)(2,1)} %get-tuple-element.39), channel_id=1, source_target_pairs={{65,64},{66,65},{67,66},{68,67},{69,68},{70,69},{71,70},{72,71},{7... | collective-permute-start | bytes 3145736 | tf_op jit(solution)/shard_map/ppermute | solution.py:314
  14.9 2.4 %copy.15 = bf16[1,4096,64]{2,1,0:T(8,128)(2,1)} copy(bf16[1,4096,64]{1,2,0:T(8,128)(2,1)} %param.12) | data formatting | bytes 1048576 | tf_op args[3]
  17.4 0.1 copy.16.lens_ref
  17.5 0.1 pad_add_fusion.rank_ref.place_ref
  17.5 1.2 copy-done.2
  18.8 1.0 copy-done.5
  19.8 1.3 copy-done.11
  21.1 4.6 %forward_tile.1 = bf16[128,4096]{1,0:T(8,128)(2,1)S(1)} custom-call(s32[3]{0:T(128)S(1)} %pad_add_fusion.rank_ref.place_ref, s32[2,64,8]{2,1,0:T(8,128)S(1)} %copy.16.lens_ref, s32[2,64]{1,0:T(2,128)S(1)} %copy-done.12, f32[102]{0:T(128)S(1)} %copy-done.14, bf16[128,5120]{1,0:T(8,128)(2,1)S(1)} %bitcast.31, bf16[4096,64]{1,0:T(8,128)(2,1)S(1)} %bitcast.24, ...), custom_call_target="tpu_custom_call" | custom-call | flops 1048576 | bytes 1048576 | tf_op jit(solution)/shard_map/forward_tile/pallas_call | solution.py:240
  25.8 1.3 collective-permute-start.3
  27.1 0.0 copy-start.6
  27.2 1.0 copy-done.6
  28.2 4.3 %prepare_tile.1 = (f32[4096,128]{1,0:T(8,128)S(1)}, bf16[128,4096]{1,0:T(8,128)(2,1)S(1)}, bf16[128,64]{1,0:T(8,128)(2,1)S(1)}, bf16[128,128]{1,0:T(8,128)(2,1)S...) custom-call(s32[3]{0:T(128)S(1)} %pad_add_fusion.rank_ref.place_ref, s32[2,64,8]{2,1,0:T(8,128)S(1)} %copy.16.lens_ref, ...), custom_call_target="tpu_custom_call" | custom-call | flops 1048576 | bytes 1048576 | tf_op jit(solution)/shard_map/prepare_tile/pallas_call | solution.py:254
  32.5 0.0 copy-start.10
  32.5 1.3 copy-done.10
  33.8 0.0 collective-permute-done.1.left_ref
  33.8 0.2 collective-permute-done.2.right_ref
  34.0 0.0 collective-permute-done.3
  34.0 0.7 collective-permute-start.4
  34.7 0.7 collective-permute-start.5
  35.5 0.0 copy-start.1
  35.5 8.7 %backward_tile.1 = (bf16[128,5120]{1,0:T(8,128)(2,1)}, bf16[128,4096]{1,0:T(8,128)(2,1)S(1)}, bf16[128,64]{1,0:T(8,128)(2,1)S(1)}) custom-call(s32[3]{0:T(128)S(1)} %pad_add_fusion.rank_ref.place_ref, s32[2,64]{1,0:T(2,128)S(1)} %copy-done.12, s32[2,64]{1,0:T(2,128)S(1)} %copy-done.13, f32[102]{0:T(128)S(1)} %copy-done.14, bf16[128,5120]{1,0:T(8,128)(2,1)} %bitcast.26, ...), custom_call_target="tpu_custom_call" | custom-call | flops 1048576 | bytes 1048576 | tf_op jit(solution)/shard_map/backward_tile/pallas_call | solution.py:286
  44.2 0.7 collective-permute-start.6
  44.9 0.7 collective-permute-start.7
  45.6 0.0 slice-start
  45.6 2.7 %adapter_terms.1 = bf16[4096,128]{1,0:T(8,128)(2,1)} custom-call(s32[3]{0:T(128)S(1)} %pad_add_fusion.rank_ref.place_ref, s32[2,64]{1,0:T(2,128)S(1)} %copy-done.12, s32[2,64]{1,0:T(2,128)S(1)} %copy-done.13, f32[102]{0:T(128)S(1)} %copy-done.14, bf16[128,4096]{1,0:T(8,128)(2,1)S(1)} %get-tuple-element.33.attn_ref, bf16[384,4096]{1,0:T(8,128)(2,1)S(1)} %bitcast.22, ...), custom_call_target="tpu_custom_call" | custom-call | flops 1048576 | bytes 1048576 | tf_op jit(solution)/shard_map/adapter_terms/pallas_call | solution.py:273
  48.3 6.8 %all-to-all-start = ((bf16[16,256,128]{2,1,0:T(8,128)(2,1)}), bf16[16,256,128]{2,1,0:T(8,128)(2,1)S(1)}, u32[]{:S(2)}, u32[]{:S(2)}) async-start(bf16[16,256,128]{2,1,0:T(8,128)(2,1)} %bitcast.10), calls=%async_computation | async-start | bytes 2097152 | tf_op jit(solution)/shard_map/all_to_all | solution.py:338
  55.1 23.4 %collective-permute-start = (bf16[128,4096]{1,0:T(8,128)(2,1)S(1)}, bf16[128,4096]{1,0:T(8,128)(2,1)}, u32[]{:S(2)}, u32[]{:S(2)}) collective-permute-start(bf16[128,4096]{1,0:T(8,128)(2,1)S(1)} %copy-done.9), channel_id=1, source_target_pairs={{64,128},{65,129},{66,130},{67,131},{68,132},{69,133},{70,134},{71... | collective-permute-start | bytes 3145736 | tf_op jit(solution)/shard_map/ppermute | solution.py:314
  78.6 0.6 constant_dynamic-slice_fusion.2
  79.8 2.6 %collective-permute-start.10 = (bf16[128,4096]{1,0:T(8,128)(2,1)}, bf16[128,4096]{1,0:T(8,128)(2,1)}, u32[]{:S(2)}, u32[]{:S(2)}) collective-permute-start(bf16[128,4096]{1,0:T(8,128)(2,1)} %collective-permute-done.3), channel_id=1, source_target_pairs={{64,65},{65,66},{66,67},{67,68},{68,69},{69,70},{70,71},{71,72},{7... | collective-permute-start | bytes 3145736 | tf_op jit(solution)/shard_map/ppermute | solution.py:314
  82.4 7.5 %collective-permute-start.11 = (bf16[128,4096]{1,0:T(8,128)(2,1)}, bf16[128,4096]{1,0:T(8,128)(2,1)}, u32[]{:S(2)}, u32[]{:S(2)}) collective-permute-start(bf16[128,4096]{1,0:T(8,128)(2,1)} %collective-permute-done.3), channel_id=1, source_target_pairs={{65,64},{66,65},{67,66},{68,67},{69,68},{70,69},{71,70},{72,71},{7... | collective-permute-start | bytes 3145736 | tf_op jit(solution)/shard_map/ppermute | solution.py:314
  89.9 1.9 %collective-permute-start.9 = (bf16[128,5120]{1,0:T(8,128)(2,1)}, bf16[128,5120]{1,0:T(8,128)(2,1)S(1)}, u32[]{:S(2)}, u32[]{:S(2)}) collective-permute-start(bf16[128,5120]{1,0:T(8,128)(2,1)} %get-tuple-element.53), channel_id=1, source_target_pairs={{64,0},{65,1},{66,2},{67,3},{68,4},{69,5},{70,6},{71,7},{72,8},{73... | collective-permute-start | bytes 3932168 | tf_op jit(solution)/shard_map/ppermute | solution.py:314
  91.8 0.8 convert_reduce_fusion
  92.6 2.7 %select_select_fusion.1 = (bf16[128,4096]{1,0:T(8,128)(2,1)S(1)}, bf16[128,4096]{1,0:T(8,128)(2,1)}) fusion(bf16[128,4096]{1,0:T(8,128)(2,1)} %collective-permute-done, bf16[128,4096]{1,0:T(8,128)(2,1)} %collective-permute-done.3, pred[]{:T(512)S(6)} %eq.14, pred[]{:T(512)S(6)} %eq.13, bf16[128,4096]{1,0:T(8,128)(2,1)S(1)} %copy-done.9), kind=kLoop, calls=%fused_computation.3 | loop fusion | flops 1572864 | bytes 5242882 | tf_op jit(solution)/shard_map/jit(_where)/select_n | solution.py:398
  95.3 0.7 collective-permute-start.8
  96.0 12.8 %collective-permute-done.10 = bf16[128,4096]{1,0:T(8,128)(2,1)} collective-permute-done((bf16[128,4096]{1,0:T(8,128)(2,1)}, bf16[128,4096]{1,0:T(8,128)(2,1)}, u32[]{:S(2)}, u32[]{:S(2)}) %collective-permute-start.10) | collective-permute-done | bytes 1048608 | tf_op jit(solution)/shard_map/ppermute | solution.py:314
  108.8 13.4 %collective-permute-done.11 = bf16[128,4096]{1,0:T(8,128)(2,1)} collective-permute-done((bf16[128,4096]{1,0:T(8,128)(2,1)}, bf16[128,4096]{1,0:T(8,128)(2,1)}, u32[]{:S(2)}, u32[]{:S(2)}) %collective-permute-start.11) | collective-permute-done | bytes 1048608 | tf_op jit(solution)/shard_map/ppermute | solution.py:314
  122.1 9.7 %collective-permute-done.9 = bf16[128,5120]{1,0:T(8,128)(2,1)S(1)} collective-permute-done((bf16[128,5120]{1,0:T(8,128)(2,1)}, bf16[128,5120]{1,0:T(8,128)(2,1)S(1)}, u32[]{:S(2)}, u32[]{:S(2)}) %collective-permute-start.9) | collective-permute-done | bytes 1310752 | tf_op jit(solution)/shard_map/ppermute | solution.py:314
  131.9 13.6 %all-to-all-start.1 = ((f32[4,64,128]{2,1,0:T(8,128)}), f32[4,64,128]{2,1,0:T(8,128)S(1)}, u32[]{:S(2)}, u32[]{:S(2)}) async-start(f32[4,64,128]{2,1,0:T(8,128)} %bitcast.15), calls=%async_computation.1 | async-start | bytes 262144 | tf_op jit(solution)/shard_map/all_to_all | solution.py:338
  145.5 5.8 %collective-permute-start.12 = (bf16[128,4096]{1,0:T(8,128)(2,1)}, bf16[128,4096]{1,0:T(8,128)(2,1)}, u32[]{:S(2)}, u32[]{:S(2)}) collective-permute-start(bf16[128,4096]{1,0:T(8,128)(2,1)} %get-tuple-element.62), channel_id=1, source_target_pairs={{68,131},{72,135},{76,139},{80,143},{84,147},{88,151},{92,155},{96... | collective-permute-start | bytes 3145736 | tf_op jit(solution)/shard_map/ppermute | solution.py:314
  152.6 0.6 reduce_sum.19
  153.2 1.3 select_select_fusion.2
  154.6 7.9 %collective-permute-done.12 = bf16[128,4096]{1,0:T(8,128)(2,1)} collective-permute-done((bf16[128,4096]{1,0:T(8,128)(2,1)}, bf16[128,4096]{1,0:T(8,128)(2,1)}, u32[]{:S(2)}, u32[]{:S(2)}) %collective-permute-start.12) | collective-permute-done | bytes 1048608 | tf_op jit(solution)/shard_map/ppermute | solution.py:314
  162.4 1.3 select_select_fusion
  163.8 1.8 %maximum_bitcast_fusion = bf16[1,384,4096]{2,1,0:T(8,128)(2,1)} fusion(bf16[128,4096]{1,0:T(8,128)(2,1)S(1)} %select_select_fusion, bf16[128,4096]{1,0:T(8,128)(2,1)S(1)} %get-tuple-element.61, bf16[128,4096]{1,0:T(8,128)(2,1)S(1)} %select_select_fusion.2), kind=kLoop, calls=%fused_computation | loop fusion | flops 9437184 | bytes 6291456 | tf_op jit(solution)/shard_map/broadcast_in_dim | solution.py:402
  165.6 1.1 copy.19
  (32 shorter events, 0.1 us)
Async XLA Ops:
  0.6 16.7 %copy-start.15 = (s32[2,64,8]{1,2,0:T(8,128)S(1)}, s32[2,64,8]{1,2,0:T(8,128)}, u32[]{:S(2)}) copy-start(s32[2,64,8]{1,2,0:T(8,128)} %param.16) | copy-start | bytes 12292
  0.6 16.9 %copy-start.14 = (f32[102]{0:T(128)S(1)}, f32[102]{0:T(128)}, u32[]{:S(2)}) copy-start(f32[102]{0:T(128)} %table_ref.7) | copy-start | bytes 1228
  0.7 16.9 %copy-start.12 = (s32[2,64]{1,0:T(2,128)S(1)}, s32[2,64]{1,0:T(2,128)}, u32[]{:S(2)}) copy-start(s32[2,64]{1,0:T(2,128)} %langs_ref.7) | copy-start | bytes 1540
  0.7 26.4 %copy-start.13 = (s32[2,64]{1,0:T(2,128)S(1)}, s32[2,64]{1,0:T(2,128)}, u32[]{:S(2)}) copy-start(s32[2,64]{1,0:T(2,128)} %dest_ref.5) | copy-start | bytes 1540
  3.8 23.3 %copy-start = (bf16[1,384,4096]{2,1,0:T(8,128)(2,1)S(1)}, bf16[1,384,4096]{2,1,0:T(8,128)(2,1)}, u32[]{:S(2)}) copy-start(bf16[1,384,4096]{2,1,0:T(8,128)(2,1)} %param.11) | copy-start | bytes 9437188
  3.8 30.0 %collective-permute-start.1 = (bf16[128,4096]{1,0:T(8,128)(2,1)}, bf16[128,4096]{1,0:T(8,128)(2,1)}, u32[]{:S(2)}, u32[]{:S(2)}) collective-permute-start(bf16[128,4096]{1,0:T(8,128)(2,1)} %get-tuple-element.38), channel_id=1, source_target_pairs={{64,65},{65,66},{66,67},{67,68},{68,69},{69,70},{70,71},{71,72},{7... | collective-permute-start | bytes 3145736 | tf_op jit(solution)/shard_map/ppermute | solution.py:314
  7.6 26.4 %collective-permute-start.2 = (bf16[128,4096]{1,0:T(8,128)(2,1)}, bf16[128,4096]{1,0:T(8,128)(2,1)}, u32[]{:S(2)}, u32[]{:S(2)}) collective-permute-start(bf16[128,4096]{1,0:T(8,128)(2,1)} %get-tuple-element.39), channel_id=1, source_target_pairs={{65,64},{66,65},{67,66},{68,67},{69,68},{70,69},{71,70},{72,71},{7... | collective-permute-start | bytes 3145736 | tf_op jit(solution)/shard_map/ppermute | solution.py:314
  17.5 1.2 copy-start.2
  18.8 1.0 copy-start.5
  19.8 1.3 copy-start.11
  21.1 6.0 %copy-start.3 = (bf16[1,4096,64]{2,1,0:T(8,128)(2,1)S(1)}, bf16[1,4096,64]{2,1,0:T(8,128)(2,1)}, u32[]{:S(2)}) copy-start(bf16[1,4096,64]{2,1,0:T(8,128)(2,1)} %copy.15) | copy-start | bytes 1572868
  21.1 6.0 %copy-start.4 = (bf16[1,128,5120]{2,1,0:T(8,128)(2,1)S(1)}, bf16[1,128,5120]{2,1,0:T(8,128)(2,1)}, u32[]{:S(2)}) copy-start(bf16[1,128,5120]{2,1,0:T(8,128)(2,1)} %param.10) | copy-start | bytes 3932164
  25.8 9.7 %copy-start.8 = (bf16[128,4096]{1,0:T(8,128)(2,1)}, bf16[128,4096]{1,0:T(8,128)(2,1)S(1)}, u32[]{:S(2)}) copy-start(bf16[128,4096]{1,0:T(8,128)(2,1)S(1)} %forward_tile.1) | copy-start | bytes 3145732
  25.8 8.2 %collective-permute-start.3 = (bf16[128,4096]{1,0:T(8,128)(2,1)S(1)}, bf16[128,4096]{1,0:T(8,128)(2,1)}, u32[]{:S(2)}, u32[]{:S(2)}) collective-permute-start(bf16[128,4096]{1,0:T(8,128)(2,1)S(1)} %forward_tile.1), channel_id=1, source_target_pairs={{0,64},{1,65},{2,66},{3,67},{4,68},{5,69},{6,70},{7,71},{8,72},{9,... | collective-permute-start | bytes 3145736 | tf_op jit(solution)/shard_map/ppermute | solution.py:314
  27.1 1.0 copy-start.6
  28.2 7.3 %copy-start.7 = (bf16[1,64,4096]{2,1,0:T(8,128)(2,1)S(1)}, bf16[1,64,4096]{2,1,0:T(8,128)(2,1)}, u32[]{:S(2)}) copy-start(bf16[1,64,4096]{2,1,0:T(8,128)(2,1)} %param.13) | copy-start | bytes 1572868
  32.5 1.3 copy-start.10
  34.0 1.5 collective-permute-start.4
  34.7 0.7 collective-permute-start.5
  35.5 10.1 %copy-start.1 = (bf16[1,384,4096]{2,1,0:T(8,128)(2,1)S(1)}, bf16[1,384,4096]{2,1,0:T(8,128)(2,1)}, u32[]{:S(2)}) copy-start(bf16[1,384,4096]{2,1,0:T(8,128)(2,1)} %param.11) | copy-start | bytes 9437188
  44.2 1.3 collective-permute-start.6
  44.9 0.7 collective-permute-start.7
  45.6 9.6 %copy-start.9 = (bf16[128,4096]{1,0:T(8,128)(2,1)S(1)}, bf16[128,4096]{1,0:T(8,128)(2,1)}, u32[]{:S(2)}) copy-start(bf16[128,4096]{1,0:T(8,128)(2,1)} %copy-done.8) | copy-start | bytes 3145732
  45.6 33.0 %slice-start = ((s32[2,64]{1,0:T(2,128)}), s32[1,64]{1,0:T(1,128)S(1)}, s32[]{:S(2)}) async-start(s32[2,64]{1,0:T(2,128)} %dest_ref.5), calls=%async_computation.2 | async-start | bytes 1024 | tf_op jit(solution)/shard_map/slice | solution.py:395
  48.3 43.5 %all-to-all-start = ((bf16[16,256,128]{2,1,0:T(8,128)(2,1)}), bf16[16,256,128]{2,1,0:T(8,128)(2,1)S(1)}, u32[]{:S(2)}, u32[]{:S(2)}) async-start(bf16[16,256,128]{2,1,0:T(8,128)(2,1)} %bitcast.10), calls=%async_computation | async-start | bytes 2097152 | tf_op jit(solution)/shard_map/all_to_all | solution.py:338
  55.1 37.5 %collective-permute-start = (bf16[128,4096]{1,0:T(8,128)(2,1)S(1)}, bf16[128,4096]{1,0:T(8,128)(2,1)}, u32[]{:S(2)}, u32[]{:S(2)}) collective-permute-start(bf16[128,4096]{1,0:T(8,128)(2,1)S(1)} %copy-done.9), channel_id=1, source_target_pairs={{64,128},{65,129},{66,130},{67,131},{68,132},{69,133},{70,134},{71... | collective-permute-start | bytes 3145736 | tf_op jit(solution)/shard_map/ppermute | solution.py:314
  79.8 29.0 %collective-permute-start.10 = (bf16[128,4096]{1,0:T(8,128)(2,1)}, bf16[128,4096]{1,0:T(8,128)(2,1)}, u32[]{:S(2)}, u32[]{:S(2)}) collective-permute-start(bf16[128,4096]{1,0:T(8,128)(2,1)} %collective-permute-done.3), channel_id=1, source_target_pairs={{64,65},{65,66},{66,67},{67,68},{68,69},{69,70},{70,71},{71,72},{7... | collective-permute-start | bytes 3145736 | tf_op jit(solution)/shard_map/ppermute | solution.py:314
  82.4 39.7 %collective-permute-start.11 = (bf16[128,4096]{1,0:T(8,128)(2,1)}, bf16[128,4096]{1,0:T(8,128)(2,1)}, u32[]{:S(2)}, u32[]{:S(2)}) collective-permute-start(bf16[128,4096]{1,0:T(8,128)(2,1)} %collective-permute-done.3), channel_id=1, source_target_pairs={{65,64},{66,65},{67,66},{68,67},{69,68},{70,69},{71,70},{72,71},{7... | collective-permute-start | bytes 3145736 | tf_op jit(solution)/shard_map/ppermute | solution.py:314
  89.9 42.0 %collective-permute-start.9 = (bf16[128,5120]{1,0:T(8,128)(2,1)}, bf16[128,5120]{1,0:T(8,128)(2,1)S(1)}, u32[]{:S(2)}, u32[]{:S(2)}) collective-permute-start(bf16[128,5120]{1,0:T(8,128)(2,1)} %get-tuple-element.53), channel_id=1, source_target_pairs={{64,0},{65,1},{66,2},{67,3},{68,4},{69,5},{70,6},{71,7},{72,8},{73... | collective-permute-start | bytes 3932168 | tf_op jit(solution)/shard_map/ppermute | solution.py:314
  95.3 57.9 %collective-permute-start.8 = (bf16[128,4096]{1,0:T(8,128)(2,1)}, bf16[128,4096]{1,0:T(8,128)(2,1)S(1)}, u32[]{:S(2)}, u32[]{:S(2)}) collective-permute-start(bf16[128,4096]{1,0:T(8,128)(2,1)} %get-tuple-element.62), channel_id=1, source_target_pairs={{67,132},{71,136},{75,140},{79,144},{83,148},{87,152},{91,156},{95... | collective-permute-start | bytes 3145736 | tf_op jit(solution)/shard_map/ppermute | solution.py:314
  131.9 20.7 %all-to-all-start.1 = ((f32[4,64,128]{2,1,0:T(8,128)}), f32[4,64,128]{2,1,0:T(8,128)S(1)}, u32[]{:S(2)}, u32[]{:S(2)}) async-start(f32[4,64,128]{2,1,0:T(8,128)} %bitcast.15), calls=%async_computation.1 | async-start | bytes 262144 | tf_op jit(solution)/shard_map/all_to_all | solution.py:338
  145.5 16.9 %collective-permute-start.12 = (bf16[128,4096]{1,0:T(8,128)(2,1)}, bf16[128,4096]{1,0:T(8,128)(2,1)}, u32[]{:S(2)}, u32[]{:S(2)}) collective-permute-start(bf16[128,4096]{1,0:T(8,128)(2,1)} %get-tuple-element.62), channel_id=1, source_target_pairs={{68,131},{72,135},{76,139},{80,143},{84,147},{88,151},{92,155},{96... | collective-permute-start | bytes 3145736 | tf_op jit(solution)/shard_map/ppermute | solution.py:314

commit v6 on v5

--- a/solution.py
+++ b/solution.py
@@ -334,9 +334,8 @@
     return t % RUN != RUN - 1
 
 
-def spread(x, groups):
-    pieces = lax.all_to_all(x, "dp", 0, 0, axis_index_groups=groups, tiled=True)
-    return jnp.sum(pieces.astype(F32), axis=0)
+def scatter(x, groups):
+    return lax.all_to_all(x, "dp", 0, 0, axis_index_groups=groups, tiled=True)
 
 
 def shards(
@@ -379,16 +378,17 @@
     )
     planes = [[RUN * k + z for k in range(size // RUN)] for z in range(RUN)]
     columns = [[RUN * k + z for z in range(RUN)] for k in range(size // RUN)]
-    terms = spread(terms.reshape(size // RUN, -1, 2 * RANK), planes)
     far, terms = lax.optimization_barrier((far, terms))
+    pieces = scatter(terms.reshape(size // RUN, -1, 2 * RANK), planes)
     crossed = section == 2
     sent = jnp.where(crossed, far, out)
     far_before = shift(sent, [([1], 1, 1, run_end), ([2], 0, 1, not_run_end)])
     far_after = shift(sent, [([1], 1, -1, run_start), ([2], 0, -1, not_run_start)])
-    terms, handed_back, before, after = lax.optimization_barrier(
-        (terms, handed_back, before, after)
-    )
-    terms = spread(terms.reshape(RUN, -1, 2 * RANK), columns)
+    pieces, handed_back, before, after = lax.optimization_barrier(
+        (pieces, handed_back, before, after)
+    )
+    terms = jnp.sum(pieces.astype(F32), axis=0)
+    terms = jnp.sum(scatter(terms.reshape(RUN, -1, 2 * RANK), columns), axis=0)
     hop = jnp.where(crossed, far, near)
     slot0 = jnp.where(crossed, far_before, before)
     slot2 = jnp.where(crossed, far_after, after)

time: 167 us -> 139 us (0.83)
  the two profiles are of different devices: /device:TPU:7 before, /device:TPU:128 now
where the time goes in v6:
time: 139 us; the launch traced here: 138 us
  starting transfers between devices  67.7 us (49%)
  Pallas kernels  20.4 us (15%)
  local copies, waits for them, and re-layouts  20.1 us (14%)
  waiting for transfers between devices  19.8 us (14%)
  other arithmetic  7.12 us (5%)
  between operations  2.79 us (2%)
    ppermute x13, starting transfers between devices, shift(): return lax.ppermute(x, AXES, route)  35.3 us
    all_to_all x2, starting transfers between devices, scatter(): return lax.all_to_all(x, 'dp', 0, 0, axis_index_groups=groups, tiled=True)  32.4 us
    ppermute x13, waiting for transfers between devices, shift(): return lax.ppermute(x, AXES, route)  19 us
    unnamed x43, local copies, waits for them, and re-layouts  16.3 us
    pallas_call x1, Pallas kernels, run_backward(): pl.pallas_call(backward_kernel, out_shape=(jax.ShapeDtypeStruct((TILE, QW...  8.76 us
    pallas_call x1, Pallas kernels, run_forward(): pl.pallas_call(forward_kernel, out_shape=jax.ShapeDtypeStruct((TILE, QW),...  5.61 us
    pallas_call x1, Pallas kernels, run_prepare(): pl.pallas_call(prepare_kernel, out_shape=(jax.ShapeDtypeStruct((QW, TILE)...  4.28 us
    slice x1, local copies, waits for them, and re-layouts, shards(): to_up, to_down = (slots[2 * TILE:], slots[:TILE])  3.09 us
  transfers between devices with their start and end apart: 15, of which 3 were waited for; matrix products, arithmetic and copies ran while one was open for 7% of the time, Pallas kernels for 15%

profile of v6, /device:TPU:128, one launch (start us, length us, event | category | flops | bytes accessed | tf_op | source)
XLA Modules:
  0.0 137.9 jit_solution(4254165890270484948)
XLA Ops:
  0.7 0.0 copy-start.16
  0.7 3.1 %slice_bitcast_fusion = (bf16[128,4096]{1,0:T(8,128)(2,1)}, bf16[128,4096]{1,0:T(8,128)(2,1)}) fusion(bf16[1,384,4096]{2,1,0:T(8,128)(2,1)} %param.11), kind=kLoop, calls=%fused_computation.5 | loop fusion | bytes 4194304 | tf_op jit(solution)/shard_map/slice | solution.py:350
  3.8 4.2 %collective-permute-start.1 = (bf16[128,4096]{1,0:T(8,128)(2,1)}, bf16[128,4096]{1,0:T(8,128)(2,1)}, u32[]{:S(2)}, u32[]{:S(2)}) collective-permute-start(bf16[128,4096]{1,0:T(8,128)(2,1)} %get-tuple-element.38), channel_id=1, source_target_pairs={{64,65},{65,66},{66,67},{67,68},{68,69},{69,70},{70,71},{71,72},{7... | collective-permute-start | bytes 3145736 | tf_op jit(solution)/shard_map/ppermute | solution.py:314
  8.0 1.3 collective-permute-start.2
  9.2 2.4 %copy.15 = bf16[1,4096,64]{2,1,0:T(8,128)(2,1)} copy(bf16[1,4096,64]{1,2,0:T(8,128)(2,1)} %param.12) | data formatting | bytes 1048576 | tf_op args[3]
  11.7 0.1 copy.16.lens_ref
  11.8 0.1 pad_add_fusion.rank_ref.place_ref
  11.9 1.2 copy-done.2
  13.1 1.0 copy-done.5
  14.1 1.3 copy-done.10
  15.5 5.6 %forward_tile.1 = bf16[128,4096]{1,0:T(8,128)(2,1)} custom-call(s32[3]{0:T(128)S(1)} %pad_add_fusion.rank_ref.place_ref, s32[2,64,8]{2,1,0:T(8,128)S(1)} %copy.16.lens_ref, s32[2,64]{1,0:T(2,128)S(1)} %copy-done.15, f32[102]{0:T(128)S(1)} %copy-done.17, bf16[128,5120]{1,0:T(8,128)(2,1)S(1)} %bitcast.32, bf16[4096,64]{1,0:T(8,128)(2,1)S(1)} %bitcast.24, ...), custom_call_target="tpu_custom_call" | custom-call | flops 1048576 | bytes 1048576 | tf_op jit(solution)/shard_map/forward_tile/pallas_call | solution.py:240
  21.1 1.3 collective-permute-start.3
  22.5 0.0 copy-start.6
  22.5 1.0 copy-done.6
  23.5 4.3 %prepare_tile.1 = (f32[4096,128]{1,0:T(8,128)S(1)}, bf16[128,4096]{1,0:T(8,128)(2,1)S(1)}, bf16[128,64]{1,0:T(8,128)(2,1)S(1)}, bf16[128,128]{1,0:T(8,128)(2,1)S...) custom-call(s32[3]{0:T(128)S(1)} %pad_add_fusion.rank_ref.place_ref, s32[2,64,8]{2,1,0:T(8,128)S(1)} %copy.16.lens_ref, ...), custom_call_target="tpu_custom_call" | custom-call | flops 1048576 | bytes 1048576 | tf_op jit(solution)/shard_map/prepare_tile/pallas_call | solution.py:254
  27.8 0.0 copy-start.9
  27.8 1.3 copy-done.9
  29.1 1.0 copy-done.11
  30.1 5.0 %collective-permute-done.2.right_ref = bf16[128,4096]{1,0:T(8,128)(2,1)} collective-permute-done((bf16[128,4096]{1,0:T(8,128)(2,1)}, bf16[128,4096]{1,0:T(8,128)(2,1)}, u32[]{:S(2)}, u32[]{:S(2)}) %collective-permute-start.2) | collective-permute-done | bytes 1048608 | tf_op jit(solution)/shard_map/ppermute | solution.py:314
  35.1 0.7 collective-permute-start.4
  35.9 0.7 collective-permute-start.5
  36.6 1.3 collective-permute-start
  37.9 0.0 slice-start
  38.0 8.8 %backward_tile.1 = (bf16[128,5120]{1,0:T(8,128)(2,1)}, bf16[128,4096]{1,0:T(8,128)(2,1)S(1)}, bf16[128,64]{1,0:T(8,128)(2,1)S(1)}) custom-call(s32[3]{0:T(128)S(1)} %pad_add_fusion.rank_ref.place_ref, s32[2,64]{1,0:T(2,128)S(1)} %copy-done.15, s32[2,64]{1,0:T(2,128)S(1)} %copy-done.16, f32[102]{0:T(128)S(1)} %copy-done.17, bf16[128,5120]{1,0:T(8,128)(2,1)} %bitcast.26, ...), custom_call_target="tpu_custom_call" | custom-call | flops 1048576 | bytes 1048576 | tf_op jit(solution)/shard_map/backward_tile/pallas_call | solution.py:286
  46.7 1.0 copy-done.13
  47.7 0.7 collective-permute-start.6
  48.3 0.7 collective-permute-start.7
  49.0 0.7 constant_dynamic-slice_fusion.2
  50.4 1.6 %collective-permute-start.10 = (bf16[128,4096]{1,0:T(8,128)(2,1)}, bf16[128,4096]{1,0:T(8,128)(2,1)}, u32[]{:S(2)}, u32[]{:S(2)}) collective-permute-start(bf16[128,4096]{1,0:T(8,128)(2,1)} %copy-done.18), channel_id=1, source_target_pairs={{64,65},{65,66},{66,67},{67,68},{68,69},{69,70},{70,71},{71,72},{7... | collective-permute-start | bytes 3145736 | tf_op jit(solution)/shard_map/ppermute | solution.py:314
  52.0 1.7 %collective-permute-start.11 = (bf16[128,4096]{1,0:T(8,128)(2,1)}, bf16[128,4096]{1,0:T(8,128)(2,1)}, u32[]{:S(2)}, u32[]{:S(2)}) collective-permute-start(bf16[128,4096]{1,0:T(8,128)(2,1)} %copy-done.18), channel_id=1, source_target_pairs={{65,64},{66,65},{67,66},{68,67},{69,68},{70,69},{71,70},{72,71},{7... | collective-permute-start | bytes 3145736 | tf_op jit(solution)/shard_map/ppermute | solution.py:314
  53.7 10.2 %collective-permute-start.9 = (bf16[128,5120]{1,0:T(8,128)(2,1)}, bf16[128,5120]{1,0:T(8,128)(2,1)}, u32[]{:S(2)}, u32[]{:S(2)}) collective-permute-start(bf16[128,5120]{1,0:T(8,128)(2,1)} %get-tuple-element.53), channel_id=1, source_target_pairs={{64,0},{65,1},{66,2},{67,3},{68,4},{69,5},{70,6},{71,7},{72,8},{73... | collective-permute-start | bytes 3932168 | tf_op jit(solution)/shard_map/ppermute | solution.py:314
  64.0 1.2 copy-done.12
  65.2 1.2 copy-done.14
  66.4 1.7 %adapter_terms.1 = bf16[4096,128]{1,0:T(8,128)(2,1)S(1)} custom-call(s32[3]{0:T(128)S(1)} %pad_add_fusion.rank_ref.place_ref, s32[2,64]{1,0:T(2,128)S(1)} %copy-done.15, s32[2,64]{1,0:T(2,128)S(1)} %copy-done.16, f32[102]{0:T(128)S(1)} %copy-done.17, bf16[128,4096]{1,0:T(8,128)(2,1)S(1)} %copy-done.12, bf16[384,4096]{1,0:T(8,128)(2,1)S(1)} %bitcast.22, ...), custom_call_target="tpu_custom_call" | custom-call | flops 1048576 | bytes 1048576 | tf_op jit(solution)/shard_map/adapter_terms/pallas_call | solution.py:273
  68.2 1.0 copy-done.8
  69.1 10.6 %all-to-all-start = ((bf16[16,256,128]{2,1,0:T(8,128)(2,1)}), bf16[16,256,128]{2,1,0:T(8,128)(2,1)S(1)}, u32[]{:S(2)}, u32[]{:S(2)}) async-start(bf16[16,256,128]{2,1,0:T(8,128)(2,1)} %bitcast.31), calls=%async_computation | async-start | bytes 2097152 | tf_op jit(solution)/shard_map/all_to_all | solution.py:338
  79.7 2.4 %select_select_fusion.1 = (bf16[128,4096]{1,0:T(8,128)(2,1)S(1)}, bf16[128,4096]{1,0:T(8,128)(2,1)}) fusion(bf16[128,4096]{1,0:T(8,128)(2,1)} %collective-permute-done, bf16[128,4096]{1,0:T(8,128)(2,1)} %copy-done.18, pred[]{:T(512)S(6)} %eq.14, pred[]{:T(512)S(6)} %eq.13, bf16[128,4096]{1,0:T(8,128)(2,1)} %forward_tile.1), kind=kLoop, calls=%fused_computation.3 | loop fusion | flops 1572864 | bytes 5242882 | tf_op jit(solution)/shard_map/jit(_where)/select_n | solution.py:398
  82.1 9.6 %collective-permute-start.8 = (bf16[128,4096]{1,0:T(8,128)(2,1)}, bf16[128,4096]{1,0:T(8,128)(2,1)S(1)}, u32[]{:S(2)}, u32[]{:S(2)}) collective-permute-start(bf16[128,4096]{1,0:T(8,128)(2,1)} %get-tuple-element.62), channel_id=1, source_target_pairs={{67,132},{71,136},{75,140},{79,144},{83,148},{87,152},{91,156},{95... | collective-permute-start | bytes 3145736 | tf_op jit(solution)/shard_map/ppermute | solution.py:314
  92.9 1.3 collective-permute-start.12
  94.2 0.8 all-to-all-done
  95.0 0.8 convert_reduce_fusion
  95.8 21.8 %all-to-all-start.1 = ((f32[4,64,128]{2,1,0:T(8,128)}), f32[4,64,128]{2,1,0:T(8,128)S(1)}, u32[]{:S(2)}, u32[]{:S(2)}) async-start(f32[4,64,128]{2,1,0:T(8,128)} %bitcast.15), calls=%async_computation.1 | async-start | bytes 262144 | tf_op jit(solution)/shard_map/all_to_all | solution.py:338
  117.7 0.1 select_select_fusion.2
  117.8 13.9 %collective-permute-done.12 = bf16[128,4096]{1,0:T(8,128)(2,1)} collective-permute-done((bf16[128,4096]{1,0:T(8,128)(2,1)}, bf16[128,4096]{1,0:T(8,128)(2,1)}, u32[]{:S(2)}, u32[]{:S(2)}) %collective-permute-start.12) | collective-permute-done | bytes 1048608 | tf_op jit(solution)/shard_map/ppermute | solution.py:314
  131.7 1.3 select_select_fusion
  133.0 1.8 %maximum_bitcast_fusion = bf16[1,384,4096]{2,1,0:T(8,128)(2,1)} fusion(bf16[128,4096]{1,0:T(8,128)(2,1)S(1)} %select_select_fusion, bf16[128,4096]{1,0:T(8,128)(2,1)S(1)} %get-tuple-element.61, bf16[128,4096]{1,0:T(8,128)(2,1)S(1)} %select_select_fusion.2), kind=kLoop, calls=%fused_computation | loop fusion | flops 9437184 | bytes 6291456 | tf_op jit(solution)/shard_map/broadcast_in_dim | solution.py:402
  134.8 0.6 reduce_sum.19
  135.5 2.5 %copy.19 = bf16[1,128,5120]{2,1,0:T(8,128)(2,1)} copy(bf16[1,128,5120]{2,1,0:T(8,128)(2,1)} %bitcast.11) | data formatting | bytes 2621440
  (40 shorter events, 0.1 us)
Async XLA Ops:
  0.6 11.0 %copy-start.19 = (s32[2,64,8]{1,2,0:T(8,128)S(1)}, s32[2,64,8]{1,2,0:T(8,128)}, u32[]{:S(2)}) copy-start(s32[2,64,8]{1,2,0:T(8,128)} %param.16) | copy-start | bytes 12292
  0.6 11.2 %copy-start.17 = (f32[102]{0:T(128)S(1)}, f32[102]{0:T(128)}, u32[]{:S(2)}) copy-start(f32[102]{0:T(128)} %table_ref.7) | copy-start | bytes 1228
  0.7 11.2 %copy-start.15 = (s32[2,64]{1,0:T(2,128)S(1)}, s32[2,64]{1,0:T(2,128)}, u32[]{:S(2)}) copy-start(s32[2,64]{1,0:T(2,128)} %langs_ref.7) | copy-start | bytes 1540
  0.7 21.8 %copy-start.16 = (s32[2,64]{1,0:T(2,128)S(1)}, s32[2,64]{1,0:T(2,128)}, u32[]{:S(2)}) copy-start(s32[2,64]{1,0:T(2,128)} %dest_ref.5) | copy-start | bytes 1540
  3.8 18.7 %copy-start = (bf16[1,384,4096]{2,1,0:T(8,128)(2,1)S(1)}, bf16[1,384,4096]{2,1,0:T(8,128)(2,1)}, u32[]{:S(2)}) copy-start(bf16[1,384,4096]{2,1,0:T(8,128)(2,1)} %param.11) | copy-start | bytes 9437188
  3.8 26.3 %collective-permute-start.1 = (bf16[128,4096]{1,0:T(8,128)(2,1)}, bf16[128,4096]{1,0:T(8,128)(2,1)}, u32[]{:S(2)}, u32[]{:S(2)}) collective-permute-start(bf16[128,4096]{1,0:T(8,128)(2,1)} %get-tuple-element.38), channel_id=1, source_target_pairs={{64,65},{65,66},{66,67},{67,68},{68,69},{69,70},{70,71},{71,72},{7... | collective-permute-start | bytes 3145736 | tf_op jit(solution)/shard_map/ppermute | solution.py:314
  8.0 27.2 %collective-permute-start.2 = (bf16[128,4096]{1,0:T(8,128)(2,1)}, bf16[128,4096]{1,0:T(8,128)(2,1)}, u32[]{:S(2)}, u32[]{:S(2)}) collective-permute-start(bf16[128,4096]{1,0:T(8,128)(2,1)} %get-tuple-element.39), channel_id=1, source_target_pairs={{65,64},{66,65},{67,66},{68,67},{69,68},{70,69},{71,70},{72,71},{7... | collective-permute-start | bytes 3145736 | tf_op jit(solution)/shard_map/ppermute | solution.py:314
  11.9 1.2 copy-start.2
  13.1 1.0 copy-start.5
  14.1 1.3 copy-start.10
  15.4 7.0 %copy-start.3 = (bf16[1,4096,64]{2,1,0:T(8,128)(2,1)S(1)}, bf16[1,4096,64]{2,1,0:T(8,128)(2,1)}, u32[]{:S(2)}) copy-start(bf16[1,4096,64]{2,1,0:T(8,128)(2,1)} %copy.15) | copy-start | bytes 1572868
  15.5 7.0 %copy-start.4 = (bf16[1,128,5120]{2,1,0:T(8,128)(2,1)S(1)}, bf16[1,128,5120]{2,1,0:T(8,128)(2,1)}, u32[]{:S(2)}) copy-start(bf16[1,128,5120]{2,1,0:T(8,128)(2,1)} %param.10) | copy-start | bytes 3932164
  21.1 14.1 %collective-permute-start.3 = (bf16[128,4096]{1,0:T(8,128)(2,1)}, bf16[128,4096]{1,0:T(8,128)(2,1)S(1)}, u32[]{:S(2)}, u32[]{:S(2)}) collective-permute-start(bf16[128,4096]{1,0:T(8,128)(2,1)} %forward_tile.1), channel_id=1, source_target_pairs={{0,64},{1,65},{2,66},{3,67},{4,68},{5,69},{6,70},{7,71},{8,72},{9,... | collective-permute-start | bytes 3145736 | tf_op jit(solution)/shard_map/ppermute | solution.py:314
  22.5 1.0 copy-start.6
  23.5 14.4 %copy-start.7 = (bf16[1,64,4096]{2,1,0:T(8,128)(2,1)S(1)}, bf16[1,64,4096]{2,1,0:T(8,128)(2,1)}, u32[]{:S(2)}) copy-start(bf16[1,64,4096]{2,1,0:T(8,128)(2,1)} %param.13) | copy-start | bytes 1572868
  27.8 1.3 copy-start.9
  29.1 1.0 copy-start.11
  35.1 2.8 %copy-start.18 = (bf16[128,4096]{1,0:T(8,128)(2,1)}, bf16[128,4096]{1,0:T(8,128)(2,1)S(1)}, u32[]{:S(2)}) copy-start(bf16[128,4096]{1,0:T(8,128)(2,1)S(1)} %collective-permute-done.3) | copy-start | bytes 3145732
  35.1 2.8 %collective-permute-start.4 = (bf16[128,4096]{1,0:T(8,128)(2,1)}, bf16[128,4096]{1,0:T(8,128)(2,1)S(1)}, u32[]{:S(2)}, u32[]{:S(2)}) collective-permute-start(bf16[128,4096]{1,0:T(8,128)(2,1)} %get-tuple-element.38), channel_id=1, source_target_pairs={{192,193},{193,194},{194,195},{195,196},{196,197},{197,198},{198,1... | collective-permute-start | bytes 3145736 | tf_op jit(solution)/shard_map/ppermute | solution.py:314
  35.9 2.0 %collective-permute-start.5 = (bf16[128,4096]{1,0:T(8,128)(2,1)}, bf16[128,4096]{1,0:T(8,128)(2,1)S(1)}, u32[]{:S(2)}, u32[]{:S(2)}) collective-permute-start(bf16[128,4096]{1,0:T(8,128)(2,1)} %get-tuple-element.39), channel_id=1, source_target_pairs={{193,192},{194,193},{195,194},{196,195},{197,196},{198,197},{199,1... | collective-permute-start | bytes 3145736 | tf_op jit(solution)/shard_map/ppermute | solution.py:314
  36.6 32.6 %collective-permute-start = (bf16[128,4096]{1,0:T(8,128)(2,1)}, bf16[128,4096]{1,0:T(8,128)(2,1)}, u32[]{:S(2)}, u32[]{:S(2)}) collective-permute-start(bf16[128,4096]{1,0:T(8,128)(2,1)} %forward_tile.1), channel_id=1, source_target_pairs={{64,128},{65,129},{66,130},{67,131},{68,132},{69,133},{70,134},{71... | collective-permute-start | bytes 3145736 | tf_op jit(solution)/shard_map/ppermute | solution.py:314
  37.9 11.1 %slice-start = ((s32[2,64]{1,0:T(2,128)}), s32[1,64]{1,0:T(1,128)S(1)}, s32[]{:S(2)}) async-start(s32[2,64]{1,0:T(2,128)} %dest_ref.5), calls=%async_computation.2 | async-start | bytes 1024 | tf_op jit(solution)/shard_map/slice | solution.py:395
  37.9 26.0 %copy-start.1 = (bf16[1,384,4096]{2,1,0:T(8,128)(2,1)S(1)}, bf16[1,384,4096]{2,1,0:T(8,128)(2,1)}, u32[]{:S(2)}) copy-start(bf16[1,384,4096]{2,1,0:T(8,128)(2,1)} %param.11) | copy-start | bytes 9437188
  46.7 1.0 copy-start.13
  47.7 6.0 %collective-permute-start.6 = (bf16[128,128]{1,0:T(8,128)(2,1)S(1)}, bf16[128,128]{1,0:T(8,128)(2,1)S(1)}, u32[]{:S(2)}, u32[]{:S(2)}) collective-permute-start(bf16[128,128]{1,0:T(8,128)(2,1)S(1)} %get-tuple-element.45), channel_id=1, source_target_pairs={{0,1},{1,2},{2,3},{3,4},{4,5},{5,6},{6,7},{7,8},{8,9},{9,10},{10,1... | collective-permute-start | bytes 98312 | tf_op jit(solution)/shard_map/ppermute | solution.py:314
  48.3 15.6 %collective-permute-start.7 = (bf16[128,128]{1,0:T(8,128)(2,1)S(1)}, bf16[128,128]{1,0:T(8,128)(2,1)S(1)}, u32[]{:S(2)}, u32[]{:S(2)}) collective-permute-start(bf16[128,128]{1,0:T(8,128)(2,1)S(1)} %get-tuple-element.47), channel_id=1, source_target_pairs={{1,0},{2,1},{3,2},{4,3},{5,4},{6,5},{7,6},{8,7},{9,8},{10,9},{11,1... | collective-permute-start | bytes 98312 | tf_op jit(solution)/shard_map/ppermute | solution.py:314
  50.4 44.6 %collective-permute-start.10 = (bf16[128,4096]{1,0:T(8,128)(2,1)}, bf16[128,4096]{1,0:T(8,128)(2,1)}, u32[]{:S(2)}, u32[]{:S(2)}) collective-permute-start(bf16[128,4096]{1,0:T(8,128)(2,1)} %copy-done.18), channel_id=1, source_target_pairs={{64,65},{65,66},{66,67},{67,68},{68,69},{69,70},{70,71},{71,72},{7... | collective-permute-start | bytes 3145736 | tf_op jit(solution)/shard_map/ppermute | solution.py:314
  52.0 43.0 %collective-permute-start.11 = (bf16[128,4096]{1,0:T(8,128)(2,1)}, bf16[128,4096]{1,0:T(8,128)(2,1)}, u32[]{:S(2)}, u32[]{:S(2)}) collective-permute-start(bf16[128,4096]{1,0:T(8,128)(2,1)} %copy-done.18), channel_id=1, source_target_pairs={{65,64},{66,65},{67,66},{68,67},{69,68},{70,69},{71,70},{72,71},{7... | collective-permute-start | bytes 3145736 | tf_op jit(solution)/shard_map/ppermute | solution.py:314
  53.7 41.3 %collective-permute-start.9 = (bf16[128,5120]{1,0:T(8,128)(2,1)}, bf16[128,5120]{1,0:T(8,128)(2,1)}, u32[]{:S(2)}, u32[]{:S(2)}) collective-permute-start(bf16[128,5120]{1,0:T(8,128)(2,1)} %get-tuple-element.53), channel_id=1, source_target_pairs={{64,0},{65,1},{66,2},{67,3},{68,4},{69,5},{70,6},{71,7},{72,8},{73... | collective-permute-start | bytes 3932168 | tf_op jit(solution)/shard_map/ppermute | solution.py:314
  64.0 1.2 copy-start.12
  65.2 1.2 copy-start.14
  68.1 1.0 copy-start.8
  69.1 25.9 %all-to-all-start = ((bf16[16,256,128]{2,1,0:T(8,128)(2,1)}), bf16[16,256,128]{2,1,0:T(8,128)(2,1)S(1)}, u32[]{:S(2)}, u32[]{:S(2)}) async-start(bf16[16,256,128]{2,1,0:T(8,128)(2,1)} %bitcast.31), calls=%async_computation | async-start | bytes 2097152 | tf_op jit(solution)/shard_map/all_to_all | solution.py:338
  82.1 35.5 %collective-permute-start.8 = (bf16[128,4096]{1,0:T(8,128)(2,1)}, bf16[128,4096]{1,0:T(8,128)(2,1)S(1)}, u32[]{:S(2)}, u32[]{:S(2)}) collective-permute-start(bf16[128,4096]{1,0:T(8,128)(2,1)} %get-tuple-element.62), channel_id=1, source_target_pairs={{67,132},{71,136},{75,140},{79,144},{83,148},{87,152},{91,156},{95... | collective-permute-start | bytes 3145736 | tf_op jit(solution)/shard_map/ppermute | solution.py:314
  92.9 38.8 %collective-permute-start.12 = (bf16[128,4096]{1,0:T(8,128)(2,1)}, bf16[128,4096]{1,0:T(8,128)(2,1)}, u32[]{:S(2)}, u32[]{:S(2)}) collective-permute-start(bf16[128,4096]{1,0:T(8,128)(2,1)} %get-tuple-element.62), channel_id=1, source_target_pairs={{68,131},{72,135},{76,139},{80,143},{84,147},{88,151},{92,155},{96... | collective-permute-start | bytes 3145736 | tf_op jit(solution)/shard_map/ppermute | solution.py:314
  95.8 39.0 %all-to-all-start.1 = ((f32[4,64,128]{2,1,0:T(8,128)}), f32[4,64,128]{2,1,0:T(8,128)S(1)}, u32[]{:S(2)}, u32[]{:S(2)}) async-start(f32[4,64,128]{2,1,0:T(8,128)} %bitcast.15), calls=%async_computation.1 | async-start | bytes 262144 | tf_op jit(solution)/shard_map/all_to_all | solution.py:338

commit v7 on v6

--- a/solution.py
+++ b/solution.py
@@ -19,6 +19,7 @@
 KW = KV * HEAD_DIM
 GW = GROUP * HEAD_DIM
 SCALE = 1.0 / math.sqrt(HEAD_DIM)
+HALF = QW // 2
 RUN = 4
 AXES = ("section", "dp")
 BF16 = jnp.bfloat16
@@ -171,7 +172,7 @@
 
 def backward_kernel(
     place_ref, langs_ref, dest_ref, table_ref, qkv_ref, left_ref, right_ref, last_left_ref,
-    last_right_ref, slots_ref, probs_ref, down_ref, up_ref, grad_ref, scaled_ref, back_ref,
+    last_right_ref, turned_ref, slots_ref, probs_ref, down_ref, up_ref, grad_ref, scaled_ref, back_ref,
     gattn_ref,
 ):
     rank = place_ref[0]
@@ -183,8 +184,11 @@
         back = jnp.zeros((TILE, RANK), F32)
         for c in range(0, QW, 512):
             cols = slice(c, c + 512)
-            left = jnp.where(last, last_left_ref[:, cols], left_ref[:, cols])
-            right = jnp.where(last, last_right_ref[:, cols], right_ref[:, cols])
+            turned = turned_ref[:, cols]
+            left = jnp.where(run_start(rank), turned, last_left_ref[:, cols])
+            left = jnp.where(last, left, left_ref[:, cols])
+            right = jnp.where(run_end(rank), turned, last_right_ref[:, cols])
+            right = jnp.where(last, right, right_ref[:, cols])
             mid = slots_ref[TILE : 2 * TILE, cols]
             grad = jnp.where(went < 0, left, jnp.where(went > 0, right, mid))
             gattn_ref[:, cols] = grad
@@ -290,7 +294,7 @@
             jax.ShapeDtypeStruct((TILE, QW), BF16),
             jax.ShapeDtypeStruct((TILE, RANK), BF16),
         ),
-        in_specs=[SMEM] * 4 + [VMEM] * 9,
+        in_specs=[SMEM] * 4 + [VMEM] * 10,
         out_specs=(VMEM,) * 3,
         scratch_shapes=[pltpu.VMEM((TILE, QW), BF16)],
         compiler_params=pltpu.CompilerParams(vmem_limit_bytes=48 * 2**20),
@@ -324,6 +328,14 @@
 
 def run_end(t):
     return t % RUN == RUN - 1
+
+
+def after_run_start(t):
+    return t % RUN == 1
+
+
+def before_run_end(t):
+    return t % RUN == RUN - 2
 
 
 def not_run_start(t):
@@ -350,27 +362,33 @@
     to_up, to_down = slots[2 * TILE :], slots[:TILE]
     from_left = shift(to_up, [(early, 0, 1, anywhere)])
     from_right = shift(to_down, [(early, 0, -1, anywhere)])
+    turning = jnp.where(run_end(rank), to_up, to_down)
+    turned = shift(turning, [([last], -last, -1, run_end), ([last], -last, 1, run_start)])
     out = run_forward(place, lengths, languages, lang_scale, qkv_a[0], down, up)
     out, place = lax.optimization_barrier((out, place))
-    near = shift(out, [([0, 2], 1, 0, anywhere)])
-    far = shift(out, [([1], 1, 0, anywhere)])
+    near = shift(
+        out, [([0, 2], 1, 0, anywhere), ([1], 1, 1, run_end), ([1], 1, -1, run_start)]
+    )
+    far_first = shift(out[:, :HALF], [([1], 1, 0, anywhere)])
     probs, attn, low, to_left, own, to_right = run_prepare(
         place, lengths, languages, destination, lang_scale, qkv_b[0], slots, down, up
     )
     from_left, from_right, low = lax.optimization_barrier((from_left, from_right, low))
-    to_up, to_down, near, low = lax.optimization_barrier((to_up, to_down, near, low))
-    last_left = shift(to_up, [([last], 0, 1, anywhere)])
-    last_right = shift(to_down, [([last], 0, -1, anywhere)])
+    to_up, to_down, turned, near, far_first, low = lax.optimization_barrier(
+        (to_up, to_down, turned, near, far_first, low)
+    )
+    last_left = shift(to_up, [([last], 0, 1, not_run_end)])
+    last_right = shift(to_down, [([last], 0, -1, not_run_start)])
+    turned = shift(turned, [([0], last, 2, before_run_end), ([0], last, -2, after_run_start)])
     grad_qkv, scaled, back = run_backward(
         place, languages, destination, lang_scale, qkv_b[0],
-        (from_left, from_right, last_left, last_right), slots, probs, down, up,
-    )
-    grad_qkv, near, to_left, to_right = lax.optimization_barrier(
-        (grad_qkv, near, to_left, to_right)
+        (from_left, from_right, last_left, last_right, turned), slots, probs, down, up,
+    )
+    grad_qkv, near, to_left, to_right, out = lax.optimization_barrier(
+        (grad_qkv, near, to_left, to_right, out)
     )
     handed_back = shift(grad_qkv, [(every, -1, 0, anywhere)])[None]
-    before = shift(near, [([1, 3], 0, 1, anywhere)])
-    after = shift(near, [([1, 3], 0, -1, anywhere)])
+    far_second = shift(out[:, HALF:], [([1], 1, 0, anywhere)])
     left = shift(to_right, [([0], 0, 1, anywhere)])
     right = shift(to_left, [([0], 0, -1, anywhere)])
     terms = run_terms(
@@ -378,20 +396,17 @@
     )
     planes = [[RUN * k + z for k in range(size // RUN)] for z in range(RUN)]
     columns = [[RUN * k + z for z in range(RUN)] for k in range(size // RUN)]
-    far, terms = lax.optimization_barrier((far, terms))
+    far_second, terms = lax.optimization_barrier((far_second, terms))
     pieces = scatter(terms.reshape(size // RUN, -1, 2 * RANK), planes)
     crossed = section == 2
-    sent = jnp.where(crossed, far, out)
-    far_before = shift(sent, [([1], 1, 1, run_end), ([2], 0, 1, not_run_end)])
-    far_after = shift(sent, [([1], 1, -1, run_start), ([2], 0, -1, not_run_start)])
-    pieces, handed_back, before, after = lax.optimization_barrier(
-        (pieces, handed_back, before, after)
-    )
-    terms = jnp.sum(pieces.astype(F32), axis=0)
+    hop = jnp.where(crossed, jnp.concatenate([far_first, far_second], axis=1), near)
+    before = shift(hop, [([1, 3], 0, 1, anywhere), ([2], 0, 1, not_run_end)])
+    after = shift(hop, [([1, 3], 0, -1, anywhere), ([2], 0, -1, not_run_start)])
+    gate = lax.optimization_barrier((pieces, handed_back))
+    terms = jnp.sum(gate[0].astype(F32), axis=0)
     terms = jnp.sum(scatter(terms.reshape(RUN, -1, 2 * RANK), columns), axis=0)
-    hop = jnp.where(crossed, far, near)
-    slot0 = jnp.where(crossed, far_before, before)
-    slot2 = jnp.where(crossed, far_after, after)
+    slot0 = jnp.where(crossed & run_start(rank), near, before)
+    slot2 = jnp.where(crossed & run_end(rank), near, after)
     dest = destination[0]
     zero = jnp.zeros((), BF16)
     slot0 = jnp.where((dest[jnp.maximum(rank - 1, 0)] == rank) & (rank > 0), slot0, zero)

time: 139 us -> 165 us (1.19)
  the two profiles are of different devices: /device:TPU:128 before, /device:TPU:225 now
where the time goes in v7:
time: 165 us; the launch traced here: 164 us
  waiting for transfers between devices  57.6 us (35%)
  starting transfers between devices  54.6 us (33%)
  Pallas kernels  19.8 us (12%)
  local copies, waits for them, and re-layouts  18.6 us (11%)
  other arithmetic  10.8 us (7%)
  between operations  2.87 us (2%)
    ppermute x14, waiting for transfers between devices, shift(): return lax.ppermute(x, AXES, route)  55.4 us
    ppermute x14, starting transfers between devices, shift(): return lax.ppermute(x, AXES, route)  33.3 us
    all_to_all x2, starting transfers between devices, scatter(): return lax.all_to_all(x, 'dp', 0, 0, axis_index_groups=groups, tiled=True)  21.2 us
    unnamed x47, local copies, waits for them, and re-layouts  15.5 us
    pallas_call x1, Pallas kernels, run_backward(): pl.pallas_call(backward_kernel, out_shape=(jax.ShapeDtypeStruct((TILE, QW...  9.15 us
    pallas_call x1, Pallas kernels, run_forward(): pl.pallas_call(forward_kernel, out_shape=jax.ShapeDtypeStruct((TILE, QW),...  4.64 us
    pallas_call x1, Pallas kernels, run_prepare(): pl.pallas_call(prepare_kernel, out_shape=(jax.ShapeDtypeStruct((QW, TILE)...  4.28 us
  transfers between devices with their start and end apart: 16, of which 6 were waited for; matrix products, arithmetic and copies ran while one was open for 7% of the time, Pallas kernels for 6%

profile of v7, /device:TPU:225, one launch (start us, length us, event | category | flops | bytes accessed | tf_op | source)
XLA Modules:
  0.0 164.3 jit_solution(10905080461544186904)
XLA Ops:
  0.7 2.8 %broadcast_select_fusion.1 = bf16[128,4096]{1,0:T(8,128)(2,1)} fusion(pred[]{:T(512)S(6)} %eq.26, bf16[1,384,4096]{2,1,0:T(8,128)(2,1)} %param.11), kind=kLoop, calls=%fused_computation.8 | loop fusion | flops 524288 | bytes 3145729 | tf_op jit(solution)/shard_map/jit(_where)/select_n | solution.py:365
  3.5 3.4 %collective-permute-start.2 = (bf16[128,4096]{1,0:T(8,128)(2,1)}, bf16[128,4096]{1,0:T(8,128)(2,1)}, u32[]{:S(2)}, u32[]{:S(2)}) collective-permute-start(bf16[128,4096]{1,0:T(8,128)(2,1)} %broadcast_select_fusion.1), channel_id=1, source_target_pairs={{195,2},{199,6},{203,10},{207,14},{211,18},{215,22},{219,26},{223,... | collective-permute-start | bytes 3145736 | tf_op jit(solution)/shard_map/ppermute | solution.py:318
  6.9 1.5 slice_bitcast_fusion
  8.4 1.6 collective-permute-start
  10.0 1.7 %collective-permute-start.1 = (bf16[128,4096]{1,0:T(8,128)(2,1)}, bf16[128,4096]{1,0:T(8,128)(2,1)}, u32[]{:S(2)}, u32[]{:S(2)}) collective-permute-start(bf16[128,4096]{1,0:T(8,128)(2,1)} %get-tuple-element.38), channel_id=1, source_target_pairs={{65,64},{66,65},{67,66},{68,67},{69,68},{70,69},{71,70},{72,71},{7... | collective-permute-start | bytes 3145736 | tf_op jit(solution)/shard_map/ppermute | solution.py:318
  11.6 2.4 %copy.15 = bf16[1,4096,64]{2,1,0:T(8,128)(2,1)} copy(bf16[1,4096,64]{1,2,0:T(8,128)(2,1)} %param.12) | data formatting | bytes 1048576 | tf_op args[3]
  14.0 0.1 copy.16.lens_ref
  14.2 1.2 copy-done.2
  15.5 1.0 copy-done.5
  16.5 1.3 copy-done.9
  17.8 4.6 %forward_tile.1 = bf16[128,4096]{1,0:T(8,128)(2,1)S(1)} custom-call(s32[3]{0:T(128)S(1)} %pad_add_fusion.rank_ref.place_ref, s32[2,64,8]{2,1,0:T(8,128)S(1)} %copy.16.lens_ref, s32[2,64]{1,0:T(2,128)S(1)} %copy-done.14, f32[102]{0:T(128)S(1)} %copy-done.16, bf16[128,5120]{1,0:T(8,128)(2,1)S(1)} %bitcast.36, bf16[4096,64]{1,0:T(8,128)(2,1)S(1)} %bitcast.28, ...), custom_call_target="tpu_custom_call" | custom-call | flops 1048576 | bytes 1048576 | tf_op jit(solution)/shard_map/forward_tile/pallas_call | solution.py:244
  22.5 1.3 collective-permute-start.3
  23.8 0.7 collective-permute-start.4
  24.6 4.3 %prepare_tile.1 = (f32[4096,128]{1,0:T(8,128)S(1)}, bf16[128,4096]{1,0:T(8,128)(2,1)S(1)}, bf16[128,64]{1,0:T(8,128)(2,1)S(1)}, bf16[128,128]{1,0:T(8,128)(2,1)S...) custom-call(s32[3]{0:T(128)S(1)} %pad_add_fusion.rank_ref.place_ref, s32[2,64,8]{2,1,0:T(8,128)S(1)} %copy.16.lens_ref, ...), custom_call_target="tpu_custom_call" | custom-call | flops 1048576 | bytes 1048576 | tf_op jit(solution)/shard_map/prepare_tile/pallas_call | solution.py:258
  28.9 1.3 copy-done.8
  30.2 1.0 copy-done.10
  31.2 1.3 collective-permute-start.5
  32.5 4.1 %collective-permute-start.6 = (bf16[128,4096]{1,0:T(8,128)(2,1)}, bf16[128,4096]{1,0:T(8,128)(2,1)S(1)}, u32[]{:S(2)}, u32[]{:S(2)}) collective-permute-start(bf16[128,4096]{1,0:T(8,128)(2,1)} %get-tuple-element.38), channel_id=1, source_target_pairs={{193,192},{194,193},{195,194},{197,196},{198,197},{199,198},{201,2... | collective-permute-start | bytes 3145736 | tf_op jit(solution)/shard_map/ppermute | solution.py:318
  36.6 1.3 collective-permute-start.7
  37.9 9.4 %collective-permute-done.5.last_left_ref = bf16[128,4096]{1,0:T(8,128)(2,1)S(1)} collective-permute-done((bf16[128,4096]{1,0:T(8,128)(2,1)}, bf16[128,4096]{1,0:T(8,128)(2,1)S(1)}, u32[]{:S(2)}, u32[]{:S(2)}) %collective-permute-start.5) | collective-permute-done | bytes 1048608 | tf_op jit(solution)/shard_map/ppermute | solution.py:318
  47.3 5.3 %collective-permute-done.6.last_right_ref = bf16[128,4096]{1,0:T(8,128)(2,1)S(1)} collective-permute-done((bf16[128,4096]{1,0:T(8,128)(2,1)}, bf16[128,4096]{1,0:T(8,128)(2,1)S(1)}, u32[]{:S(2)}, u32[]{:S(2)}) %collective-permute-start.6) | collective-permute-done | bytes 1048608 | tf_op jit(solution)/shard_map/ppermute | solution.py:318
  52.6 9.0 %collective-permute-done.7.turned_ref = bf16[128,4096]{1,0:T(8,128)(2,1)S(1)} collective-permute-done((bf16[128,4096]{1,0:T(8,128)(2,1)}, bf16[128,4096]{1,0:T(8,128)(2,1)S(1)}, u32[]{:S(2)}, u32[]{:S(2)}) %collective-permute-start.7) | collective-permute-done | bytes 1048608 | tf_op jit(solution)/shard_map/ppermute | solution.py:318
  61.6 1.0 copy-done.19
  62.6 9.2 %backward_tile.1 = (bf16[128,5120]{1,0:T(8,128)(2,1)}, bf16[128,4096]{1,0:T(8,128)(2,1)S(1)}, bf16[128,64]{1,0:T(8,128)(2,1)S(1)}) custom-call(s32[3]{0:T(128)S(1)} %pad_add_fusion.rank_ref.place_ref, s32[2,64]{1,0:T(2,128)S(1)} %copy-done.14, s32[2,64]{1,0:T(2,128)S(1)} %copy-done.15, f32[102]{0:T(128)S(1)} %copy-done.16, bf16[128,5120]{1,0:T(8,128)(2,1)} %bitcast.30, ...), custom_call_target="tpu_custom_call" | custom-call | flops 1048576 | bytes 1048576 | tf_op jit(solution)/shard_map/backward_tile/pallas_call | solution.py:290
  71.8 0.9 slice.27
  72.7 0.2 copy-done.12
  72.9 1.5 collective-permute-start.8
  74.4 0.7 collective-permute-start.10
  75.0 0.7 collective-permute-start.9
  75.7 0.7 constant_dynamic-slice_fusion.2
  77.0 10.0 %collective-permute-start.13 = (bf16[128,5120]{1,0:T(8,128)(2,1)}, bf16[128,5120]{1,0:T(8,128)(2,1)}, u32[]{:S(2)}, u32[]{:S(2)}) collective-permute-start(bf16[128,5120]{1,0:T(8,128)(2,1)} %get-tuple-element.56), channel_id=1, source_target_pairs={{64,0},{65,1},{66,2},{67,3},{68,4},{69,5},{70,6},{71,7},{72,8},{73... | collective-permute-start | bytes 3932168 | tf_op jit(solution)/shard_map/ppermute | solution.py:318
  87.0 1.2 copy-done.11
  88.3 1.2 copy-done.13
  89.5 1.7 %adapter_terms.1 = bf16[4096,128]{1,0:T(8,128)(2,1)S(1)} custom-call(s32[3]{0:T(128)S(1)} %pad_add_fusion.rank_ref.place_ref, s32[2,64]{1,0:T(2,128)S(1)} %copy-done.14, s32[2,64]{1,0:T(2,128)S(1)} %copy-done.15, f32[102]{0:T(128)S(1)} %copy-done.16, bf16[128,4096]{1,0:T(8,128)(2,1)S(1)} %copy-done.11, bf16[384,4096]{1,0:T(8,128)(2,1)S(1)} %bitcast.26, ...), custom_call_target="tpu_custom_call" | custom-call | flops 1048576 | bytes 1048576 | tf_op jit(solution)/shard_map/adapter_terms/pallas_call | solution.py:277
  91.2 1.0 copy-done.7
  92.2 16.7 %all-to-all-start = ((bf16[16,256,128]{2,1,0:T(8,128)(2,1)}), bf16[16,256,128]{2,1,0:T(8,128)(2,1)S(1)}, u32[]{:S(2)}, u32[]{:S(2)}) async-start(bf16[16,256,128]{2,1,0:T(8,128)(2,1)} %bitcast.35), calls=%async_computation | async-start | bytes 2097152 | tf_op jit(solution)/shard_map/all_to_all | solution.py:350
  108.9 3.0 %broadcast_select_fusion = (bf16[128,4096]{1,0:T(8,128)(2,1)S(1)}, bf16[128,4096]{1,0:T(8,128)(2,1)}) fusion(pred[]{:T(512)S(6)} %eq.27, bf16[128,4096]{1,0:T(8,128)(2,1)} %copy-done.17, bf16[128,2048]{1,0:T(8,128)(2,1)} %collective-permute-done.8, bf16[128,2048]{1,0:T(8,128)(2,1)} %copy-done.20, pred[]{:T(512)S(6)} %eq.24), kind=kLoop, calls=%fused_computation.7 | loop fusion | flops 3145728 | bytes 4194306 | tf_op jit(solution)/shard_map/jit(_where)/select_n | solution.py:413
  111.9 3.1 %collective-permute-start.11 = (bf16[128,4096]{1,0:T(8,128)(2,1)}, bf16[128,4096]{1,0:T(8,128)(2,1)}, u32[]{:S(2)}, u32[]{:S(2)}) collective-permute-start(bf16[128,4096]{1,0:T(8,128)(2,1)} %get-tuple-element.60), channel_id=1, source_target_pairs={{64,65},{65,66},{66,67},{67,68},{68,69},{69,70},{70,71},{71,72},{7... | collective-permute-start | bytes 3145736 | tf_op jit(solution)/shard_map/ppermute | solution.py:318
  115.0 2.2 %collective-permute-start.12 = (bf16[128,4096]{1,0:T(8,128)(2,1)}, bf16[128,4096]{1,0:T(8,128)(2,1)}, u32[]{:S(2)}, u32[]{:S(2)}) collective-permute-start(bf16[128,4096]{1,0:T(8,128)(2,1)} %get-tuple-element.60), channel_id=1, source_target_pairs={{65,64},{66,65},{67,66},{68,67},{69,68},{70,69},{71,70},{72,71},{7... | collective-permute-start | bytes 3145736 | tf_op jit(solution)/shard_map/ppermute | solution.py:318
  118.5 2.2 %all-to-all-done = bf16[16,256,128]{2,1,0:T(8,128)(2,1)S(1)} async-done(((bf16[16,256,128]{2,1,0:T(8,128)(2,1)}), bf16[16,256,128]{2,1,0:T(8,128)(2,1)S(1)}, u32[]{:S(2)}, u32[]{:S(2)}) %all-to-all-start) | async-done | bytes 1048608 | tf_op jit(solution)/shard_map/all_to_all | solution.py:350
  120.7 0.8 convert_reduce_fusion
  121.5 4.5 %all-to-all-start.1 = ((f32[4,64,128]{2,1,0:T(8,128)}), f32[4,64,128]{2,1,0:T(8,128)S(1)}, u32[]{:S(2)}, u32[]{:S(2)}) async-start(f32[4,64,128]{2,1,0:T(8,128)} %bitcast.15), calls=%async_computation.1 | async-start | bytes 262144 | tf_op jit(solution)/shard_map/all_to_all | solution.py:350
  126.1 7.4 %collective-permute-done.11 = bf16[128,4096]{1,0:T(8,128)(2,1)} collective-permute-done((bf16[128,4096]{1,0:T(8,128)(2,1)}, bf16[128,4096]{1,0:T(8,128)(2,1)}, u32[]{:S(2)}, u32[]{:S(2)}) %collective-permute-start.11) | collective-permute-done | bytes 1048608 | tf_op jit(solution)/shard_map/ppermute | solution.py:318
  133.5 24.2 %collective-permute-done.12 = bf16[128,4096]{1,0:T(8,128)(2,1)} collective-permute-done((bf16[128,4096]{1,0:T(8,128)(2,1)}, bf16[128,4096]{1,0:T(8,128)(2,1)}, u32[]{:S(2)}, u32[]{:S(2)}) %collective-permute-start.12) | collective-permute-done | bytes 1048608 | tf_op jit(solution)/shard_map/ppermute | solution.py:318
  157.7 1.7 %select_select_fusion.1 = (bf16[128,4096]{1,0:T(8,128)(2,1)S(1)}, bf16[128,4096]{1,0:T(8,128)(2,1)S(1)}) fusion(bf16[128,4096]{1,0:T(8,128)(2,1)S(1)} %copy-done.18, bf16[128,4096]{1,0:T(8,128)(2,1)} %collective-permute-done.11, pred[]{:T(512)S(6)} %and.23, pred[]{:T(512)S(6)} %and.21, bf16[128,4096]{1,0:T(8,128)(2,1)} %collective-permute-done.12, ...), kind=kLoop, calls=%fused_computation.4 | loop fusion | flops 2097152 | bytes 5242884 | tf_op jit(solution)/shard_map/jit(_where)/select_n | solution.py:412
  159.4 1.8 %maximum_bitcast_fusion = bf16[1,384,4096]{2,1,0:T(8,128)(2,1)} fusion(bf16[128,4096]{1,0:T(8,128)(2,1)S(1)} %get-tuple-element.64, bf16[128,4096]{1,0:T(8,128)(2,1)S(1)} %get-tuple-element.59, bf16[128,4096]{1,0:T(8,128)(2,1)S(1)} %get-tuple-element.63), kind=kLoop, calls=%fused_computation | loop fusion | flops 9437184 | bytes 6291456 | tf_op jit(solution)/shard_map/broadcast_in_dim | solution.py:417
  161.2 0.6 reduce_sum.19
  161.8 2.5 %copy.19 = bf16[1,128,5120]{2,1,0:T(8,128)(2,1)} copy(bf16[1,128,5120]{2,1,0:T(8,128)(2,1)} %bitcast.13) | data formatting | bytes 2621440
  (48 shorter events, 0.2 us)
Async XLA Ops:
  0.6 6.2 %copy-start = (bf16[1,384,4096]{2,1,0:T(8,128)(2,1)S(1)}, bf16[1,384,4096]{2,1,0:T(8,128)(2,1)}, u32[]{:S(2)}) copy-start(bf16[1,384,4096]{2,1,0:T(8,128)(2,1)} %param.11) | copy-start | bytes 9437188
  3.5 10.6 %copy-start.21 = (s32[2,64,8]{1,2,0:T(8,128)S(1)}, s32[2,64,8]{1,2,0:T(8,128)}, u32[]{:S(2)}) copy-start(s32[2,64,8]{1,2,0:T(8,128)} %param.16) | copy-start | bytes 12292
  3.5 10.8 %copy-start.14 = (s32[2,64]{1,0:T(2,128)S(1)}, s32[2,64]{1,0:T(2,128)}, u32[]{:S(2)}) copy-start(s32[2,64]{1,0:T(2,128)} %langs_ref.7) | copy-start | bytes 1540
  3.5 10.8 %copy-start.16 = (f32[102]{0:T(128)S(1)}, f32[102]{0:T(128)}, u32[]{:S(2)}) copy-start(f32[102]{0:T(128)} %table_ref.7) | copy-start | bytes 1228
  3.5 27.7 %collective-permute-start.2 = (bf16[128,4096]{1,0:T(8,128)(2,1)}, bf16[128,4096]{1,0:T(8,128)(2,1)}, u32[]{:S(2)}, u32[]{:S(2)}) collective-permute-start(bf16[128,4096]{1,0:T(8,128)(2,1)} %broadcast_select_fusion.1), channel_id=1, source_target_pairs={{195,2},{199,6},{203,10},{207,14},{211,18},{215,22},{219,26},{223,... | collective-permute-start | bytes 3145736 | tf_op jit(solution)/shard_map/ppermute | solution.py:318
  8.4 22.8 %collective-permute-start = (bf16[128,4096]{1,0:T(8,128)(2,1)}, bf16[128,4096]{1,0:T(8,128)(2,1)}, u32[]{:S(2)}, u32[]{:S(2)}) collective-permute-start(bf16[128,4096]{1,0:T(8,128)(2,1)} %get-tuple-element.37), channel_id=1, source_target_pairs={{64,65},{65,66},{66,67},{67,68},{68,69},{69,70},{70,71},{71,72},{7... | collective-permute-start | bytes 3145736 | tf_op jit(solution)/shard_map/ppermute | solution.py:318
  10.0 21.2 %collective-permute-start.1 = (bf16[128,4096]{1,0:T(8,128)(2,1)}, bf16[128,4096]{1,0:T(8,128)(2,1)}, u32[]{:S(2)}, u32[]{:S(2)}) collective-permute-start(bf16[128,4096]{1,0:T(8,128)(2,1)} %get-tuple-element.38), channel_id=1, source_target_pairs={{65,64},{66,65},{67,66},{68,67},{69,68},{70,69},{71,70},{72,71},{7... | collective-permute-start | bytes 3145736 | tf_op jit(solution)/shard_map/ppermute | solution.py:318
  11.6 12.9 %copy-start.15 = (s32[2,64]{1,0:T(2,128)S(1)}, s32[2,64]{1,0:T(2,128)}, u32[]{:S(2)}) copy-start(s32[2,64]{1,0:T(2,128)} %dest_ref.5) | copy-start | bytes 1540
  14.2 1.2 copy-start.2
  15.5 1.0 copy-start.5
  16.5 1.3 copy-start.9
  17.8 6.7 %copy-start.3 = (bf16[1,4096,64]{2,1,0:T(8,128)(2,1)S(1)}, bf16[1,4096,64]{2,1,0:T(8,128)(2,1)}, u32[]{:S(2)}) copy-start(bf16[1,4096,64]{2,1,0:T(8,128)(2,1)} %copy.15) | copy-start | bytes 1572868
  17.8 6.7 %copy-start.4 = (bf16[1,128,5120]{2,1,0:T(8,128)(2,1)S(1)}, bf16[1,128,5120]{2,1,0:T(8,128)(2,1)}, u32[]{:S(2)}) copy-start(bf16[1,128,5120]{2,1,0:T(8,128)(2,1)} %param.10) | copy-start | bytes 3932164
  17.8 6.7 %copy-start.6 = (bf16[1,64,4096]{2,1,0:T(8,128)(2,1)S(1)}, bf16[1,64,4096]{2,1,0:T(8,128)(2,1)}, u32[]{:S(2)}) copy-start(bf16[1,64,4096]{2,1,0:T(8,128)(2,1)} %param.13) | copy-start | bytes 1572868
  22.5 8.7 %collective-permute-start.3 = (bf16[128,4096]{1,0:T(8,128)(2,1)S(1)}, bf16[128,4096]{1,0:T(8,128)(2,1)S(1)}, u32[]{:S(2)}, u32[]{:S(2)}) collective-permute-start(bf16[128,4096]{1,0:T(8,128)(2,1)S(1)} %forward_tile.1), channel_id=1, source_target_pairs={{0,64},{1,65},{2,66},{3,67},{4,68},{5,69},{6,70},{7,71},{8,72},{9,... | collective-permute-start | bytes 3145736 | tf_op jit(solution)/shard_map/ppermute | solution.py:318
  23.8 7.4 %collective-permute-start.4 = (bf16[128,2048]{1,0:T(8,128)(2,1)S(1)}, bf16[128,2048]{1,0:T(8,128)(2,1)S(1)}, u32[]{:S(2)}, u32[]{:S(2)}) collective-permute-start(bf16[128,2048]{1,0:T(8,128)(2,1)S(1)} %slice.26), channel_id=1, source_target_pairs={{64,128},{65,129},{66,130},{67,131},{68,132},{69,133},{70,134},{71... | collective-permute-start | bytes 1572872 | tf_op jit(solution)/shard_map/ppermute | solution.py:318
  28.9 1.3 copy-start.8
  30.2 1.0 copy-start.10
  31.2 30.4 %copy-start.20 = (bf16[128,2048]{1,0:T(8,128)(2,1)}, bf16[128,2048]{1,0:T(8,128)(2,1)S(1)}, u32[]{:S(2)}) copy-start(bf16[128,2048]{1,0:T(8,128)(2,1)S(1)} %collective-permute-done.4) | copy-start | bytes 1572868
  31.2 30.4 %copy-start.17 = (bf16[128,4096]{1,0:T(8,128)(2,1)}, bf16[128,4096]{1,0:T(8,128)(2,1)S(1)}, u32[]{:S(2)}) copy-start(bf16[128,4096]{1,0:T(8,128)(2,1)S(1)} %collective-permute-done.3) | copy-start | bytes 3145732
  31.2 16.0 %collective-permute-start.5 = (bf16[128,4096]{1,0:T(8,128)(2,1)}, bf16[128,4096]{1,0:T(8,128)(2,1)S(1)}, u32[]{:S(2)}, u32[]{:S(2)}) collective-permute-start(bf16[128,4096]{1,0:T(8,128)(2,1)} %get-tuple-element.37), channel_id=1, source_target_pairs={{192,193},{193,194},{194,195},{196,197},{197,198},{198,199},{200,2... | collective-permute-start | bytes 3145736 | tf_op jit(solution)/shard_map/ppermute | solution.py:318
  32.5 20.1 %collective-permute-start.6 = (bf16[128,4096]{1,0:T(8,128)(2,1)}, bf16[128,4096]{1,0:T(8,128)(2,1)S(1)}, u32[]{:S(2)}, u32[]{:S(2)}) collective-permute-start(bf16[128,4096]{1,0:T(8,128)(2,1)} %get-tuple-element.38), channel_id=1, source_target_pairs={{193,192},{194,193},{195,194},{197,196},{198,197},{199,198},{201,2... | collective-permute-start | bytes 3145736 | tf_op jit(solution)/shard_map/ppermute | solution.py:318
  36.6 25.0 %collective-permute-start.7 = (bf16[128,4096]{1,0:T(8,128)(2,1)}, bf16[128,4096]{1,0:T(8,128)(2,1)S(1)}, u32[]{:S(2)}, u32[]{:S(2)}) collective-permute-start(bf16[128,4096]{1,0:T(8,128)(2,1)} %collective-permute-done.2), channel_id=1, source_target_pairs={{2,196},{6,200},{10,204},{14,208},{18,212},{22,216},{26,220},{30,2... | collective-permute-start | bytes 3145736 | tf_op jit(solution)/shard_map/ppermute | solution.py:318
  61.6 1.0 copy-start.19
  62.6 13.1 %slice-start = ((s32[2,64]{1,0:T(2,128)}), s32[1,64]{1,0:T(1,128)S(1)}, s32[]{:S(2)}) async-start(s32[2,64]{1,0:T(2,128)} %dest_ref.5), calls=%async_computation.2 | async-start | bytes 1024 | tf_op jit(solution)/shard_map/slice | solution.py:410
  62.6 24.4 %copy-start.1 = (bf16[1,384,4096]{2,1,0:T(8,128)(2,1)S(1)}, bf16[1,384,4096]{2,1,0:T(8,128)(2,1)}, u32[]{:S(2)}) copy-start(bf16[1,384,4096]{2,1,0:T(8,128)(2,1)} %param.11) | copy-start | bytes 9437188
  71.8 1.1 copy-start.12
  72.9 19.3 %collective-permute-start.8 = (bf16[128,2048]{1,0:T(8,128)(2,1)}, bf16[128,2048]{1,0:T(8,128)(2,1)}, u32[]{:S(2)}, u32[]{:S(2)}) collective-permute-start(bf16[128,2048]{1,0:T(8,128)(2,1)} %slice.27), channel_id=1, source_target_pairs={{64,128},{65,129},{66,130},{67,131},{68,132},{69,133},{70,134},{71... | collective-permute-start | bytes 1572872 | tf_op jit(solution)/shard_map/ppermute | solution.py:318
  74.4 12.6 %collective-permute-start.10 = (bf16[128,128]{1,0:T(8,128)(2,1)S(1)}, bf16[128,128]{1,0:T(8,128)(2,1)S(1)}, u32[]{:S(2)}, u32[]{:S(2)}) collective-permute-start(bf16[128,128]{1,0:T(8,128)(2,1)S(1)} %get-tuple-element.51), channel_id=1, source_target_pairs={{1,0},{2,1},{3,2},{4,3},{5,4},{6,5},{7,6},{8,7},{9,8},{10,9},{11,1... | collective-permute-start | bytes 98312 | tf_op jit(solution)/shard_map/ppermute | solution.py:318
  75.0 12.0 %collective-permute-start.9 = (bf16[128,128]{1,0:T(8,128)(2,1)S(1)}, bf16[128,128]{1,0:T(8,128)(2,1)S(1)}, u32[]{:S(2)}, u32[]{:S(2)}) collective-permute-start(bf16[128,128]{1,0:T(8,128)(2,1)S(1)} %get-tuple-element.49), channel_id=1, source_target_pairs={{0,1},{1,2},{2,3},{3,4},{4,5},{5,6},{6,7},{7,8},{8,9},{9,10},{10,1... | collective-permute-start | bytes 98312 | tf_op jit(solution)/shard_map/ppermute | solution.py:318
  77.0 41.5 %collective-permute-start.13 = (bf16[128,5120]{1,0:T(8,128)(2,1)}, bf16[128,5120]{1,0:T(8,128)(2,1)}, u32[]{:S(2)}, u32[]{:S(2)}) collective-permute-start(bf16[128,5120]{1,0:T(8,128)(2,1)} %get-tuple-element.56), channel_id=1, source_target_pairs={{64,0},{65,1},{66,2},{67,3},{68,4},{69,5},{70,6},{71,7},{72,8},{73... | collective-permute-start | bytes 3932168 | tf_op jit(solution)/shard_map/ppermute | solution.py:318
  87.0 1.2 copy-start.11
  88.3 1.2 copy-start.13
  91.2 1.0 copy-start.7
  92.2 28.6 %all-to-all-start = ((bf16[16,256,128]{2,1,0:T(8,128)(2,1)}), bf16[16,256,128]{2,1,0:T(8,128)(2,1)S(1)}, u32[]{:S(2)}, u32[]{:S(2)}) async-start(bf16[16,256,128]{2,1,0:T(8,128)(2,1)} %bitcast.35), calls=%async_computation | async-start | bytes 2097152 | tf_op jit(solution)/shard_map/all_to_all | solution.py:350
  108.9 48.8 %copy-start.18 = (bf16[128,4096]{1,0:T(8,128)(2,1)S(1)}, bf16[128,4096]{1,0:T(8,128)(2,1)}, u32[]{:S(2)}) copy-start(bf16[128,4096]{1,0:T(8,128)(2,1)} %copy-done.17) | copy-start | bytes 3145732
  111.9 21.6 %collective-permute-start.11 = (bf16[128,4096]{1,0:T(8,128)(2,1)}, bf16[128,4096]{1,0:T(8,128)(2,1)}, u32[]{:S(2)}, u32[]{:S(2)}) collective-permute-start(bf16[128,4096]{1,0:T(8,128)(2,1)} %get-tuple-element.60), channel_id=1, source_target_pairs={{64,65},{65,66},{66,67},{67,68},{68,69},{69,70},{70,71},{71,72},{7... | collective-permute-start | bytes 3145736 | tf_op jit(solution)/shard_map/ppermute | solution.py:318
  115.0 42.7 %collective-permute-start.12 = (bf16[128,4096]{1,0:T(8,128)(2,1)}, bf16[128,4096]{1,0:T(8,128)(2,1)}, u32[]{:S(2)}, u32[]{:S(2)}) collective-permute-start(bf16[128,4096]{1,0:T(8,128)(2,1)} %get-tuple-element.60), channel_id=1, source_target_pairs={{65,64},{66,65},{67,66},{68,67},{69,68},{70,69},{71,70},{72,71},{7... | collective-permute-start | bytes 3145736 | tf_op jit(solution)/shard_map/ppermute | solution.py:318
  121.5 39.7 %all-to-all-start.1 = ((f32[4,64,128]{2,1,0:T(8,128)}), f32[4,64,128]{2,1,0:T(8,128)S(1)}, u32[]{:S(2)}, u32[]{:S(2)}) async-start(f32[4,64,128]{2,1,0:T(8,128)} %bitcast.15), calls=%async_computation.1 | async-start | bytes 262144 | tf_op jit(solution)/shard_map/all_to_all | solution.py:350

commit v8 on v6

--- a/solution.py
+++ b/solution.py
@@ -299,6 +299,55 @@
     )(place, languages, dest, table, qkv, *moved, slots, probs, down, up)
 
 
+def place_kernel(
+    place_ref, dest_ref, before_ref, hop_ref, after_ref, ends_ref, back_ref,
+    placed_ref, handed_ref, zero_ref, sems,
+):
+    rank, section = place_ref[0], place_ref[1]
+    tiles = dest_ref.shape[1]
+    zero_ref[...] = jnp.zeros(zero_ref.shape, BF16)
+    handed = pltpu.make_async_copy(back_ref, handed_ref, sems.at[0])
+    handed.start()
+    copies = []
+    for k, (near_ref, edge) in enumerate(
+        ((before_ref, run_start(rank)), (hop_ref, False), (after_ref, run_end(rank)))
+    ):
+        tile = rank + (k - 1)
+        held = jnp.clip(tile, 0, tiles - 1)
+        live = (tile == held) & (dest_ref[0, held] == rank) & (section > 0)
+        crossed = (section == 2) & edge
+        slot = placed_ref.at[pl.ds(k * TILE, TILE), :]
+        for source, chosen in (
+            (near_ref, live & jnp.logical_not(crossed)),
+            (ends_ref, live & crossed),
+            (zero_ref, jnp.logical_not(live)),
+        ):
+            copy = pltpu.make_async_copy(source, slot, sems.at[k + 1])
+            copies.append((copy, chosen))
+    for copy, chosen in copies:
+        pl.when(chosen)(copy.start)
+    for copy, chosen in copies:
+        pl.when(chosen)(copy.wait)
+    handed.wait()
+
+
+def run_place(place, dest, before, hop, after, ends, back):
+    hbm = pl.BlockSpec(memory_space=pl.ANY)
+    return pl.pallas_call(
+        place_kernel,
+        out_shape=(
+            jax.ShapeDtypeStruct((3 * TILE, QW), BF16),
+            jax.ShapeDtypeStruct(back.shape, BF16),
+        ),
+        in_specs=[SMEM] * 2 + [VMEM] * 5,
+        out_specs=(hbm, hbm),
+        scratch_shapes=[pltpu.VMEM((TILE, QW), BF16), pltpu.SemaphoreType.DMA((4,))],
+        compiler_params=pltpu.CompilerParams(vmem_limit_bytes=24 * 2**20),
+        cost_estimate=COST,
+        name="place_outputs",
+    )(place, dest, before, hop, after, ends, back)
+
+
 def sections():
     return lax.axis_size("section")
 
@@ -352,25 +401,25 @@
     from_right = shift(to_down, [(early, 0, -1, anywhere)])
     out = run_forward(place, lengths, languages, lang_scale, qkv_a[0], down, up)
     out, place = lax.optimization_barrier((out, place))
-    near = shift(out, [([0, 2], 1, 0, anywhere)])
-    far = shift(out, [([1], 1, 0, anywhere)])
+    hop = shift(out, [(every, 1, 0, anywhere)])
     probs, attn, low, to_left, own, to_right = run_prepare(
         place, lengths, languages, destination, lang_scale, qkv_b[0], slots, down, up
     )
     from_left, from_right, low = lax.optimization_barrier((from_left, from_right, low))
-    to_up, to_down, near, low = lax.optimization_barrier((to_up, to_down, near, low))
+    to_up, to_down, hop, low = lax.optimization_barrier((to_up, to_down, hop, low))
     last_left = shift(to_up, [([last], 0, 1, anywhere)])
     last_right = shift(to_down, [([last], 0, -1, anywhere)])
     grad_qkv, scaled, back = run_backward(
         place, languages, destination, lang_scale, qkv_b[0],
         (from_left, from_right, last_left, last_right), slots, probs, down, up,
     )
-    grad_qkv, near, to_left, to_right = lax.optimization_barrier(
-        (grad_qkv, near, to_left, to_right)
-    )
-    handed_back = shift(grad_qkv, [(every, -1, 0, anywhere)])[None]
-    before = shift(near, [([1, 3], 0, 1, anywhere)])
-    after = shift(near, [([1, 3], 0, -1, anywhere)])
+    grad_qkv, hop, to_left, to_right, out = lax.optimization_barrier(
+        (grad_qkv, hop, to_left, to_right, out)
+    )
+    handed_back = shift(grad_qkv, [(every, -1, 0, anywhere)])
+    ends = shift(out, [([1], 1, 1, run_end), ([1], 1, -1, run_start)])
+    before = shift(hop, [([1, 3], 0, 1, anywhere), ([2], 0, 1, not_run_end)])
+    after = shift(hop, [([1, 3], 0, -1, anywhere), ([2], 0, -1, not_run_start)])
     left = shift(to_right, [([0], 0, 1, anywhere)])
     right = shift(to_left, [([0], 0, -1, anywhere)])
     terms = run_terms(
@@ -378,29 +427,14 @@
     )
     planes = [[RUN * k + z for k in range(size // RUN)] for z in range(RUN)]
     columns = [[RUN * k + z for z in range(RUN)] for k in range(size // RUN)]
-    far, terms = lax.optimization_barrier((far, terms))
     pieces = scatter(terms.reshape(size // RUN, -1, 2 * RANK), planes)
-    crossed = section == 2
-    sent = jnp.where(crossed, far, out)
-    far_before = shift(sent, [([1], 1, 1, run_end), ([2], 0, 1, not_run_end)])
-    far_after = shift(sent, [([1], 1, -1, run_start), ([2], 0, -1, not_run_start)])
-    pieces, handed_back, before, after = lax.optimization_barrier(
-        (pieces, handed_back, before, after)
-    )
+    pieces, gated, before = lax.optimization_barrier((pieces, handed_back, before))
     terms = jnp.sum(pieces.astype(F32), axis=0)
     terms = jnp.sum(scatter(terms.reshape(RUN, -1, 2 * RANK), columns), axis=0)
-    hop = jnp.where(crossed, far, near)
-    slot0 = jnp.where(crossed, far_before, before)
-    slot2 = jnp.where(crossed, far_after, after)
-    dest = destination[0]
-    zero = jnp.zeros((), BF16)
-    slot0 = jnp.where((dest[jnp.maximum(rank - 1, 0)] == rank) & (rank > 0), slot0, zero)
-    slot1 = jnp.where(dest[rank] == rank, hop, zero)
-    slot2 = jnp.where(
-        (dest[jnp.minimum(rank + 1, size - 1)] == rank) & (rank < size - 1), slot2, zero
-    )
-    handed_forward = jnp.concatenate([slot0, slot1, slot2], axis=0)[None]
-    return (handed_forward, handed_back, terms[None])
+    handed_forward, handed_back = run_place(
+        place, destination, before, hop, after, ends, handed_back
+    )
+    return (handed_forward[None], handed_back[None], terms[None])
 
 
 def solution(mesh):

time: 139 us -> 145 us (1.043)
  the two profiles are of different devices: /device:TPU:128 before, /device:TPU:166 now
where the time goes in v8:
time: 145 us; the launch traced here: 144 us
  starting transfers between devices  64.6 us (45%)
  waiting for transfers between devices  44.5 us (31%)
  Pallas kernels  24.5 us (17%)
  local copies, waits for them, and re-layouts  6.86 us (5%)
  other arithmetic  2.73 us (2%)
    all_to_all x2, starting transfers between devices, scatter(): return lax.all_to_all(x, 'dp', 0, 0, axis_index_groups=groups, tiled=True)  43.9 us
    ppermute x11, waiting for transfers between devices, shift(): return lax.ppermute(x, AXES, route)  35.8 us
    ppermute x11, starting transfers between devices, shift(): return lax.ppermute(x, AXES, route)  20.7 us
    pallas_call x1, Pallas kernels, run_backward(): pl.pallas_call(backward_kernel, out_shape=(jax.ShapeDtypeStruct((TILE, QW...  8.85 us
    all_to_all x2, waiting for transfers between devices, scatter(): return lax.all_to_all(x, 'dp', 0, 0, axis_index_groups=groups, tiled=True)  8.73 us
    pallas_call x1, Pallas kernels, run_forward(): pl.pallas_call(forward_kernel, out_shape=jax.ShapeDtypeStruct((TILE, QW),...  4.65 us
    pallas_call x1, Pallas kernels, run_prepare(): pl.pallas_call(prepare_kernel, out_shape=(jax.ShapeDtypeStruct((QW, TILE)...  4.28 us
    pallas_call x1, Pallas kernels, run_place(): pl.pallas_call(place_kernel, out_shape=(jax.ShapeDtypeStruct((3 * TILE, Q...  3.99 us
  transfers between devices with their start and end apart: 13, of which 5 were waited for; matrix products, arithmetic and copies ran while one was open for 2% of the time, Pallas kernels for 11%

profile of v8, /device:TPU:166, one launch (start us, length us, event | category | flops | bytes accessed | tf_op | source)
XLA Modules:
  0.0 144.1 jit_solution(9761339082194544817)
XLA Ops:
  0.7 3.2 %slice_bitcast_fusion = (bf16[128,4096]{1,0:T(8,128)(2,1)}, bf16[128,4096]{1,0:T(8,128)(2,1)}) fusion(bf16[1,384,4096]{2,1,0:T(8,128)(2,1)} %param.11), kind=kLoop, calls=%fused_computation.1 | loop fusion | bytes 4194304 | tf_op jit(solution)/shard_map/slice | solution.py:399
  3.9 2.9 %collective-permute-start.1 = (bf16[128,4096]{1,0:T(8,128)(2,1)}, bf16[128,4096]{1,0:T(8,128)(2,1)}, u32[]{:S(2)}, u32[]{:S(2)}) collective-permute-start(bf16[128,4096]{1,0:T(8,128)(2,1)} %get-tuple-element.38), channel_id=1, source_target_pairs={{65,64},{66,65},{67,66},{68,67},{69,68},{70,69},{71,70},{72,71},{7... | collective-permute-start | bytes 3145736 | tf_op jit(solution)/shard_map/ppermute | solution.py:363
  6.8 2.9 %collective-permute-start = (bf16[128,4096]{1,0:T(8,128)(2,1)}, bf16[128,4096]{1,0:T(8,128)(2,1)}, u32[]{:S(2)}, u32[]{:S(2)}) collective-permute-start(bf16[128,4096]{1,0:T(8,128)(2,1)} %get-tuple-element.37), channel_id=1, source_target_pairs={{64,65},{65,66},{66,67},{67,68},{68,69},{69,70},{70,71},{71,72},{7... | collective-permute-start | bytes 3145736 | tf_op jit(solution)/shard_map/ppermute | solution.py:363
  9.7 0.0 copy-done.13
  9.7 0.1 copy.16.lens_ref
  9.8 0.0 copy-start.3
  9.8 0.0 copy-start.10
  9.9 0.5 copy.15
  10.4 0.0 copy-start
  10.4 0.1 pad_add_fusion.rank_ref.place_ref
  10.4 0.0 copy-done.9
  10.4 0.0 copy-done.4
  10.5 0.0 copy-start.6
  10.5 1.7 %copy-done.6 = bf16[1,128,5120]{2,1,0:T(8,128)(2,1)S(1)} copy-done((bf16[1,128,5120]{2,1,0:T(8,128)(2,1)S(1)}, bf16[1,128,5120]{2,1,0:T(8,128)(2,1)}, u32[]{:S(2)}) %copy-start.6) | copy-done | bytes 1310744
  12.2 4.7 %forward_tile.1 = bf16[128,4096]{1,0:T(8,128)(2,1)S(1)} custom-call(s32[3]{0:T(128)S(1)} %pad_add_fusion.rank_ref.place_ref, s32[2,64,8]{2,1,0:T(8,128)S(1)} %copy.16.lens_ref, s32[2,64]{1,0:T(2,128)S(1)} %copy-done.9, f32[102]{0:T(128)S(1)} %copy-done.11, bf16[128,5120]{1,0:T(8,128)(2,1)S(1)} %bitcast.27, bf16[4096,64]{1,0:T(8,128)(2,1)S(1)} %bitcast.19, ...), custom_call_target="tpu_custom_call" | custom-call | flops 1048576 | bytes 1048576 | tf_op jit(solution)/shard_map/forward_tile/pallas_call | solution.py:240
  16.9 1.9 %collective-permute-start.2 = (bf16[128,4096]{1,0:T(8,128)(2,1)S(1)}, bf16[128,4096]{1,0:T(8,128)(2,1)}, u32[]{:S(2)}, u32[]{:S(2)}) collective-permute-start(bf16[128,4096]{1,0:T(8,128)(2,1)S(1)} %forward_tile.1), channel_id=1, source_target_pairs={{0,64},{1,65},{2,66},{3,67},{4,68},{5,69},{6,70},{7,71},{8,72},{9,... | collective-permute-start | bytes 3145736 | tf_op jit(solution)/shard_map/ppermute | solution.py:363
  18.8 4.3 %prepare_tile.1 = (f32[4096,128]{1,0:T(8,128)S(1)}, bf16[128,4096]{1,0:T(8,128)(2,1)S(1)}, bf16[128,64]{1,0:T(8,128)(2,1)S(1)}, bf16[128,128]{1,0:T(8,128)(2,1)S...) custom-call(s32[3]{0:T(128)S(1)} %pad_add_fusion.rank_ref.place_ref, s32[2,64,8]{2,1,0:T(8,128)S(1)} %copy.16.lens_ref, ...), custom_call_target="tpu_custom_call" | custom-call | flops 1048576 | bytes 1048576 | tf_op jit(solution)/shard_map/prepare_tile/pallas_call | solution.py:254
  23.1 0.0 copy-start.5
  23.2 1.3 copy-done.5
  24.5 0.0 collective-permute-done.1.right_ref
  24.5 21.7 %collective-permute-done.left_ref = bf16[128,4096]{1,0:T(8,128)(2,1)} collective-permute-done((bf16[128,4096]{1,0:T(8,128)(2,1)}, bf16[128,4096]{1,0:T(8,128)(2,1)}, u32[]{:S(2)}, u32[]{:S(2)}) %collective-permute-start) | collective-permute-done | bytes 1048608 | tf_op jit(solution)/shard_map/ppermute | solution.py:363
  46.2 8.7 %collective-permute-done.2.hop_ref = bf16[128,4096]{1,0:T(8,128)(2,1)} collective-permute-done((bf16[128,4096]{1,0:T(8,128)(2,1)S(1)}, bf16[128,4096]{1,0:T(8,128)(2,1)}, u32[]{:S(2)}, u32[]{:S(2)}) %collective-permute-start.2) | collective-permute-done | bytes 1048608 | tf_op jit(solution)/shard_map/ppermute | solution.py:363
  54.8 0.7 collective-permute-start.3
  55.5 0.7 collective-permute-start.4
  56.3 0.0 collective-permute-done.3.last_left_ref
  56.3 0.0 collective-permute-done.4.last_right_ref
  56.3 0.0 copy-start.1
  56.3 8.8 %backward_tile.1 = (bf16[128,5120]{1,0:T(8,128)(2,1)}, bf16[128,4096]{1,0:T(8,128)(2,1)S(1)}, bf16[128,64]{1,0:T(8,128)(2,1)S(1)}) custom-call(s32[3]{0:T(128)S(1)} %pad_add_fusion.rank_ref.place_ref, s32[2,64]{1,0:T(2,128)S(1)} %copy-done.9, s32[2,64]{1,0:T(2,128)S(1)} %copy-done.10, f32[102]{0:T(128)S(1)} %copy-done.11, bf16[128,5120]{1,0:T(8,128)(2,1)} %bitcast.22, ...), custom_call_target="tpu_custom_call" | custom-call | flops 1048576 | bytes 1048576 | tf_op jit(solution)/shard_map/backward_tile/pallas_call | solution.py:286
  65.2 1.9 %collective-permute-start.7 = (bf16[128,5120]{1,0:T(8,128)(2,1)}, bf16[128,5120]{1,0:T(8,128)(2,1)S(1)}, u32[]{:S(2)}, u32[]{:S(2)}) collective-permute-start(bf16[128,5120]{1,0:T(8,128)(2,1)} %get-tuple-element.50), channel_id=1, source_target_pairs={{64,0},{65,1},{66,2},{67,3},{68,4},{69,5},{70,6},{71,7},{72,8},{73... | collective-permute-start | bytes 3932168 | tf_op jit(solution)/shard_map/ppermute | solution.py:363
  67.1 4.7 %collective-permute-start.8 = (bf16[128,4096]{1,0:T(8,128)(2,1)}, bf16[128,4096]{1,0:T(8,128)(2,1)S(1)}, u32[]{:S(2)}, u32[]{:S(2)}) collective-permute-start(bf16[128,4096]{1,0:T(8,128)(2,1)} %collective-permute-done.2.hop_ref), channel_id=1, source_target_pairs={{64,65},{65,66},{66,67},{67,68},{68,69},{69,70},{70,71},{71,72},{7... | collective-permute-start | bytes 3145736 | tf_op jit(solution)/shard_map/ppermute | solution.py:363
  71.8 0.7 collective-permute-start.5
  72.5 0.7 collective-permute-start.6
  73.1 0.0 collective-permute-done.5.left_ref
  73.1 0.0 collective-permute-done.6.right_ref
  73.2 2.7 %adapter_terms.1 = bf16[4096,128]{1,0:T(8,128)(2,1)} custom-call(s32[3]{0:T(128)S(1)} %pad_add_fusion.rank_ref.place_ref, s32[2,64]{1,0:T(2,128)S(1)} %copy-done.9, s32[2,64]{1,0:T(2,128)S(1)} %copy-done.10, f32[102]{0:T(128)S(1)} %copy-done.11, bf16[128,4096]{1,0:T(8,128)(2,1)S(1)} %get-tuple-element.31.attn_ref, bf16[384,4096]{1,0:T(8,128)(2,1)S(1)} %bitcast.18, ...), custom_call_target="tpu_custom_call" | custom-call | flops 1048576 | bytes 1048576 | tf_op jit(solution)/shard_map/adapter_terms/pallas_call | solution.py:273
  75.8 7.3 %all-to-all-start = ((bf16[16,256,128]{2,1,0:T(8,128)(2,1)}), bf16[16,256,128]{2,1,0:T(8,128)(2,1)}, u32[]{:S(2)}, u32[]{:S(2)}) async-start(bf16[16,256,128]{2,1,0:T(8,128)(2,1)} %bitcast.9), calls=%async_computation | async-start | bytes 2097152 | tf_op jit(solution)/shard_map/all_to_all | solution.py:387
  83.2 1.6 %collective-permute-start.10 = (bf16[128,4096]{1,0:T(8,128)(2,1)S(1)}, bf16[128,4096]{1,0:T(8,128)(2,1)}, u32[]{:S(2)}, u32[]{:S(2)}) collective-permute-start(bf16[128,4096]{1,0:T(8,128)(2,1)S(1)} %copy-done.8), channel_id=1, source_target_pairs={{67,132},{71,136},{75,140},{79,144},{83,148},{87,152},{91,156},{95... | collective-permute-start | bytes 3145736 | tf_op jit(solution)/shard_map/ppermute | solution.py:363
  84.8 1.9 %collective-permute-start.9 = (bf16[128,4096]{1,0:T(8,128)(2,1)}, bf16[128,4096]{1,0:T(8,128)(2,1)}, u32[]{:S(2)}, u32[]{:S(2)}) collective-permute-start(bf16[128,4096]{1,0:T(8,128)(2,1)} %collective-permute-done.2.hop_ref), channel_id=1, source_target_pairs={{65,64},{66,65},{67,66},{68,67},{69,68},{70,69},{71,70},{72,71},{7... | collective-permute-start | bytes 3145736 | tf_op jit(solution)/shard_map/ppermute | solution.py:363
  86.7 7.6 %all-to-all-done = bf16[16,256,128]{2,1,0:T(8,128)(2,1)} async-done(((bf16[16,256,128]{2,1,0:T(8,128)(2,1)}), bf16[16,256,128]{2,1,0:T(8,128)(2,1)}, u32[]{:S(2)}, u32[]{:S(2)}) %all-to-all-start) | async-done | bytes 1048608 | tf_op jit(solution)/shard_map/all_to_all | solution.py:387
  94.3 5.4 %collective-permute-done.8.before_ref = bf16[128,4096]{1,0:T(8,128)(2,1)S(1)} collective-permute-done((bf16[128,4096]{1,0:T(8,128)(2,1)}, bf16[128,4096]{1,0:T(8,128)(2,1)S(1)}, u32[]{:S(2)}, u32[]{:S(2)}) %collective-permute-start.8) | collective-permute-done | bytes 1048608 | tf_op jit(solution)/shard_map/ppermute | solution.py:363
  99.7 0.0 collective-permute-done.7.back_ref
  99.7 2.0 %convert_reduce_fusion = f32[256,128]{1,0:T(8,128)} fusion(bf16[16,256,128]{2,1,0:T(8,128)(2,1)} %all-to-all-done), kind=kLoop, calls=%fused_computation | loop fusion | flops 1015808 | bytes 1179648 | tf_op jit(solution)/shard_map/reduce_sum | solution.py:432
  101.7 36.6 %all-to-all-start.1 = ((f32[4,64,128]{2,1,0:T(8,128)}), f32[4,64,128]{2,1,0:T(8,128)S(1)}, u32[]{:S(2)}, u32[]{:S(2)}) async-start(f32[4,64,128]{2,1,0:T(8,128)} %bitcast.12), calls=%async_computation.1 | async-start | bytes 262144 | tf_op jit(solution)/shard_map/all_to_all | solution.py:387
  138.3 0.0 collective-permute-done.10.ends_ref
  138.3 0.0 collective-permute-done.9.after_ref
  138.3 4.0 %place_outputs.1 = (bf16[384,4096]{1,0:T(8,128)(2,1)}, bf16[128,5120]{1,0:T(8,128)(2,1)}) custom-call(s32[3]{0:T(128)S(1)} %pad_add_fusion.rank_ref.place_ref, s32[2,64]{1,0:T(2,128)S(1)} %copy-done.10, bf16[128,4096]{1,0:T(8,128)(2,1)S(1)} %collective-permute-done.8.before_ref, bf16[128,4096]{1,0:T(8,128)(2,1)} %collective-permute-done.2.hop_ref, ...), custom_call_target="tpu_custom_call" | custom-call | flops 1048576 | bytes 1048576 | tf_op jit(solution)/shard_map/place_outputs/pallas_call | solution.py:336
  142.3 1.2 all-to-all-done.1
  143.5 0.6 reduce_sum.19
  (17 shorter events, 0.0 us)
Async XLA Ops:
  0.6 9.1 %copy-start.13 = (s32[2,64,8]{1,2,0:T(8,128)S(1)}, s32[2,64,8]{1,2,0:T(8,128)}, u32[]{:S(2)}) copy-start(s32[2,64,8]{1,2,0:T(8,128)} %param.16) | copy-start | bytes 12292
  0.6 9.2 %copy-start.12 = (bf16[1,4096,64]{1,2,0:T(8,128)(2,1)S(1)}, bf16[1,4096,64]{1,2,0:T(8,128)(2,1)}, u32[]{:S(2)}) copy-start(bf16[1,4096,64]{1,2,0:T(8,128)(2,1)} %param.12) | copy-start | bytes 1572868
  0.7 9.8 %copy-start.9 = (s32[2,64]{1,0:T(2,128)S(1)}, s32[2,64]{1,0:T(2,128)}, u32[]{:S(2)}) copy-start(s32[2,64]{1,0:T(2,128)} %langs_ref.7) | copy-start | bytes 1540
  0.7 9.8 %copy-start.11 = (f32[102]{0:T(128)S(1)}, f32[102]{0:T(128)}, u32[]{:S(2)}) copy-start(f32[102]{0:T(128)} %table_ref.7) | copy-start | bytes 1228
  0.7 9.8 %copy-start.4 = (bf16[1,64,4096]{2,1,0:T(8,128)(2,1)S(1)}, bf16[1,64,4096]{2,1,0:T(8,128)(2,1)}, u32[]{:S(2)}) copy-start(bf16[1,64,4096]{2,1,0:T(8,128)(2,1)} %param.13) | copy-start | bytes 1572868
  3.9 20.6 %collective-permute-start.1 = (bf16[128,4096]{1,0:T(8,128)(2,1)}, bf16[128,4096]{1,0:T(8,128)(2,1)}, u32[]{:S(2)}, u32[]{:S(2)}) collective-permute-start(bf16[128,4096]{1,0:T(8,128)(2,1)} %get-tuple-element.38), channel_id=1, source_target_pairs={{65,64},{66,65},{67,66},{68,67},{69,68},{70,69},{71,70},{72,71},{7... | collective-permute-start | bytes 3145736 | tf_op jit(solution)/shard_map/ppermute | solution.py:363
  6.8 39.4 %collective-permute-start = (bf16[128,4096]{1,0:T(8,128)(2,1)}, bf16[128,4096]{1,0:T(8,128)(2,1)}, u32[]{:S(2)}, u32[]{:S(2)}) collective-permute-start(bf16[128,4096]{1,0:T(8,128)(2,1)} %get-tuple-element.37), channel_id=1, source_target_pairs={{64,65},{65,66},{66,67},{67,68},{68,69},{69,70},{70,71},{71,72},{7... | collective-permute-start | bytes 3145736 | tf_op jit(solution)/shard_map/ppermute | solution.py:363
  9.8 9.0 %copy-start.3 = (bf16[1,128,5120]{2,1,0:T(8,128)(2,1)S(1)}, bf16[1,128,5120]{2,1,0:T(8,128)(2,1)}, u32[]{:S(2)}) copy-start(bf16[1,128,5120]{2,1,0:T(8,128)(2,1)} %param.10) | copy-start | bytes 3932164
  9.8 9.0 %copy-start.10 = (s32[2,64]{1,0:T(2,128)S(1)}, s32[2,64]{1,0:T(2,128)}, u32[]{:S(2)}) copy-start(s32[2,64]{1,0:T(2,128)} %dest_ref.7) | copy-start | bytes 1540
  10.3 12.8 %copy-start.2 = (bf16[1,4096,64]{2,1,0:T(8,128)(2,1)}, bf16[1,4096,64]{2,1,0:T(8,128)(2,1)S(1)}, u32[]{:S(2)}) copy-start(bf16[1,4096,64]{2,1,0:T(8,128)(2,1)S(1)} %copy.15) | copy-start | bytes 1572868
  10.4 8.5 %copy-start = (bf16[1,384,4096]{2,1,0:T(8,128)(2,1)S(1)}, bf16[1,384,4096]{2,1,0:T(8,128)(2,1)}, u32[]{:S(2)}) copy-start(bf16[1,384,4096]{2,1,0:T(8,128)(2,1)} %param.11) | copy-start | bytes 9437188
  10.5 1.8 %copy-start.6 = (bf16[1,128,5120]{2,1,0:T(8,128)(2,1)S(1)}, bf16[1,128,5120]{2,1,0:T(8,128)(2,1)}, u32[]{:S(2)}) copy-start(bf16[1,128,5120]{2,1,0:T(8,128)(2,1)} %param.9) | copy-start | bytes 3932164
  16.9 6.3 %copy-start.7 = (bf16[128,4096]{1,0:T(8,128)(2,1)}, bf16[128,4096]{1,0:T(8,128)(2,1)S(1)}, u32[]{:S(2)}) copy-start(bf16[128,4096]{1,0:T(8,128)(2,1)S(1)} %forward_tile.1) | copy-start | bytes 3145732
  16.9 37.9 %collective-permute-start.2 = (bf16[128,4096]{1,0:T(8,128)(2,1)S(1)}, bf16[128,4096]{1,0:T(8,128)(2,1)}, u32[]{:S(2)}, u32[]{:S(2)}) collective-permute-start(bf16[128,4096]{1,0:T(8,128)(2,1)S(1)} %forward_tile.1), channel_id=1, source_target_pairs={{0,64},{1,65},{2,66},{3,67},{4,68},{5,69},{6,70},{7,71},{8,72},{9,... | collective-permute-start | bytes 3145736 | tf_op jit(solution)/shard_map/ppermute | solution.py:363
  23.1 1.3 copy-start.5
  54.8 1.5 %collective-permute-start.3 = (bf16[128,4096]{1,0:T(8,128)(2,1)}, bf16[128,4096]{1,0:T(8,128)(2,1)S(1)}, u32[]{:S(2)}, u32[]{:S(2)}) collective-permute-start(bf16[128,4096]{1,0:T(8,128)(2,1)} %get-tuple-element.37), channel_id=1, source_target_pairs={{192,193},{193,194},{194,195},{195,196},{196,197},{197,198},{198,1... | collective-permute-start | bytes 3145736 | tf_op jit(solution)/shard_map/ppermute | solution.py:363
  55.5 0.7 collective-permute-start.4
  56.3 16.9 %copy-start.1 = (bf16[1,384,4096]{2,1,0:T(8,128)(2,1)S(1)}, bf16[1,384,4096]{2,1,0:T(8,128)(2,1)}, u32[]{:S(2)}) copy-start(bf16[1,384,4096]{2,1,0:T(8,128)(2,1)} %param.11) | copy-start | bytes 9437188
  65.2 34.6 %collective-permute-start.7 = (bf16[128,5120]{1,0:T(8,128)(2,1)}, bf16[128,5120]{1,0:T(8,128)(2,1)S(1)}, u32[]{:S(2)}, u32[]{:S(2)}) collective-permute-start(bf16[128,5120]{1,0:T(8,128)(2,1)} %get-tuple-element.50), channel_id=1, source_target_pairs={{64,0},{65,1},{66,2},{67,3},{68,4},{69,5},{70,6},{71,7},{72,8},{73... | collective-permute-start | bytes 3932168 | tf_op jit(solution)/shard_map/ppermute | solution.py:363
  67.1 32.6 %collective-permute-start.8 = (bf16[128,4096]{1,0:T(8,128)(2,1)}, bf16[128,4096]{1,0:T(8,128)(2,1)S(1)}, u32[]{:S(2)}, u32[]{:S(2)}) collective-permute-start(bf16[128,4096]{1,0:T(8,128)(2,1)} %collective-permute-done.2.hop_ref), channel_id=1, source_target_pairs={{64,65},{65,66},{66,67},{67,68},{68,69},{69,70},{70,71},{71,72},{7... | collective-permute-start | bytes 3145736 | tf_op jit(solution)/shard_map/ppermute | solution.py:363
  71.8 1.3 collective-permute-start.5
  72.5 0.7 collective-permute-start.6
  75.8 7.3 %copy-start.8 = (bf16[128,4096]{1,0:T(8,128)(2,1)S(1)}, bf16[128,4096]{1,0:T(8,128)(2,1)}, u32[]{:S(2)}) copy-start(bf16[128,4096]{1,0:T(8,128)(2,1)} %copy-done.7) | copy-start | bytes 3145732
  75.8 18.4 %all-to-all-start = ((bf16[16,256,128]{2,1,0:T(8,128)(2,1)}), bf16[16,256,128]{2,1,0:T(8,128)(2,1)}, u32[]{:S(2)}, u32[]{:S(2)}) async-start(bf16[16,256,128]{2,1,0:T(8,128)(2,1)} %bitcast.9), calls=%async_computation | async-start | bytes 2097152 | tf_op jit(solution)/shard_map/all_to_all | solution.py:387
  83.2 55.1 %collective-permute-start.10 = (bf16[128,4096]{1,0:T(8,128)(2,1)S(1)}, bf16[128,4096]{1,0:T(8,128)(2,1)}, u32[]{:S(2)}, u32[]{:S(2)}) collective-permute-start(bf16[128,4096]{1,0:T(8,128)(2,1)S(1)} %copy-done.8), channel_id=1, source_target_pairs={{67,132},{71,136},{75,140},{79,144},{83,148},{87,152},{91,156},{95... | collective-permute-start | bytes 3145736 | tf_op jit(solution)/shard_map/ppermute | solution.py:363
  84.8 53.5 %collective-permute-start.9 = (bf16[128,4096]{1,0:T(8,128)(2,1)}, bf16[128,4096]{1,0:T(8,128)(2,1)}, u32[]{:S(2)}, u32[]{:S(2)}) collective-permute-start(bf16[128,4096]{1,0:T(8,128)(2,1)} %collective-permute-done.2.hop_ref), channel_id=1, source_target_pairs={{65,64},{66,65},{67,66},{68,67},{69,68},{70,69},{71,70},{72,71},{7... | collective-permute-start | bytes 3145736 | tf_op jit(solution)/shard_map/ppermute | solution.py:363
  101.7 41.7 %all-to-all-start.1 = ((f32[4,64,128]{2,1,0:T(8,128)}), f32[4,64,128]{2,1,0:T(8,128)S(1)}, u32[]{:S(2)}, u32[]{:S(2)}) async-start(f32[4,64,128]{2,1,0:T(8,128)} %bitcast.12), calls=%async_computation.1 | async-start | bytes 262144 | tf_op jit(solution)/shard_map/all_to_all | solution.py:387

commit v9 on v8

--- a/solution.py
+++ b/solution.py
@@ -139,7 +139,8 @@
 
 def terms_kernel(
     place_ref, langs_ref, dest_ref, table_ref, attn_ref, slots_ref, left_ref, own_ref, right_ref,
-    scaled_ref, back_ref, low_ref, terms_ref, slot_scaled_ref,
+    one_scaled_ref, one_back_ref, more_scaled_ref, more_back_ref, low_ref, terms_ref,
+    slot_scaled_ref,
 ):
     rank = place_ref[0]
     tiles = dest_ref.shape[1]
@@ -160,31 +161,41 @@
             terms = jnp.concatenate([one[:, RANK:], two[:, :RANK]], axis=1)
             terms_ref[cols, :] = terms.astype(terms_ref.dtype)
 
-    @pl.when(place_ref[1] != 0)
-    def _():
+    def at_home(scaled_ref, back_ref):
         for c in range(0, QW, 512):
             cols = slice(c, c + 512)
             one = dot(attn_ref[:, cols], back_ref[...], TN)
             two = dot(scaled_ref[:, cols], low_ref[...], TN)
             terms_ref[cols, :] = jnp.concatenate([one, two], axis=1).astype(terms_ref.dtype)
 
+    @pl.when(place_ref[1] == 2)
+    def _():
+        at_home(one_scaled_ref, one_back_ref)
+
+    @pl.when((place_ref[1] != 0) & (place_ref[1] != 2))
+    def _():
+        at_home(more_scaled_ref, more_back_ref)
+
 
 def backward_kernel(
-    place_ref, langs_ref, dest_ref, table_ref, qkv_ref, left_ref, right_ref, last_left_ref,
-    last_right_ref, slots_ref, probs_ref, down_ref, up_ref, grad_ref, scaled_ref, back_ref,
+    wanted, place_ref, langs_ref, dest_ref, table_ref, qkv_ref, left_ref, right_ref, more_left_ref,
+    more_right_ref, slots_ref, probs_ref, down_ref, up_ref, grad_ref, scaled_ref, back_ref,
     gattn_ref,
 ):
     rank = place_ref[0]
     rate = table_ref[langs_ref[1, rank]]
     went = dest_ref[1, rank] - rank
-    last = place_ref[1] == place_ref[2] - 1
+    more = place_ref[1] == place_ref[2] - 1
+    active = functools.reduce(jnp.logical_or, [place_ref[1] == s for s in wanted])
 
     def chosen():
         back = jnp.zeros((TILE, RANK), F32)
         for c in range(0, QW, 512):
             cols = slice(c, c + 512)
-            left = jnp.where(last, last_left_ref[:, cols], left_ref[:, cols])
-            right = jnp.where(last, last_right_ref[:, cols], right_ref[:, cols])
+            left, right = left_ref[:, cols], right_ref[:, cols]
+            if more_left_ref is not None:
+                left = jnp.where(more, more_left_ref[:, cols], left)
+                right = jnp.where(more, more_right_ref[:, cols], right)
             mid = slots_ref[TILE : 2 * TILE, cols]
             grad = jnp.where(went < 0, left, jnp.where(went > 0, right, mid))
             gattn_ref[:, cols] = grad
@@ -193,7 +204,7 @@
             back = back + dot(scaled, up_ref[:, cols], NT)
         return back.astype(BF16)
 
-    @pl.when(place_ref[1] != 0)
+    @pl.when(active)
     def _():
         back = chosen()
         back_ref[...] = back
@@ -224,11 +235,14 @@
             cols = slice(QW + KW + j * HEAD_DIM, QW + KW + (j + 1) * HEAD_DIM)
             grad_ref[:, cols] = dot(probs_low, grads, TN).astype(BF16)
 
-    @pl.when(place_ref[1] == 0)
-    def _():
-        grad_ref[...] = jnp.zeros(grad_ref.shape, BF16)
+    @pl.when(jnp.logical_not(active))
+    def _():
         scaled_ref[...] = jnp.zeros(scaled_ref.shape, BF16)
         back_ref[...] = jnp.zeros(back_ref.shape, BF16)
+
+
+def backward_one_kernel(wanted, *refs):
+    backward_kernel(wanted, *refs[:7], None, None, *refs[7:])
 
 
 COST = pl.CostEstimate(flops=2**20, bytes_accessed=2**20, transcendentals=0)
@@ -269,28 +283,29 @@
     )(place, lengths, languages, dest, table, qkv, slots, down, up)
 
 
-def run_terms(place, languages, dest, table, attn, slots, left, own, right, scaled, back, low):
+def run_terms(place, languages, dest, table, attn, slots, left, own, right, one, more, low):
     return pl.pallas_call(
         terms_kernel,
         out_shape=jax.ShapeDtypeStruct((QW, 2 * RANK), BF16),
-        in_specs=[SMEM] * 4 + [VMEM] * 8,
+        in_specs=[SMEM] * 4 + [VMEM] * 10,
         out_specs=VMEM,
         scratch_shapes=[pltpu.VMEM((3 * TILE, 512), BF16)],
         compiler_params=pltpu.CompilerParams(vmem_limit_bytes=40 * 2**20),
         cost_estimate=COST,
         name="adapter_terms",
-    )(place, languages, dest, table, attn, slots, left, own, right, scaled, back, low)
-
-
-def run_backward(place, languages, dest, table, qkv, moved, slots, probs, down, up):
+    )(place, languages, dest, table, attn, slots, left, own, right, *one, *more, low)
+
+
+def run_backward(wanted, place, languages, dest, table, qkv, moved, slots, probs, down, up):
+    kernel = backward_one_kernel if len(moved) == 2 else backward_kernel
     return pl.pallas_call(
-        backward_kernel,
+        functools.partial(kernel, wanted),
         out_shape=(
             jax.ShapeDtypeStruct((TILE, QW + 2 * KW), BF16),
             jax.ShapeDtypeStruct((TILE, QW), BF16),
             jax.ShapeDtypeStruct((TILE, RANK), BF16),
         ),
-        in_specs=[SMEM] * 4 + [VMEM] * 9,
+        in_specs=[SMEM] * 4 + [VMEM] * (5 + len(moved)),
         out_specs=(VMEM,) * 3,
         scratch_shapes=[pltpu.VMEM((TILE, QW), BF16)],
         compiler_params=pltpu.CompilerParams(vmem_limit_bytes=48 * 2**20),
@@ -300,52 +315,50 @@
 
 
 def place_kernel(
-    place_ref, dest_ref, before_ref, hop_ref, after_ref, ends_ref, back_ref,
-    placed_ref, handed_ref, zero_ref, sems,
+    place_ref, dest_ref, before_ref, near_ref, after_ref, far_before_ref, far_ref, far_after_ref,
+    back_one_ref, back_more_ref, placed_ref, handed_ref, zero_ref, sems,
 ):
     rank, section = place_ref[0], place_ref[1]
     tiles = dest_ref.shape[1]
     zero_ref[...] = jnp.zeros(zero_ref.shape, BF16)
-    handed = pltpu.make_async_copy(back_ref, handed_ref, sems.at[0])
-    handed.start()
-    copies = []
-    for k, (near_ref, edge) in enumerate(
-        ((before_ref, run_start(rank)), (hop_ref, False), (after_ref, run_end(rank)))
+    copies = [
+        (pltpu.make_async_copy(back_one_ref, handed_ref, sems.at[0]), section == 1),
+        (pltpu.make_async_copy(back_more_ref, handed_ref, sems.at[0]), section != 1),
+    ]
+    for k, (near, far) in enumerate(
+        ((before_ref, far_before_ref), (near_ref, far_ref), (after_ref, far_after_ref))
     ):
         tile = rank + (k - 1)
         held = jnp.clip(tile, 0, tiles - 1)
         live = (tile == held) & (dest_ref[0, held] == rank) & (section > 0)
-        crossed = (section == 2) & edge
         slot = placed_ref.at[pl.ds(k * TILE, TILE), :]
         for source, chosen in (
-            (near_ref, live & jnp.logical_not(crossed)),
-            (ends_ref, live & crossed),
+            (near, live & (section != 2)),
+            (far, live & (section == 2)),
             (zero_ref, jnp.logical_not(live)),
         ):
-            copy = pltpu.make_async_copy(source, slot, sems.at[k + 1])
-            copies.append((copy, chosen))
+            copies.append((pltpu.make_async_copy(source, slot, sems.at[k + 1]), chosen))
     for copy, chosen in copies:
         pl.when(chosen)(copy.start)
     for copy, chosen in copies:
         pl.when(chosen)(copy.wait)
-    handed.wait()
-
-
-def run_place(place, dest, before, hop, after, ends, back):
+
+
+def run_place(place, dest, *tiles):
     hbm = pl.BlockSpec(memory_space=pl.ANY)
     return pl.pallas_call(
         place_kernel,
         out_shape=(
             jax.ShapeDtypeStruct((3 * TILE, QW), BF16),
-            jax.ShapeDtypeStruct(back.shape, BF16),
+            jax.ShapeDtypeStruct(tiles[-1].shape, BF16),
         ),
-        in_specs=[SMEM] * 2 + [VMEM] * 5,
+        in_specs=[SMEM] * 2 + [VMEM] * len(tiles),
         out_specs=(hbm, hbm),
         scratch_shapes=[pltpu.VMEM((TILE, QW), BF16), pltpu.SemaphoreType.DMA((4,))],
         compiler_params=pltpu.CompilerParams(vmem_limit_bytes=24 * 2**20),
         cost_estimate=COST,
         name="place_outputs",
-    )(place, dest, before, hop, after, ends, back)
+    )(place, dest, *tiles)
 
 
 def sections():
@@ -401,38 +414,44 @@
     from_right = shift(to_down, [(early, 0, -1, anywhere)])
     out = run_forward(place, lengths, languages, lang_scale, qkv_a[0], down, up)
     out, place = lax.optimization_barrier((out, place))
-    hop = shift(out, [(every, 1, 0, anywhere)])
+    near = shift(out, [([0, 2], 1, 0, anywhere)])
+    far = shift(out, [([1], 1, 0, anywhere)])
     probs, attn, low, to_left, own, to_right = run_prepare(
         place, lengths, languages, destination, lang_scale, qkv_b[0], slots, down, up
     )
     from_left, from_right, low = lax.optimization_barrier((from_left, from_right, low))
-    to_up, to_down, hop, low = lax.optimization_barrier((to_up, to_down, hop, low))
+    to_up, to_down, near, low = lax.optimization_barrier((to_up, to_down, near, low))
     last_left = shift(to_up, [([last], 0, 1, anywhere)])
     last_right = shift(to_down, [([last], 0, -1, anywhere)])
-    grad_qkv, scaled, back = run_backward(
-        place, languages, destination, lang_scale, qkv_b[0],
-        (from_left, from_right, last_left, last_right), slots, probs, down, up,
-    )
-    grad_qkv, hop, to_left, to_right, out = lax.optimization_barrier(
-        (grad_qkv, hop, to_left, to_right, out)
-    )
-    handed_back = shift(grad_qkv, [(every, -1, 0, anywhere)])
-    ends = shift(out, [([1], 1, 1, run_end), ([1], 1, -1, run_start)])
-    before = shift(hop, [([1, 3], 0, 1, anywhere), ([2], 0, 1, not_run_end)])
-    after = shift(hop, [([1, 3], 0, -1, anywhere), ([2], 0, -1, not_run_start)])
+    shared = (place, languages, destination, lang_scale, qkv_b[0])
+    grad_one, *one = run_backward((2,), *shared, (from_left, from_right), slots, probs, down, up)
+    back_one = shift(grad_one, [([2], -1, 0, anywhere)])
+    grad_more, *more = run_backward(
+        (1, 3), *shared, (from_left, from_right, last_left, last_right), slots, probs, down, up
+    )
+    grad_more, near, to_left, to_right = lax.optimization_barrier(
+        (grad_more, near, to_left, to_right)
+    )
+    back_more = shift(grad_more, [([1, 3], -1, 0, anywhere)])
+    before = shift(near, [([1, 3], 0, 1, anywhere)])
+    after = shift(near, [([1, 3], 0, -1, anywhere)])
     left = shift(to_right, [([0], 0, 1, anywhere)])
     right = shift(to_left, [([0], 0, -1, anywhere)])
     terms = run_terms(
-        place, languages, destination, lang_scale, attn, slots, left, own, right, scaled, back, low
+        place, languages, destination, lang_scale, attn, slots, left, own, right, one, more, low
     )
     planes = [[RUN * k + z for k in range(size // RUN)] for z in range(RUN)]
     columns = [[RUN * k + z for z in range(RUN)] for k in range(size // RUN)]
+    far, terms = lax.optimization_barrier((far, terms))
     pieces = scatter(terms.reshape(size // RUN, -1, 2 * RANK), planes)
-    pieces, gated, before = lax.optimization_barrier((pieces, handed_back, before))
+    sent = jnp.where(section == 2, far, out)
+    far_before = shift(sent, [([1], 1, 1, run_end), ([2], 0, 1, not_run_end)])
+    far_after = shift(sent, [([1], 1, -1, run_start), ([2], 0, -1, not_run_start)])
+    pieces, _, before, after = lax.optimization_barrier((pieces, back_one, before, after))
     terms = jnp.sum(pieces.astype(F32), axis=0)
     terms = jnp.sum(scatter(terms.reshape(RUN, -1, 2 * RANK), columns), axis=0)
     handed_forward, handed_back = run_place(
-        place, destination, before, hop, after, ends, handed_back
+        place, destination, before, near, after, far_before, far, far_after, back_one, back_more
     )
     return (handed_forward[None], handed_back[None], terms[None])
 

time: 145 us -> 147 us (1.014)
  the two profiles are of different devices: /device:TPU:166 before, /device:TPU:161 now
where the time goes in v9:
time: 147 us; the launch traced here: 146 us
  waiting for transfers between devices  39.5 us (27%)
  Pallas kernels  28.9 us (20%)
  blocking collectives  26.2 us (18%)
  starting transfers between devices  25.7 us (17%)
  local copies, waits for them, and re-layouts  21.8 us (15%)
  other arithmetic  3.16 us (2%)
    ppermute x14, waiting for transfers between devices, shift(): return lax.ppermute(x, AXES, route)  31.6 us
    all_to_all x1, blocking collectives, scatter(): return lax.all_to_all(x, 'dp', 0, 0, axis_index_groups=groups, tiled=True)  26.2 us
    ppermute x14, starting transfers between devices, shift(): return lax.ppermute(x, AXES, route)  22 us
    unnamed x52, local copies, waits for them, and re-layouts  18.6 us
    pallas_call x2, Pallas kernels, run_backward(): pl.pallas_call(functools.partial(kernel, wanted), out_shape=(jax.ShapeDty...  12.4 us
    all_to_all x1, waiting for transfers between devices, scatter(): return lax.all_to_all(x, 'dp', 0, 0, axis_index_groups=groups, tiled=True)  7.93 us
    pallas_call x1, Pallas kernels, run_forward(): pl.pallas_call(forward_kernel, out_shape=jax.ShapeDtypeStruct((TILE, QW),...  5.61 us
    pallas_call x1, Pallas kernels, run_place(): pl.pallas_call(place_kernel, out_shape=(jax.ShapeDtypeStruct((3 * TILE, Q...  5.12 us
  transfers between devices with their start and end apart: 15, of which 3 were waited for; matrix products, arithmetic and copies ran while one was open for 4% of the time, Pallas kernels for 16%

profile of v9, /device:TPU:161, one launch (start us, length us, event | category | flops | bytes accessed | tf_op | source)
XLA Modules:
  0.0 146.3 jit_solution(14008614038527534923)
XLA Ops:
  0.6 3.1 %slice_bitcast_fusion = (bf16[128,4096]{1,0:T(8,128)(2,1)}, bf16[128,4096]{1,0:T(8,128)(2,1)}) fusion(bf16[1,384,4096]{2,1,0:T(8,128)(2,1)} %param.11), kind=kLoop, calls=%fused_computation.1 | loop fusion | bytes 4194304 | tf_op jit(solution)/shard_map/slice | solution.py:412
  3.8 0.9 collective-permute-start.2
  4.7 0.7 collective-permute-start.1
  5.4 0.1 copy.16.lens_ref
  5.5 2.4 %copy.15 = bf16[1,4096,64]{2,1,0:T(8,128)(2,1)} copy(bf16[1,4096,64]{1,2,0:T(8,128)(2,1)} %param.12) | data formatting | bytes 1048576 | tf_op args[3]
  7.9 0.1 pad_add_fusion.rank_ref.place_ref.refs_0_
  8.0 1.2 copy-done.2
  9.2 1.0 copy-done.7
  10.2 5.6 %forward_tile.1 = bf16[128,4096]{1,0:T(8,128)(2,1)} custom-call(s32[3]{0:T(128)S(1)} %pad_add_fusion.rank_ref.place_ref.refs_0_, s32[2,64,8]{2,1,0:T(8,128)S(1)} %copy.16.lens_ref, s32[2,64]{1,0:T(2,128)S(1)} %copy-done.21, f32[102]{0:T(128)S(1)} %copy-done.23, bf16[128,5120]{1,0:T(8,128)(2,1)S(1)} %bitcast.32, bf16[4096,64]{1,0:T(8,128)(2,1)S(1)} %bitcast.21, ...), custom_call_target="tpu_custom_call" | custom-call | flops 1048576 | bytes 1048576 | tf_op jit(solution)/shard_map/forward_tile/pallas_call | solution.py:254
  15.8 1.3 collective-permute-start.3
  17.2 1.2 copy-done.3
  18.4 1.3 copy-done.5
  19.7 4.3 %prepare_tile.1 = (f32[4096,128]{1,0:T(8,128)S(1)}, bf16[128,4096]{1,0:T(8,128)(2,1)S(1)}, bf16[128,64]{1,0:T(8,128)(2,1)S(1)}, bf16[128,128]{1,0:T(8,128)(2,1)S...) custom-call(s32[3]{0:T(128)S(1)} %pad_add_fusion.rank_ref.place_ref.refs_0_, ...), custom_call_target="tpu_custom_call" | custom-call | flops 1048576 | bytes 1048576 | tf_op jit(solution)/shard_map/prepare_tile/pallas_call | solution.py:268
  24.0 0.0 copy-start.6
  24.0 1.3 copy-done.6
  25.3 1.0 copy-done.15
  26.3 0.0 collective-permute-done.2.right_ref.refs_6_
  26.3 2.7 %collective-permute-start.4 = (bf16[128,4096]{1,0:T(8,128)(2,1)}, bf16[128,4096]{1,0:T(8,128)(2,1)S(1)}, u32[]{:S(2)}, u32[]{:S(2)}) collective-permute-start(bf16[128,4096]{1,0:T(8,128)(2,1)} %get-tuple-element.42), channel_id=1, source_target_pairs={{192,193},{193,194},{194,195},{195,196},{196,197},{197,198},{198,1... | collective-permute-start | bytes 3145736 | tf_op jit(solution)/shard_map/ppermute | solution.py:376
  29.0 2.7 %collective-permute-start.5 = (bf16[128,4096]{1,0:T(8,128)(2,1)}, bf16[128,4096]{1,0:T(8,128)(2,1)S(1)}, u32[]{:S(2)}, u32[]{:S(2)}) collective-permute-start(bf16[128,4096]{1,0:T(8,128)(2,1)} %get-tuple-element.43), channel_id=1, source_target_pairs={{193,192},{194,193},{195,194},{196,195},{197,196},{198,197},{199,1... | collective-permute-start | bytes 3145736 | tf_op jit(solution)/shard_map/ppermute | solution.py:376
  31.7 1.6 %collective-permute-start = (bf16[128,4096]{1,0:T(8,128)(2,1)}, bf16[128,4096]{1,0:T(8,128)(2,1)}, u32[]{:S(2)}, u32[]{:S(2)}) collective-permute-start(bf16[128,4096]{1,0:T(8,128)(2,1)} %forward_tile.1), channel_id=1, source_target_pairs={{64,128},{65,129},{66,130},{67,131},{68,132},{69,133},{70,134},{71... | collective-permute-start | bytes 3145736 | tf_op jit(solution)/shard_map/ppermute | solution.py:376
  33.4 4.1 %backward_tile.3 = (bf16[128,5120]{1,0:T(8,128)(2,1)}, bf16[128,4096]{1,0:T(8,128)(2,1)S(1)}, bf16[128,64]{1,0:T(8,128)(2,1)S(1)}) custom-call(s32[3]{0:T(128)S(1)} %pad_add_fusion.rank_ref.place_ref.refs_0_, s32[2,64]{1,0:T(2,128)S(1)} %copy-done.21, s32[2,64]{1,0:T(2,128)S(1)} %copy-done.22, f32[102]{0:T(128)S(1)} %copy-done.23, ...), custom_call_target="tpu_custom_call" | custom-call | flops 1048576 | bytes 1048576 | tf_op jit(solution)/shard_map/backward_tile/pallas_call | solution.py:301
  37.5 1.0 copy-done.17
  38.4 1.7 %collective-permute-start.8 = (bf16[128,5120]{1,0:T(8,128)(2,1)}, bf16[128,5120]{1,0:T(8,128)(2,1)}, u32[]{:S(2)}, u32[]{:S(2)}) collective-permute-start(bf16[128,5120]{1,0:T(8,128)(2,1)} %get-tuple-element.58), channel_id=1, source_target_pairs={{128,64},{129,65},{130,66},{131,67},{132,68},{133,69},{134,70},{13... | collective-permute-start | bytes 3932168 | tf_op jit(solution)/shard_map/ppermute | solution.py:376
  40.1 3.4 %collective-permute-done.4.more_left_ref = bf16[128,4096]{1,0:T(8,128)(2,1)S(1)} collective-permute-done((bf16[128,4096]{1,0:T(8,128)(2,1)}, bf16[128,4096]{1,0:T(8,128)(2,1)S(1)}, u32[]{:S(2)}, u32[]{:S(2)}) %collective-permute-start.4) | collective-permute-done | bytes 1048608 | tf_op jit(solution)/shard_map/ppermute | solution.py:376
  43.5 28.2 %collective-permute-done.5.more_right_ref = bf16[128,4096]{1,0:T(8,128)(2,1)S(1)} collective-permute-done((bf16[128,4096]{1,0:T(8,128)(2,1)}, bf16[128,4096]{1,0:T(8,128)(2,1)S(1)}, u32[]{:S(2)}, u32[]{:S(2)}) %collective-permute-start.5) | collective-permute-done | bytes 1048608 | tf_op jit(solution)/shard_map/ppermute | solution.py:376
  71.7 1.2 copy-done.11
  72.9 1.2 copy-done.13
  74.2 8.3 %backward_tile.2 = (bf16[128,5120]{1,0:T(8,128)(2,1)}, bf16[128,4096]{1,0:T(8,128)(2,1)S(1)}, bf16[128,64]{1,0:T(8,128)(2,1)S(1)}) custom-call(s32[3]{0:T(128)S(1)} %pad_add_fusion.rank_ref.place_ref.refs_0_, s32[2,64]{1,0:T(2,128)S(1)} %copy-done.21, s32[2,64]{1,0:T(2,128)S(1)} %copy-done.22, f32[102]{0:T(128)S(1)} %copy-done.23, ...), custom_call_target="tpu_custom_call" | custom-call | flops 1048576 | bytes 1048576 | tf_op jit(solution)/shard_map/backward_tile/pallas_call | solution.py:301
  82.5 1.0 copy-done.19
  83.4 0.7 collective-permute-start.6
  84.1 0.7 collective-permute-start.7
  84.8 1.9 %collective-permute-start.10 = (bf16[128,4096]{1,0:T(8,128)(2,1)}, bf16[128,4096]{1,0:T(8,128)(2,1)}, u32[]{:S(2)}, u32[]{:S(2)}) collective-permute-start(bf16[128,4096]{1,0:T(8,128)(2,1)} %collective-permute-done.3.near_ref), channel_id=1, source_target_pairs={{65,64},{66,65},{67,66},{68,67},{69,68},{70,69},{71,70},{72,71},{7... | collective-permute-start | bytes 3145736 | tf_op jit(solution)/shard_map/ppermute | solution.py:376
  86.7 3.4 %collective-permute-start.9 = (bf16[128,4096]{1,0:T(8,128)(2,1)}, bf16[128,4096]{1,0:T(8,128)(2,1)}, u32[]{:S(2)}, u32[]{:S(2)}) collective-permute-start(bf16[128,4096]{1,0:T(8,128)(2,1)} %collective-permute-done.3.near_ref), channel_id=1, source_target_pairs={{64,65},{65,66},{66,67},{67,68},{68,69},{69,70},{70,71},{71,72},{7... | collective-permute-start | bytes 3145736 | tf_op jit(solution)/shard_map/ppermute | solution.py:376
  90.1 2.4 %collective-permute-start.13 = (bf16[128,5120]{1,0:T(8,128)(2,1)}, bf16[128,5120]{1,0:T(8,128)(2,1)}, u32[]{:S(2)}, u32[]{:S(2)}) collective-permute-start(bf16[128,5120]{1,0:T(8,128)(2,1)} %get-tuple-element.63), channel_id=1, source_target_pairs={{64,0},{65,1},{66,2},{67,3},{68,4},{69,5},{70,6},{71,7},{72,8},{73... | collective-permute-start | bytes 3932168 | tf_op jit(solution)/shard_map/ppermute | solution.py:376
  92.5 1.2 copy-done.16
  93.7 1.2 copy-done.18
  94.9 1.2 copy-done.20
  96.1 1.5 %adapter_terms.1 = bf16[4096,128]{1,0:T(8,128)(2,1)S(1)} custom-call(s32[3]{0:T(128)S(1)} %pad_add_fusion.rank_ref.place_ref.refs_0_, s32[2,64]{1,0:T(2,128)S(1)} %copy-done.21, s32[2,64]{1,0:T(2,128)S(1)} %copy-done.22, f32[102]{0:T(128)S(1)} %copy-done.23, bf16[128,4096]{1,0:T(8,128)(2,1)S(1)} %copy-done.16, bf16[384,4096]{1,0:T(8,128)(2,1)S(1)} %bitcast.19, ...), custom_call_target="tpu_custom_call" | custom-call | flops 1048576 | bytes 1048576 | tf_op jit(solution)/shard_map/adapter_terms/pallas_call | solution.py:287
  97.7 1.0 copy-done.9
  98.7 3.7 %all-to-all-start = ((bf16[16,256,128]{2,1,0:T(8,128)(2,1)}), bf16[16,256,128]{2,1,0:T(8,128)(2,1)S(1)}, u32[]{:S(2)}, u32[]{:S(2)}) async-start(bf16[16,256,128]{2,1,0:T(8,128)(2,1)} %bitcast.31), calls=%async_computation | async-start | bytes 2097152 | tf_op jit(solution)/shard_map/all_to_all | solution.py:400
  102.3 2.3 %broadcast_select_fusion = bf16[128,4096]{1,0:T(8,128)(2,1)} fusion(bf16[128,4096]{1,0:T(8,128)(2,1)} %collective-permute-done.far_ref, bf16[128,4096]{1,0:T(8,128)(2,1)} %forward_tile.1, pred[]{:T(512)S(6)} %eq.3), kind=kLoop, calls=%fused_computation.3 | loop fusion | flops 524288 | bytes 3145729 | tf_op jit(solution)/shard_map/jit(_where)/select_n | solution.py:447
  104.7 0.7 collective-permute-start.12
  105.4 0.7 collective-permute-start.11
  106.1 7.9 %all-to-all-done = bf16[16,256,128]{2,1,0:T(8,128)(2,1)S(1)} async-done(((bf16[16,256,128]{2,1,0:T(8,128)(2,1)}), bf16[16,256,128]{2,1,0:T(8,128)(2,1)S(1)}, u32[]{:S(2)}, u32[]{:S(2)}) %all-to-all-start) | async-done | bytes 1048608 | tf_op jit(solution)/shard_map/all_to_all | solution.py:400
  114.1 0.1 convert_reduce_fusion
  114.2 26.2 %all_to_all.10 = f32[4,64,128]{2,1,0:T(8,128)S(1)} all-to-all(f32[4,64,128]{2,1,0:T(8,128)S(1)} %bitcast.33), channel_id=1, replica_groups={{0,1,2,3},{4,5,6,7},{8,9,10,11},{12,13,14,15},{16,17,18,19},{20,21,22,2..., dimensions={0} | all-to-all | bytes 262144 | tf_op jit(solution)/shard_map/all_to_all | solution.py:400
  140.4 0.6 reduce_sum.19
  141.0 5.1 %place_outputs.1 = (bf16[384,4096]{1,0:T(8,128)(2,1)}, bf16[128,5120]{1,0:T(8,128)(2,1)}) custom-call(s32[3]{0:T(128)S(1)} %pad_add_fusion.rank_ref.place_ref.refs_0_, s32[2,64]{1,0:T(2,128)S(1)} %copy-done.22, bf16[128,4096]{1,0:T(8,128)(2,1)} %collective-permute-done.9.before_ref, bf16[128,4096]{1,0:T(8,128)(2,1)} %collective-permute-done.3.near_ref, ...), custom_call_target="tpu_custom_call" | custom-call | flops 1048576 | bytes 1048576 | tf_op jit(solution)/shard_map/place_outputs/pallas_call | solution.py:349
  (46 shorter events, 0.1 us)
Async XLA Ops:
  0.6 4.8 %copy-start.24 = (s32[2,64,8]{1,2,0:T(8,128)S(1)}, s32[2,64,8]{1,2,0:T(8,128)}, u32[]{:S(2)}) copy-start(s32[2,64,8]{1,2,0:T(8,128)} %param.16) | copy-start | bytes 12292
  3.8 4.2 %copy-start.14 = (bf16[1,128,5120]{2,1,0:T(8,128)(2,1)S(1)}, bf16[1,128,5120]{2,1,0:T(8,128)(2,1)}, u32[]{:S(2)}) copy-start(bf16[1,128,5120]{2,1,0:T(8,128)(2,1)} %param.9) | copy-start | bytes 3932164
  3.8 4.2 %copy-start.21 = (s32[2,64]{1,0:T(2,128)S(1)}, s32[2,64]{1,0:T(2,128)}, u32[]{:S(2)}) copy-start(s32[2,64]{1,0:T(2,128)} %langs_ref.7) | copy-start | bytes 1540
  3.8 4.2 %copy-start.23 = (f32[102]{0:T(128)S(1)}, f32[102]{0:T(128)}, u32[]{:S(2)}) copy-start(f32[102]{0:T(128)} %table_ref.7) | copy-start | bytes 1228
  3.8 22.5 %collective-permute-start.2 = (bf16[128,4096]{1,0:T(8,128)(2,1)}, bf16[128,4096]{1,0:T(8,128)(2,1)S(1)}, u32[]{:S(2)}, u32[]{:S(2)}) collective-permute-start(bf16[128,4096]{1,0:T(8,128)(2,1)} %get-tuple-element.43), channel_id=1, source_target_pairs={{65,64},{66,65},{67,66},{68,67},{69,68},{70,69},{71,70},{72,71},{7... | collective-permute-start | bytes 3145736 | tf_op jit(solution)/shard_map/ppermute | solution.py:376
  4.7 21.7 %collective-permute-start.1 = (bf16[128,4096]{1,0:T(8,128)(2,1)}, bf16[128,4096]{1,0:T(8,128)(2,1)S(1)}, u32[]{:S(2)}, u32[]{:S(2)}) collective-permute-start(bf16[128,4096]{1,0:T(8,128)(2,1)} %get-tuple-element.42), channel_id=1, source_target_pairs={{64,65},{65,66},{66,67},{67,68},{68,69},{69,70},{70,71},{71,72},{7... | collective-permute-start | bytes 3145736 | tf_op jit(solution)/shard_map/ppermute | solution.py:376
  8.0 1.2 copy-start.2
  9.2 1.0 copy-start.7
  10.2 6.9 %copy-start = (bf16[1,384,4096]{2,1,0:T(8,128)(2,1)S(1)}, bf16[1,384,4096]{2,1,0:T(8,128)(2,1)}, u32[]{:S(2)}) copy-start(bf16[1,384,4096]{2,1,0:T(8,128)(2,1)} %param.11) | copy-start | bytes 9437188
  10.2 6.9 %copy-start.8 = (bf16[1,64,4096]{2,1,0:T(8,128)(2,1)S(1)}, bf16[1,64,4096]{2,1,0:T(8,128)(2,1)}, u32[]{:S(2)}) copy-start(bf16[1,64,4096]{2,1,0:T(8,128)(2,1)} %param.13) | copy-start | bytes 1572868
  10.2 6.9 %copy-start.22 = (s32[2,64]{1,0:T(2,128)S(1)}, s32[2,64]{1,0:T(2,128)}, u32[]{:S(2)}) copy-start(s32[2,64]{1,0:T(2,128)} %dest_ref.7) | copy-start | bytes 1540
  15.8 10.5 %collective-permute-start.3 = (bf16[128,4096]{1,0:T(8,128)(2,1)}, bf16[128,4096]{1,0:T(8,128)(2,1)}, u32[]{:S(2)}, u32[]{:S(2)}) collective-permute-start(bf16[128,4096]{1,0:T(8,128)(2,1)} %forward_tile.1), channel_id=1, source_target_pairs={{0,64},{1,65},{2,66},{3,67},{4,68},{5,69},{6,70},{7,71},{8,72},{9,... | collective-permute-start | bytes 3145736 | tf_op jit(solution)/shard_map/ppermute | solution.py:376
  17.2 1.2 copy-start.3
  18.4 1.3 copy-start.5
  19.7 13.6 %copy-start.4 = (bf16[1,4096,64]{2,1,0:T(8,128)(2,1)S(1)}, bf16[1,4096,64]{2,1,0:T(8,128)(2,1)}, u32[]{:S(2)}) copy-start(bf16[1,4096,64]{2,1,0:T(8,128)(2,1)} %copy.15) | copy-start | bytes 1572868
  24.0 1.3 copy-start.6
  25.3 1.0 copy-start.15
  26.3 11.1 %copy-start.10 = (bf16[128,4096]{1,0:T(8,128)(2,1)}, bf16[128,4096]{1,0:T(8,128)(2,1)S(1)}, u32[]{:S(2)}) copy-start(bf16[128,4096]{1,0:T(8,128)(2,1)S(1)} %collective-permute-done.2.right_ref.refs_6_) | copy-start | bytes 3145732
  26.3 11.1 %copy-start.12 = (bf16[128,4096]{1,0:T(8,128)(2,1)}, bf16[128,4096]{1,0:T(8,128)(2,1)S(1)}, u32[]{:S(2)}) copy-start(bf16[128,4096]{1,0:T(8,128)(2,1)S(1)} %collective-permute-done.1.left_ref.refs_5_) | copy-start | bytes 3145732
  26.3 17.2 %collective-permute-start.4 = (bf16[128,4096]{1,0:T(8,128)(2,1)}, bf16[128,4096]{1,0:T(8,128)(2,1)S(1)}, u32[]{:S(2)}, u32[]{:S(2)}) collective-permute-start(bf16[128,4096]{1,0:T(8,128)(2,1)} %get-tuple-element.42), channel_id=1, source_target_pairs={{192,193},{193,194},{194,195},{195,196},{196,197},{197,198},{198,1... | collective-permute-start | bytes 3145736 | tf_op jit(solution)/shard_map/ppermute | solution.py:376
  29.0 42.7 %collective-permute-start.5 = (bf16[128,4096]{1,0:T(8,128)(2,1)}, bf16[128,4096]{1,0:T(8,128)(2,1)S(1)}, u32[]{:S(2)}, u32[]{:S(2)}) collective-permute-start(bf16[128,4096]{1,0:T(8,128)(2,1)} %get-tuple-element.43), channel_id=1, source_target_pairs={{193,192},{194,193},{195,194},{196,195},{197,196},{198,197},{199,1... | collective-permute-start | bytes 3145736 | tf_op jit(solution)/shard_map/ppermute | solution.py:376
  31.7 67.0 %collective-permute-start = (bf16[128,4096]{1,0:T(8,128)(2,1)}, bf16[128,4096]{1,0:T(8,128)(2,1)}, u32[]{:S(2)}, u32[]{:S(2)}) collective-permute-start(bf16[128,4096]{1,0:T(8,128)(2,1)} %forward_tile.1), channel_id=1, source_target_pairs={{64,128},{65,129},{66,130},{67,131},{68,132},{69,133},{70,134},{71... | collective-permute-start | bytes 3145736 | tf_op jit(solution)/shard_map/ppermute | solution.py:376
  37.5 1.0 copy-start.17
  38.4 67.0 %collective-permute-start.8 = (bf16[128,5120]{1,0:T(8,128)(2,1)}, bf16[128,5120]{1,0:T(8,128)(2,1)}, u32[]{:S(2)}, u32[]{:S(2)}) collective-permute-start(bf16[128,5120]{1,0:T(8,128)(2,1)} %get-tuple-element.58), channel_id=1, source_target_pairs={{128,64},{129,65},{130,66},{131,67},{132,68},{133,69},{134,70},{13... | collective-permute-start | bytes 3932168 | tf_op jit(solution)/shard_map/ppermute | solution.py:376
  71.7 1.2 copy-start.11
  72.9 1.2 copy-start.13
  74.2 18.3 %copy-start.1 = (bf16[1,384,4096]{2,1,0:T(8,128)(2,1)S(1)}, bf16[1,384,4096]{2,1,0:T(8,128)(2,1)}, u32[]{:S(2)}) copy-start(bf16[1,384,4096]{2,1,0:T(8,128)(2,1)} %param.11) | copy-start | bytes 9437188
  82.5 1.0 copy-start.19
  83.4 3.3 %collective-permute-start.6 = (bf16[128,128]{1,0:T(8,128)(2,1)S(1)}, bf16[128,128]{1,0:T(8,128)(2,1)S(1)}, u32[]{:S(2)}, u32[]{:S(2)}) collective-permute-start(bf16[128,128]{1,0:T(8,128)(2,1)S(1)} %get-tuple-element.49), channel_id=1, source_target_pairs={{0,1},{1,2},{2,3},{3,4},{4,5},{5,6},{6,7},{7,8},{8,9},{9,10},{10,1... | collective-permute-start | bytes 98312 | tf_op jit(solution)/shard_map/ppermute | solution.py:376
  84.1 6.0 %collective-permute-start.7 = (bf16[128,128]{1,0:T(8,128)(2,1)S(1)}, bf16[128,128]{1,0:T(8,128)(2,1)S(1)}, u32[]{:S(2)}, u32[]{:S(2)}) collective-permute-start(bf16[128,128]{1,0:T(8,128)(2,1)S(1)} %get-tuple-element.51), channel_id=1, source_target_pairs={{1,0},{2,1},{3,2},{4,3},{5,4},{6,5},{7,6},{8,7},{9,8},{10,9},{11,1... | collective-permute-start | bytes 98312 | tf_op jit(solution)/shard_map/ppermute | solution.py:376
  84.8 29.3 %collective-permute-start.10 = (bf16[128,4096]{1,0:T(8,128)(2,1)}, bf16[128,4096]{1,0:T(8,128)(2,1)}, u32[]{:S(2)}, u32[]{:S(2)}) collective-permute-start(bf16[128,4096]{1,0:T(8,128)(2,1)} %collective-permute-done.3.near_ref), channel_id=1, source_target_pairs={{65,64},{66,65},{67,66},{68,67},{69,68},{70,69},{71,70},{72,71},{7... | collective-permute-start | bytes 3145736 | tf_op jit(solution)/shard_map/ppermute | solution.py:376
  86.7 27.4 %collective-permute-start.9 = (bf16[128,4096]{1,0:T(8,128)(2,1)}, bf16[128,4096]{1,0:T(8,128)(2,1)}, u32[]{:S(2)}, u32[]{:S(2)}) collective-permute-start(bf16[128,4096]{1,0:T(8,128)(2,1)} %collective-permute-done.3.near_ref), channel_id=1, source_target_pairs={{64,65},{65,66},{66,67},{67,68},{68,69},{69,70},{70,71},{71,72},{7... | collective-permute-start | bytes 3145736 | tf_op jit(solution)/shard_map/ppermute | solution.py:376
  90.1 50.9 %collective-permute-start.13 = (bf16[128,5120]{1,0:T(8,128)(2,1)}, bf16[128,5120]{1,0:T(8,128)(2,1)}, u32[]{:S(2)}, u32[]{:S(2)}) collective-permute-start(bf16[128,5120]{1,0:T(8,128)(2,1)} %get-tuple-element.63), channel_id=1, source_target_pairs={{64,0},{65,1},{66,2},{67,3},{68,4},{69,5},{70,6},{71,7},{72,8},{73... | collective-permute-start | bytes 3932168 | tf_op jit(solution)/shard_map/ppermute | solution.py:376
  92.5 1.2 copy-start.16
  93.7 1.2 copy-start.18
  94.9 1.2 copy-start.20
  97.7 1.0 copy-start.9
  98.7 15.4 %all-to-all-start = ((bf16[16,256,128]{2,1,0:T(8,128)(2,1)}), bf16[16,256,128]{2,1,0:T(8,128)(2,1)S(1)}, u32[]{:S(2)}, u32[]{:S(2)}) async-start(bf16[16,256,128]{2,1,0:T(8,128)(2,1)} %bitcast.31), calls=%async_computation | async-start | bytes 2097152 | tf_op jit(solution)/shard_map/all_to_all | solution.py:400
  104.7 36.4 %collective-permute-start.12 = (bf16[128,4096]{1,0:T(8,128)(2,1)}, bf16[128,4096]{1,0:T(8,128)(2,1)S(1)}, u32[]{:S(2)}, u32[]{:S(2)}) collective-permute-start(bf16[128,4096]{1,0:T(8,128)(2,1)} %broadcast_select_fusion), channel_id=1, source_target_pairs={{68,131},{72,135},{76,139},{80,143},{84,147},{88,151},{92,155},{96... | collective-permute-start | bytes 3145736 | tf_op jit(solution)/shard_map/ppermute | solution.py:376
  105.4 35.6 %collective-permute-start.11 = (bf16[128,4096]{1,0:T(8,128)(2,1)}, bf16[128,4096]{1,0:T(8,128)(2,1)S(1)}, u32[]{:S(2)}, u32[]{:S(2)}) collective-permute-start(bf16[128,4096]{1,0:T(8,128)(2,1)} %broadcast_select_fusion), channel_id=1, source_target_pairs={{67,132},{71,136},{75,140},{79,144},{83,148},{87,152},{91,156},{95... | collective-permute-start | bytes 3145736 | tf_op jit(solution)/shard_map/ppermute | solution.py:376

commit v10 on v8

--- a/solution.py
+++ b/solution.py
@@ -104,10 +104,12 @@
 
 def prepare_kernel(
     place_ref, lens_ref, langs_ref, dest_ref, table_ref, qkv_ref, slots_ref, down_ref, up_ref,
-    probs_ref, attn_ref, low_ref, left_ref, own_ref, right_ref,
+    probs_ref, attn_ref, low_ref, left_ref, own_ref, right_ref, held_ref, sem,
 ):
     rank = place_ref[0]
     tiles = lens_ref.shape[1]
+    fetch = pltpu.make_async_copy(slots_ref, held_ref, sem)
+    pl.when(place_ref[1] == 0)(fetch.start)
     bias = mask_bias(lens_ref, 1, rank)
     low = jnp.zeros((TILE, RANK), F32)
     for j in range(KV):
@@ -121,12 +123,13 @@
 
     @pl.when(place_ref[1] == 0)
     def _():
+        fetch.wait()
         for k, out_ref in enumerate((left_ref, own_ref, right_ref)):
             rate = slot_rate(k, rank, tiles, langs_ref, dest_ref, table_ref)
             back = jnp.zeros((TILE, RANK), F32)
             for c in range(0, QW, 512):
                 cols = slice(c, c + 512)
-                grad = slots_ref[k * TILE : (k + 1) * TILE, cols]
+                grad = held_ref[k * TILE : (k + 1) * TILE, cols]
                 scaled = (rate * grad.astype(F32)).astype(BF16)
                 back = back + dot(scaled, up_ref[:, cols], NT)
             out_ref[...] = jnp.concatenate([low, back], axis=1).astype(BF16)
@@ -139,13 +142,16 @@
 
 def terms_kernel(
     place_ref, langs_ref, dest_ref, table_ref, attn_ref, slots_ref, left_ref, own_ref, right_ref,
-    scaled_ref, back_ref, low_ref, terms_ref, slot_scaled_ref,
+    scaled_ref, back_ref, low_ref, terms_ref, slot_scaled_ref, held_ref, sem,
 ):
     rank = place_ref[0]
     tiles = dest_ref.shape[1]
+    fetch = pltpu.make_async_copy(slots_ref, held_ref, sem)
 
     @pl.when(place_ref[1] == 0)
     def _():
+        fetch.start()
+        fetch.wait()
         went = dest_ref[1, rank] - rank
         back = jnp.where(went < 0, left_ref[...], jnp.where(went > 0, right_ref[...], own_ref[...]))
         lows = jnp.concatenate([left_ref[...], own_ref[...], right_ref[...]], axis=0)
@@ -154,7 +160,7 @@
             for k in range(3):
                 rows = slice(k * TILE, (k + 1) * TILE)
                 rate = slot_rate(k, rank, tiles, langs_ref, dest_ref, table_ref)
-                slot_scaled_ref[rows, :] = (rate * slots_ref[rows, cols].astype(F32)).astype(BF16)
+                slot_scaled_ref[rows, :] = (rate * held_ref[rows, cols].astype(F32)).astype(BF16)
             one = dot(attn_ref[:, cols], back, TN)
             two = dot(slot_scaled_ref[...], lows, TN)
             terms = jnp.concatenate([one[:, RANK:], two[:, :RANK]], axis=1)
@@ -172,20 +178,24 @@
 def backward_kernel(
     place_ref, langs_ref, dest_ref, table_ref, qkv_ref, left_ref, right_ref, last_left_ref,
     last_right_ref, slots_ref, probs_ref, down_ref, up_ref, grad_ref, scaled_ref, back_ref,
-    gattn_ref,
+    gattn_ref, mid_ref, sem,
 ):
     rank = place_ref[0]
     rate = table_ref[langs_ref[1, rank]]
     went = dest_ref[1, rank] - rank
     last = place_ref[1] == place_ref[2] - 1
+    active = place_ref[1] != 0
+    fetch = pltpu.make_async_copy(slots_ref.at[pl.ds(TILE, TILE), :], mid_ref, sem)
 
     def chosen():
+        fetch.start()
+        fetch.wait()
         back = jnp.zeros((TILE, RANK), F32)
         for c in range(0, QW, 512):
             cols = slice(c, c + 512)
             left = jnp.where(last, last_left_ref[:, cols], left_ref[:, cols])
             right = jnp.where(last, last_right_ref[:, cols], right_ref[:, cols])
-            mid = slots_ref[TILE : 2 * TILE, cols]
+            mid = mid_ref[:, cols]
             grad = jnp.where(went < 0, left, jnp.where(went > 0, right, mid))
             gattn_ref[:, cols] = grad
             scaled = (rate * grad.astype(F32)).astype(BF16)
@@ -193,7 +203,7 @@
             back = back + dot(scaled, up_ref[:, cols], NT)
         return back.astype(BF16)
 
-    @pl.when(place_ref[1] != 0)
+    @pl.when(active)
     def _():
         back = chosen()
         back_ref[...] = back
@@ -224,16 +234,11 @@
             cols = slice(QW + KW + j * HEAD_DIM, QW + KW + (j + 1) * HEAD_DIM)
             grad_ref[:, cols] = dot(probs_low, grads, TN).astype(BF16)
 
-    @pl.when(place_ref[1] == 0)
-    def _():
-        grad_ref[...] = jnp.zeros(grad_ref.shape, BF16)
-        scaled_ref[...] = jnp.zeros(scaled_ref.shape, BF16)
-        back_ref[...] = jnp.zeros(back_ref.shape, BF16)
-
 
 COST = pl.CostEstimate(flops=2**20, bytes_accessed=2**20, transcendentals=0)
 SMEM = pl.BlockSpec(memory_space=pltpu.SMEM)
 VMEM = pl.BlockSpec(memory_space=pltpu.VMEM)
+ANY = pl.BlockSpec(memory_space=pl.ANY)
 
 
 def run_forward(rank, lengths, languages, table, qkv, down, up):
@@ -243,7 +248,7 @@
         in_specs=[SMEM] * 4 + [VMEM] * 3,
         out_specs=VMEM,
         scratch_shapes=[pltpu.VMEM((GROUP * TILE, TILE), F32)],
-        compiler_params=pltpu.CompilerParams(vmem_limit_bytes=24 * 2**20),
+        compiler_params=pltpu.CompilerParams(vmem_limit_bytes=16 * 2**20),
         cost_estimate=COST,
         name="forward_tile",
     )(rank, lengths, languages, table, qkv, down, up)
@@ -261,9 +266,10 @@
             message,
             message,
         ),
-        in_specs=[SMEM] * 5 + [VMEM] * 4,
+        in_specs=[SMEM] * 5 + [VMEM, ANY, VMEM, VMEM],
         out_specs=(VMEM,) * 6,
-        compiler_params=pltpu.CompilerParams(vmem_limit_bytes=40 * 2**20),
+        scratch_shapes=[pltpu.VMEM((3 * TILE, QW), BF16), pltpu.SemaphoreType.DMA],
+        compiler_params=pltpu.CompilerParams(vmem_limit_bytes=22 * 2**20),
         cost_estimate=COST,
         name="prepare_tile",
     )(place, lengths, languages, dest, table, qkv, slots, down, up)
@@ -273,10 +279,14 @@
     return pl.pallas_call(
         terms_kernel,
         out_shape=jax.ShapeDtypeStruct((QW, 2 * RANK), BF16),
-        in_specs=[SMEM] * 4 + [VMEM] * 8,
+        in_specs=[SMEM] * 4 + [VMEM, ANY] + [VMEM] * 6,
         out_specs=VMEM,
-        scratch_shapes=[pltpu.VMEM((3 * TILE, 512), BF16)],
-        compiler_params=pltpu.CompilerParams(vmem_limit_bytes=40 * 2**20),
+        scratch_shapes=[
+            pltpu.VMEM((3 * TILE, 512), BF16),
+            pltpu.VMEM((3 * TILE, QW), BF16),
+            pltpu.SemaphoreType.DMA,
+        ],
+        compiler_params=pltpu.CompilerParams(vmem_limit_bytes=22 * 2**20),
         cost_estimate=COST,
         name="adapter_terms",
     )(place, languages, dest, table, attn, slots, left, own, right, scaled, back, low)
@@ -290,10 +300,14 @@
             jax.ShapeDtypeStruct((TILE, QW), BF16),
             jax.ShapeDtypeStruct((TILE, RANK), BF16),
         ),
-        in_specs=[SMEM] * 4 + [VMEM] * 9,
+        in_specs=[SMEM] * 4 + [VMEM] * (1 + len(moved)) + [ANY] + [VMEM] * 3,
         out_specs=(VMEM,) * 3,
-        scratch_shapes=[pltpu.VMEM((TILE, QW), BF16)],
-        compiler_params=pltpu.CompilerParams(vmem_limit_bytes=48 * 2**20),
+        scratch_shapes=[
+            pltpu.VMEM((TILE, QW), BF16),
+            pltpu.VMEM((TILE, QW), BF16),
+            pltpu.SemaphoreType.DMA,
+        ],
+        compiler_params=pltpu.CompilerParams(vmem_limit_bytes=24 * 2**20),
         cost_estimate=COST,
         name="backward_tile",
     )(place, languages, dest, table, qkv, *moved, slots, probs, down, up)
@@ -309,7 +323,7 @@
     handed = pltpu.make_async_copy(back_ref, handed_ref, sems.at[0])
     handed.start()
     copies = []
-    for k, (near_ref, edge) in enumerate(
+    for k, (near, edge) in enumerate(
         ((before_ref, run_start(rank)), (hop_ref, False), (after_ref, run_end(rank)))
     ):
         tile = rank + (k - 1)
@@ -318,12 +332,11 @@
         crossed = (section == 2) & edge
         slot = placed_ref.at[pl.ds(k * TILE, TILE), :]
         for source, chosen in (
-            (near_ref, live & jnp.logical_not(crossed)),
+            (near, live & jnp.logical_not(crossed)),
             (ends_ref, live & crossed),
             (zero_ref, jnp.logical_not(live)),
         ):
-            copy = pltpu.make_async_copy(source, slot, sems.at[k + 1])
-            copies.append((copy, chosen))
+            copies.append((pltpu.make_async_copy(source, slot, sems.at[k + 1]), chosen))
     for copy, chosen in copies:
         pl.when(chosen)(copy.start)
     for copy, chosen in copies:
@@ -331,21 +344,20 @@
     handed.wait()
 
 
-def run_place(place, dest, before, hop, after, ends, back):
-    hbm = pl.BlockSpec(memory_space=pl.ANY)
+def run_place(place, dest, *tiles):
     return pl.pallas_call(
         place_kernel,
         out_shape=(
             jax.ShapeDtypeStruct((3 * TILE, QW), BF16),
-            jax.ShapeDtypeStruct(back.shape, BF16),
+            jax.ShapeDtypeStruct(tiles[-1].shape, BF16),
         ),
-        in_specs=[SMEM] * 2 + [VMEM] * 5,
-        out_specs=(hbm, hbm),
+        in_specs=[SMEM] * 2 + [VMEM] * len(tiles),
+        out_specs=(ANY, ANY),
         scratch_shapes=[pltpu.VMEM((TILE, QW), BF16), pltpu.SemaphoreType.DMA((4,))],
         compiler_params=pltpu.CompilerParams(vmem_limit_bytes=24 * 2**20),
         cost_estimate=COST,
         name="place_outputs",
-    )(place, dest, before, hop, after, ends, back)
+    )(place, dest, *tiles)
 
 
 def sections():
@@ -373,6 +385,14 @@
 
 def run_end(t):
     return t % RUN == RUN - 1
+
+
+def after_run_start(t):
+    return t % RUN == 1
+
+
+def before_run_end(t):
+    return t % RUN == RUN - 2
 
 
 def not_run_start(t):
@@ -401,25 +421,26 @@
     from_right = shift(to_down, [(early, 0, -1, anywhere)])
     out = run_forward(place, lengths, languages, lang_scale, qkv_a[0], down, up)
     out, place = lax.optimization_barrier((out, place))
-    hop = shift(out, [(every, 1, 0, anywhere)])
+    near = shift(out, [([0, 2], 1, 0, anywhere)])
     probs, attn, low, to_left, own, to_right = run_prepare(
         place, lengths, languages, destination, lang_scale, qkv_b[0], slots, down, up
     )
     from_left, from_right, low = lax.optimization_barrier((from_left, from_right, low))
-    to_up, to_down, hop, low = lax.optimization_barrier((to_up, to_down, hop, low))
+    to_up, to_down, near, low = lax.optimization_barrier((to_up, to_down, near, low))
     last_left = shift(to_up, [([last], 0, 1, anywhere)])
     last_right = shift(to_down, [([last], 0, -1, anywhere)])
+    far = shift(
+        jnp.where(section == last, near, out),
+        [([1], 1, 0, anywhere), ([last], -last, -1, run_end), ([last], -last, 1, run_start)],
+    )
     grad_qkv, scaled, back = run_backward(
         place, languages, destination, lang_scale, qkv_b[0],
         (from_left, from_right, last_left, last_right), slots, probs, down, up,
     )
-    grad_qkv, hop, to_left, to_right, out = lax.optimization_barrier(
-        (grad_qkv, hop, to_left, to_right, out)
+    grad_qkv, near, to_left, to_right = lax.optimization_barrier(
+        (grad_qkv, near, to_left, to_right)
     )
     handed_back = shift(grad_qkv, [(every, -1, 0, anywhere)])
-    ends = shift(out, [([1], 1, 1, run_end), ([1], 1, -1, run_start)])
-    before = shift(hop, [([1, 3], 0, 1, anywhere), ([2], 0, 1, not_run_end)])
-    after = shift(hop, [([1, 3], 0, -1, anywhere), ([2], 0, -1, not_run_start)])
     left = shift(to_right, [([0], 0, 1, anywhere)])
     right = shift(to_left, [([0], 0, -1, anywhere)])
     terms = run_terms(
@@ -427,8 +448,19 @@
     )
     planes = [[RUN * k + z for k in range(size // RUN)] for z in range(RUN)]
     columns = [[RUN * k + z for z in range(RUN)] for k in range(size // RUN)]
+    far, terms, out = lax.optimization_barrier((far, terms, out))
     pieces = scatter(terms.reshape(size // RUN, -1, 2 * RANK), planes)
-    pieces, gated, before = lax.optimization_barrier((pieces, handed_back, before))
+    hop = jnp.where((section == 1) | (section == last), near, far)
+    before = shift(
+        hop,
+        [([1], 0, 1, anywhere), ([2, last], 0, 1, not_run_end), ([0], last, 2, before_run_end)],
+    )
+    after = shift(
+        hop,
+        [([1], 0, -1, anywhere), ([2, last], 0, -1, not_run_start), ([0], last, -2, after_run_start)],
+    )
+    ends = shift(out, [([1], 1, 1, run_end), ([1], 1, -1, run_start)])
+    pieces, _ = lax.optimization_barrier((pieces, handed_back))
     terms = jnp.sum(pieces.astype(F32), axis=0)
     terms = jnp.sum(scatter(terms.reshape(RUN, -1, 2 * RANK), columns), axis=0)
     handed_forward, handed_back = run_place(

time: 145 us -> 139 us (0.959)
  the two profiles are of different devices: /device:TPU:166 before, /device:TPU:227 now
where the time goes in v10:
time: 139 us; the launch traced here: 136 us
  waiting for transfers between devices  51.5 us (37%)
  starting transfers between devices  38.1 us (27%)
  Pallas kernels  20.9 us (15%)
  local copies, waits for them, and re-layouts  18.4 us (13%)
  other arithmetic  6.39 us (5%)
    ppermute x12, waiting for transfers between devices, shift(): return lax.ppermute(x, AXES, route)  35.9 us
    ppermute x12, starting transfers between devices, shift(): return lax.ppermute(x, AXES, route)  25.2 us
    all_to_all x2, waiting for transfers between devices, scatter(): return lax.all_to_all(x, 'dp', 0, 0, axis_index_groups=groups, tiled=True)  15.6 us
    unnamed x44, local copies, waits for them, and re-layouts  15.2 us
    all_to_all x2, starting transfers between devices, scatter(): return lax.all_to_all(x, 'dp', 0, 0, axis_index_groups=groups, tiled=True)  12.9 us
    pallas_call x1, Pallas kernels, run_forward(): pl.pallas_call(forward_kernel, out_shape=jax.ShapeDtypeStruct((TILE, QW),...  5.62 us
    pallas_call x1, Pallas kernels, run_backward(): pl.pallas_call(backward_kernel, out_shape=(jax.ShapeDtypeStruct((TILE, QW...  5.51 us
    pallas_call x1, Pallas kernels, run_prepare(): pl.pallas_call(prepare_kernel, out_shape=(jax.ShapeDtypeStruct((QW, TILE)...  4.3 us
  transfers between devices with their start and end apart: 14, of which 3 were waited for; matrix products, arithmetic and copies ran while one was open for 5% of the time, Pallas kernels for 15%

profile of v10, /device:TPU:227, one launch (start us, length us, event | category | flops | bytes accessed | tf_op | source)
XLA Modules:
  0.0 136.2 jit_solution(866921469090672956)
XLA Ops:
  0.7 3.2 %slice_bitcast_fusion = (bf16[128,4096]{1,0:T(8,128)(2,1)}, bf16[128,4096]{1,0:T(8,128)(2,1)}) fusion(bf16[1,384,4096]{2,1,0:T(8,128)(2,1)} %param.11), kind=kLoop, calls=%fused_computation.1 | loop fusion | bytes 4194304 | tf_op jit(solution)/shard_map/slice | solution.py:419
  3.8 1.6 %collective-permute-start = (bf16[128,4096]{1,0:T(8,128)(2,1)}, bf16[128,4096]{1,0:T(8,128)(2,1)}, u32[]{:S(2)}, u32[]{:S(2)}) collective-permute-start(bf16[128,4096]{1,0:T(8,128)(2,1)} %get-tuple-element.37), channel_id=1, source_target_pairs={{64,65},{65,66},{66,67},{67,68},{68,69},{69,70},{70,71},{71,72},{7... | collective-permute-start | bytes 3145736 | tf_op jit(solution)/shard_map/ppermute | solution.py:375
  5.5 1.7 %collective-permute-start.1 = (bf16[128,4096]{1,0:T(8,128)(2,1)}, bf16[128,4096]{1,0:T(8,128)(2,1)}, u32[]{:S(2)}, u32[]{:S(2)}) collective-permute-start(bf16[128,4096]{1,0:T(8,128)(2,1)} %get-tuple-element.38), channel_id=1, source_target_pairs={{65,64},{66,65},{67,66},{68,67},{69,68},{70,69},{71,70},{72,71},{7... | collective-permute-start | bytes 3145736 | tf_op jit(solution)/shard_map/ppermute | solution.py:375
  7.2 1.3 copy.15
  8.5 0.1 copy.16.lens_ref
  8.6 0.1 pad_add_fusion.rank_ref.place_ref
  8.7 0.0 copy-start.1
  8.7 1.4 %copy-done.1 = bf16[1,4096,64]{2,1,0:T(8,128)(2,1)S(1)} copy-done((bf16[1,4096,64]{2,1,0:T(8,128)(2,1)S(1)}, bf16[1,4096,64]{2,1,0:T(8,128)(2,1)}, u32[]{:S(2)}) %copy-start.1) | copy-done | bytes 524312
  10.0 1.0 copy-done.6
  11.1 1.3 copy-done.10
  12.4 5.6 %forward_tile.1 = bf16[128,4096]{1,0:T(8,128)(2,1)} custom-call(s32[3]{0:T(128)S(1)} %pad_add_fusion.rank_ref.place_ref, s32[2,64,8]{2,1,0:T(8,128)S(1)} %copy.16.lens_ref, s32[2,64]{1,0:T(2,128)S(1)} %copy-done.15, f32[102]{0:T(128)S(1)} %copy-done.17, bf16[128,5120]{1,0:T(8,128)(2,1)S(1)} %bitcast.28, bf16[4096,64]{1,0:T(8,128)(2,1)S(1)} %bitcast.19, ...), custom_call_target="tpu_custom_call" | custom-call | flops 1048576 | bytes 1048576 | tf_op jit(solution)/shard_map/forward_tile/pallas_call | solution.py:245
  18.0 1.3 collective-permute-start.2
  19.3 0.0 copy-start.2
  19.3 1.2 copy-done.2
  20.6 1.3 copy-done.4
  21.9 1.0 copy-done.7
  22.9 4.3 %prepare_tile.1 = (f32[4096,128]{1,0:T(8,128)S(1)}, bf16[128,4096]{1,0:T(8,128)(2,1)S(1)}, bf16[128,64]{1,0:T(8,128)(2,1)S(1)}, bf16[128,128]{1,0:T(8,128)(2,1)S...) custom-call(s32[3]{0:T(128)S(1)} %pad_add_fusion.rank_ref.place_ref, s32[2,64,8]{2,1,0:T(8,128)S(1)} %copy.16.lens_ref, ...), custom_call_target="tpu_custom_call" | custom-call | flops 1048576 | bytes 1048576 | tf_op jit(solution)/shard_map/prepare_tile/pallas_call | solution.py:259
  27.2 1.0 copy-done.11
  28.2 0.0 collective-permute-done.1.right_ref
  28.3 4.8 %collective-permute-start.3 = (bf16[128,4096]{1,0:T(8,128)(2,1)}, bf16[128,4096]{1,0:T(8,128)(2,1)S(1)}, u32[]{:S(2)}, u32[]{:S(2)}) collective-permute-start(bf16[128,4096]{1,0:T(8,128)(2,1)} %get-tuple-element.37), channel_id=1, source_target_pairs={{192,193},{193,194},{194,195},{195,196},{196,197},{197,198},{198,1... | collective-permute-start | bytes 3145736 | tf_op jit(solution)/shard_map/ppermute | solution.py:375
  33.1 1.9 %collective-permute-start.4 = (bf16[128,4096]{1,0:T(8,128)(2,1)}, bf16[128,4096]{1,0:T(8,128)(2,1)S(1)}, u32[]{:S(2)}, u32[]{:S(2)}) collective-permute-start(bf16[128,4096]{1,0:T(8,128)(2,1)} %get-tuple-element.38), channel_id=1, source_target_pairs={{193,192},{194,193},{195,194},{196,195},{197,196},{198,197},{199,1... | collective-permute-start | bytes 3145736 | tf_op jit(solution)/shard_map/ppermute | solution.py:375
  35.0 2.3 %broadcast_select_fusion = bf16[128,4096]{1,0:T(8,128)(2,1)} fusion(bf16[128,4096]{1,0:T(8,128)(2,1)} %collective-permute-done.2, bf16[128,4096]{1,0:T(8,128)(2,1)} %forward_tile.1, pred[]{:T(512)S(6)} %eq.8), kind=kLoop, calls=%fused_computation.3 | loop fusion | flops 524288 | bytes 3145729 | tf_op jit(solution)/shard_map/jit(_where)/select_n | solution.py:433
  37.3 2.9 %collective-permute-start.5 = (bf16[128,4096]{1,0:T(8,128)(2,1)}, bf16[128,4096]{1,0:T(8,128)(2,1)}, u32[]{:S(2)}, u32[]{:S(2)}) collective-permute-start(bf16[128,4096]{1,0:T(8,128)(2,1)} %broadcast_select_fusion), channel_id=1, source_target_pairs={{64,128},{65,129},{66,130},{67,131},{68,132},{69,133},{70,134},{71... | collective-permute-start | bytes 3145736 | tf_op jit(solution)/shard_map/ppermute | solution.py:375
  40.3 4.9 %collective-permute-done.3.last_left_ref = bf16[128,4096]{1,0:T(8,128)(2,1)S(1)} collective-permute-done((bf16[128,4096]{1,0:T(8,128)(2,1)}, bf16[128,4096]{1,0:T(8,128)(2,1)S(1)}, u32[]{:S(2)}, u32[]{:S(2)}) %collective-permute-start.3) | collective-permute-done | bytes 1048608 | tf_op jit(solution)/shard_map/ppermute | solution.py:375
  45.2 31.0 %collective-permute-done.4.last_right_ref = bf16[128,4096]{1,0:T(8,128)(2,1)S(1)} collective-permute-done((bf16[128,4096]{1,0:T(8,128)(2,1)}, bf16[128,4096]{1,0:T(8,128)(2,1)S(1)}, u32[]{:S(2)}, u32[]{:S(2)}) %collective-permute-start.4) | collective-permute-done | bytes 1048608 | tf_op jit(solution)/shard_map/ppermute | solution.py:375
  76.2 5.5 %backward_tile.1 = (bf16[128,5120]{1,0:T(8,128)(2,1)S(1)}, bf16[128,4096]{1,0:T(8,128)(2,1)S(1)}, bf16[128,64]{1,0:T(8,128)(2,1)S(1)}) custom-call(s32[3]{0:T(128)S(1)} %pad_add_fusion.rank_ref.place_ref, s32[2,64]{1,0:T(2,128)S(1)} %copy-done.15, s32[2,64]{1,0:T(2,128)S(1)} %copy-done.16, f32[102]{0:T(128)S(1)} %copy-done.17, ...), custom_call_target="tpu_custom_call" | custom-call | flops 1048576 | bytes 1048576 | tf_op jit(solution)/shard_map/backward_tile/pallas_call | solution.py:296
  81.7 1.0 copy-done.13
  82.7 1.1 copy-done.18
  83.7 0.7 collective-permute-start.6
  84.4 0.7 collective-permute-start.7
  85.1 2.4 %collective-permute-start.11 = (bf16[128,5120]{1,0:T(8,128)(2,1)}, bf16[128,5120]{1,0:T(8,128)(2,1)}, u32[]{:S(2)}, u32[]{:S(2)}) collective-permute-start(bf16[128,5120]{1,0:T(8,128)(2,1)} %copy-done.18), channel_id=1, source_target_pairs={{64,0},{65,1},{66,2},{67,3},{68,4},{69,5},{70,6},{71,7},{72,8},{73... | collective-permute-start | bytes 3932168 | tf_op jit(solution)/shard_map/ppermute | solution.py:375
  87.4 0.0 collective-permute-done.6.left_ref
  87.4 1.2 copy-done.12
  88.7 1.2 copy-done.14
  89.9 1.7 %adapter_terms.1 = bf16[4096,128]{1,0:T(8,128)(2,1)S(1)} custom-call(s32[3]{0:T(128)S(1)} %pad_add_fusion.rank_ref.place_ref, s32[2,64]{1,0:T(2,128)S(1)} %copy-done.15, s32[2,64]{1,0:T(2,128)S(1)} %copy-done.16, f32[102]{0:T(128)S(1)} %copy-done.17, bf16[128,4096]{1,0:T(8,128)(2,1)S(1)} %copy-done.12, bf16[384,4096]{1,0:T(8,128)(2,1)S(1)} %bitcast.18, ...), custom_call_target="tpu_custom_call" | custom-call | flops 1048576 | bytes 1048576 | tf_op jit(solution)/shard_map/adapter_terms/pallas_call | solution.py:279
  91.6 1.0 copy-done.9
  92.6 0.0 collective-permute-done.5
  92.6 8.3 %all-to-all-start = ((bf16[16,256,128]{2,1,0:T(8,128)(2,1)}), bf16[16,256,128]{2,1,0:T(8,128)(2,1)}, u32[]{:S(2)}, u32[]{:S(2)}) async-start(bf16[16,256,128]{2,1,0:T(8,128)(2,1)} %bitcast.27), calls=%async_computation | async-start | bytes 2097152 | tf_op jit(solution)/shard_map/all_to_all | solution.py:407
  101.0 1.3 broadcast_select_fusion.1.hop_ref
  102.3 1.3 collective-permute-start.8
  103.6 4.4 %collective-permute-start.9 = (bf16[128,4096]{1,0:T(8,128)(2,1)S(1)}, bf16[128,4096]{1,0:T(8,128)(2,1)S(1)}, u32[]{:S(2)}, u32[]{:S(2)}) collective-permute-start(bf16[128,4096]{1,0:T(8,128)(2,1)S(1)} %broadcast_select_fusion.1.hop_ref), channel_id=1, source_target_pairs={{65,64},{66,65},{67,66},{68,67},{69,68},{70,69},{71,70},{72,71},{7... | collective-permute-start | bytes 3145736 | tf_op jit(solution)/shard_map/ppermute | solution.py:375
  108.0 1.7 %collective-permute-start.10 = (bf16[128,4096]{1,0:T(8,128)(2,1)}, bf16[128,4096]{1,0:T(8,128)(2,1)}, u32[]{:S(2)}, u32[]{:S(2)}) collective-permute-start(bf16[128,4096]{1,0:T(8,128)(2,1)} %forward_tile.1), channel_id=1, source_target_pairs={{67,132},{71,136},{75,140},{79,144},{83,148},{87,152},{91,156},{95... | collective-permute-start | bytes 3145736 | tf_op jit(solution)/shard_map/ppermute | solution.py:375
  109.6 15.6 %all-to-all-done = bf16[16,256,128]{2,1,0:T(8,128)(2,1)} async-done(((bf16[16,256,128]{2,1,0:T(8,128)(2,1)}), bf16[16,256,128]{2,1,0:T(8,128)(2,1)}, u32[]{:S(2)}, u32[]{:S(2)}) %all-to-all-start) | async-done | bytes 1048608 | tf_op jit(solution)/shard_map/all_to_all | solution.py:407
  125.2 2.0 %convert_reduce_fusion = f32[256,128]{1,0:T(8,128)} fusion(bf16[16,256,128]{2,1,0:T(8,128)(2,1)} %all-to-all-done), kind=kLoop, calls=%fused_computation | loop fusion | flops 1015808 | bytes 1179648 | tf_op jit(solution)/shard_map/reduce_sum | solution.py:464
  127.3 4.5 %all-to-all-start.1 = ((f32[4,64,128]{2,1,0:T(8,128)}), f32[4,64,128]{2,1,0:T(8,128)S(1)}, u32[]{:S(2)}, u32[]{:S(2)}) async-start(f32[4,64,128]{2,1,0:T(8,128)} %bitcast.12), calls=%async_computation.1 | async-start | bytes 262144 | tf_op jit(solution)/shard_map/all_to_all | solution.py:407
  131.8 0.0 collective-permute-done.8.before_ref
  131.8 3.8 %place_outputs.1 = (bf16[384,4096]{1,0:T(8,128)(2,1)}, bf16[128,5120]{1,0:T(8,128)(2,1)}) custom-call(s32[3]{0:T(128)S(1)} %pad_add_fusion.rank_ref.place_ref, s32[2,64]{1,0:T(2,128)S(1)} %copy-done.16, bf16[128,4096]{1,0:T(8,128)(2,1)S(1)} %collective-permute-done.8.before_ref, bf16[128,4096]{1,0:T(8,128)(2,1)S(1)} %broadcast_select_fusion.1.hop_ref, ...), custom_call_target="tpu_custom_call" | custom-call | flops 1048576 | bytes 1048576 | tf_op jit(solution)/shard_map/place_outputs/pallas_call | solution.py:348
  135.6 0.6 reduce_sum.19
  (35 shorter events, 0.1 us)
Async XLA Ops:
  0.6 6.5 %copy-start.19 = (bf16[1,4096,64]{1,2,0:T(8,128)(2,1)S(1)}, bf16[1,4096,64]{1,2,0:T(8,128)(2,1)}, u32[]{:S(2)}) copy-start(bf16[1,4096,64]{1,2,0:T(8,128)(2,1)} %param.12) | copy-start | bytes 1572868
  0.6 7.8 %copy-start.20 = (s32[2,64,8]{1,2,0:T(8,128)S(1)}, s32[2,64,8]{1,2,0:T(8,128)}, u32[]{:S(2)}) copy-start(s32[2,64,8]{1,2,0:T(8,128)} %param.16) | copy-start | bytes 12292
  0.7 8.0 %copy-start.17 = (f32[102]{0:T(128)S(1)}, f32[102]{0:T(128)}, u32[]{:S(2)}) copy-start(f32[102]{0:T(128)} %table_ref.7) | copy-start | bytes 1228
  0.7 8.0 %copy-start.15 = (s32[2,64]{1,0:T(2,128)S(1)}, s32[2,64]{1,0:T(2,128)}, u32[]{:S(2)}) copy-start(s32[2,64]{1,0:T(2,128)} %langs_ref.7) | copy-start | bytes 1540
  3.8 24.4 %collective-permute-start = (bf16[128,4096]{1,0:T(8,128)(2,1)}, bf16[128,4096]{1,0:T(8,128)(2,1)}, u32[]{:S(2)}, u32[]{:S(2)}) collective-permute-start(bf16[128,4096]{1,0:T(8,128)(2,1)} %get-tuple-element.37), channel_id=1, source_target_pairs={{64,65},{65,66},{66,67},{67,68},{68,69},{69,70},{70,71},{71,72},{7... | collective-permute-start | bytes 3145736 | tf_op jit(solution)/shard_map/ppermute | solution.py:375
  5.5 22.8 %collective-permute-start.1 = (bf16[128,4096]{1,0:T(8,128)(2,1)}, bf16[128,4096]{1,0:T(8,128)(2,1)}, u32[]{:S(2)}, u32[]{:S(2)}) collective-permute-start(bf16[128,4096]{1,0:T(8,128)(2,1)} %get-tuple-element.38), channel_id=1, source_target_pairs={{65,64},{66,65},{67,66},{68,67},{69,68},{70,69},{71,70},{72,71},{7... | collective-permute-start | bytes 3145736 | tf_op jit(solution)/shard_map/ppermute | solution.py:375
  7.2 12.2 %copy-start.16 = (s32[2,64]{1,0:T(2,128)S(1)}, s32[2,64]{1,0:T(2,128)}, u32[]{:S(2)}) copy-start(s32[2,64]{1,0:T(2,128)} %dest_ref.7) | copy-start | bytes 1540
  8.5 10.9 %copy-start = (bf16[1,384,4096]{2,1,0:T(8,128)(2,1)S(1)}, bf16[1,384,4096]{2,1,0:T(8,128)(2,1)}, u32[]{:S(2)}) copy-start(bf16[1,384,4096]{2,1,0:T(8,128)(2,1)} %param.11) | copy-start | bytes 9437188
  8.7 1.4 %copy-start.1 = (bf16[1,4096,64]{2,1,0:T(8,128)(2,1)S(1)}, bf16[1,4096,64]{2,1,0:T(8,128)(2,1)}, u32[]{:S(2)}) copy-start(bf16[1,4096,64]{2,1,0:T(8,128)(2,1)} %copy.15) | copy-start | bytes 1572868
  10.0 1.0 copy-start.6
  11.1 1.3 copy-start.10
  18.0 10.2 %collective-permute-start.2 = (bf16[128,4096]{1,0:T(8,128)(2,1)}, bf16[128,4096]{1,0:T(8,128)(2,1)}, u32[]{:S(2)}, u32[]{:S(2)}) collective-permute-start(bf16[128,4096]{1,0:T(8,128)(2,1)} %forward_tile.1), channel_id=1, source_target_pairs={{0,64},{1,65},{2,66},{3,67},{4,68},{5,69},{6,70},{7,71},{8,72},{9,... | collective-permute-start | bytes 3145736 | tf_op jit(solution)/shard_map/ppermute | solution.py:375
  19.3 1.2 copy-start.2
  20.6 1.3 copy-start.4
  21.9 1.0 copy-start.7
  27.2 1.0 copy-start.11
  28.2 47.9 %copy-start.3 = (bf16[1,4096,64]{2,1,0:T(8,128)(2,1)S(1)}, bf16[1,4096,64]{2,1,0:T(8,128)(2,1)}, u32[]{:S(2)}) copy-start(bf16[1,4096,64]{2,1,0:T(8,128)(2,1)} %copy.15) | copy-start | bytes 1572868
  28.2 47.9 %copy-start.5 = (bf16[1,128,5120]{2,1,0:T(8,128)(2,1)S(1)}, bf16[1,128,5120]{2,1,0:T(8,128)(2,1)}, u32[]{:S(2)}) copy-start(bf16[1,128,5120]{2,1,0:T(8,128)(2,1)} %param.10) | copy-start | bytes 3932164
  28.2 47.9 %copy-start.8 = (bf16[1,64,4096]{2,1,0:T(8,128)(2,1)S(1)}, bf16[1,64,4096]{2,1,0:T(8,128)(2,1)}, u32[]{:S(2)}) copy-start(bf16[1,64,4096]{2,1,0:T(8,128)(2,1)} %param.13) | copy-start | bytes 1572868
  28.3 16.9 %collective-permute-start.3 = (bf16[128,4096]{1,0:T(8,128)(2,1)}, bf16[128,4096]{1,0:T(8,128)(2,1)S(1)}, u32[]{:S(2)}, u32[]{:S(2)}) collective-permute-start(bf16[128,4096]{1,0:T(8,128)(2,1)} %get-tuple-element.37), channel_id=1, source_target_pairs={{192,193},{193,194},{194,195},{195,196},{196,197},{197,198},{198,1... | collective-permute-start | bytes 3145736 | tf_op jit(solution)/shard_map/ppermute | solution.py:375
  33.1 43.1 %collective-permute-start.4 = (bf16[128,4096]{1,0:T(8,128)(2,1)}, bf16[128,4096]{1,0:T(8,128)(2,1)S(1)}, u32[]{:S(2)}, u32[]{:S(2)}) collective-permute-start(bf16[128,4096]{1,0:T(8,128)(2,1)} %get-tuple-element.38), channel_id=1, source_target_pairs={{193,192},{194,193},{195,194},{196,195},{197,196},{198,197},{199,1... | collective-permute-start | bytes 3145736 | tf_op jit(solution)/shard_map/ppermute | solution.py:375
  37.3 55.3 %collective-permute-start.5 = (bf16[128,4096]{1,0:T(8,128)(2,1)}, bf16[128,4096]{1,0:T(8,128)(2,1)}, u32[]{:S(2)}, u32[]{:S(2)}) collective-permute-start(bf16[128,4096]{1,0:T(8,128)(2,1)} %broadcast_select_fusion), channel_id=1, source_target_pairs={{64,128},{65,129},{66,130},{67,131},{68,132},{69,133},{70,134},{71... | collective-permute-start | bytes 3145736 | tf_op jit(solution)/shard_map/ppermute | solution.py:375
  81.7 1.0 copy-start.13
  82.7 1.1 copy-start.18
  83.7 3.7 %collective-permute-start.6 = (bf16[128,128]{1,0:T(8,128)(2,1)S(1)}, bf16[128,128]{1,0:T(8,128)(2,1)S(1)}, u32[]{:S(2)}, u32[]{:S(2)}) collective-permute-start(bf16[128,128]{1,0:T(8,128)(2,1)S(1)} %get-tuple-element.46), channel_id=1, source_target_pairs={{0,1},{1,2},{2,3},{3,4},{4,5},{5,6},{6,7},{7,8},{8,9},{9,10},{10,1... | collective-permute-start | bytes 98312 | tf_op jit(solution)/shard_map/ppermute | solution.py:375
  84.4 3.1 %collective-permute-start.7 = (bf16[128,128]{1,0:T(8,128)(2,1)S(1)}, bf16[128,128]{1,0:T(8,128)(2,1)S(1)}, u32[]{:S(2)}, u32[]{:S(2)}) collective-permute-start(bf16[128,128]{1,0:T(8,128)(2,1)S(1)} %get-tuple-element.48), channel_id=1, source_target_pairs={{1,0},{2,1},{3,2},{4,3},{5,4},{6,5},{7,6},{8,7},{9,8},{10,9},{11,1... | collective-permute-start | bytes 98312 | tf_op jit(solution)/shard_map/ppermute | solution.py:375
  85.1 40.2 %collective-permute-start.11 = (bf16[128,5120]{1,0:T(8,128)(2,1)}, bf16[128,5120]{1,0:T(8,128)(2,1)}, u32[]{:S(2)}, u32[]{:S(2)}) collective-permute-start(bf16[128,5120]{1,0:T(8,128)(2,1)} %copy-done.18), channel_id=1, source_target_pairs={{64,0},{65,1},{66,2},{67,3},{68,4},{69,5},{70,6},{71,7},{72,8},{73... | collective-permute-start | bytes 3932168 | tf_op jit(solution)/shard_map/ppermute | solution.py:375
  87.4 1.2 copy-start.12
  88.7 1.2 copy-start.14
  91.6 1.0 copy-start.9
  92.6 32.6 %all-to-all-start = ((bf16[16,256,128]{2,1,0:T(8,128)(2,1)}), bf16[16,256,128]{2,1,0:T(8,128)(2,1)}, u32[]{:S(2)}, u32[]{:S(2)}) async-start(bf16[16,256,128]{2,1,0:T(8,128)(2,1)} %bitcast.27), calls=%async_computation | async-start | bytes 2097152 | tf_op jit(solution)/shard_map/all_to_all | solution.py:407
  102.3 29.5 %collective-permute-start.8 = (bf16[128,4096]{1,0:T(8,128)(2,1)S(1)}, bf16[128,4096]{1,0:T(8,128)(2,1)S(1)}, u32[]{:S(2)}, u32[]{:S(2)}) collective-permute-start(bf16[128,4096]{1,0:T(8,128)(2,1)S(1)} %broadcast_select_fusion.1.hop_ref), channel_id=1, source_target_pairs={{64,65},{65,66},{66,67},{67,68},{68,69},{69,70},{70,71},{71,72},{7... | collective-permute-start | bytes 3145736 | tf_op jit(solution)/shard_map/ppermute | solution.py:375
  103.6 28.2 %collective-permute-start.9 = (bf16[128,4096]{1,0:T(8,128)(2,1)S(1)}, bf16[128,4096]{1,0:T(8,128)(2,1)S(1)}, u32[]{:S(2)}, u32[]{:S(2)}) collective-permute-start(bf16[128,4096]{1,0:T(8,128)(2,1)S(1)} %broadcast_select_fusion.1.hop_ref), channel_id=1, source_target_pairs={{65,64},{66,65},{67,66},{68,67},{69,68},{70,69},{71,70},{72,71},{7... | collective-permute-start | bytes 3145736 | tf_op jit(solution)/shard_map/ppermute | solution.py:375
  108.0 23.9 %collective-permute-start.10 = (bf16[128,4096]{1,0:T(8,128)(2,1)}, bf16[128,4096]{1,0:T(8,128)(2,1)}, u32[]{:S(2)}, u32[]{:S(2)}) collective-permute-start(bf16[128,4096]{1,0:T(8,128)(2,1)} %forward_tile.1), channel_id=1, source_target_pairs={{67,132},{71,136},{75,140},{79,144},{83,148},{87,152},{91,156},{95... | collective-permute-start | bytes 3145736 | tf_op jit(solution)/shard_map/ppermute | solution.py:375
  127.3 8.3 %all-to-all-start.1 = ((f32[4,64,128]{2,1,0:T(8,128)}), f32[4,64,128]{2,1,0:T(8,128)S(1)}, u32[]{:S(2)}, u32[]{:S(2)}) async-start(f32[4,64,128]{2,1,0:T(8,128)} %bitcast.12), calls=%async_computation.1 | async-start | bytes 262144 | tf_op jit(solution)/shard_map/all_to_all | solution.py:407

commit v11 on v10

--- a/solution.py
+++ b/solution.py
@@ -88,7 +88,8 @@
         for h in range(GROUP):
             cols = slice(j * GW + h * HEAD_DIM, j * GW + (h + 1) * HEAD_DIM)
             out_ref[:, cols] = attn[h * TILE : (h + 1) * TILE]
-        low = low + dot(out_ref[:, j * GW : (j + 1) * GW], down_ref[j * GW : (j + 1) * GW, :], NN)
+        block = slice(j * GW, (j + 1) * GW)
+        low = low + dot(out_ref[:, block], down_ref[:, block], NT)
     low = low.astype(BF16)
     for c in range(0, QW, 512):
         lift = dot(low, up_ref[:, c : c + 512], NN)
@@ -118,7 +119,7 @@
         for h in range(GROUP):
             cols = slice(j * GW + h * HEAD_DIM, j * GW + (h + 1) * HEAD_DIM)
             attn_ref[:, cols] = attn[h * TILE : (h + 1) * TILE]
-        low = low + dot(attn_ref[:, block], down_ref[block, :], NN)
+        low = low + dot(attn_ref[:, block], down_ref[:, block], NT)
     low_ref[...] = low.astype(BF16)
 
     @pl.when(place_ref[1] == 0)
@@ -142,7 +143,7 @@
 
 def terms_kernel(
     place_ref, langs_ref, dest_ref, table_ref, attn_ref, slots_ref, left_ref, own_ref, right_ref,
-    scaled_ref, back_ref, low_ref, terms_ref, slot_scaled_ref, held_ref, sem,
+    home_ref, terms_ref, slot_scaled_ref, held_ref, summed_ref, sem,
 ):
     rank = place_ref[0]
     tiles = dest_ref.shape[1]
@@ -164,21 +165,16 @@
             one = dot(attn_ref[:, cols], back, TN)
             two = dot(slot_scaled_ref[...], lows, TN)
             terms = jnp.concatenate([one[:, RANK:], two[:, :RANK]], axis=1)
-            terms_ref[cols, :] = terms.astype(terms_ref.dtype)
-
-    @pl.when(place_ref[1] != 0)
-    def _():
-        for c in range(0, QW, 512):
-            cols = slice(c, c + 512)
-            one = dot(attn_ref[:, cols], back_ref[...], TN)
-            two = dot(scaled_ref[:, cols], low_ref[...], TN)
-            terms_ref[cols, :] = jnp.concatenate([one, two], axis=1).astype(terms_ref.dtype)
+            summed_ref[cols, :] = terms.astype(BF16)
+        store = pltpu.make_async_copy(summed_ref, terms_ref, sem)
+        store.start()
+        store.wait()
 
 
 def backward_kernel(
     place_ref, langs_ref, dest_ref, table_ref, qkv_ref, left_ref, right_ref, last_left_ref,
-    last_right_ref, slots_ref, probs_ref, down_ref, up_ref, grad_ref, scaled_ref, back_ref,
-    gattn_ref, mid_ref, sem,
+    last_right_ref, slots_ref, probs_ref, attn_ref, low_ref, down_ref, up_ref, grad_ref, terms_ref,
+    gattn_ref, scaled_ref, mid_ref, sem,
 ):
     rank = place_ref[0]
     rate = table_ref[langs_ref[1, rank]]
@@ -206,10 +202,9 @@
     @pl.when(active)
     def _():
         back = chosen()
-        back_ref[...] = back
         for j in range(KV):
             block = slice(j * GW, (j + 1) * GW)
-            gattn = gattn_ref[:, block].astype(F32) + dot(back, down_ref[block, :], NT)
+            gattn = gattn_ref[:, block].astype(F32) + dot(back, down_ref[:, block], NN)
             gattn_ref[:, block] = gattn.astype(BF16)
             queries = stacked(qkv_ref, j * GW)
             keys = qkv_ref[:, QW + j * HEAD_DIM : QW + (j + 1) * HEAD_DIM]
@@ -233,6 +228,11 @@
             grad_ref[:, cols] = dot(grad_scores, queries, TN).astype(BF16)
             cols = slice(QW + KW + j * HEAD_DIM, QW + KW + (j + 1) * HEAD_DIM)
             grad_ref[:, cols] = dot(probs_low, grads, TN).astype(BF16)
+        for c in range(0, QW, 512):
+            cols = slice(c, c + 512)
+            one = dot(attn_ref[:, cols], back, TN)
+            two = dot(scaled_ref[:, cols], low_ref[...], TN)
+            terms_ref[cols, :] = jnp.concatenate([one, two], axis=1).astype(terms_ref.dtype)
 
 
 COST = pl.CostEstimate(flops=2**20, bytes_accessed=2**20, transcendentals=0)
@@ -275,34 +275,36 @@
     )(place, lengths, languages, dest, table, qkv, slots, down, up)
 
 
-def run_terms(place, languages, dest, table, attn, slots, left, own, right, scaled, back, low):
+def run_terms(place, languages, dest, table, attn, slots, left, own, right, home):
     return pl.pallas_call(
         terms_kernel,
         out_shape=jax.ShapeDtypeStruct((QW, 2 * RANK), BF16),
-        in_specs=[SMEM] * 4 + [VMEM, ANY] + [VMEM] * 6,
-        out_specs=VMEM,
+        in_specs=[SMEM] * 4 + [VMEM, ANY] + [VMEM] * 3 + [ANY],
+        input_output_aliases={9: 0},
+        out_specs=ANY,
         scratch_shapes=[
             pltpu.VMEM((3 * TILE, 512), BF16),
             pltpu.VMEM((3 * TILE, QW), BF16),
+            pltpu.VMEM((QW, 2 * RANK), BF16),
             pltpu.SemaphoreType.DMA,
         ],
         compiler_params=pltpu.CompilerParams(vmem_limit_bytes=22 * 2**20),
         cost_estimate=COST,
         name="adapter_terms",
-    )(place, languages, dest, table, attn, slots, left, own, right, scaled, back, low)
-
-
-def run_backward(place, languages, dest, table, qkv, moved, slots, probs, down, up):
+    )(place, languages, dest, table, attn, slots, left, own, right, home)
+
+
+def run_backward(place, languages, dest, table, qkv, moved, slots, probs, attn, low, down, up):
     return pl.pallas_call(
         backward_kernel,
         out_shape=(
             jax.ShapeDtypeStruct((TILE, QW + 2 * KW), BF16),
-            jax.ShapeDtypeStruct((TILE, QW), BF16),
-            jax.ShapeDtypeStruct((TILE, RANK), BF16),
+            jax.ShapeDtypeStruct((QW, 2 * RANK), BF16),
         ),
-        in_specs=[SMEM] * 4 + [VMEM] * (1 + len(moved)) + [ANY] + [VMEM] * 3,
-        out_specs=(VMEM,) * 3,
+        in_specs=[SMEM] * 4 + [VMEM] * 5 + [ANY] + [VMEM] * 5,
+        out_specs=(VMEM, VMEM),
         scratch_shapes=[
+            pltpu.VMEM((TILE, QW), BF16),
             pltpu.VMEM((TILE, QW), BF16),
             pltpu.VMEM((TILE, QW), BF16),
             pltpu.SemaphoreType.DMA,
@@ -310,7 +312,7 @@
         compiler_params=pltpu.CompilerParams(vmem_limit_bytes=24 * 2**20),
         cost_estimate=COST,
         name="backward_tile",
-    )(place, languages, dest, table, qkv, *moved, slots, probs, down, up)
+    )(place, languages, dest, table, qkv, *moved, slots, probs, attn, low, down, up)
 
 
 def place_kernel(
@@ -351,7 +353,7 @@
             jax.ShapeDtypeStruct((3 * TILE, QW), BF16),
             jax.ShapeDtypeStruct(tiles[-1].shape, BF16),
         ),
-        in_specs=[SMEM] * 2 + [VMEM] * len(tiles),
+        in_specs=[SMEM] * 2 + [ANY] * len(tiles),
         out_specs=(ANY, ANY),
         scratch_shapes=[pltpu.VMEM((TILE, QW), BF16), pltpu.SemaphoreType.DMA((4,))],
         compiler_params=pltpu.CompilerParams(vmem_limit_bytes=24 * 2**20),
@@ -387,14 +389,6 @@
     return t % RUN == RUN - 1
 
 
-def after_run_start(t):
-    return t % RUN == 1
-
-
-def before_run_end(t):
-    return t % RUN == RUN - 2
-
-
 def not_run_start(t):
     return t % RUN != 0
 
@@ -413,7 +407,7 @@
     rank, size = lax.axis_index("dp"), lax.axis_size("dp")
     section, last = lax.axis_index("section"), sections() - 1
     place = jnp.stack([rank, section, jnp.int32(sections())]).astype(jnp.int32)
-    down, up = adapter_down[0], adapter_up[0]
+    down, up = adapter_down[0].T, adapter_up[0]
     slots = slot_grad_b[0]
     every, early = range(sections()), range(1, last)
     to_up, to_down = slots[2 * TILE :], slots[:TILE]
@@ -429,13 +423,10 @@
     to_up, to_down, near, low = lax.optimization_barrier((to_up, to_down, near, low))
     last_left = shift(to_up, [([last], 0, 1, anywhere)])
     last_right = shift(to_down, [([last], 0, -1, anywhere)])
-    far = shift(
-        jnp.where(section == last, near, out),
-        [([1], 1, 0, anywhere), ([last], -last, -1, run_end), ([last], -last, 1, run_start)],
-    )
-    grad_qkv, scaled, back = run_backward(
+    far = shift(out, [([1], 1, 0, anywhere)])
+    grad_qkv, terms = run_backward(
         place, languages, destination, lang_scale, qkv_b[0],
-        (from_left, from_right, last_left, last_right), slots, probs, down, up,
+        (from_left, from_right, last_left, last_right), slots, probs, attn, low, down, up,
     )
     grad_qkv, near, to_left, to_right = lax.optimization_barrier(
         (grad_qkv, near, to_left, to_right)
@@ -444,21 +435,15 @@
     left = shift(to_right, [([0], 0, 1, anywhere)])
     right = shift(to_left, [([0], 0, -1, anywhere)])
     terms = run_terms(
-        place, languages, destination, lang_scale, attn, slots, left, own, right, scaled, back, low
+        place, languages, destination, lang_scale, attn, slots, left, own, right, terms
     )
     planes = [[RUN * k + z for k in range(size // RUN)] for z in range(RUN)]
     columns = [[RUN * k + z for z in range(RUN)] for k in range(size // RUN)]
     far, terms, out = lax.optimization_barrier((far, terms, out))
     pieces = scatter(terms.reshape(size // RUN, -1, 2 * RANK), planes)
-    hop = jnp.where((section == 1) | (section == last), near, far)
-    before = shift(
-        hop,
-        [([1], 0, 1, anywhere), ([2, last], 0, 1, not_run_end), ([0], last, 2, before_run_end)],
-    )
-    after = shift(
-        hop,
-        [([1], 0, -1, anywhere), ([2, last], 0, -1, not_run_start), ([0], last, -2, after_run_start)],
-    )
+    hop = jnp.where(section == 2, far, near)
+    before = shift(hop, [([1, last], 0, 1, anywhere), ([2], 0, 1, not_run_end)])
+    after = shift(hop, [([1, last], 0, -1, anywhere), ([2], 0, -1, not_run_start)])
     ends = shift(out, [([1], 1, 1, run_end), ([1], 1, -1, run_start)])
     pieces, _ = lax.optimization_barrier((pieces, handed_back))
     terms = jnp.sum(pieces.astype(F32), axis=0)

time: 139 us -> 212 us (1.53)
  the two profiles are of different devices: /device:TPU:227 before, /device:TPU:136 now
where the time goes in v11:
time: 212 us; the launch traced here: 211 us
  Pallas kernels  89.5 us (42%)
  waiting for transfers between devices  52.7 us (25%)
  starting transfers between devices  44.4 us (21%)
  local copies, waits for them, and re-layouts  19.9 us (9%)
  other arithmetic  4.07 us (2%)
    pallas_call x1, Pallas kernels, run_place(): pl.pallas_call(place_kernel, out_shape=(jax.ShapeDtypeStruct((3 * TILE, Q...  73.2 us
    ppermute x12, waiting for transfers between devices, shift(): return lax.ppermute(x, AXES, route)  47.5 us
    ppermute x12, starting transfers between devices, shift(): return lax.ppermute(x, AXES, route)  29.3 us
    unnamed x49, local copies, waits for them, and re-layouts  16.8 us
    all_to_all x2, starting transfers between devices, scatter(): return lax.all_to_all(x, 'dp', 0, 0, axis_index_groups=groups, tiled=True)  15.1 us
    pallas_call x1, Pallas kernels, run_backward(): pl.pallas_call(backward_kernel, out_shape=(jax.ShapeDtypeStruct((TILE, QW...  6.06 us
    pallas_call x1, Pallas kernels, run_forward(): pl.pallas_call(forward_kernel, out_shape=jax.ShapeDtypeStruct((TILE, QW),...  5.54 us
    all_to_all x2, waiting for transfers between devices, scatter(): return lax.all_to_all(x, 'dp', 0, 0, axis_index_groups=groups, tiled=True)  5.19 us
  transfers between devices with their start and end apart: 14, of which 4 were waited for; matrix products, arithmetic and copies ran while one was open for 2% of the time, Pallas kernels for 42%

profile of v11, /device:TPU:136, one launch (start us, length us, event | category | flops | bytes accessed | tf_op | source)
XLA Modules:
  0.0 211.4 jit_solution(18165463388043641307)
XLA Ops:
  0.7 3.1 %slice_bitcast_fusion = (bf16[128,4096]{1,0:T(8,128)(2,1)}, bf16[128,4096]{1,0:T(8,128)(2,1)}) fusion(bf16[1,384,4096]{2,1,0:T(8,128)(2,1)} %param.11), kind=kLoop, calls=%fused_computation.1 | loop fusion | bytes 4194304 | tf_op jit(solution)/shard_map/slice | solution.py:413
  3.8 3.2 %collective-permute-start.1 = (bf16[128,4096]{1,0:T(8,128)(2,1)}, bf16[128,4096]{1,0:T(8,128)(2,1)}, u32[]{:S(2)}, u32[]{:S(2)}) collective-permute-start(bf16[128,4096]{1,0:T(8,128)(2,1)} %get-tuple-element.37), channel_id=1, source_target_pairs={{64,65},{65,66},{66,67},{67,68},{68,69},{69,70},{70,71},{71,72},{7... | collective-permute-start | bytes 3145736 | tf_op jit(solution)/shard_map/ppermute | solution.py:377
  7.0 5.6 %collective-permute-start.2 = (bf16[128,4096]{1,0:T(8,128)(2,1)}, bf16[128,4096]{1,0:T(8,128)(2,1)}, u32[]{:S(2)}, u32[]{:S(2)}) collective-permute-start(bf16[128,4096]{1,0:T(8,128)(2,1)} %get-tuple-element.38), channel_id=1, source_target_pairs={{65,64},{66,65},{67,66},{68,67},{69,68},{70,69},{71,70},{72,71},{7... | collective-permute-start | bytes 3145736 | tf_op jit(solution)/shard_map/ppermute | solution.py:377
  12.6 0.1 copy.15.lens_ref
  12.7 0.1 pad_add_fusion.rank_ref.place_ref
  12.8 1.0 copy-done.3
  13.8 1.0 copy-done.6
  14.9 1.3 copy-done.14
  16.2 5.5 %forward_tile.1 = bf16[128,4096]{1,0:T(8,128)(2,1)} custom-call(s32[3]{0:T(128)S(1)} %pad_add_fusion.rank_ref.place_ref, s32[2,64,8]{2,1,0:T(8,128)S(1)} %copy.15.lens_ref, s32[2,64]{1,0:T(2,128)S(1)} %copy-done.19, f32[102]{0:T(128)S(1)} %copy-done.21, bf16[128,5120]{1,0:T(8,128)(2,1)S(1)} %bitcast.30, bf16[64,4096]{1,0:T(8,128)(2,1)S(1)} %bitcast.23, ...), custom_call_target="tpu_custom_call" | custom-call | flops 1048576 | bytes 1048576 | tf_op jit(solution)/shard_map/forward_tile/pallas_call | solution.py:245
  21.7 2.3 %collective-permute-start.3 = (bf16[128,4096]{1,0:T(8,128)(2,1)}, bf16[128,4096]{1,0:T(8,128)(2,1)}, u32[]{:S(2)}, u32[]{:S(2)}) collective-permute-start(bf16[128,4096]{1,0:T(8,128)(2,1)} %forward_tile.1), channel_id=1, source_target_pairs={{0,64},{1,65},{2,66},{3,67},{4,68},{5,69},{6,70},{7,71},{8,72},{9,... | collective-permute-start | bytes 3145736 | tf_op jit(solution)/shard_map/ppermute | solution.py:377
  24.0 1.3 copy-done.1
  25.3 1.0 copy-done.4
  26.3 1.0 copy-done.7
  27.4 3.9 %prepare_tile.1 = (f32[4096,128]{1,0:T(8,128)S(1)}, bf16[128,4096]{1,0:T(8,128)(2,1)S(1)}, bf16[128,64]{1,0:T(8,128)(2,1)S(1)}, bf16[128,128]{1,0:T(8,128)(2,1)S...) custom-call(s32[3]{0:T(128)S(1)} %pad_add_fusion.rank_ref.place_ref, s32[2,64,8]{2,1,0:T(8,128)S(1)} %copy.15.lens_ref, ...), custom_call_target="tpu_custom_call" | custom-call | flops 1048576 | bytes 1048576 | tf_op jit(solution)/shard_map/prepare_tile/pallas_call | solution.py:259
  31.3 17.3 %collective-permute-done.2.right_ref = bf16[128,4096]{1,0:T(8,128)(2,1)} collective-permute-done((bf16[128,4096]{1,0:T(8,128)(2,1)}, bf16[128,4096]{1,0:T(8,128)(2,1)}, u32[]{:S(2)}, u32[]{:S(2)}) %collective-permute-start.2) | collective-permute-done | bytes 1048608 | tf_op jit(solution)/shard_map/ppermute | solution.py:377
  48.6 0.7 collective-permute-start.4
  49.3 0.7 collective-permute-start.5
  50.1 1.3 collective-permute-start
  51.4 0.0 collective-permute-done.4.last_left_ref
  51.4 0.0 collective-permute-done.5.last_right_ref
  51.4 6.1 %backward_tile.1 = (bf16[128,5120]{1,0:T(8,128)(2,1)S(1)}, bf16[4096,128]{1,0:T(8,128)(2,1)S(1)}) custom-call(s32[3]{0:T(128)S(1)} %pad_add_fusion.rank_ref.place_ref, s32[2,64]{1,0:T(2,128)S(1)} %copy-done.19, s32[2,64]{1,0:T(2,128)S(1)} %copy-done.20, f32[102]{0:T(128)S(1)} %copy-done.21, bf16[128,5120]{1,0:T(8,128)(2,1)S(1)} %bitcast.22, ...), custom_call_target="tpu_custom_call" | custom-call | flops 1048576 | bytes 1048576 | tf_op jit(solution)/shard_map/backward_tile/pallas_call | solution.py:298
  57.5 1.0 copy-done.9
  58.5 1.1 copy-done.22
  59.5 0.7 collective-permute-start.6
  60.2 0.7 collective-permute-start.7
  60.9 9.1 %collective-permute-start.11 = (bf16[128,5120]{1,0:T(8,128)(2,1)}, bf16[128,5120]{1,0:T(8,128)(2,1)}, u32[]{:S(2)}, u32[]{:S(2)}) collective-permute-start(bf16[128,5120]{1,0:T(8,128)(2,1)} %copy-done.22), channel_id=1, source_target_pairs={{64,0},{65,1},{66,2},{67,3},{68,4},{69,5},{70,6},{71,7},{72,8},{73... | collective-permute-start | bytes 3932168 | tf_op jit(solution)/shard_map/ppermute | solution.py:377
  70.0 0.0 collective-permute-done.6.left_ref
  70.0 0.0 collective-permute-done.7.right_ref
  70.0 1.2 copy-done.10
  71.3 1.2 copy-done.13
  72.5 0.8 adapter_terms.1
  73.3 1.0 copy-done.11
  74.3 6.8 %all-to-all-start = ((bf16[16,256,128]{2,1,0:T(8,128)(2,1)}), bf16[16,256,128]{2,1,0:T(8,128)(2,1)}, u32[]{:S(2)}, u32[]{:S(2)}) async-start(bf16[16,256,128]{2,1,0:T(8,128)(2,1)} %bitcast.29), calls=%async_computation | async-start | bytes 2097152 | tf_op jit(solution)/shard_map/all_to_all | solution.py:401
  81.1 1.3 broadcast_select_fusion.hop_ref
  82.4 2.5 %collective-permute-start.8 = (bf16[128,4096]{1,0:T(8,128)(2,1)S(1)}, bf16[128,4096]{1,0:T(8,128)(2,1)S(1)}, u32[]{:S(2)}, u32[]{:S(2)}) collective-permute-start(bf16[128,4096]{1,0:T(8,128)(2,1)S(1)} %broadcast_select_fusion.hop_ref), channel_id=1, source_target_pairs={{64,65},{65,66},{66,67},{67,68},{68,69},{69,70},{70,71},{71,72},{7... | collective-permute-start | bytes 3145736 | tf_op jit(solution)/shard_map/ppermute | solution.py:377
  84.9 1.3 collective-permute-start.9
  86.2 1.3 collective-permute-start.10
  87.5 5.2 %all-to-all-done = bf16[16,256,128]{2,1,0:T(8,128)(2,1)} async-done(((bf16[16,256,128]{2,1,0:T(8,128)(2,1)}), bf16[16,256,128]{2,1,0:T(8,128)(2,1)}, u32[]{:S(2)}, u32[]{:S(2)}) %all-to-all-start) | async-done | bytes 1048608 | tf_op jit(solution)/shard_map/all_to_all | solution.py:401
  92.7 2.0 convert_reduce_fusion
  94.8 8.3 %all-to-all-start.1 = ((f32[4,64,128]{2,1,0:T(8,128)}), f32[4,64,128]{2,1,0:T(8,128)S(1)}, u32[]{:S(2)}, u32[]{:S(2)}) async-start(f32[4,64,128]{2,1,0:T(8,128)} %bitcast.14), calls=%async_computation.1 | async-start | bytes 262144 | tf_op jit(solution)/shard_map/all_to_all | solution.py:401
  103.0 8.4 %collective-permute-done.8.before_ref = bf16[128,4096]{1,0:T(8,128)(2,1)S(1)} collective-permute-done((bf16[128,4096]{1,0:T(8,128)(2,1)S(1)}, bf16[128,4096]{1,0:T(8,128)(2,1)S(1)}, u32[]{:S(2)}, u32[]{:S(2)}) %collective-permute-start.8) | collective-permute-done | bytes 1048608 | tf_op jit(solution)/shard_map/ppermute | solution.py:377
  111.4 1.0 copy-done.15
  112.4 21.7 %collective-permute-done.9.after_ref = bf16[128,4096]{1,0:T(8,128)(2,1)S(1)} collective-permute-done((bf16[128,4096]{1,0:T(8,128)(2,1)S(1)}, bf16[128,4096]{1,0:T(8,128)(2,1)S(1)}, u32[]{:S(2)}, u32[]{:S(2)}) %collective-permute-start.9) | collective-permute-done | bytes 1048608 | tf_op jit(solution)/shard_map/ppermute | solution.py:377
  134.1 1.0 copy-done.17
  135.1 1.2 copy-done.16
  136.3 1.2 copy-done.18
  137.6 73.2 %place_outputs.1 = (bf16[384,4096]{1,0:T(8,128)(2,1)}, bf16[128,5120]{1,0:T(8,128)(2,1)}) custom-call(s32[3]{0:T(128)S(1)} %pad_add_fusion.rank_ref.place_ref, s32[2,64]{1,0:T(2,128)S(1)} %copy-done.20, bf16[128,4096]{1,0:T(8,128)(2,1)S(1)} %copy-done.16, bf16[128,4096]{1,0:T(8,128)(2,1)S(1)} %broadcast_select_fusion.hop_ref, ...), custom_call_target="tpu_custom_call" | custom-call | flops 1048576 | bytes 1048576 | tf_op jit(solution)/shard_map/place_outputs/pallas_call | solution.py:350
  210.8 0.6 reduce_sum.19
  (39 shorter events, 0.1 us)
Async XLA Ops:
  0.6 12.0 %copy-start.23 = (s32[2,64,8]{1,2,0:T(8,128)S(1)}, s32[2,64,8]{1,2,0:T(8,128)}, u32[]{:S(2)}) copy-start(s32[2,64,8]{1,2,0:T(8,128)} %param.16) | copy-start | bytes 12292
  0.6 12.1 %copy-start.21 = (f32[102]{0:T(128)S(1)}, f32[102]{0:T(128)}, u32[]{:S(2)}) copy-start(f32[102]{0:T(128)} %table_ref.7) | copy-start | bytes 1228
  0.7 12.1 %copy-start.19 = (s32[2,64]{1,0:T(2,128)S(1)}, s32[2,64]{1,0:T(2,128)}, u32[]{:S(2)}) copy-start(s32[2,64]{1,0:T(2,128)} %langs_ref.7) | copy-start | bytes 1540
  0.7 23.3 %copy-start.20 = (s32[2,64]{1,0:T(2,128)S(1)}, s32[2,64]{1,0:T(2,128)}, u32[]{:S(2)}) copy-start(s32[2,64]{1,0:T(2,128)} %dest_ref.7) | copy-start | bytes 1540
  3.8 20.2 %copy-start = (bf16[1,384,4096]{2,1,0:T(8,128)(2,1)S(1)}, bf16[1,384,4096]{2,1,0:T(8,128)(2,1)}, u32[]{:S(2)}) copy-start(bf16[1,384,4096]{2,1,0:T(8,128)(2,1)} %param.11) | copy-start | bytes 9437188
  3.8 27.5 %collective-permute-start.1 = (bf16[128,4096]{1,0:T(8,128)(2,1)}, bf16[128,4096]{1,0:T(8,128)(2,1)}, u32[]{:S(2)}, u32[]{:S(2)}) collective-permute-start(bf16[128,4096]{1,0:T(8,128)(2,1)} %get-tuple-element.37), channel_id=1, source_target_pairs={{64,65},{65,66},{66,67},{67,68},{68,69},{69,70},{70,71},{71,72},{7... | collective-permute-start | bytes 3145736 | tf_op jit(solution)/shard_map/ppermute | solution.py:377
  7.0 41.7 %collective-permute-start.2 = (bf16[128,4096]{1,0:T(8,128)(2,1)}, bf16[128,4096]{1,0:T(8,128)(2,1)}, u32[]{:S(2)}, u32[]{:S(2)}) collective-permute-start(bf16[128,4096]{1,0:T(8,128)(2,1)} %get-tuple-element.38), channel_id=1, source_target_pairs={{65,64},{66,65},{67,66},{68,67},{69,68},{70,69},{71,70},{72,71},{7... | collective-permute-start | bytes 3145736 | tf_op jit(solution)/shard_map/ppermute | solution.py:377
  12.8 1.0 copy-start.3
  13.8 1.0 copy-start.6
  14.9 1.3 copy-start.14
  21.7 26.9 %collective-permute-start.3 = (bf16[128,4096]{1,0:T(8,128)(2,1)}, bf16[128,4096]{1,0:T(8,128)(2,1)}, u32[]{:S(2)}, u32[]{:S(2)}) collective-permute-start(bf16[128,4096]{1,0:T(8,128)(2,1)} %forward_tile.1), channel_id=1, source_target_pairs={{0,64},{1,65},{2,66},{3,67},{4,68},{5,69},{6,70},{7,71},{8,72},{9,... | collective-permute-start | bytes 3145736 | tf_op jit(solution)/shard_map/ppermute | solution.py:377
  24.0 1.3 copy-start.1
  25.3 1.0 copy-start.4
  26.3 1.0 copy-start.7
  27.4 24.0 %copy-start.2 = (bf16[1,128,5120]{2,1,0:T(8,128)(2,1)S(1)}, bf16[1,128,5120]{2,1,0:T(8,128)(2,1)}, u32[]{:S(2)}) copy-start(bf16[1,128,5120]{2,1,0:T(8,128)(2,1)} %param.10) | copy-start | bytes 3932164
  27.4 24.0 %copy-start.5 = (bf16[1,4096,64]{1,2,0:T(8,128)(2,1)S(1)}, bf16[1,4096,64]{1,2,0:T(8,128)(2,1)}, u32[]{:S(2)}) copy-start(bf16[1,4096,64]{1,2,0:T(8,128)(2,1)} %param.12) | copy-start | bytes 1572868
  27.4 24.0 %copy-start.8 = (bf16[1,64,4096]{2,1,0:T(8,128)(2,1)S(1)}, bf16[1,64,4096]{2,1,0:T(8,128)(2,1)}, u32[]{:S(2)}) copy-start(bf16[1,64,4096]{2,1,0:T(8,128)(2,1)} %param.13) | copy-start | bytes 1572868
  31.3 26.2 %copy-start.12 = (bf16[128,4096]{1,0:T(8,128)(2,1)}, bf16[128,4096]{1,0:T(8,128)(2,1)S(1)}, u32[]{:S(2)}) copy-start(bf16[128,4096]{1,0:T(8,128)(2,1)S(1)} %get-tuple-element.32.attn_ref) | copy-start | bytes 3145732
  48.6 2.8 %collective-permute-start.4 = (bf16[128,4096]{1,0:T(8,128)(2,1)}, bf16[128,4096]{1,0:T(8,128)(2,1)S(1)}, u32[]{:S(2)}, u32[]{:S(2)}) collective-permute-start(bf16[128,4096]{1,0:T(8,128)(2,1)} %get-tuple-element.37), channel_id=1, source_target_pairs={{192,193},{193,194},{194,195},{195,196},{196,197},{197,198},{198,1... | collective-permute-start | bytes 3145736 | tf_op jit(solution)/shard_map/ppermute | solution.py:377
  49.3 2.0 collective-permute-start.5
  50.1 24.2 %collective-permute-start = (bf16[128,4096]{1,0:T(8,128)(2,1)}, bf16[128,4096]{1,0:T(8,128)(2,1)}, u32[]{:S(2)}, u32[]{:S(2)}) collective-permute-start(bf16[128,4096]{1,0:T(8,128)(2,1)} %forward_tile.1), channel_id=1, source_target_pairs={{64,128},{65,129},{66,130},{67,131},{68,132},{69,133},{70,134},{71... | collective-permute-start | bytes 3145736 | tf_op jit(solution)/shard_map/ppermute | solution.py:377
  57.5 1.0 copy-start.9
  58.5 1.1 copy-start.22
  59.5 10.5 %collective-permute-start.6 = (bf16[128,128]{1,0:T(8,128)(2,1)S(1)}, bf16[128,128]{1,0:T(8,128)(2,1)S(1)}, u32[]{:S(2)}, u32[]{:S(2)}) collective-permute-start(bf16[128,128]{1,0:T(8,128)(2,1)S(1)} %get-tuple-element.45), channel_id=1, source_target_pairs={{0,1},{1,2},{2,3},{3,4},{4,5},{5,6},{6,7},{7,8},{8,9},{9,10},{10,1... | collective-permute-start | bytes 98312 | tf_op jit(solution)/shard_map/ppermute | solution.py:377
  60.2 9.8 %collective-permute-start.7 = (bf16[128,128]{1,0:T(8,128)(2,1)S(1)}, bf16[128,128]{1,0:T(8,128)(2,1)S(1)}, u32[]{:S(2)}, u32[]{:S(2)}) collective-permute-start(bf16[128,128]{1,0:T(8,128)(2,1)S(1)} %get-tuple-element.47), channel_id=1, source_target_pairs={{1,0},{2,1},{3,2},{4,3},{5,4},{6,5},{7,6},{8,7},{9,8},{10,9},{11,1... | collective-permute-start | bytes 98312 | tf_op jit(solution)/shard_map/ppermute | solution.py:377
  60.9 31.8 %collective-permute-start.11 = (bf16[128,5120]{1,0:T(8,128)(2,1)}, bf16[128,5120]{1,0:T(8,128)(2,1)}, u32[]{:S(2)}, u32[]{:S(2)}) collective-permute-start(bf16[128,5120]{1,0:T(8,128)(2,1)} %copy-done.22), channel_id=1, source_target_pairs={{64,0},{65,1},{66,2},{67,3},{68,4},{69,5},{70,6},{71,7},{72,8},{73... | collective-permute-start | bytes 3932168 | tf_op jit(solution)/shard_map/ppermute | solution.py:377
  70.0 1.2 copy-start.10
  71.3 1.2 copy-start.13
  73.3 1.0 copy-start.11
  74.3 18.5 %all-to-all-start = ((bf16[16,256,128]{2,1,0:T(8,128)(2,1)}), bf16[16,256,128]{2,1,0:T(8,128)(2,1)}, u32[]{:S(2)}, u32[]{:S(2)}) async-start(bf16[16,256,128]{2,1,0:T(8,128)(2,1)} %bitcast.29), calls=%async_computation | async-start | bytes 2097152 | tf_op jit(solution)/shard_map/all_to_all | solution.py:401
  82.4 29.0 %collective-permute-start.8 = (bf16[128,4096]{1,0:T(8,128)(2,1)S(1)}, bf16[128,4096]{1,0:T(8,128)(2,1)S(1)}, u32[]{:S(2)}, u32[]{:S(2)}) collective-permute-start(bf16[128,4096]{1,0:T(8,128)(2,1)S(1)} %broadcast_select_fusion.hop_ref), channel_id=1, source_target_pairs={{64,65},{65,66},{66,67},{67,68},{68,69},{69,70},{70,71},{71,72},{7... | collective-permute-start | bytes 3145736 | tf_op jit(solution)/shard_map/ppermute | solution.py:377
  84.9 49.2 %collective-permute-start.9 = (bf16[128,4096]{1,0:T(8,128)(2,1)S(1)}, bf16[128,4096]{1,0:T(8,128)(2,1)S(1)}, u32[]{:S(2)}, u32[]{:S(2)}) collective-permute-start(bf16[128,4096]{1,0:T(8,128)(2,1)S(1)} %broadcast_select_fusion.hop_ref), channel_id=1, source_target_pairs={{65,64},{66,65},{67,66},{68,67},{69,68},{70,69},{71,70},{72,71},{7... | collective-permute-start | bytes 3145736 | tf_op jit(solution)/shard_map/ppermute | solution.py:377
  86.2 48.9 %collective-permute-start.10 = (bf16[128,4096]{1,0:T(8,128)(2,1)}, bf16[128,4096]{1,0:T(8,128)(2,1)}, u32[]{:S(2)}, u32[]{:S(2)}) collective-permute-start(bf16[128,4096]{1,0:T(8,128)(2,1)} %forward_tile.1), channel_id=1, source_target_pairs={{67,132},{71,136},{75,140},{79,144},{83,148},{87,152},{91,156},{95... | collective-permute-start | bytes 3145736 | tf_op jit(solution)/shard_map/ppermute | solution.py:377
  94.8 116.0 %all-to-all-start.1 = ((f32[4,64,128]{2,1,0:T(8,128)}), f32[4,64,128]{2,1,0:T(8,128)S(1)}, u32[]{:S(2)}, u32[]{:S(2)}) async-start(f32[4,64,128]{2,1,0:T(8,128)} %bitcast.14), calls=%async_computation.1 | async-start | bytes 262144 | tf_op jit(solution)/shard_map/all_to_all | solution.py:401
  111.4 1.0 copy-start.15
  134.1 1.0 copy-start.17
  135.1 1.2 copy-start.16
  136.3 1.2 copy-start.18

commit v12 on v11

--- a/solution.py
+++ b/solution.py
@@ -353,7 +353,7 @@
             jax.ShapeDtypeStruct((3 * TILE, QW), BF16),
             jax.ShapeDtypeStruct(tiles[-1].shape, BF16),
         ),
-        in_specs=[SMEM] * 2 + [ANY] * len(tiles),
+        in_specs=[SMEM] * 2 + [VMEM] * len(tiles),
         out_specs=(ANY, ANY),
         scratch_shapes=[pltpu.VMEM((TILE, QW), BF16), pltpu.SemaphoreType.DMA((4,))],
         compiler_params=pltpu.CompilerParams(vmem_limit_bytes=24 * 2**20),
@@ -387,6 +387,14 @@
 
 def run_end(t):
     return t % RUN == RUN - 1
+
+
+def after_run_start(t):
+    return t % RUN == 1
+
+
+def before_run_end(t):
+    return t % RUN == RUN - 2
 
 
 def not_run_start(t):
@@ -423,7 +431,10 @@
     to_up, to_down, near, low = lax.optimization_barrier((to_up, to_down, near, low))
     last_left = shift(to_up, [([last], 0, 1, anywhere)])
     last_right = shift(to_down, [([last], 0, -1, anywhere)])
-    far = shift(out, [([1], 1, 0, anywhere)])
+    far = shift(
+        jnp.where(section == last, near, out),
+        [([1], 1, 0, anywhere), ([last], -last, -1, run_end), ([last], -last, 1, run_start)],
+    )
     grad_qkv, terms = run_backward(
         place, languages, destination, lang_scale, qkv_b[0],
         (from_left, from_right, last_left, last_right), slots, probs, attn, low, down, up,
@@ -441,9 +452,15 @@
     columns = [[RUN * k + z for z in range(RUN)] for k in range(size // RUN)]
     far, terms, out = lax.optimization_barrier((far, terms, out))
     pieces = scatter(terms.reshape(size // RUN, -1, 2 * RANK), planes)
-    hop = jnp.where(section == 2, far, near)
-    before = shift(hop, [([1, last], 0, 1, anywhere), ([2], 0, 1, not_run_end)])
-    after = shift(hop, [([1, last], 0, -1, anywhere), ([2], 0, -1, not_run_start)])
+    hop = jnp.where((section == 1) | (section == last), near, far)
+    before = shift(
+        hop,
+        [([1], 0, 1, anywhere), ([2, last], 0, 1, not_run_end), ([0], last, 2, before_run_end)],
+    )
+    after = shift(
+        hop,
+        [([1], 0, -1, anywhere), ([2, last], 0, -1, not_run_start), ([0], last, -2, after_run_start)],
+    )
     ends = shift(out, [([1], 1, 1, run_end), ([1], 1, -1, run_start)])
     pieces, _ = lax.optimization_barrier((pieces, handed_back))
     terms = jnp.sum(pieces.astype(F32), axis=0)

time: 212 us -> 146 us (0.69)
  the two profiles are of different devices: /device:TPU:136 before, /device:TPU:227 now
where the time goes in v12:
time: 146 us; the launch traced here: 143 us
  starting transfers between devices  53.9 us (37%)
  waiting for transfers between devices  42 us (29%)
  Pallas kernels  20 us (14%)
  local copies, waits for them, and re-layouts  19.9 us (14%)
  other arithmetic  6.39 us (4%)
    all_to_all x2, starting transfers between devices, scatter(): return lax.all_to_all(x, 'dp', 0, 0, axis_index_groups=groups, tiled=True)  28.6 us
    ppermute x12, starting transfers between devices, shift(): return lax.ppermute(x, AXES, route)  25.2 us
    all_to_all x2, waiting for transfers between devices, scatter(): return lax.all_to_all(x, 'dp', 0, 0, axis_index_groups=groups, tiled=True)  22.7 us
    ppermute x12, waiting for transfers between devices, shift(): return lax.ppermute(x, AXES, route)  19.3 us
    unnamed x49, local copies, waits for them, and re-layouts  16.8 us
    pallas_call x1, Pallas kernels, run_backward(): pl.pallas_call(backward_kernel, out_shape=(jax.ShapeDtypeStruct((TILE, QW...  6.06 us
    pallas_call x1, Pallas kernels, run_forward(): pl.pallas_call(forward_kernel, out_shape=jax.ShapeDtypeStruct((TILE, QW),...  5.54 us
    pallas_call x1, Pallas kernels, run_prepare(): pl.pallas_call(prepare_kernel, out_shape=(jax.ShapeDtypeStruct((QW, TILE)...  3.89 us
  transfers between devices with their start and end apart: 14, of which 3 were waited for; matrix products, arithmetic and copies ran while one was open for 4% of the time, Pallas kernels for 14%

profile of v12, /device:TPU:227, one launch (start us, length us, event | category | flops | bytes accessed | tf_op | source)
XLA Modules:
  0.0 143.1 jit_solution(2444306959760081821)
XLA Ops:
  0.7 3.1 %slice_bitcast_fusion = (bf16[128,4096]{1,0:T(8,128)(2,1)}, bf16[128,4096]{1,0:T(8,128)(2,1)}) fusion(bf16[1,384,4096]{2,1,0:T(8,128)(2,1)} %param.11), kind=kLoop, calls=%fused_computation.1 | loop fusion | bytes 4194304 | tf_op jit(solution)/shard_map/slice | solution.py:421
  3.8 1.8 %collective-permute-start = (bf16[128,4096]{1,0:T(8,128)(2,1)}, bf16[128,4096]{1,0:T(8,128)(2,1)}, u32[]{:S(2)}, u32[]{:S(2)}) collective-permute-start(bf16[128,4096]{1,0:T(8,128)(2,1)} %get-tuple-element.36), channel_id=1, source_target_pairs={{64,65},{65,66},{66,67},{67,68},{68,69},{69,70},{70,71},{71,72},{7... | collective-permute-start | bytes 3145736 | tf_op jit(solution)/shard_map/ppermute | solution.py:377
  5.6 1.6 %collective-permute-start.1 = (bf16[128,4096]{1,0:T(8,128)(2,1)}, bf16[128,4096]{1,0:T(8,128)(2,1)}, u32[]{:S(2)}, u32[]{:S(2)}) collective-permute-start(bf16[128,4096]{1,0:T(8,128)(2,1)} %get-tuple-element.37), channel_id=1, source_target_pairs={{65,64},{66,65},{67,66},{68,67},{69,68},{70,69},{71,70},{72,71},{7... | collective-permute-start | bytes 3145736 | tf_op jit(solution)/shard_map/ppermute | solution.py:377
  7.2 0.1 copy.15.lens_ref
  7.3 0.1 pad_add_fusion.rank_ref.place_ref
  7.4 1.0 copy-done.3
  8.4 1.0 copy-done.6
  9.5 1.3 copy-done.14
  10.8 5.5 %forward_tile.1 = bf16[128,4096]{1,0:T(8,128)(2,1)} custom-call(s32[3]{0:T(128)S(1)} %pad_add_fusion.rank_ref.place_ref, s32[2,64,8]{2,1,0:T(8,128)S(1)} %copy.15.lens_ref, s32[2,64]{1,0:T(2,128)S(1)} %copy-done.19, f32[102]{0:T(128)S(1)} %copy-done.21, bf16[128,5120]{1,0:T(8,128)(2,1)S(1)} %bitcast.30, bf16[64,4096]{1,0:T(8,128)(2,1)S(1)} %bitcast.23, ...), custom_call_target="tpu_custom_call" | custom-call | flops 1048576 | bytes 1048576 | tf_op jit(solution)/shard_map/forward_tile/pallas_call | solution.py:245
  16.3 1.3 collective-permute-start.2
  17.6 0.0 copy-start.1
  17.6 1.3 copy-done.1
  18.9 1.0 copy-done.4
  20.0 1.0 copy-done.7
  21.0 3.9 %prepare_tile.1 = (f32[4096,128]{1,0:T(8,128)S(1)}, bf16[128,4096]{1,0:T(8,128)(2,1)S(1)}, bf16[128,64]{1,0:T(8,128)(2,1)S(1)}, bf16[128,128]{1,0:T(8,128)(2,1)S...) custom-call(s32[3]{0:T(128)S(1)} %pad_add_fusion.rank_ref.place_ref, s32[2,64,8]{2,1,0:T(8,128)S(1)} %copy.15.lens_ref, ...), custom_call_target="tpu_custom_call" | custom-call | flops 1048576 | bytes 1048576 | tf_op jit(solution)/shard_map/prepare_tile/pallas_call | solution.py:259
  24.9 0.0 copy-start.2
  24.9 0.0 copy-start.5
  25.0 0.0 copy-start.8
  25.0 5.7 %collective-permute-start.3 = (bf16[128,4096]{1,0:T(8,128)(2,1)}, bf16[128,4096]{1,0:T(8,128)(2,1)S(1)}, u32[]{:S(2)}, u32[]{:S(2)}) collective-permute-start(bf16[128,4096]{1,0:T(8,128)(2,1)} %get-tuple-element.36), channel_id=1, source_target_pairs={{192,193},{193,194},{194,195},{195,196},{196,197},{197,198},{198,1... | collective-permute-start | bytes 3145736 | tf_op jit(solution)/shard_map/ppermute | solution.py:377
  30.7 1.9 %collective-permute-start.4 = (bf16[128,4096]{1,0:T(8,128)(2,1)}, bf16[128,4096]{1,0:T(8,128)(2,1)S(1)}, u32[]{:S(2)}, u32[]{:S(2)}) collective-permute-start(bf16[128,4096]{1,0:T(8,128)(2,1)} %get-tuple-element.37), channel_id=1, source_target_pairs={{193,192},{194,193},{195,194},{196,195},{197,196},{198,197},{199,1... | collective-permute-start | bytes 3145736 | tf_op jit(solution)/shard_map/ppermute | solution.py:377
  32.6 2.3 %broadcast_select_fusion = bf16[128,4096]{1,0:T(8,128)(2,1)} fusion(bf16[128,4096]{1,0:T(8,128)(2,1)} %collective-permute-done.2, bf16[128,4096]{1,0:T(8,128)(2,1)} %forward_tile.1, pred[]{:T(512)S(6)} %eq.8), kind=kLoop, calls=%fused_computation.3 | loop fusion | flops 524288 | bytes 3145729 | tf_op jit(solution)/shard_map/jit(_where)/select_n | solution.py:435
  34.9 2.3 %collective-permute-start.5 = (bf16[128,4096]{1,0:T(8,128)(2,1)}, bf16[128,4096]{1,0:T(8,128)(2,1)}, u32[]{:S(2)}, u32[]{:S(2)}) collective-permute-start(bf16[128,4096]{1,0:T(8,128)(2,1)} %broadcast_select_fusion), channel_id=1, source_target_pairs={{64,128},{65,129},{66,130},{67,131},{68,132},{69,133},{70,134},{71... | collective-permute-start | bytes 3145736 | tf_op jit(solution)/shard_map/ppermute | solution.py:377
  37.3 7.0 %collective-permute-done.3.last_left_ref = bf16[128,4096]{1,0:T(8,128)(2,1)S(1)} collective-permute-done((bf16[128,4096]{1,0:T(8,128)(2,1)}, bf16[128,4096]{1,0:T(8,128)(2,1)S(1)}, u32[]{:S(2)}, u32[]{:S(2)}) %collective-permute-start.3) | collective-permute-done | bytes 1048608 | tf_op jit(solution)/shard_map/ppermute | solution.py:377
  44.3 12.2 %collective-permute-done.4.last_right_ref = bf16[128,4096]{1,0:T(8,128)(2,1)S(1)} collective-permute-done((bf16[128,4096]{1,0:T(8,128)(2,1)}, bf16[128,4096]{1,0:T(8,128)(2,1)S(1)}, u32[]{:S(2)}, u32[]{:S(2)}) %collective-permute-start.4) | collective-permute-done | bytes 1048608 | tf_op jit(solution)/shard_map/ppermute | solution.py:377
  56.5 6.1 %backward_tile.1 = (bf16[128,5120]{1,0:T(8,128)(2,1)S(1)}, bf16[4096,128]{1,0:T(8,128)(2,1)S(1)}) custom-call(s32[3]{0:T(128)S(1)} %pad_add_fusion.rank_ref.place_ref, s32[2,64]{1,0:T(2,128)S(1)} %copy-done.19, s32[2,64]{1,0:T(2,128)S(1)} %copy-done.20, f32[102]{0:T(128)S(1)} %copy-done.21, bf16[128,5120]{1,0:T(8,128)(2,1)S(1)} %bitcast.22, ...), custom_call_target="tpu_custom_call" | custom-call | flops 1048576 | bytes 1048576 | tf_op jit(solution)/shard_map/backward_tile/pallas_call | solution.py:298
  62.6 1.0 copy-done.9
  63.6 1.1 copy-done.22
  64.7 0.7 collective-permute-start.6
  65.3 0.7 collective-permute-start.7
  66.0 2.4 %collective-permute-start.11 = (bf16[128,5120]{1,0:T(8,128)(2,1)}, bf16[128,5120]{1,0:T(8,128)(2,1)}, u32[]{:S(2)}, u32[]{:S(2)}) collective-permute-start(bf16[128,5120]{1,0:T(8,128)(2,1)} %copy-done.22), channel_id=1, source_target_pairs={{64,0},{65,1},{66,2},{67,3},{68,4},{69,5},{70,6},{71,7},{72,8},{73... | collective-permute-start | bytes 3932168 | tf_op jit(solution)/shard_map/ppermute | solution.py:377
  68.4 1.2 copy-done.10
  69.6 1.2 copy-done.13
  70.8 0.8 adapter_terms.1
  71.6 1.0 copy-done.11
  72.6 24.1 %all-to-all-start = ((bf16[16,256,128]{2,1,0:T(8,128)(2,1)}), bf16[16,256,128]{2,1,0:T(8,128)(2,1)}, u32[]{:S(2)}, u32[]{:S(2)}) async-start(bf16[16,256,128]{2,1,0:T(8,128)(2,1)} %bitcast.29), calls=%async_computation | async-start | bytes 2097152 | tf_op jit(solution)/shard_map/all_to_all | solution.py:409
  96.7 1.3 broadcast_select_fusion.1.hop_ref
  98.0 1.3 collective-permute-start.8
  99.3 4.0 %collective-permute-start.9 = (bf16[128,4096]{1,0:T(8,128)(2,1)S(1)}, bf16[128,4096]{1,0:T(8,128)(2,1)S(1)}, u32[]{:S(2)}, u32[]{:S(2)}) collective-permute-start(bf16[128,4096]{1,0:T(8,128)(2,1)S(1)} %broadcast_select_fusion.1.hop_ref), channel_id=1, source_target_pairs={{65,64},{66,65},{67,66},{68,67},{69,68},{70,69},{71,70},{72,71},{7... | collective-permute-start | bytes 3145736 | tf_op jit(solution)/shard_map/ppermute | solution.py:377
  103.3 1.6 %collective-permute-start.10 = (bf16[128,4096]{1,0:T(8,128)(2,1)}, bf16[128,4096]{1,0:T(8,128)(2,1)}, u32[]{:S(2)}, u32[]{:S(2)}) collective-permute-start(bf16[128,4096]{1,0:T(8,128)(2,1)} %forward_tile.1), channel_id=1, source_target_pairs={{67,132},{71,136},{75,140},{79,144},{83,148},{87,152},{91,156},{95... | collective-permute-start | bytes 3145736 | tf_op jit(solution)/shard_map/ppermute | solution.py:377
  105.0 22.7 %all-to-all-done = bf16[16,256,128]{2,1,0:T(8,128)(2,1)} async-done(((bf16[16,256,128]{2,1,0:T(8,128)(2,1)}), bf16[16,256,128]{2,1,0:T(8,128)(2,1)}, u32[]{:S(2)}, u32[]{:S(2)}) %all-to-all-start) | async-done | bytes 1048608 | tf_op jit(solution)/shard_map/all_to_all | solution.py:409
  127.7 2.0 %convert_reduce_fusion = f32[256,128]{1,0:T(8,128)} fusion(bf16[16,256,128]{2,1,0:T(8,128)(2,1)} %all-to-all-done), kind=kLoop, calls=%fused_computation | loop fusion | flops 1015808 | bytes 1179648 | tf_op jit(solution)/shard_map/reduce_sum | solution.py:466
  129.8 4.5 %all-to-all-start.1 = ((f32[4,64,128]{2,1,0:T(8,128)}), f32[4,64,128]{2,1,0:T(8,128)S(1)}, u32[]{:S(2)}, u32[]{:S(2)}) async-start(f32[4,64,128]{2,1,0:T(8,128)} %bitcast.14), calls=%async_computation.1 | async-start | bytes 262144 | tf_op jit(solution)/shard_map/all_to_all | solution.py:409
  134.3 1.0 copy-done.15
  135.3 1.0 copy-done.17
  136.2 1.2 copy-done.16
  137.5 1.2 copy-done.18
  138.7 3.8 %place_outputs.1 = (bf16[384,4096]{1,0:T(8,128)(2,1)}, bf16[128,5120]{1,0:T(8,128)(2,1)}) custom-call(s32[3]{0:T(128)S(1)} %pad_add_fusion.rank_ref.place_ref, s32[2,64]{1,0:T(2,128)S(1)} %copy-done.20, bf16[128,4096]{1,0:T(8,128)(2,1)S(1)} %copy-done.16, bf16[128,4096]{1,0:T(8,128)(2,1)S(1)} %broadcast_select_fusion.1.hop_ref, ...), custom_call_target="tpu_custom_call" | custom-call | flops 1048576 | bytes 1048576 | tf_op jit(solution)/shard_map/place_outputs/pallas_call | solution.py:350
  142.5 0.6 reduce_sum.19
  (40 shorter events, 0.1 us)
Async XLA Ops:
  0.6 6.6 %copy-start.23 = (s32[2,64,8]{1,2,0:T(8,128)S(1)}, s32[2,64,8]{1,2,0:T(8,128)}, u32[]{:S(2)}) copy-start(s32[2,64,8]{1,2,0:T(8,128)} %param.16) | copy-start | bytes 12292
  0.6 6.7 %copy-start.21 = (f32[102]{0:T(128)S(1)}, f32[102]{0:T(128)}, u32[]{:S(2)}) copy-start(f32[102]{0:T(128)} %table_ref.7) | copy-start | bytes 1228
  0.7 6.7 %copy-start.19 = (s32[2,64]{1,0:T(2,128)S(1)}, s32[2,64]{1,0:T(2,128)}, u32[]{:S(2)}) copy-start(s32[2,64]{1,0:T(2,128)} %langs_ref.7) | copy-start | bytes 1540
  0.7 16.9 %copy-start.20 = (s32[2,64]{1,0:T(2,128)S(1)}, s32[2,64]{1,0:T(2,128)}, u32[]{:S(2)}) copy-start(s32[2,64]{1,0:T(2,128)} %dest_ref.7) | copy-start | bytes 1540
  3.8 13.8 %copy-start = (bf16[1,384,4096]{2,1,0:T(8,128)(2,1)S(1)}, bf16[1,384,4096]{2,1,0:T(8,128)(2,1)}, u32[]{:S(2)}) copy-start(bf16[1,384,4096]{2,1,0:T(8,128)(2,1)} %param.11) | copy-start | bytes 9437188
  3.8 21.2 %collective-permute-start = (bf16[128,4096]{1,0:T(8,128)(2,1)}, bf16[128,4096]{1,0:T(8,128)(2,1)}, u32[]{:S(2)}, u32[]{:S(2)}) collective-permute-start(bf16[128,4096]{1,0:T(8,128)(2,1)} %get-tuple-element.36), channel_id=1, source_target_pairs={{64,65},{65,66},{66,67},{67,68},{68,69},{69,70},{70,71},{71,72},{7... | collective-permute-start | bytes 3145736 | tf_op jit(solution)/shard_map/ppermute | solution.py:377
  5.6 19.4 %collective-permute-start.1 = (bf16[128,4096]{1,0:T(8,128)(2,1)}, bf16[128,4096]{1,0:T(8,128)(2,1)}, u32[]{:S(2)}, u32[]{:S(2)}) collective-permute-start(bf16[128,4096]{1,0:T(8,128)(2,1)} %get-tuple-element.37), channel_id=1, source_target_pairs={{65,64},{66,65},{67,66},{68,67},{69,68},{70,69},{71,70},{72,71},{7... | collective-permute-start | bytes 3145736 | tf_op jit(solution)/shard_map/ppermute | solution.py:377
  7.4 1.1 copy-start.3
  8.4 1.0 copy-start.6
  9.5 1.3 copy-start.14
  16.3 8.7 %collective-permute-start.2 = (bf16[128,4096]{1,0:T(8,128)(2,1)}, bf16[128,4096]{1,0:T(8,128)(2,1)}, u32[]{:S(2)}, u32[]{:S(2)}) collective-permute-start(bf16[128,4096]{1,0:T(8,128)(2,1)} %forward_tile.1), channel_id=1, source_target_pairs={{0,64},{1,65},{2,66},{3,67},{4,68},{5,69},{6,70},{7,71},{8,72},{9,... | collective-permute-start | bytes 3145736 | tf_op jit(solution)/shard_map/ppermute | solution.py:377
  17.6 1.3 copy-start.1
  18.9 1.0 copy-start.4
  20.0 1.0 copy-start.7
  24.9 37.7 %copy-start.12 = (bf16[128,4096]{1,0:T(8,128)(2,1)}, bf16[128,4096]{1,0:T(8,128)(2,1)S(1)}, u32[]{:S(2)}) copy-start(bf16[128,4096]{1,0:T(8,128)(2,1)S(1)} %get-tuple-element.39.attn_ref) | copy-start | bytes 3145732
  24.9 31.6 %copy-start.2 = (bf16[1,128,5120]{2,1,0:T(8,128)(2,1)S(1)}, bf16[1,128,5120]{2,1,0:T(8,128)(2,1)}, u32[]{:S(2)}) copy-start(bf16[1,128,5120]{2,1,0:T(8,128)(2,1)} %param.10) | copy-start | bytes 3932164
  24.9 31.6 %copy-start.5 = (bf16[1,4096,64]{1,2,0:T(8,128)(2,1)S(1)}, bf16[1,4096,64]{1,2,0:T(8,128)(2,1)}, u32[]{:S(2)}) copy-start(bf16[1,4096,64]{1,2,0:T(8,128)(2,1)} %param.12) | copy-start | bytes 1572868
  25.0 31.6 %copy-start.8 = (bf16[1,64,4096]{2,1,0:T(8,128)(2,1)S(1)}, bf16[1,64,4096]{2,1,0:T(8,128)(2,1)}, u32[]{:S(2)}) copy-start(bf16[1,64,4096]{2,1,0:T(8,128)(2,1)} %param.13) | copy-start | bytes 1572868
  25.0 19.3 %collective-permute-start.3 = (bf16[128,4096]{1,0:T(8,128)(2,1)}, bf16[128,4096]{1,0:T(8,128)(2,1)S(1)}, u32[]{:S(2)}, u32[]{:S(2)}) collective-permute-start(bf16[128,4096]{1,0:T(8,128)(2,1)} %get-tuple-element.36), channel_id=1, source_target_pairs={{192,193},{193,194},{194,195},{195,196},{196,197},{197,198},{198,1... | collective-permute-start | bytes 3145736 | tf_op jit(solution)/shard_map/ppermute | solution.py:377
  30.7 25.8 %collective-permute-start.4 = (bf16[128,4096]{1,0:T(8,128)(2,1)}, bf16[128,4096]{1,0:T(8,128)(2,1)S(1)}, u32[]{:S(2)}, u32[]{:S(2)}) collective-permute-start(bf16[128,4096]{1,0:T(8,128)(2,1)} %get-tuple-element.37), channel_id=1, source_target_pairs={{193,192},{194,193},{195,194},{196,195},{197,196},{198,197},{199,1... | collective-permute-start | bytes 3145736 | tf_op jit(solution)/shard_map/ppermute | solution.py:377
  34.9 37.7 %collective-permute-start.5 = (bf16[128,4096]{1,0:T(8,128)(2,1)}, bf16[128,4096]{1,0:T(8,128)(2,1)}, u32[]{:S(2)}, u32[]{:S(2)}) collective-permute-start(bf16[128,4096]{1,0:T(8,128)(2,1)} %broadcast_select_fusion), channel_id=1, source_target_pairs={{64,128},{65,129},{66,130},{67,131},{68,132},{69,133},{70,134},{71... | collective-permute-start | bytes 3145736 | tf_op jit(solution)/shard_map/ppermute | solution.py:377
  62.6 1.0 copy-start.9
  63.6 1.1 copy-start.22
  64.7 3.7 %collective-permute-start.6 = (bf16[128,128]{1,0:T(8,128)(2,1)S(1)}, bf16[128,128]{1,0:T(8,128)(2,1)S(1)}, u32[]{:S(2)}, u32[]{:S(2)}) collective-permute-start(bf16[128,128]{1,0:T(8,128)(2,1)S(1)} %get-tuple-element.46), channel_id=1, source_target_pairs={{0,1},{1,2},{2,3},{3,4},{4,5},{5,6},{6,7},{7,8},{8,9},{9,10},{10,1... | collective-permute-start | bytes 98312 | tf_op jit(solution)/shard_map/ppermute | solution.py:377
  65.3 3.1 %collective-permute-start.7 = (bf16[128,128]{1,0:T(8,128)(2,1)S(1)}, bf16[128,128]{1,0:T(8,128)(2,1)S(1)}, u32[]{:S(2)}, u32[]{:S(2)}) collective-permute-start(bf16[128,128]{1,0:T(8,128)(2,1)S(1)} %get-tuple-element.48), channel_id=1, source_target_pairs={{1,0},{2,1},{3,2},{4,3},{5,4},{6,5},{7,6},{8,7},{9,8},{10,9},{11,1... | collective-permute-start | bytes 98312 | tf_op jit(solution)/shard_map/ppermute | solution.py:377
  66.0 61.7 %collective-permute-start.11 = (bf16[128,5120]{1,0:T(8,128)(2,1)}, bf16[128,5120]{1,0:T(8,128)(2,1)}, u32[]{:S(2)}, u32[]{:S(2)}) collective-permute-start(bf16[128,5120]{1,0:T(8,128)(2,1)} %copy-done.22), channel_id=1, source_target_pairs={{64,0},{65,1},{66,2},{67,3},{68,4},{69,5},{70,6},{71,7},{72,8},{73... | collective-permute-start | bytes 3932168 | tf_op jit(solution)/shard_map/ppermute | solution.py:377
  68.4 1.2 copy-start.10
  69.6 1.2 copy-start.13
  71.6 1.0 copy-start.11
  72.6 55.1 %all-to-all-start = ((bf16[16,256,128]{2,1,0:T(8,128)(2,1)}), bf16[16,256,128]{2,1,0:T(8,128)(2,1)}, u32[]{:S(2)}, u32[]{:S(2)}) async-start(bf16[16,256,128]{2,1,0:T(8,128)(2,1)} %bitcast.29), calls=%async_computation | async-start | bytes 2097152 | tf_op jit(solution)/shard_map/all_to_all | solution.py:409
  98.0 36.3 %collective-permute-start.8 = (bf16[128,4096]{1,0:T(8,128)(2,1)S(1)}, bf16[128,4096]{1,0:T(8,128)(2,1)S(1)}, u32[]{:S(2)}, u32[]{:S(2)}) collective-permute-start(bf16[128,4096]{1,0:T(8,128)(2,1)S(1)} %broadcast_select_fusion.1.hop_ref), channel_id=1, source_target_pairs={{64,65},{65,66},{66,67},{67,68},{68,69},{69,70},{70,71},{71,72},{7... | collective-permute-start | bytes 3145736 | tf_op jit(solution)/shard_map/ppermute | solution.py:377
  99.3 35.9 %collective-permute-start.9 = (bf16[128,4096]{1,0:T(8,128)(2,1)S(1)}, bf16[128,4096]{1,0:T(8,128)(2,1)S(1)}, u32[]{:S(2)}, u32[]{:S(2)}) collective-permute-start(bf16[128,4096]{1,0:T(8,128)(2,1)S(1)} %broadcast_select_fusion.1.hop_ref), channel_id=1, source_target_pairs={{65,64},{66,65},{67,66},{68,67},{69,68},{70,69},{71,70},{72,71},{7... | collective-permute-start | bytes 3145736 | tf_op jit(solution)/shard_map/ppermute | solution.py:377
  103.3 32.9 %collective-permute-start.10 = (bf16[128,4096]{1,0:T(8,128)(2,1)}, bf16[128,4096]{1,0:T(8,128)(2,1)}, u32[]{:S(2)}, u32[]{:S(2)}) collective-permute-start(bf16[128,4096]{1,0:T(8,128)(2,1)} %forward_tile.1), channel_id=1, source_target_pairs={{67,132},{71,136},{75,140},{79,144},{83,148},{87,152},{91,156},{95... | collective-permute-start | bytes 3145736 | tf_op jit(solution)/shard_map/ppermute | solution.py:377
  129.8 12.7 %all-to-all-start.1 = ((f32[4,64,128]{2,1,0:T(8,128)}), f32[4,64,128]{2,1,0:T(8,128)S(1)}, u32[]{:S(2)}, u32[]{:S(2)}) async-start(f32[4,64,128]{2,1,0:T(8,128)} %bitcast.14), calls=%async_computation.1 | async-start | bytes 262144 | tf_op jit(solution)/shard_map/all_to_all | solution.py:409
  134.3 1.0 copy-start.15
  135.3 1.0 copy-start.17
  136.2 1.2 copy-start.16
  137.5 1.2 copy-start.18

commit v13 on v11

--- a/solution.py
+++ b/solution.py
@@ -316,8 +316,8 @@
 
 
 def place_kernel(
-    place_ref, dest_ref, before_ref, hop_ref, after_ref, ends_ref, back_ref,
-    placed_ref, handed_ref, zero_ref, sems,
+    place_ref, dest_ref, before_ref, near_ref, after_ref, far_before_ref, far_ref, far_after_ref,
+    back_ref, placed_ref, handed_ref, zero_ref, sems,
 ):
     rank, section = place_ref[0], place_ref[1]
     tiles = dest_ref.shape[1]
@@ -325,17 +325,16 @@
     handed = pltpu.make_async_copy(back_ref, handed_ref, sems.at[0])
     handed.start()
     copies = []
-    for k, (near, edge) in enumerate(
-        ((before_ref, run_start(rank)), (hop_ref, False), (after_ref, run_end(rank)))
+    for k, (near, far) in enumerate(
+        ((before_ref, far_before_ref), (near_ref, far_ref), (after_ref, far_after_ref))
     ):
         tile = rank + (k - 1)
         held = jnp.clip(tile, 0, tiles - 1)
         live = (tile == held) & (dest_ref[0, held] == rank) & (section > 0)
-        crossed = (section == 2) & edge
         slot = placed_ref.at[pl.ds(k * TILE, TILE), :]
         for source, chosen in (
-            (near, live & jnp.logical_not(crossed)),
-            (ends_ref, live & crossed),
+            (near, live & (section != 2)),
+            (far, live & (section == 2)),
             (zero_ref, jnp.logical_not(live)),
         ):
             copies.append((pltpu.make_async_copy(source, slot, sems.at[k + 1]), chosen))
@@ -353,7 +352,7 @@
             jax.ShapeDtypeStruct((3 * TILE, QW), BF16),
             jax.ShapeDtypeStruct(tiles[-1].shape, BF16),
         ),
-        in_specs=[SMEM] * 2 + [ANY] * len(tiles),
+        in_specs=[SMEM] * 2 + [VMEM] * len(tiles),
         out_specs=(ANY, ANY),
         scratch_shapes=[pltpu.VMEM((TILE, QW), BF16), pltpu.SemaphoreType.DMA((4,))],
         compiler_params=pltpu.CompilerParams(vmem_limit_bytes=24 * 2**20),
@@ -416,6 +415,7 @@
     out = run_forward(place, lengths, languages, lang_scale, qkv_a[0], down, up)
     out, place = lax.optimization_barrier((out, place))
     near = shift(out, [([0, 2], 1, 0, anywhere)])
+    far = shift(out, [([1], 1, 0, anywhere)])
     probs, attn, low, to_left, own, to_right = run_prepare(
         place, lengths, languages, destination, lang_scale, qkv_b[0], slots, down, up
     )
@@ -423,7 +423,6 @@
     to_up, to_down, near, low = lax.optimization_barrier((to_up, to_down, near, low))
     last_left = shift(to_up, [([last], 0, 1, anywhere)])
     last_right = shift(to_down, [([last], 0, -1, anywhere)])
-    far = shift(out, [([1], 1, 0, anywhere)])
     grad_qkv, terms = run_backward(
         place, languages, destination, lang_scale, qkv_b[0],
         (from_left, from_right, last_left, last_right), slots, probs, attn, low, down, up,
@@ -432,6 +431,8 @@
         (grad_qkv, near, to_left, to_right)
     )
     handed_back = shift(grad_qkv, [(every, -1, 0, anywhere)])
+    before = shift(near, [([1, last], 0, 1, anywhere)])
+    after = shift(near, [([1, last], 0, -1, anywhere)])
     left = shift(to_right, [([0], 0, 1, anywhere)])
     right = shift(to_left, [([0], 0, -1, anywhere)])
     terms = run_terms(
@@ -439,17 +440,16 @@
     )
     planes = [[RUN * k + z for k in range(size // RUN)] for z in range(RUN)]
     columns = [[RUN * k + z for z in range(RUN)] for k in range(size // RUN)]
-    far, terms, out = lax.optimization_barrier((far, terms, out))
+    far, terms = lax.optimization_barrier((far, terms))
     pieces = scatter(terms.reshape(size // RUN, -1, 2 * RANK), planes)
-    hop = jnp.where(section == 2, far, near)
-    before = shift(hop, [([1, last], 0, 1, anywhere), ([2], 0, 1, not_run_end)])
-    after = shift(hop, [([1, last], 0, -1, anywhere), ([2], 0, -1, not_run_start)])
-    ends = shift(out, [([1], 1, 1, run_end), ([1], 1, -1, run_start)])
-    pieces, _ = lax.optimization_barrier((pieces, handed_back))
+    sent = jnp.where(section == 2, far, out)
+    far_before = shift(sent, [([1], 1, 1, run_end), ([2], 0, 1, not_run_end)])
+    far_after = shift(sent, [([1], 1, -1, run_start), ([2], 0, -1, not_run_start)])
+    pieces, _, before, after = lax.optimization_barrier((pieces, handed_back, before, after))
     terms = jnp.sum(pieces.astype(F32), axis=0)
     terms = jnp.sum(scatter(terms.reshape(RUN, -1, 2 * RANK), columns), axis=0)
     handed_forward, handed_back = run_place(
-        place, destination, before, hop, after, ends, handed_back
+        place, destination, before, near, after, far_before, far, far_after, handed_back
     )
     return (handed_forward[None], handed_back[None], terms[None])
 

time: 212 us -> 152 us (0.72)
  the two profiles are of different devices: /device:TPU:136 before, /device:TPU:227 now
where the time goes in v13:
time: 152 us; the launch traced here: 151 us
  starting transfers between devices  55.1 us (36%)
  waiting for transfers between devices  49.1 us (32%)
  local copies, waits for them, and re-layouts  21.1 us (14%)
  Pallas kernels  20.7 us (14%)
  other arithmetic  3.81 us (3%)
    all_to_all x2, starting transfers between devices, scatter(): return lax.all_to_all(x, 'dp', 0, 0, axis_index_groups=groups, tiled=True)  30.2 us
    ppermute x13, waiting for transfers between devices, shift(): return lax.ppermute(x, AXES, route)  26.1 us
    ppermute x13, starting transfers between devices, shift(): return lax.ppermute(x, AXES, route)  24.9 us
    all_to_all x2, waiting for transfers between devices, scatter(): return lax.all_to_all(x, 'dp', 0, 0, axis_index_groups=groups, tiled=True)  23 us
    unnamed x53, local copies, waits for them, and re-layouts  18 us
    pallas_call x1, Pallas kernels, run_backward(): pl.pallas_call(backward_kernel, out_shape=(jax.ShapeDtypeStruct((TILE, QW...  6.06 us
    pallas_call x1, Pallas kernels, run_forward(): pl.pallas_call(forward_kernel, out_shape=jax.ShapeDtypeStruct((TILE, QW),...  5.54 us
    pallas_call x1, Pallas kernels, run_place(): pl.pallas_call(place_kernel, out_shape=(jax.ShapeDtypeStruct((3 * TILE, Q...  4.4 us
  transfers between devices with their start and end apart: 15, of which 5 were waited for; matrix products, arithmetic and copies ran while one was open for 2% of the time, Pallas kernels for 14%

profile of v13, /device:TPU:227, one launch (start us, length us, event | category | flops | bytes accessed | tf_op | source)
XLA Modules:
  0.0 150.7 jit_solution(2380901097542611311)
XLA Ops:
  0.7 3.1 %slice_bitcast_fusion = (bf16[128,4096]{1,0:T(8,128)(2,1)}, bf16[128,4096]{1,0:T(8,128)(2,1)}) fusion(bf16[1,384,4096]{2,1,0:T(8,128)(2,1)} %param.11), kind=kLoop, calls=%fused_computation.1 | loop fusion | bytes 4194304 | tf_op jit(solution)/shard_map/slice | solution.py:412
  3.8 1.8 %collective-permute-start.2 = (bf16[128,4096]{1,0:T(8,128)(2,1)}, bf16[128,4096]{1,0:T(8,128)(2,1)}, u32[]{:S(2)}, u32[]{:S(2)}) collective-permute-start(bf16[128,4096]{1,0:T(8,128)(2,1)} %get-tuple-element.39), channel_id=1, source_target_pairs={{65,64},{66,65},{67,66},{68,67},{69,68},{70,69},{71,70},{72,71},{7... | collective-permute-start | bytes 3145736 | tf_op jit(solution)/shard_map/ppermute | solution.py:376
  5.6 1.6 %collective-permute-start.1 = (bf16[128,4096]{1,0:T(8,128)(2,1)}, bf16[128,4096]{1,0:T(8,128)(2,1)}, u32[]{:S(2)}, u32[]{:S(2)}) collective-permute-start(bf16[128,4096]{1,0:T(8,128)(2,1)} %get-tuple-element.38), channel_id=1, source_target_pairs={{64,65},{65,66},{66,67},{67,68},{68,69},{69,70},{70,71},{71,72},{7... | collective-permute-start | bytes 3145736 | tf_op jit(solution)/shard_map/ppermute | solution.py:376
  7.2 0.1 copy.15.lens_ref
  7.3 0.1 pad_add_fusion.rank_ref.place_ref
  7.4 1.0 copy-done.3
  8.4 1.0 copy-done.6
  9.5 1.3 copy-done.14
  10.8 5.5 %forward_tile.1 = bf16[128,4096]{1,0:T(8,128)(2,1)} custom-call(s32[3]{0:T(128)S(1)} %pad_add_fusion.rank_ref.place_ref, s32[2,64,8]{2,1,0:T(8,128)S(1)} %copy.15.lens_ref, s32[2,64]{1,0:T(2,128)S(1)} %copy-done.21, f32[102]{0:T(128)S(1)} %copy-done.23, bf16[128,5120]{1,0:T(8,128)(2,1)S(1)} %bitcast.30, bf16[64,4096]{1,0:T(8,128)(2,1)S(1)} %bitcast.23, ...), custom_call_target="tpu_custom_call" | custom-call | flops 1048576 | bytes 1048576 | tf_op jit(solution)/shard_map/forward_tile/pallas_call | solution.py:245
  16.3 1.3 collective-permute-start.3
  17.6 0.0 copy-start.1
  17.6 1.3 copy-done.1
  19.0 1.0 copy-done.4
  20.0 1.0 copy-done.7
  21.0 3.9 %prepare_tile.1 = (f32[4096,128]{1,0:T(8,128)S(1)}, bf16[128,4096]{1,0:T(8,128)(2,1)S(1)}, bf16[128,64]{1,0:T(8,128)(2,1)S(1)}, bf16[128,128]{1,0:T(8,128)(2,1)S...) custom-call(s32[3]{0:T(128)S(1)} %pad_add_fusion.rank_ref.place_ref, s32[2,64,8]{2,1,0:T(8,128)S(1)} %copy.15.lens_ref, ...), custom_call_target="tpu_custom_call" | custom-call | flops 1048576 | bytes 1048576 | tf_op jit(solution)/shard_map/prepare_tile/pallas_call | solution.py:259
  25.0 1.1 collective-permute-done.3.near_ref
  26.0 3.5 %collective-permute-start.4 = (bf16[128,4096]{1,0:T(8,128)(2,1)}, bf16[128,4096]{1,0:T(8,128)(2,1)S(1)}, u32[]{:S(2)}, u32[]{:S(2)}) collective-permute-start(bf16[128,4096]{1,0:T(8,128)(2,1)} %get-tuple-element.38), channel_id=1, source_target_pairs={{192,193},{193,194},{194,195},{195,196},{196,197},{197,198},{198,1... | collective-permute-start | bytes 3145736 | tf_op jit(solution)/shard_map/ppermute | solution.py:376
  29.5 1.9 %collective-permute-start.5 = (bf16[128,4096]{1,0:T(8,128)(2,1)}, bf16[128,4096]{1,0:T(8,128)(2,1)S(1)}, u32[]{:S(2)}, u32[]{:S(2)}) collective-permute-start(bf16[128,4096]{1,0:T(8,128)(2,1)} %get-tuple-element.39), channel_id=1, source_target_pairs={{193,192},{194,193},{195,194},{196,195},{197,196},{198,197},{199,1... | collective-permute-start | bytes 3145736 | tf_op jit(solution)/shard_map/ppermute | solution.py:376
  31.5 1.6 %collective-permute-start = (bf16[128,4096]{1,0:T(8,128)(2,1)}, bf16[128,4096]{1,0:T(8,128)(2,1)}, u32[]{:S(2)}, u32[]{:S(2)}) collective-permute-start(bf16[128,4096]{1,0:T(8,128)(2,1)} %forward_tile.1), channel_id=1, source_target_pairs={{64,128},{65,129},{66,130},{67,131},{68,132},{69,133},{70,134},{71... | collective-permute-start | bytes 3145736 | tf_op jit(solution)/shard_map/ppermute | solution.py:376
  33.1 13.2 %collective-permute-done.4.last_left_ref = bf16[128,4096]{1,0:T(8,128)(2,1)S(1)} collective-permute-done((bf16[128,4096]{1,0:T(8,128)(2,1)}, bf16[128,4096]{1,0:T(8,128)(2,1)S(1)}, u32[]{:S(2)}, u32[]{:S(2)}) %collective-permute-start.4) | collective-permute-done | bytes 1048608 | tf_op jit(solution)/shard_map/ppermute | solution.py:376
  46.3 11.5 %collective-permute-done.5.last_right_ref = bf16[128,4096]{1,0:T(8,128)(2,1)S(1)} collective-permute-done((bf16[128,4096]{1,0:T(8,128)(2,1)}, bf16[128,4096]{1,0:T(8,128)(2,1)S(1)}, u32[]{:S(2)}, u32[]{:S(2)}) %collective-permute-start.5) | collective-permute-done | bytes 1048608 | tf_op jit(solution)/shard_map/ppermute | solution.py:376
  57.9 6.1 %backward_tile.1 = (bf16[128,5120]{1,0:T(8,128)(2,1)S(1)}, bf16[4096,128]{1,0:T(8,128)(2,1)S(1)}) custom-call(s32[3]{0:T(128)S(1)} %pad_add_fusion.rank_ref.place_ref, s32[2,64]{1,0:T(2,128)S(1)} %copy-done.21, s32[2,64]{1,0:T(2,128)S(1)} %copy-done.22, f32[102]{0:T(128)S(1)} %copy-done.23, bf16[128,5120]{1,0:T(8,128)(2,1)S(1)} %bitcast.22, ...), custom_call_target="tpu_custom_call" | custom-call | flops 1048576 | bytes 1048576 | tf_op jit(solution)/shard_map/backward_tile/pallas_call | solution.py:298
  64.0 1.0 copy-done.9
  65.0 1.1 copy-done.24
  66.0 0.7 collective-permute-start.6
  66.7 0.7 collective-permute-start.7
  67.3 1.9 %collective-permute-start.10 = (bf16[128,4096]{1,0:T(8,128)(2,1)}, bf16[128,4096]{1,0:T(8,128)(2,1)}, u32[]{:S(2)}, u32[]{:S(2)}) collective-permute-start(bf16[128,4096]{1,0:T(8,128)(2,1)} %copy-done.15), channel_id=1, source_target_pairs={{65,64},{66,65},{67,66},{68,67},{69,68},{70,69},{71,70},{72,71},{7... | collective-permute-start | bytes 3145736 | tf_op jit(solution)/shard_map/ppermute | solution.py:376
  69.3 6.1 %collective-permute-start.9 = (bf16[128,4096]{1,0:T(8,128)(2,1)}, bf16[128,4096]{1,0:T(8,128)(2,1)}, u32[]{:S(2)}, u32[]{:S(2)}) collective-permute-start(bf16[128,4096]{1,0:T(8,128)(2,1)} %copy-done.15), channel_id=1, source_target_pairs={{64,65},{65,66},{66,67},{67,68},{68,69},{69,70},{70,71},{71,72},{7... | collective-permute-start | bytes 3145736 | tf_op jit(solution)/shard_map/ppermute | solution.py:376
  75.3 2.4 %collective-permute-start.8 = (bf16[128,5120]{1,0:T(8,128)(2,1)}, bf16[128,5120]{1,0:T(8,128)(2,1)}, u32[]{:S(2)}, u32[]{:S(2)}) collective-permute-start(bf16[128,5120]{1,0:T(8,128)(2,1)} %copy-done.24), channel_id=1, source_target_pairs={{64,0},{65,1},{66,2},{67,3},{68,4},{69,5},{70,6},{71,7},{72,8},{73... | collective-permute-start | bytes 3932168 | tf_op jit(solution)/shard_map/ppermute | solution.py:376
  77.7 1.2 copy-done.10
  79.0 1.2 copy-done.13
  80.2 0.8 adapter_terms.1
  81.0 1.0 copy-done.11
  82.0 11.2 %all-to-all-start = ((bf16[16,256,128]{2,1,0:T(8,128)(2,1)}), bf16[16,256,128]{2,1,0:T(8,128)(2,1)S(1)}, u32[]{:S(2)}, u32[]{:S(2)}) async-start(bf16[16,256,128]{2,1,0:T(8,128)(2,1)} %bitcast.29), calls=%async_computation | async-start | bytes 2097152 | tf_op jit(solution)/shard_map/all_to_all | solution.py:400
  93.2 2.3 %broadcast_select_fusion = bf16[128,4096]{1,0:T(8,128)(2,1)} fusion(bf16[128,4096]{1,0:T(8,128)(2,1)} %collective-permute-done.far_ref, bf16[128,4096]{1,0:T(8,128)(2,1)} %forward_tile.1, pred[]{:T(512)S(6)} %eq.3), kind=kLoop, calls=%fused_computation.3 | loop fusion | flops 524288 | bytes 3145729 | tf_op jit(solution)/shard_map/jit(_where)/select_n | solution.py:445
  95.5 0.7 collective-permute-start.12
  96.2 0.7 collective-permute-start.11
  97.0 23.0 %all-to-all-done = bf16[16,256,128]{2,1,0:T(8,128)(2,1)S(1)} async-done(((bf16[16,256,128]{2,1,0:T(8,128)(2,1)}), bf16[16,256,128]{2,1,0:T(8,128)(2,1)S(1)}, u32[]{:S(2)}, u32[]{:S(2)}) %all-to-all-start) | async-done | bytes 1048608 | tf_op jit(solution)/shard_map/all_to_all | solution.py:400
  120.0 0.2 collective-permute-done.9.before_ref
  120.2 0.8 convert_reduce_fusion
  121.0 19.0 %all-to-all-start.1 = ((f32[4,64,128]{2,1,0:T(8,128)}), f32[4,64,128]{2,1,0:T(8,128)S(1)}, u32[]{:S(2)}, u32[]{:S(2)}) async-start(f32[4,64,128]{2,1,0:T(8,128)} %bitcast.14), calls=%async_computation.1 | async-start | bytes 262144 | tf_op jit(solution)/shard_map/all_to_all | solution.py:400
  140.0 1.0 copy-done.17
  141.0 1.0 copy-done.19
  142.0 1.2 copy-done.16
  143.2 1.2 copy-done.18
  144.4 1.2 copy-done.20
  145.7 4.4 %place_outputs.1 = (bf16[384,4096]{1,0:T(8,128)(2,1)}, bf16[128,5120]{1,0:T(8,128)(2,1)}) custom-call(s32[3]{0:T(128)S(1)} %pad_add_fusion.rank_ref.place_ref, s32[2,64]{1,0:T(2,128)S(1)} %copy-done.22, bf16[128,4096]{1,0:T(8,128)(2,1)} %collective-permute-done.9.before_ref, bf16[128,4096]{1,0:T(8,128)(2,1)S(1)} %copy-done.16, ...), custom_call_target="tpu_custom_call" | custom-call | flops 1048576 | bytes 1048576 | tf_op jit(solution)/shard_map/place_outputs/pallas_call | solution.py:349
  150.1 0.6 reduce_sum.19
  (45 shorter events, 0.1 us)
Async XLA Ops:
  0.6 6.6 %copy-start.25 = (s32[2,64,8]{1,2,0:T(8,128)S(1)}, s32[2,64,8]{1,2,0:T(8,128)}, u32[]{:S(2)}) copy-start(s32[2,64,8]{1,2,0:T(8,128)} %param.16) | copy-start | bytes 12292
  0.6 6.7 %copy-start.21 = (s32[2,64]{1,0:T(2,128)S(1)}, s32[2,64]{1,0:T(2,128)}, u32[]{:S(2)}) copy-start(s32[2,64]{1,0:T(2,128)} %langs_ref.7) | copy-start | bytes 1540
  0.7 6.7 %copy-start.23 = (f32[102]{0:T(128)S(1)}, f32[102]{0:T(128)}, u32[]{:S(2)}) copy-start(f32[102]{0:T(128)} %table_ref.7) | copy-start | bytes 1228
  0.7 17.0 %copy-start.22 = (s32[2,64]{1,0:T(2,128)S(1)}, s32[2,64]{1,0:T(2,128)}, u32[]{:S(2)}) copy-start(s32[2,64]{1,0:T(2,128)} %dest_ref.7) | copy-start | bytes 1540
  3.8 13.8 %copy-start = (bf16[1,384,4096]{2,1,0:T(8,128)(2,1)S(1)}, bf16[1,384,4096]{2,1,0:T(8,128)(2,1)}, u32[]{:S(2)}) copy-start(bf16[1,384,4096]{2,1,0:T(8,128)(2,1)} %param.11) | copy-start | bytes 9437188
  3.8 21.2 %collective-permute-start.2 = (bf16[128,4096]{1,0:T(8,128)(2,1)}, bf16[128,4096]{1,0:T(8,128)(2,1)}, u32[]{:S(2)}, u32[]{:S(2)}) collective-permute-start(bf16[128,4096]{1,0:T(8,128)(2,1)} %get-tuple-element.39), channel_id=1, source_target_pairs={{65,64},{66,65},{67,66},{68,67},{69,68},{70,69},{71,70},{72,71},{7... | collective-permute-start | bytes 3145736 | tf_op jit(solution)/shard_map/ppermute | solution.py:376
  5.6 19.4 %collective-permute-start.1 = (bf16[128,4096]{1,0:T(8,128)(2,1)}, bf16[128,4096]{1,0:T(8,128)(2,1)}, u32[]{:S(2)}, u32[]{:S(2)}) collective-permute-start(bf16[128,4096]{1,0:T(8,128)(2,1)} %get-tuple-element.38), channel_id=1, source_target_pairs={{64,65},{65,66},{66,67},{67,68},{68,69},{69,70},{70,71},{71,72},{7... | collective-permute-start | bytes 3145736 | tf_op jit(solution)/shard_map/ppermute | solution.py:376
  7.4 1.0 copy-start.3
  8.4 1.0 copy-start.6
  9.5 1.3 copy-start.14
  16.3 9.7 %collective-permute-start.3 = (bf16[128,4096]{1,0:T(8,128)(2,1)}, bf16[128,4096]{1,0:T(8,128)(2,1)S(1)}, u32[]{:S(2)}, u32[]{:S(2)}) collective-permute-start(bf16[128,4096]{1,0:T(8,128)(2,1)} %forward_tile.1), channel_id=1, source_target_pairs={{0,64},{1,65},{2,66},{3,67},{4,68},{5,69},{6,70},{7,71},{8,72},{9,... | collective-permute-start | bytes 3145736 | tf_op jit(solution)/shard_map/ppermute | solution.py:376
  17.6 1.3 copy-start.1
  18.9 1.0 copy-start.4
  20.0 1.0 copy-start.7
  21.0 36.8 %copy-start.2 = (bf16[1,128,5120]{2,1,0:T(8,128)(2,1)S(1)}, bf16[1,128,5120]{2,1,0:T(8,128)(2,1)}, u32[]{:S(2)}) copy-start(bf16[1,128,5120]{2,1,0:T(8,128)(2,1)} %param.10) | copy-start | bytes 3932164
  21.0 36.8 %copy-start.5 = (bf16[1,4096,64]{1,2,0:T(8,128)(2,1)S(1)}, bf16[1,4096,64]{1,2,0:T(8,128)(2,1)}, u32[]{:S(2)}) copy-start(bf16[1,4096,64]{1,2,0:T(8,128)(2,1)} %param.12) | copy-start | bytes 1572868
  21.0 36.9 %copy-start.8 = (bf16[1,64,4096]{2,1,0:T(8,128)(2,1)S(1)}, bf16[1,64,4096]{2,1,0:T(8,128)(2,1)}, u32[]{:S(2)}) copy-start(bf16[1,64,4096]{2,1,0:T(8,128)(2,1)} %param.13) | copy-start | bytes 1572868
  24.9 39.0 %copy-start.12 = (bf16[128,4096]{1,0:T(8,128)(2,1)}, bf16[128,4096]{1,0:T(8,128)(2,1)S(1)}, u32[]{:S(2)}) copy-start(bf16[128,4096]{1,0:T(8,128)(2,1)S(1)} %get-tuple-element.33.attn_ref) | copy-start | bytes 3145732
  26.0 31.8 %copy-start.15 = (bf16[128,4096]{1,0:T(8,128)(2,1)}, bf16[128,4096]{1,0:T(8,128)(2,1)S(1)}, u32[]{:S(2)}) copy-start(bf16[128,4096]{1,0:T(8,128)(2,1)S(1)} %collective-permute-done.3.near_ref) | copy-start | bytes 3145732
  26.0 20.3 %collective-permute-start.4 = (bf16[128,4096]{1,0:T(8,128)(2,1)}, bf16[128,4096]{1,0:T(8,128)(2,1)S(1)}, u32[]{:S(2)}, u32[]{:S(2)}) collective-permute-start(bf16[128,4096]{1,0:T(8,128)(2,1)} %get-tuple-element.38), channel_id=1, source_target_pairs={{192,193},{193,194},{194,195},{195,196},{196,197},{197,198},{198,1... | collective-permute-start | bytes 3145736 | tf_op jit(solution)/shard_map/ppermute | solution.py:376
  29.5 28.3 %collective-permute-start.5 = (bf16[128,4096]{1,0:T(8,128)(2,1)}, bf16[128,4096]{1,0:T(8,128)(2,1)S(1)}, u32[]{:S(2)}, u32[]{:S(2)}) collective-permute-start(bf16[128,4096]{1,0:T(8,128)(2,1)} %get-tuple-element.39), channel_id=1, source_target_pairs={{193,192},{194,193},{195,194},{196,195},{197,196},{198,197},{199,1... | collective-permute-start | bytes 3145736 | tf_op jit(solution)/shard_map/ppermute | solution.py:376
  31.5 50.5 %collective-permute-start = (bf16[128,4096]{1,0:T(8,128)(2,1)}, bf16[128,4096]{1,0:T(8,128)(2,1)}, u32[]{:S(2)}, u32[]{:S(2)}) collective-permute-start(bf16[128,4096]{1,0:T(8,128)(2,1)} %forward_tile.1), channel_id=1, source_target_pairs={{64,128},{65,129},{66,130},{67,131},{68,132},{69,133},{70,134},{71... | collective-permute-start | bytes 3145736 | tf_op jit(solution)/shard_map/ppermute | solution.py:376
  64.0 1.0 copy-start.9
  64.9 1.1 copy-start.24
  66.0 9.3 %collective-permute-start.6 = (bf16[128,128]{1,0:T(8,128)(2,1)S(1)}, bf16[128,128]{1,0:T(8,128)(2,1)S(1)}, u32[]{:S(2)}, u32[]{:S(2)}) collective-permute-start(bf16[128,128]{1,0:T(8,128)(2,1)S(1)} %get-tuple-element.46), channel_id=1, source_target_pairs={{0,1},{1,2},{2,3},{3,4},{4,5},{5,6},{6,7},{7,8},{8,9},{9,10},{10,1... | collective-permute-start | bytes 98312 | tf_op jit(solution)/shard_map/ppermute | solution.py:376
  66.7 11.1 %collective-permute-start.7 = (bf16[128,128]{1,0:T(8,128)(2,1)S(1)}, bf16[128,128]{1,0:T(8,128)(2,1)S(1)}, u32[]{:S(2)}, u32[]{:S(2)}) collective-permute-start(bf16[128,128]{1,0:T(8,128)(2,1)S(1)} %get-tuple-element.48), channel_id=1, source_target_pairs={{1,0},{2,1},{3,2},{4,3},{5,4},{6,5},{7,6},{8,7},{9,8},{10,9},{11,1... | collective-permute-start | bytes 98312 | tf_op jit(solution)/shard_map/ppermute | solution.py:376
  67.3 52.6 %collective-permute-start.10 = (bf16[128,4096]{1,0:T(8,128)(2,1)}, bf16[128,4096]{1,0:T(8,128)(2,1)}, u32[]{:S(2)}, u32[]{:S(2)}) collective-permute-start(bf16[128,4096]{1,0:T(8,128)(2,1)} %copy-done.15), channel_id=1, source_target_pairs={{65,64},{66,65},{67,66},{68,67},{69,68},{70,69},{71,70},{72,71},{7... | collective-permute-start | bytes 3145736 | tf_op jit(solution)/shard_map/ppermute | solution.py:376
  69.3 50.9 %collective-permute-start.9 = (bf16[128,4096]{1,0:T(8,128)(2,1)}, bf16[128,4096]{1,0:T(8,128)(2,1)}, u32[]{:S(2)}, u32[]{:S(2)}) collective-permute-start(bf16[128,4096]{1,0:T(8,128)(2,1)} %copy-done.15), channel_id=1, source_target_pairs={{64,65},{65,66},{66,67},{67,68},{68,69},{69,70},{70,71},{71,72},{7... | collective-permute-start | bytes 3145736 | tf_op jit(solution)/shard_map/ppermute | solution.py:376
  75.3 44.9 %collective-permute-start.8 = (bf16[128,5120]{1,0:T(8,128)(2,1)}, bf16[128,5120]{1,0:T(8,128)(2,1)}, u32[]{:S(2)}, u32[]{:S(2)}) collective-permute-start(bf16[128,5120]{1,0:T(8,128)(2,1)} %copy-done.24), channel_id=1, source_target_pairs={{64,0},{65,1},{66,2},{67,3},{68,4},{69,5},{70,6},{71,7},{72,8},{73... | collective-permute-start | bytes 3932168 | tf_op jit(solution)/shard_map/ppermute | solution.py:376
  77.7 1.2 copy-start.10
  79.0 1.2 copy-start.13
  81.0 1.0 copy-start.11
  82.0 38.0 %all-to-all-start = ((bf16[16,256,128]{2,1,0:T(8,128)(2,1)}), bf16[16,256,128]{2,1,0:T(8,128)(2,1)S(1)}, u32[]{:S(2)}, u32[]{:S(2)}) async-start(bf16[16,256,128]{2,1,0:T(8,128)(2,1)} %bitcast.29), calls=%async_computation | async-start | bytes 2097152 | tf_op jit(solution)/shard_map/all_to_all | solution.py:400
  95.5 44.5 %collective-permute-start.12 = (bf16[128,4096]{1,0:T(8,128)(2,1)}, bf16[128,4096]{1,0:T(8,128)(2,1)S(1)}, u32[]{:S(2)}, u32[]{:S(2)}) collective-permute-start(bf16[128,4096]{1,0:T(8,128)(2,1)} %broadcast_select_fusion), channel_id=1, source_target_pairs={{68,131},{72,135},{76,139},{80,143},{84,147},{88,151},{92,155},{96... | collective-permute-start | bytes 3145736 | tf_op jit(solution)/shard_map/ppermute | solution.py:376
  96.2 44.8 %collective-permute-start.11 = (bf16[128,4096]{1,0:T(8,128)(2,1)}, bf16[128,4096]{1,0:T(8,128)(2,1)S(1)}, u32[]{:S(2)}, u32[]{:S(2)}) collective-permute-start(bf16[128,4096]{1,0:T(8,128)(2,1)} %broadcast_select_fusion), channel_id=1, source_target_pairs={{67,132},{71,136},{75,140},{79,144},{83,148},{87,152},{91,156},{95... | collective-permute-start | bytes 3145736 | tf_op jit(solution)/shard_map/ppermute | solution.py:376
  121.0 29.1 %all-to-all-start.1 = ((f32[4,64,128]{2,1,0:T(8,128)}), f32[4,64,128]{2,1,0:T(8,128)S(1)}, u32[]{:S(2)}, u32[]{:S(2)}) async-start(f32[4,64,128]{2,1,0:T(8,128)} %bitcast.14), calls=%async_computation.1 | async-start | bytes 262144 | tf_op jit(solution)/shard_map/all_to_all | solution.py:400
  140.0 1.0 copy-start.17
  141.0 1.0 copy-start.19
  142.0 1.2 copy-start.16
  143.2 1.2 copy-start.18
  144.4 1.2 copy-start.20

commit v14 on v8

--- a/solution.py
+++ b/solution.py
@@ -300,8 +300,8 @@
 
 
 def place_kernel(
-    place_ref, dest_ref, before_ref, hop_ref, after_ref, ends_ref, back_ref,
-    placed_ref, handed_ref, zero_ref, sems,
+    place_ref, dest_ref, before_ref, near_ref, after_ref, far_before_ref, far_ref, far_after_ref,
+    back_ref, placed_ref, handed_ref, zero_ref, sems,
 ):
     rank, section = place_ref[0], place_ref[1]
     tiles = dest_ref.shape[1]
@@ -309,21 +309,19 @@
     handed = pltpu.make_async_copy(back_ref, handed_ref, sems.at[0])
     handed.start()
     copies = []
-    for k, (near_ref, edge) in enumerate(
-        ((before_ref, run_start(rank)), (hop_ref, False), (after_ref, run_end(rank)))
+    for k, (near, far) in enumerate(
+        ((before_ref, far_before_ref), (near_ref, far_ref), (after_ref, far_after_ref))
     ):
         tile = rank + (k - 1)
         held = jnp.clip(tile, 0, tiles - 1)
         live = (tile == held) & (dest_ref[0, held] == rank) & (section > 0)
-        crossed = (section == 2) & edge
         slot = placed_ref.at[pl.ds(k * TILE, TILE), :]
         for source, chosen in (
-            (near_ref, live & jnp.logical_not(crossed)),
-            (ends_ref, live & crossed),
+            (near, live & (section != 2)),
+            (far, live & (section == 2)),
             (zero_ref, jnp.logical_not(live)),
         ):
-            copy = pltpu.make_async_copy(source, slot, sems.at[k + 1])
-            copies.append((copy, chosen))
+            copies.append((pltpu.make_async_copy(source, slot, sems.at[k + 1]), chosen))
     for copy, chosen in copies:
         pl.when(chosen)(copy.start)
     for copy, chosen in copies:
@@ -331,21 +329,20 @@
     handed.wait()
 
 
-def run_place(place, dest, before, hop, after, ends, back):
-    hbm = pl.BlockSpec(memory_space=pl.ANY)
+def run_place(place, dest, *tiles):
     return pl.pallas_call(
         place_kernel,
         out_shape=(
             jax.ShapeDtypeStruct((3 * TILE, QW), BF16),
-            jax.ShapeDtypeStruct(back.shape, BF16),
+            jax.ShapeDtypeStruct(tiles[-1].shape, BF16),
         ),
-        in_specs=[SMEM] * 2 + [VMEM] * 5,
-        out_specs=(hbm, hbm),
+        in_specs=[SMEM] * 2 + [VMEM] * len(tiles),
+        out_specs=(pl.BlockSpec(memory_space=pl.ANY),) * 2,
         scratch_shapes=[pltpu.VMEM((TILE, QW), BF16), pltpu.SemaphoreType.DMA((4,))],
         compiler_params=pltpu.CompilerParams(vmem_limit_bytes=24 * 2**20),
         cost_estimate=COST,
         name="place_outputs",
-    )(place, dest, before, hop, after, ends, back)
+    )(place, dest, *tiles)
 
 
 def sections():
@@ -401,25 +398,25 @@
     from_right = shift(to_down, [(early, 0, -1, anywhere)])
     out = run_forward(place, lengths, languages, lang_scale, qkv_a[0], down, up)
     out, place = lax.optimization_barrier((out, place))
-    hop = shift(out, [(every, 1, 0, anywhere)])
+    near = shift(out, [([0, 2], 1, 0, anywhere)])
+    far = shift(out, [([1], 1, 0, anywhere)])
     probs, attn, low, to_left, own, to_right = run_prepare(
         place, lengths, languages, destination, lang_scale, qkv_b[0], slots, down, up
     )
     from_left, from_right, low = lax.optimization_barrier((from_left, from_right, low))
-    to_up, to_down, hop, low = lax.optimization_barrier((to_up, to_down, hop, low))
+    to_up, to_down, near, low = lax.optimization_barrier((to_up, to_down, near, low))
     last_left = shift(to_up, [([last], 0, 1, anywhere)])
     last_right = shift(to_down, [([last], 0, -1, anywhere)])
     grad_qkv, scaled, back = run_backward(
         place, languages, destination, lang_scale, qkv_b[0],
         (from_left, from_right, last_left, last_right), slots, probs, down, up,
     )
-    grad_qkv, hop, to_left, to_right, out = lax.optimization_barrier(
-        (grad_qkv, hop, to_left, to_right, out)
-    )
-    handed_back = shift(grad_qkv, [(every, -1, 0, anywhere)])
-    ends = shift(out, [([1], 1, 1, run_end), ([1], 1, -1, run_start)])
-    before = shift(hop, [([1, 3], 0, 1, anywhere), ([2], 0, 1, not_run_end)])
-    after = shift(hop, [([1, 3], 0, -1, anywhere), ([2], 0, -1, not_run_start)])
+    grad_qkv, near, to_left, to_right = lax.optimization_barrier(
+        (grad_qkv, near, to_left, to_right)
+    )
+    handed_back = shift(grad_qkv, [(every, -1, 0, anywhere)])[None]
+    before = shift(near, [([1, 3], 0, 1, anywhere)])
+    after = shift(near, [([1, 3], 0, -1, anywhere)])
     left = shift(to_right, [([0], 0, 1, anywhere)])
     right = shift(to_left, [([0], 0, -1, anywhere)])
     terms = run_terms(
@@ -427,12 +424,19 @@
     )
     planes = [[RUN * k + z for k in range(size // RUN)] for z in range(RUN)]
     columns = [[RUN * k + z for z in range(RUN)] for k in range(size // RUN)]
+    far, terms = lax.optimization_barrier((far, terms))
     pieces = scatter(terms.reshape(size // RUN, -1, 2 * RANK), planes)
-    pieces, gated, before = lax.optimization_barrier((pieces, handed_back, before))
+    crossed = section == 2
+    sent = jnp.where(crossed, far, out)
+    far_before = shift(sent, [([1], 1, 1, run_end), ([2], 0, 1, not_run_end)])
+    far_after = shift(sent, [([1], 1, -1, run_start), ([2], 0, -1, not_run_start)])
+    pieces, handed_back, before, after = lax.optimization_barrier(
+        (pieces, handed_back, before, after)
+    )
     terms = jnp.sum(pieces.astype(F32), axis=0)
     terms = jnp.sum(scatter(terms.reshape(RUN, -1, 2 * RANK), columns), axis=0)
     handed_forward, handed_back = run_place(
-        place, destination, before, hop, after, ends, handed_back
+        place, destination, before, near, after, far_before, far, far_after, handed_back[0]
     )
     return (handed_forward[None], handed_back[None], terms[None])
 

time: 145 us -> 136 us (0.938)
  the two profiles are of different devices: /device:TPU:166 before, /device:TPU:227 now
where the time goes in v14:
time: 136 us; the launch traced here: 135 us
  waiting for transfers between devices  47 us (35%)
  starting transfers between devices  39.9 us (29%)
  Pallas kernels  24.8 us (18%)
  local copies, waits for them, and re-layouts  17.6 us (13%)
  other arithmetic  5.16 us (4%)
    ppermute x13, waiting for transfers between devices, shift(): return lax.ppermute(x, AXES, route)  37.4 us
    ppermute x13, starting transfers between devices, shift(): return lax.ppermute(x, AXES, route)  25.8 us
    unnamed x44, local copies, waits for them, and re-layouts  14.4 us
    all_to_all x2, starting transfers between devices, scatter(): return lax.all_to_all(x, 'dp', 0, 0, axis_index_groups=groups, tiled=True)  14 us
    all_to_all x2, waiting for transfers between devices, scatter(): return lax.all_to_all(x, 'dp', 0, 0, axis_index_groups=groups, tiled=True)  9.62 us
    pallas_call x1, Pallas kernels, run_backward(): pl.pallas_call(backward_kernel, out_shape=(jax.ShapeDtypeStruct((TILE, QW...  8.76 us
    pallas_call x1, Pallas kernels, run_forward(): pl.pallas_call(forward_kernel, out_shape=jax.ShapeDtypeStruct((TILE, QW),...  5.62 us
    pallas_call x1, Pallas kernels, run_place(): pl.pallas_call(place_kernel, out_shape=(jax.ShapeDtypeStruct((3 * TILE, Q...  4.41 us
  transfers between devices with their start and end apart: 15, of which 4 were waited for; matrix products, arithmetic and copies ran while one was open for 4% of the time, Pallas kernels for 18%

profile of v14, /device:TPU:227, one launch (start us, length us, event | category | flops | bytes accessed | tf_op | source)
XLA Modules:
  0.0 135.3 jit_solution(13135255713724127779)
XLA Ops:
  0.7 3.2 %slice_bitcast_fusion = (bf16[128,4096]{1,0:T(8,128)(2,1)}, bf16[128,4096]{1,0:T(8,128)(2,1)}) fusion(bf16[1,384,4096]{2,1,0:T(8,128)(2,1)} %param.11), kind=kLoop, calls=%fused_computation.1 | loop fusion | bytes 4194304 | tf_op jit(solution)/shard_map/slice | solution.py:396
  3.8 1.6 %collective-permute-start.1 = (bf16[128,4096]{1,0:T(8,128)(2,1)}, bf16[128,4096]{1,0:T(8,128)(2,1)}, u32[]{:S(2)}, u32[]{:S(2)}) collective-permute-start(bf16[128,4096]{1,0:T(8,128)(2,1)} %get-tuple-element.40), channel_id=1, source_target_pairs={{64,65},{65,66},{66,67},{67,68},{68,69},{69,70},{70,71},{71,72},{7... | collective-permute-start | bytes 3145736 | tf_op jit(solution)/shard_map/ppermute | solution.py:360
  5.5 1.7 %collective-permute-start.2 = (bf16[128,4096]{1,0:T(8,128)(2,1)}, bf16[128,4096]{1,0:T(8,128)(2,1)}, u32[]{:S(2)}, u32[]{:S(2)}) collective-permute-start(bf16[128,4096]{1,0:T(8,128)(2,1)} %get-tuple-element.41), channel_id=1, source_target_pairs={{65,64},{66,65},{67,66},{68,67},{69,68},{70,69},{71,70},{72,71},{7... | collective-permute-start | bytes 3145736 | tf_op jit(solution)/shard_map/ppermute | solution.py:360
  7.2 1.3 copy.15
  8.5 0.1 copy.16.lens_ref
  8.6 0.1 pad_add_fusion.rank_ref.place_ref
  8.7 1.4 %copy-done.2 = bf16[1,4096,64]{2,1,0:T(8,128)(2,1)S(1)} copy-done((bf16[1,4096,64]{2,1,0:T(8,128)(2,1)S(1)}, bf16[1,4096,64]{2,1,0:T(8,128)(2,1)}, u32[]{:S(2)}) %copy-start.2) | copy-done | bytes 524312
  10.1 1.0 copy-done.5
  11.1 1.3 copy-done.9
  12.4 5.6 %forward_tile.1 = bf16[128,4096]{1,0:T(8,128)(2,1)} custom-call(s32[3]{0:T(128)S(1)} %pad_add_fusion.rank_ref.place_ref, s32[2,64,8]{2,1,0:T(8,128)S(1)} %copy.16.lens_ref, s32[2,64]{1,0:T(2,128)S(1)} %copy-done.16, f32[102]{0:T(128)S(1)} %copy-done.18, bf16[128,5120]{1,0:T(8,128)(2,1)S(1)} %bitcast.30, bf16[4096,64]{1,0:T(8,128)(2,1)S(1)} %bitcast.22, ...), custom_call_target="tpu_custom_call" | custom-call | flops 1048576 | bytes 1048576 | tf_op jit(solution)/shard_map/forward_tile/pallas_call | solution.py:240
  18.0 1.3 collective-permute-start.3
  19.4 1.2 copy-done.3
  20.6 1.3 copy-done.4
  21.9 4.3 %prepare_tile.1 = (f32[4096,128]{1,0:T(8,128)S(1)}, bf16[128,4096]{1,0:T(8,128)(2,1)S(1)}, bf16[128,64]{1,0:T(8,128)(2,1)S(1)}, bf16[128,128]{1,0:T(8,128)(2,1)S...) custom-call(s32[3]{0:T(128)S(1)} %pad_add_fusion.rank_ref.place_ref, s32[2,64,8]{2,1,0:T(8,128)S(1)} %copy.16.lens_ref, ...), custom_call_target="tpu_custom_call" | custom-call | flops 1048576 | bytes 1048576 | tf_op jit(solution)/shard_map/prepare_tile/pallas_call | solution.py:254
  26.2 0.0 copy-start.8
  26.2 1.3 copy-done.8
  27.5 1.0 copy-done.10
  28.5 0.0 collective-permute-done.1.left_ref
  28.5 0.0 collective-permute-done.2.right_ref
  28.5 0.0 collective-permute-done.3.near_ref
  28.5 4.5 %collective-permute-start.4 = (bf16[128,4096]{1,0:T(8,128)(2,1)}, bf16[128,4096]{1,0:T(8,128)(2,1)S(1)}, u32[]{:S(2)}, u32[]{:S(2)}) collective-permute-start(bf16[128,4096]{1,0:T(8,128)(2,1)} %get-tuple-element.40), channel_id=1, source_target_pairs={{192,193},{193,194},{194,195},{195,196},{196,197},{197,198},{198,1... | collective-permute-start | bytes 3145736 | tf_op jit(solution)/shard_map/ppermute | solution.py:360
  33.1 1.9 %collective-permute-start.5 = (bf16[128,4096]{1,0:T(8,128)(2,1)}, bf16[128,4096]{1,0:T(8,128)(2,1)S(1)}, u32[]{:S(2)}, u32[]{:S(2)}) collective-permute-start(bf16[128,4096]{1,0:T(8,128)(2,1)} %get-tuple-element.41), channel_id=1, source_target_pairs={{193,192},{194,193},{195,194},{196,195},{197,196},{198,197},{199,1... | collective-permute-start | bytes 3145736 | tf_op jit(solution)/shard_map/ppermute | solution.py:360
  35.0 1.6 %collective-permute-start = (bf16[128,4096]{1,0:T(8,128)(2,1)}, bf16[128,4096]{1,0:T(8,128)(2,1)}, u32[]{:S(2)}, u32[]{:S(2)}) collective-permute-start(bf16[128,4096]{1,0:T(8,128)(2,1)} %forward_tile.1), channel_id=1, source_target_pairs={{64,128},{65,129},{66,130},{67,131},{68,132},{69,133},{70,134},{71... | collective-permute-start | bytes 3145736 | tf_op jit(solution)/shard_map/ppermute | solution.py:360
  36.6 9.1 %collective-permute-done.4.last_left_ref = bf16[128,4096]{1,0:T(8,128)(2,1)S(1)} collective-permute-done((bf16[128,4096]{1,0:T(8,128)(2,1)}, bf16[128,4096]{1,0:T(8,128)(2,1)S(1)}, u32[]{:S(2)}, u32[]{:S(2)}) %collective-permute-start.4) | collective-permute-done | bytes 1048608 | tf_op jit(solution)/shard_map/ppermute | solution.py:360
  45.7 22.8 %collective-permute-done.5.last_right_ref = bf16[128,4096]{1,0:T(8,128)(2,1)S(1)} collective-permute-done((bf16[128,4096]{1,0:T(8,128)(2,1)}, bf16[128,4096]{1,0:T(8,128)(2,1)S(1)}, u32[]{:S(2)}, u32[]{:S(2)}) %collective-permute-start.5) | collective-permute-done | bytes 1048608 | tf_op jit(solution)/shard_map/ppermute | solution.py:360
  68.5 8.8 %backward_tile.1 = (bf16[128,5120]{1,0:T(8,128)(2,1)}, bf16[128,4096]{1,0:T(8,128)(2,1)S(1)}, bf16[128,64]{1,0:T(8,128)(2,1)S(1)}) custom-call(s32[3]{0:T(128)S(1)} %pad_add_fusion.rank_ref.place_ref, s32[2,64]{1,0:T(2,128)S(1)} %copy-done.16, s32[2,64]{1,0:T(2,128)S(1)} %copy-done.17, f32[102]{0:T(128)S(1)} %copy-done.18, bf16[128,5120]{1,0:T(8,128)(2,1)} %bitcast.24, ...), custom_call_target="tpu_custom_call" | custom-call | flops 1048576 | bytes 1048576 | tf_op jit(solution)/shard_map/backward_tile/pallas_call | solution.py:286
  77.3 1.0 copy-done.12
  78.2 0.7 collective-permute-start.6
  78.9 0.7 collective-permute-start.7
  79.6 4.1 %collective-permute-start.10 = (bf16[128,4096]{1,0:T(8,128)(2,1)}, bf16[128,4096]{1,0:T(8,128)(2,1)}, u32[]{:S(2)}, u32[]{:S(2)}) collective-permute-start(bf16[128,4096]{1,0:T(8,128)(2,1)} %copy-done.14), channel_id=1, source_target_pairs={{65,64},{66,65},{67,66},{68,67},{69,68},{70,69},{71,70},{72,71},{7... | collective-permute-start | bytes 3145736 | tf_op jit(solution)/shard_map/ppermute | solution.py:360
  83.7 3.9 %collective-permute-start.9 = (bf16[128,4096]{1,0:T(8,128)(2,1)}, bf16[128,4096]{1,0:T(8,128)(2,1)}, u32[]{:S(2)}, u32[]{:S(2)}) collective-permute-start(bf16[128,4096]{1,0:T(8,128)(2,1)} %copy-done.14), channel_id=1, source_target_pairs={{64,65},{65,66},{66,67},{67,68},{68,69},{69,70},{70,71},{71,72},{7... | collective-permute-start | bytes 3145736 | tf_op jit(solution)/shard_map/ppermute | solution.py:360
  87.6 2.4 %collective-permute-start.8 = (bf16[128,5120]{1,0:T(8,128)(2,1)}, bf16[128,5120]{1,0:T(8,128)(2,1)}, u32[]{:S(2)}, u32[]{:S(2)}) collective-permute-start(bf16[128,5120]{1,0:T(8,128)(2,1)} %get-tuple-element.54), channel_id=1, source_target_pairs={{64,0},{65,1},{66,2},{67,3},{68,4},{69,5},{70,6},{71,7},{72,8},{73... | collective-permute-start | bytes 3932168 | tf_op jit(solution)/shard_map/ppermute | solution.py:360
  89.9 0.0 collective-permute-done.7.right_ref
  90.0 1.2 copy-done.11
  91.2 1.2 copy-done.13
  92.4 1.7 %adapter_terms.1 = bf16[4096,128]{1,0:T(8,128)(2,1)S(1)} custom-call(s32[3]{0:T(128)S(1)} %pad_add_fusion.rank_ref.place_ref, s32[2,64]{1,0:T(2,128)S(1)} %copy-done.16, s32[2,64]{1,0:T(2,128)S(1)} %copy-done.17, f32[102]{0:T(128)S(1)} %copy-done.18, bf16[128,4096]{1,0:T(8,128)(2,1)S(1)} %copy-done.11, bf16[384,4096]{1,0:T(8,128)(2,1)S(1)} %bitcast.20, ...), custom_call_target="tpu_custom_call" | custom-call | flops 1048576 | bytes 1048576 | tf_op jit(solution)/shard_map/adapter_terms/pallas_call | solution.py:273
  94.1 1.0 copy-done.7
  95.2 8.5 %all-to-all-start = ((bf16[16,256,128]{2,1,0:T(8,128)(2,1)}), bf16[16,256,128]{2,1,0:T(8,128)(2,1)}, u32[]{:S(2)}, u32[]{:S(2)}) async-start(bf16[16,256,128]{2,1,0:T(8,128)(2,1)} %bitcast.29), calls=%async_computation | async-start | bytes 2097152 | tf_op jit(solution)/shard_map/all_to_all | solution.py:384
  103.6 2.4 %broadcast_select_fusion = bf16[128,4096]{1,0:T(8,128)(2,1)} fusion(bf16[128,4096]{1,0:T(8,128)(2,1)} %collective-permute-done.far_ref, bf16[128,4096]{1,0:T(8,128)(2,1)} %forward_tile.1, pred[]{:T(512)S(6)} %eq.3), kind=kLoop, calls=%fused_computation.3 | loop fusion | flops 524288 | bytes 3145729 | tf_op jit(solution)/shard_map/jit(_where)/select_n | solution.py:430
  106.0 0.7 collective-permute-start.11
  106.8 0.7 collective-permute-start.12
  107.5 9.6 %all-to-all-done = bf16[16,256,128]{2,1,0:T(8,128)(2,1)} async-done(((bf16[16,256,128]{2,1,0:T(8,128)(2,1)}), bf16[16,256,128]{2,1,0:T(8,128)(2,1)}, u32[]{:S(2)}, u32[]{:S(2)}) %all-to-all-start) | async-done | bytes 1048608 | tf_op jit(solution)/shard_map/all_to_all | solution.py:384
  117.1 0.0 collective-permute-done.10.after_ref
  117.1 5.5 %collective-permute-done.9.before_ref = bf16[128,4096]{1,0:T(8,128)(2,1)} collective-permute-done((bf16[128,4096]{1,0:T(8,128)(2,1)}, bf16[128,4096]{1,0:T(8,128)(2,1)}, u32[]{:S(2)}, u32[]{:S(2)}) %collective-permute-start.9) | collective-permute-done | bytes 1048608 | tf_op jit(solution)/shard_map/ppermute | solution.py:360
  122.6 2.0 %convert_reduce_fusion = f32[256,128]{1,0:T(8,128)} fusion(bf16[16,256,128]{2,1,0:T(8,128)(2,1)} %all-to-all-done), kind=kLoop, calls=%fused_computation | loop fusion | flops 1015808 | bytes 1179648 | tf_op jit(solution)/shard_map/reduce_sum | solution.py:436
  124.7 5.6 %all-to-all-start.1 = ((f32[4,64,128]{2,1,0:T(8,128)}), f32[4,64,128]{2,1,0:T(8,128)S(1)}, u32[]{:S(2)}, u32[]{:S(2)}) async-start(f32[4,64,128]{2,1,0:T(8,128)} %bitcast.14), calls=%async_computation.1 | async-start | bytes 262144 | tf_op jit(solution)/shard_map/all_to_all | solution.py:384
  130.2 4.4 %place_outputs.1 = (bf16[384,4096]{1,0:T(8,128)(2,1)}, bf16[128,5120]{1,0:T(8,128)(2,1)}) custom-call(s32[3]{0:T(128)S(1)} %pad_add_fusion.rank_ref.place_ref, s32[2,64]{1,0:T(2,128)S(1)} %copy-done.17, bf16[128,4096]{1,0:T(8,128)(2,1)} %collective-permute-done.9.before_ref, bf16[128,4096]{1,0:T(8,128)(2,1)S(1)} %copy-done.15, ...), custom_call_target="tpu_custom_call" | custom-call | flops 1048576 | bytes 1048576 | tf_op jit(solution)/shard_map/place_outputs/pallas_call | solution.py:333
  134.7 0.6 reduce_sum.19
  (36 shorter events, 0.1 us)
Async XLA Ops:
  0.6 6.5 %copy-start.19 = (bf16[1,4096,64]{1,2,0:T(8,128)(2,1)S(1)}, bf16[1,4096,64]{1,2,0:T(8,128)(2,1)}, u32[]{:S(2)}) copy-start(bf16[1,4096,64]{1,2,0:T(8,128)(2,1)} %param.12) | copy-start | bytes 1572868
  0.6 7.9 %copy-start.20 = (s32[2,64,8]{1,2,0:T(8,128)S(1)}, s32[2,64,8]{1,2,0:T(8,128)}, u32[]{:S(2)}) copy-start(s32[2,64,8]{1,2,0:T(8,128)} %param.16) | copy-start | bytes 12292
  0.7 8.0 %copy-start.18 = (f32[102]{0:T(128)S(1)}, f32[102]{0:T(128)}, u32[]{:S(2)}) copy-start(f32[102]{0:T(128)} %table_ref.7) | copy-start | bytes 1228
  0.7 8.0 %copy-start.16 = (s32[2,64]{1,0:T(2,128)S(1)}, s32[2,64]{1,0:T(2,128)}, u32[]{:S(2)}) copy-start(s32[2,64]{1,0:T(2,128)} %langs_ref.7) | copy-start | bytes 1540
  3.8 24.7 %collective-permute-start.1 = (bf16[128,4096]{1,0:T(8,128)(2,1)}, bf16[128,4096]{1,0:T(8,128)(2,1)}, u32[]{:S(2)}, u32[]{:S(2)}) collective-permute-start(bf16[128,4096]{1,0:T(8,128)(2,1)} %get-tuple-element.40), channel_id=1, source_target_pairs={{64,65},{65,66},{66,67},{67,68},{68,69},{69,70},{70,71},{71,72},{7... | collective-permute-start | bytes 3145736 | tf_op jit(solution)/shard_map/ppermute | solution.py:360
  5.5 23.0 %collective-permute-start.2 = (bf16[128,4096]{1,0:T(8,128)(2,1)}, bf16[128,4096]{1,0:T(8,128)(2,1)}, u32[]{:S(2)}, u32[]{:S(2)}) collective-permute-start(bf16[128,4096]{1,0:T(8,128)(2,1)} %get-tuple-element.41), channel_id=1, source_target_pairs={{65,64},{66,65},{67,66},{68,67},{69,68},{70,69},{71,70},{72,71},{7... | collective-permute-start | bytes 3145736 | tf_op jit(solution)/shard_map/ppermute | solution.py:360
  7.2 12.2 %copy-start.17 = (s32[2,64]{1,0:T(2,128)S(1)}, s32[2,64]{1,0:T(2,128)}, u32[]{:S(2)}) copy-start(s32[2,64]{1,0:T(2,128)} %dest_ref.7) | copy-start | bytes 1540
  8.5 10.8 %copy-start = (bf16[1,384,4096]{2,1,0:T(8,128)(2,1)S(1)}, bf16[1,384,4096]{2,1,0:T(8,128)(2,1)}, u32[]{:S(2)}) copy-start(bf16[1,384,4096]{2,1,0:T(8,128)(2,1)} %param.11) | copy-start | bytes 9437188
  8.7 1.4 %copy-start.2 = (bf16[1,4096,64]{2,1,0:T(8,128)(2,1)S(1)}, bf16[1,4096,64]{2,1,0:T(8,128)(2,1)}, u32[]{:S(2)}) copy-start(bf16[1,4096,64]{2,1,0:T(8,128)(2,1)} %copy.15) | copy-start | bytes 1572868
  10.1 1.0 copy-start.5
  11.1 1.3 copy-start.9
  12.4 6.9 %copy-start.6 = (bf16[1,64,4096]{2,1,0:T(8,128)(2,1)S(1)}, bf16[1,64,4096]{2,1,0:T(8,128)(2,1)}, u32[]{:S(2)}) copy-start(bf16[1,64,4096]{2,1,0:T(8,128)(2,1)} %param.13) | copy-start | bytes 1572868
  18.0 10.5 %collective-permute-start.3 = (bf16[128,4096]{1,0:T(8,128)(2,1)}, bf16[128,4096]{1,0:T(8,128)(2,1)S(1)}, u32[]{:S(2)}, u32[]{:S(2)}) collective-permute-start(bf16[128,4096]{1,0:T(8,128)(2,1)} %forward_tile.1), channel_id=1, source_target_pairs={{0,64},{1,65},{2,66},{3,67},{4,68},{5,69},{6,70},{7,71},{8,72},{9,... | collective-permute-start | bytes 3145736 | tf_op jit(solution)/shard_map/ppermute | solution.py:360
  19.4 1.2 copy-start.3
  20.6 1.3 copy-start.4
  26.2 1.3 copy-start.8
  27.5 1.0 copy-start.10
  28.5 40.0 %copy-start.14 = (bf16[128,4096]{1,0:T(8,128)(2,1)}, bf16[128,4096]{1,0:T(8,128)(2,1)S(1)}, u32[]{:S(2)}) copy-start(bf16[128,4096]{1,0:T(8,128)(2,1)S(1)} %collective-permute-done.3.near_ref) | copy-start | bytes 3145732
  28.5 17.2 %collective-permute-start.4 = (bf16[128,4096]{1,0:T(8,128)(2,1)}, bf16[128,4096]{1,0:T(8,128)(2,1)S(1)}, u32[]{:S(2)}, u32[]{:S(2)}) collective-permute-start(bf16[128,4096]{1,0:T(8,128)(2,1)} %get-tuple-element.40), channel_id=1, source_target_pairs={{192,193},{193,194},{194,195},{195,196},{196,197},{197,198},{198,1... | collective-permute-start | bytes 3145736 | tf_op jit(solution)/shard_map/ppermute | solution.py:360
  33.1 35.4 %collective-permute-start.5 = (bf16[128,4096]{1,0:T(8,128)(2,1)}, bf16[128,4096]{1,0:T(8,128)(2,1)S(1)}, u32[]{:S(2)}, u32[]{:S(2)}) collective-permute-start(bf16[128,4096]{1,0:T(8,128)(2,1)} %get-tuple-element.41), channel_id=1, source_target_pairs={{193,192},{194,193},{195,194},{196,195},{197,196},{198,197},{199,1... | collective-permute-start | bytes 3145736 | tf_op jit(solution)/shard_map/ppermute | solution.py:360
  35.0 60.2 %collective-permute-start = (bf16[128,4096]{1,0:T(8,128)(2,1)}, bf16[128,4096]{1,0:T(8,128)(2,1)}, u32[]{:S(2)}, u32[]{:S(2)}) collective-permute-start(bf16[128,4096]{1,0:T(8,128)(2,1)} %forward_tile.1), channel_id=1, source_target_pairs={{64,128},{65,129},{66,130},{67,131},{68,132},{69,133},{70,134},{71... | collective-permute-start | bytes 3145736 | tf_op jit(solution)/shard_map/ppermute | solution.py:360
  68.5 21.5 %copy-start.1 = (bf16[1,384,4096]{2,1,0:T(8,128)(2,1)S(1)}, bf16[1,384,4096]{2,1,0:T(8,128)(2,1)}, u32[]{:S(2)}) copy-start(bf16[1,384,4096]{2,1,0:T(8,128)(2,1)} %param.11) | copy-start | bytes 9437188
  77.2 1.0 copy-start.12
  78.2 9.3 %collective-permute-start.6 = (bf16[128,128]{1,0:T(8,128)(2,1)S(1)}, bf16[128,128]{1,0:T(8,128)(2,1)S(1)}, u32[]{:S(2)}, u32[]{:S(2)}) collective-permute-start(bf16[128,128]{1,0:T(8,128)(2,1)S(1)} %get-tuple-element.47), channel_id=1, source_target_pairs={{0,1},{1,2},{2,3},{3,4},{4,5},{5,6},{6,7},{7,8},{8,9},{9,10},{10,1... | collective-permute-start | bytes 98312 | tf_op jit(solution)/shard_map/ppermute | solution.py:360
  78.9 11.1 %collective-permute-start.7 = (bf16[128,128]{1,0:T(8,128)(2,1)S(1)}, bf16[128,128]{1,0:T(8,128)(2,1)S(1)}, u32[]{:S(2)}, u32[]{:S(2)}) collective-permute-start(bf16[128,128]{1,0:T(8,128)(2,1)S(1)} %get-tuple-element.49), channel_id=1, source_target_pairs={{1,0},{2,1},{3,2},{4,3},{5,4},{6,5},{7,6},{8,7},{9,8},{10,9},{11,1... | collective-permute-start | bytes 98312 | tf_op jit(solution)/shard_map/ppermute | solution.py:360
  79.6 37.6 %collective-permute-start.10 = (bf16[128,4096]{1,0:T(8,128)(2,1)}, bf16[128,4096]{1,0:T(8,128)(2,1)}, u32[]{:S(2)}, u32[]{:S(2)}) collective-permute-start(bf16[128,4096]{1,0:T(8,128)(2,1)} %copy-done.14), channel_id=1, source_target_pairs={{65,64},{66,65},{67,66},{68,67},{69,68},{70,69},{71,70},{72,71},{7... | collective-permute-start | bytes 3145736 | tf_op jit(solution)/shard_map/ppermute | solution.py:360
  83.7 38.9 %collective-permute-start.9 = (bf16[128,4096]{1,0:T(8,128)(2,1)}, bf16[128,4096]{1,0:T(8,128)(2,1)}, u32[]{:S(2)}, u32[]{:S(2)}) collective-permute-start(bf16[128,4096]{1,0:T(8,128)(2,1)} %copy-done.14), channel_id=1, source_target_pairs={{64,65},{65,66},{66,67},{67,68},{68,69},{69,70},{70,71},{71,72},{7... | collective-permute-start | bytes 3145736 | tf_op jit(solution)/shard_map/ppermute | solution.py:360
  87.6 35.0 %collective-permute-start.8 = (bf16[128,5120]{1,0:T(8,128)(2,1)}, bf16[128,5120]{1,0:T(8,128)(2,1)}, u32[]{:S(2)}, u32[]{:S(2)}) collective-permute-start(bf16[128,5120]{1,0:T(8,128)(2,1)} %get-tuple-element.54), channel_id=1, source_target_pairs={{64,0},{65,1},{66,2},{67,3},{68,4},{69,5},{70,6},{71,7},{72,8},{73... | collective-permute-start | bytes 3932168 | tf_op jit(solution)/shard_map/ppermute | solution.py:360
  89.9 1.2 copy-start.11
  91.2 1.2 copy-start.13
  94.1 1.0 copy-start.7
  95.2 21.9 %all-to-all-start = ((bf16[16,256,128]{2,1,0:T(8,128)(2,1)}), bf16[16,256,128]{2,1,0:T(8,128)(2,1)}, u32[]{:S(2)}, u32[]{:S(2)}) async-start(bf16[16,256,128]{2,1,0:T(8,128)(2,1)} %bitcast.29), calls=%async_computation | async-start | bytes 2097152 | tf_op jit(solution)/shard_map/all_to_all | solution.py:384
  103.6 26.6 %copy-start.15 = (bf16[128,4096]{1,0:T(8,128)(2,1)S(1)}, bf16[128,4096]{1,0:T(8,128)(2,1)}, u32[]{:S(2)}) copy-start(bf16[128,4096]{1,0:T(8,128)(2,1)} %copy-done.14) | copy-start | bytes 3145732
  106.0 24.2 %collective-permute-start.11 = (bf16[128,4096]{1,0:T(8,128)(2,1)}, bf16[128,4096]{1,0:T(8,128)(2,1)S(1)}, u32[]{:S(2)}, u32[]{:S(2)}) collective-permute-start(bf16[128,4096]{1,0:T(8,128)(2,1)} %broadcast_select_fusion), channel_id=1, source_target_pairs={{67,132},{71,136},{75,140},{79,144},{83,148},{87,152},{91,156},{95... | collective-permute-start | bytes 3145736 | tf_op jit(solution)/shard_map/ppermute | solution.py:360
  106.8 23.5 %collective-permute-start.12 = (bf16[128,4096]{1,0:T(8,128)(2,1)}, bf16[128,4096]{1,0:T(8,128)(2,1)S(1)}, u32[]{:S(2)}, u32[]{:S(2)}) collective-permute-start(bf16[128,4096]{1,0:T(8,128)(2,1)} %broadcast_select_fusion), channel_id=1, source_target_pairs={{68,131},{72,135},{76,139},{80,143},{84,147},{88,151},{92,155},{96... | collective-permute-start | bytes 3145736 | tf_op jit(solution)/shard_map/ppermute | solution.py:360
  124.7 10.0 %all-to-all-start.1 = ((f32[4,64,128]{2,1,0:T(8,128)}), f32[4,64,128]{2,1,0:T(8,128)S(1)}, u32[]{:S(2)}, u32[]{:S(2)}) async-start(f32[4,64,128]{2,1,0:T(8,128)} %bitcast.14), calls=%async_computation.1 | async-start | bytes 262144 | tf_op jit(solution)/shard_map/all_to_all | solution.py:384

commit v15 on v14

--- a/solution.py
+++ b/solution.py
@@ -172,20 +172,24 @@
 def backward_kernel(
     place_ref, langs_ref, dest_ref, table_ref, qkv_ref, left_ref, right_ref, last_left_ref,
     last_right_ref, slots_ref, probs_ref, down_ref, up_ref, grad_ref, scaled_ref, back_ref,
-    gattn_ref,
+    gattn_ref, mid_ref, sem,
 ):
     rank = place_ref[0]
     rate = table_ref[langs_ref[1, rank]]
     went = dest_ref[1, rank] - rank
     last = place_ref[1] == place_ref[2] - 1
 
+    fetch = pltpu.make_async_copy(slots_ref.at[pl.ds(TILE, TILE), :], mid_ref, sem)
+
     def chosen():
+        fetch.start()
+        fetch.wait()
         back = jnp.zeros((TILE, RANK), F32)
         for c in range(0, QW, 512):
             cols = slice(c, c + 512)
             left = jnp.where(last, last_left_ref[:, cols], left_ref[:, cols])
             right = jnp.where(last, last_right_ref[:, cols], right_ref[:, cols])
-            mid = slots_ref[TILE : 2 * TILE, cols]
+            mid = mid_ref[:, cols]
             grad = jnp.where(went < 0, left, jnp.where(went > 0, right, mid))
             gattn_ref[:, cols] = grad
             scaled = (rate * grad.astype(F32)).astype(BF16)
@@ -290,9 +294,13 @@
             jax.ShapeDtypeStruct((TILE, QW), BF16),
             jax.ShapeDtypeStruct((TILE, RANK), BF16),
         ),
-        in_specs=[SMEM] * 4 + [VMEM] * 9,
+        in_specs=[SMEM] * 4 + [VMEM] * 5 + [pl.BlockSpec(memory_space=pl.ANY)] + [VMEM] * 3,
         out_specs=(VMEM,) * 3,
-        scratch_shapes=[pltpu.VMEM((TILE, QW), BF16)],
+        scratch_shapes=[
+            pltpu.VMEM((TILE, QW), BF16),
+            pltpu.VMEM((TILE, QW), BF16),
+            pltpu.SemaphoreType.DMA,
+        ],
         compiler_params=pltpu.CompilerParams(vmem_limit_bytes=48 * 2**20),
         cost_estimate=COST,
         name="backward_tile",

time: 136 us -> 137 us (level)
  no operation moved by 1% of the time
where the time goes in v15:
time: 137 us; the launch traced here: 136 us
  waiting for transfers between devices  46.3 us (34%)
  starting transfers between devices  40.9 us (30%)
  Pallas kernels  25.1 us (18%)
  local copies, waits for them, and re-layouts  17.6 us (13%)
  other arithmetic  5.16 us (4%)
    ppermute x13, waiting for transfers between devices, shift(): return lax.ppermute(x, AXES, route)  36.7 us
    ppermute x13, starting transfers between devices, shift(): return lax.ppermute(x, AXES, route)  25.8 us
    all_to_all x2, starting transfers between devices, scatter(): return lax.all_to_all(x, 'dp', 0, 0, axis_index_groups=groups, tiled=True)  15.1 us
    unnamed x44, local copies, waits for them, and re-layouts  14.4 us
    all_to_all x2, waiting for transfers between devices, scatter(): return lax.all_to_all(x, 'dp', 0, 0, axis_index_groups=groups, tiled=True)  9.62 us
    pallas_call x1, Pallas kernels, run_backward(): pl.pallas_call(backward_kernel, out_shape=(jax.ShapeDtypeStruct((TILE, QW...  9.09 us
    pallas_call x1, Pallas kernels, run_forward(): pl.pallas_call(forward_kernel, out_shape=jax.ShapeDtypeStruct((TILE, QW),...  5.62 us
    pallas_call x1, Pallas kernels, run_place(): pl.pallas_call(place_kernel, out_shape=(jax.ShapeDtypeStruct((3 * TILE, Q...  4.41 us
  transfers between devices with their start and end apart: 15, of which 4 were waited for; matrix products, arithmetic and copies ran while one was open for 4% of the time, Pallas kernels for 18%

profile of v15, /device:TPU:227, one launch (start us, length us, event | category | flops | bytes accessed | tf_op | source)
XLA Modules:
  0.0 136.0 jit_solution(15526241308235191252)
XLA Ops:
  0.7 3.2 %slice_bitcast_fusion = (bf16[128,4096]{1,0:T(8,128)(2,1)}, bf16[128,4096]{1,0:T(8,128)(2,1)}) fusion(bf16[1,384,4096]{2,1,0:T(8,128)(2,1)} %param.11), kind=kLoop, calls=%fused_computation.1 | loop fusion | bytes 4194304 | tf_op jit(solution)/shard_map/slice | solution.py:404
  3.8 1.6 %collective-permute-start.1 = (bf16[128,4096]{1,0:T(8,128)(2,1)}, bf16[128,4096]{1,0:T(8,128)(2,1)}, u32[]{:S(2)}, u32[]{:S(2)}) collective-permute-start(bf16[128,4096]{1,0:T(8,128)(2,1)} %get-tuple-element.40), channel_id=1, source_target_pairs={{64,65},{65,66},{66,67},{67,68},{68,69},{69,70},{70,71},{71,72},{7... | collective-permute-start | bytes 3145736 | tf_op jit(solution)/shard_map/ppermute | solution.py:368
  5.5 1.7 %collective-permute-start.2 = (bf16[128,4096]{1,0:T(8,128)(2,1)}, bf16[128,4096]{1,0:T(8,128)(2,1)}, u32[]{:S(2)}, u32[]{:S(2)}) collective-permute-start(bf16[128,4096]{1,0:T(8,128)(2,1)} %get-tuple-element.41), channel_id=1, source_target_pairs={{65,64},{66,65},{67,66},{68,67},{69,68},{70,69},{71,70},{72,71},{7... | collective-permute-start | bytes 3145736 | tf_op jit(solution)/shard_map/ppermute | solution.py:368
  7.2 1.3 copy.15
  8.5 0.1 copy.16.lens_ref
  8.6 0.1 pad_add_fusion.rank_ref.place_ref
  8.7 1.4 %copy-done.2 = bf16[1,4096,64]{2,1,0:T(8,128)(2,1)S(1)} copy-done((bf16[1,4096,64]{2,1,0:T(8,128)(2,1)S(1)}, bf16[1,4096,64]{2,1,0:T(8,128)(2,1)}, u32[]{:S(2)}) %copy-start.2) | copy-done | bytes 524312
  10.1 1.0 copy-done.5
  11.1 1.3 copy-done.9
  12.4 5.6 %forward_tile.1 = bf16[128,4096]{1,0:T(8,128)(2,1)} custom-call(s32[3]{0:T(128)S(1)} %pad_add_fusion.rank_ref.place_ref, s32[2,64,8]{2,1,0:T(8,128)S(1)} %copy.16.lens_ref, s32[2,64]{1,0:T(2,128)S(1)} %copy-done.16, f32[102]{0:T(128)S(1)} %copy-done.18, bf16[128,5120]{1,0:T(8,128)(2,1)S(1)} %bitcast.30, bf16[4096,64]{1,0:T(8,128)(2,1)S(1)} %bitcast.22, ...), custom_call_target="tpu_custom_call" | custom-call | flops 1048576 | bytes 1048576 | tf_op jit(solution)/shard_map/forward_tile/pallas_call | solution.py:244
  18.0 1.3 collective-permute-start.3
  19.4 1.2 copy-done.3
  20.6 1.3 copy-done.4
  21.9 4.3 %prepare_tile.1 = (f32[4096,128]{1,0:T(8,128)S(1)}, bf16[128,4096]{1,0:T(8,128)(2,1)S(1)}, bf16[128,64]{1,0:T(8,128)(2,1)S(1)}, bf16[128,128]{1,0:T(8,128)(2,1)S...) custom-call(s32[3]{0:T(128)S(1)} %pad_add_fusion.rank_ref.place_ref, s32[2,64,8]{2,1,0:T(8,128)S(1)} %copy.16.lens_ref, ...), custom_call_target="tpu_custom_call" | custom-call | flops 1048576 | bytes 1048576 | tf_op jit(solution)/shard_map/prepare_tile/pallas_call | solution.py:258
  26.2 0.0 copy-start.8
  26.2 1.3 copy-done.8
  27.5 1.0 copy-done.10
  28.5 4.5 %collective-permute-start.4 = (bf16[128,4096]{1,0:T(8,128)(2,1)}, bf16[128,4096]{1,0:T(8,128)(2,1)S(1)}, u32[]{:S(2)}, u32[]{:S(2)}) collective-permute-start(bf16[128,4096]{1,0:T(8,128)(2,1)} %get-tuple-element.40), channel_id=1, source_target_pairs={{192,193},{193,194},{194,195},{195,196},{196,197},{197,198},{198,1... | collective-permute-start | bytes 3145736 | tf_op jit(solution)/shard_map/ppermute | solution.py:368
  33.1 1.9 %collective-permute-start.5 = (bf16[128,4096]{1,0:T(8,128)(2,1)}, bf16[128,4096]{1,0:T(8,128)(2,1)S(1)}, u32[]{:S(2)}, u32[]{:S(2)}) collective-permute-start(bf16[128,4096]{1,0:T(8,128)(2,1)} %get-tuple-element.41), channel_id=1, source_target_pairs={{193,192},{194,193},{195,194},{196,195},{197,196},{198,197},{199,1... | collective-permute-start | bytes 3145736 | tf_op jit(solution)/shard_map/ppermute | solution.py:368
  35.0 1.6 %collective-permute-start = (bf16[128,4096]{1,0:T(8,128)(2,1)}, bf16[128,4096]{1,0:T(8,128)(2,1)}, u32[]{:S(2)}, u32[]{:S(2)}) collective-permute-start(bf16[128,4096]{1,0:T(8,128)(2,1)} %forward_tile.1), channel_id=1, source_target_pairs={{64,128},{65,129},{66,130},{67,131},{68,132},{69,133},{70,134},{71... | collective-permute-start | bytes 3145736 | tf_op jit(solution)/shard_map/ppermute | solution.py:368
  36.6 9.1 %collective-permute-done.4.last_left_ref = bf16[128,4096]{1,0:T(8,128)(2,1)S(1)} collective-permute-done((bf16[128,4096]{1,0:T(8,128)(2,1)}, bf16[128,4096]{1,0:T(8,128)(2,1)S(1)}, u32[]{:S(2)}, u32[]{:S(2)}) %collective-permute-start.4) | collective-permute-done | bytes 1048608 | tf_op jit(solution)/shard_map/ppermute | solution.py:368
  45.7 22.5 %collective-permute-done.5.last_right_ref = bf16[128,4096]{1,0:T(8,128)(2,1)S(1)} collective-permute-done((bf16[128,4096]{1,0:T(8,128)(2,1)}, bf16[128,4096]{1,0:T(8,128)(2,1)S(1)}, u32[]{:S(2)}, u32[]{:S(2)}) %collective-permute-start.5) | collective-permute-done | bytes 1048608 | tf_op jit(solution)/shard_map/ppermute | solution.py:368
  68.1 9.1 %backward_tile.1 = (bf16[128,5120]{1,0:T(8,128)(2,1)}, bf16[128,4096]{1,0:T(8,128)(2,1)S(1)}, bf16[128,64]{1,0:T(8,128)(2,1)S(1)}) custom-call(s32[3]{0:T(128)S(1)} %pad_add_fusion.rank_ref.place_ref, s32[2,64]{1,0:T(2,128)S(1)} %copy-done.16, s32[2,64]{1,0:T(2,128)S(1)} %copy-done.17, f32[102]{0:T(128)S(1)} %copy-done.18, bf16[128,5120]{1,0:T(8,128)(2,1)} %bitcast.24, ...), custom_call_target="tpu_custom_call" | custom-call | flops 1048576 | bytes 1048576 | tf_op jit(solution)/shard_map/backward_tile/pallas_call | solution.py:290
  77.2 0.0 copy-start.12
  77.3 1.0 copy-done.12
  78.2 0.7 collective-permute-start.6
  78.9 0.7 collective-permute-start.7
  79.6 4.1 %collective-permute-start.10 = (bf16[128,4096]{1,0:T(8,128)(2,1)}, bf16[128,4096]{1,0:T(8,128)(2,1)}, u32[]{:S(2)}, u32[]{:S(2)}) collective-permute-start(bf16[128,4096]{1,0:T(8,128)(2,1)} %copy-done.14), channel_id=1, source_target_pairs={{65,64},{66,65},{67,66},{68,67},{69,68},{70,69},{71,70},{72,71},{7... | collective-permute-start | bytes 3145736 | tf_op jit(solution)/shard_map/ppermute | solution.py:368
  83.7 3.9 %collective-permute-start.9 = (bf16[128,4096]{1,0:T(8,128)(2,1)}, bf16[128,4096]{1,0:T(8,128)(2,1)}, u32[]{:S(2)}, u32[]{:S(2)}) collective-permute-start(bf16[128,4096]{1,0:T(8,128)(2,1)} %copy-done.14), channel_id=1, source_target_pairs={{64,65},{65,66},{66,67},{67,68},{68,69},{69,70},{70,71},{71,72},{7... | collective-permute-start | bytes 3145736 | tf_op jit(solution)/shard_map/ppermute | solution.py:368
  87.6 2.4 %collective-permute-start.8 = (bf16[128,5120]{1,0:T(8,128)(2,1)}, bf16[128,5120]{1,0:T(8,128)(2,1)}, u32[]{:S(2)}, u32[]{:S(2)}) collective-permute-start(bf16[128,5120]{1,0:T(8,128)(2,1)} %get-tuple-element.54), channel_id=1, source_target_pairs={{64,0},{65,1},{66,2},{67,3},{68,4},{69,5},{70,6},{71,7},{72,8},{73... | collective-permute-start | bytes 3932168 | tf_op jit(solution)/shard_map/ppermute | solution.py:368
  90.0 1.2 copy-done.11
  91.2 1.2 copy-done.13
  92.4 1.7 %adapter_terms.1 = bf16[4096,128]{1,0:T(8,128)(2,1)S(1)} custom-call(s32[3]{0:T(128)S(1)} %pad_add_fusion.rank_ref.place_ref, s32[2,64]{1,0:T(2,128)S(1)} %copy-done.16, s32[2,64]{1,0:T(2,128)S(1)} %copy-done.17, f32[102]{0:T(128)S(1)} %copy-done.18, bf16[128,4096]{1,0:T(8,128)(2,1)S(1)} %copy-done.11, bf16[384,4096]{1,0:T(8,128)(2,1)S(1)} %bitcast.20, ...), custom_call_target="tpu_custom_call" | custom-call | flops 1048576 | bytes 1048576 | tf_op jit(solution)/shard_map/adapter_terms/pallas_call | solution.py:277
  94.1 1.0 copy-done.7
  95.2 0.0 collective-permute-done.far_ref
  95.2 8.8 %all-to-all-start = ((bf16[16,256,128]{2,1,0:T(8,128)(2,1)}), bf16[16,256,128]{2,1,0:T(8,128)(2,1)}, u32[]{:S(2)}, u32[]{:S(2)}) async-start(bf16[16,256,128]{2,1,0:T(8,128)(2,1)} %bitcast.29), calls=%async_computation | async-start | bytes 2097152 | tf_op jit(solution)/shard_map/all_to_all | solution.py:392
  104.0 2.4 %broadcast_select_fusion = bf16[128,4096]{1,0:T(8,128)(2,1)} fusion(bf16[128,4096]{1,0:T(8,128)(2,1)} %collective-permute-done.far_ref, bf16[128,4096]{1,0:T(8,128)(2,1)} %forward_tile.1, pred[]{:T(512)S(6)} %eq.3), kind=kLoop, calls=%fused_computation.3 | loop fusion | flops 524288 | bytes 3145729 | tf_op jit(solution)/shard_map/jit(_where)/select_n | solution.py:438
  106.4 0.7 collective-permute-start.11
  107.1 0.7 collective-permute-start.12
  107.8 9.6 %all-to-all-done = bf16[16,256,128]{2,1,0:T(8,128)(2,1)} async-done(((bf16[16,256,128]{2,1,0:T(8,128)(2,1)}), bf16[16,256,128]{2,1,0:T(8,128)(2,1)}, u32[]{:S(2)}, u32[]{:S(2)}) %all-to-all-start) | async-done | bytes 1048608 | tf_op jit(solution)/shard_map/all_to_all | solution.py:392
  117.5 5.1 %collective-permute-done.9.before_ref = bf16[128,4096]{1,0:T(8,128)(2,1)} collective-permute-done((bf16[128,4096]{1,0:T(8,128)(2,1)}, bf16[128,4096]{1,0:T(8,128)(2,1)}, u32[]{:S(2)}, u32[]{:S(2)}) %collective-permute-start.9) | collective-permute-done | bytes 1048608 | tf_op jit(solution)/shard_map/ppermute | solution.py:368
  122.6 0.0 collective-permute-done.8
  122.6 2.0 %convert_reduce_fusion = f32[256,128]{1,0:T(8,128)} fusion(bf16[16,256,128]{2,1,0:T(8,128)(2,1)} %all-to-all-done), kind=kLoop, calls=%fused_computation | loop fusion | flops 1015808 | bytes 1179648 | tf_op jit(solution)/shard_map/reduce_sum | solution.py:444
  124.7 6.2 %all-to-all-start.1 = ((f32[4,64,128]{2,1,0:T(8,128)}), f32[4,64,128]{2,1,0:T(8,128)S(1)}, u32[]{:S(2)}, u32[]{:S(2)}) async-start(f32[4,64,128]{2,1,0:T(8,128)} %bitcast.14), calls=%async_computation.1 | async-start | bytes 262144 | tf_op jit(solution)/shard_map/all_to_all | solution.py:392
  130.9 0.0 collective-permute-done.11.far_before_ref
  130.9 0.0 collective-permute-done.12.far_after_ref
  130.9 4.4 %place_outputs.1 = (bf16[384,4096]{1,0:T(8,128)(2,1)}, bf16[128,5120]{1,0:T(8,128)(2,1)}) custom-call(s32[3]{0:T(128)S(1)} %pad_add_fusion.rank_ref.place_ref, s32[2,64]{1,0:T(2,128)S(1)} %copy-done.17, bf16[128,4096]{1,0:T(8,128)(2,1)} %collective-permute-done.9.before_ref, bf16[128,4096]{1,0:T(8,128)(2,1)S(1)} %copy-done.15, ...), custom_call_target="tpu_custom_call" | custom-call | flops 1048576 | bytes 1048576 | tf_op jit(solution)/shard_map/place_outputs/pallas_call | solution.py:341
  135.3 0.6 reduce_sum.19
  (36 shorter events, 0.1 us)
Async XLA Ops:
  0.6 6.5 %copy-start.19 = (bf16[1,4096,64]{1,2,0:T(8,128)(2,1)S(1)}, bf16[1,4096,64]{1,2,0:T(8,128)(2,1)}, u32[]{:S(2)}) copy-start(bf16[1,4096,64]{1,2,0:T(8,128)(2,1)} %param.12) | copy-start | bytes 1572868
  0.6 7.9 %copy-start.20 = (s32[2,64,8]{1,2,0:T(8,128)S(1)}, s32[2,64,8]{1,2,0:T(8,128)}, u32[]{:S(2)}) copy-start(s32[2,64,8]{1,2,0:T(8,128)} %param.16) | copy-start | bytes 12292
  0.7 8.0 %copy-start.18 = (f32[102]{0:T(128)S(1)}, f32[102]{0:T(128)}, u32[]{:S(2)}) copy-start(f32[102]{0:T(128)} %table_ref.7) | copy-start | bytes 1228
  0.7 8.0 %copy-start.16 = (s32[2,64]{1,0:T(2,128)S(1)}, s32[2,64]{1,0:T(2,128)}, u32[]{:S(2)}) copy-start(s32[2,64]{1,0:T(2,128)} %langs_ref.7) | copy-start | bytes 1540
  3.8 24.7 %collective-permute-start.1 = (bf16[128,4096]{1,0:T(8,128)(2,1)}, bf16[128,4096]{1,0:T(8,128)(2,1)}, u32[]{:S(2)}, u32[]{:S(2)}) collective-permute-start(bf16[128,4096]{1,0:T(8,128)(2,1)} %get-tuple-element.40), channel_id=1, source_target_pairs={{64,65},{65,66},{66,67},{67,68},{68,69},{69,70},{70,71},{71,72},{7... | collective-permute-start | bytes 3145736 | tf_op jit(solution)/shard_map/ppermute | solution.py:368
  5.5 23.0 %collective-permute-start.2 = (bf16[128,4096]{1,0:T(8,128)(2,1)}, bf16[128,4096]{1,0:T(8,128)(2,1)}, u32[]{:S(2)}, u32[]{:S(2)}) collective-permute-start(bf16[128,4096]{1,0:T(8,128)(2,1)} %get-tuple-element.41), channel_id=1, source_target_pairs={{65,64},{66,65},{67,66},{68,67},{69,68},{70,69},{71,70},{72,71},{7... | collective-permute-start | bytes 3145736 | tf_op jit(solution)/shard_map/ppermute | solution.py:368
  7.2 12.2 %copy-start.17 = (s32[2,64]{1,0:T(2,128)S(1)}, s32[2,64]{1,0:T(2,128)}, u32[]{:S(2)}) copy-start(s32[2,64]{1,0:T(2,128)} %dest_ref.7) | copy-start | bytes 1540
  8.5 10.8 %copy-start = (bf16[1,384,4096]{2,1,0:T(8,128)(2,1)S(1)}, bf16[1,384,4096]{2,1,0:T(8,128)(2,1)}, u32[]{:S(2)}) copy-start(bf16[1,384,4096]{2,1,0:T(8,128)(2,1)} %param.11) | copy-start | bytes 9437188
  8.7 1.4 %copy-start.2 = (bf16[1,4096,64]{2,1,0:T(8,128)(2,1)S(1)}, bf16[1,4096,64]{2,1,0:T(8,128)(2,1)}, u32[]{:S(2)}) copy-start(bf16[1,4096,64]{2,1,0:T(8,128)(2,1)} %copy.15) | copy-start | bytes 1572868
  10.1 1.0 copy-start.5
  11.1 1.3 copy-start.9
  12.4 6.9 %copy-start.6 = (bf16[1,64,4096]{2,1,0:T(8,128)(2,1)S(1)}, bf16[1,64,4096]{2,1,0:T(8,128)(2,1)}, u32[]{:S(2)}) copy-start(bf16[1,64,4096]{2,1,0:T(8,128)(2,1)} %param.13) | copy-start | bytes 1572868
  18.0 10.5 %collective-permute-start.3 = (bf16[128,4096]{1,0:T(8,128)(2,1)}, bf16[128,4096]{1,0:T(8,128)(2,1)S(1)}, u32[]{:S(2)}, u32[]{:S(2)}) collective-permute-start(bf16[128,4096]{1,0:T(8,128)(2,1)} %forward_tile.1), channel_id=1, source_target_pairs={{0,64},{1,65},{2,66},{3,67},{4,68},{5,69},{6,70},{7,71},{8,72},{9,... | collective-permute-start | bytes 3145736 | tf_op jit(solution)/shard_map/ppermute | solution.py:368
  19.4 1.2 copy-start.3
  20.6 1.3 copy-start.4
  26.2 1.3 copy-start.8
  27.5 1.0 copy-start.10
  28.5 39.6 %copy-start.14 = (bf16[128,4096]{1,0:T(8,128)(2,1)}, bf16[128,4096]{1,0:T(8,128)(2,1)S(1)}, u32[]{:S(2)}) copy-start(bf16[128,4096]{1,0:T(8,128)(2,1)S(1)} %collective-permute-done.3.near_ref) | copy-start | bytes 3145732
  28.5 17.2 %collective-permute-start.4 = (bf16[128,4096]{1,0:T(8,128)(2,1)}, bf16[128,4096]{1,0:T(8,128)(2,1)S(1)}, u32[]{:S(2)}, u32[]{:S(2)}) collective-permute-start(bf16[128,4096]{1,0:T(8,128)(2,1)} %get-tuple-element.40), channel_id=1, source_target_pairs={{192,193},{193,194},{194,195},{195,196},{196,197},{197,198},{198,1... | collective-permute-start | bytes 3145736 | tf_op jit(solution)/shard_map/ppermute | solution.py:368
  33.1 35.1 %collective-permute-start.5 = (bf16[128,4096]{1,0:T(8,128)(2,1)}, bf16[128,4096]{1,0:T(8,128)(2,1)S(1)}, u32[]{:S(2)}, u32[]{:S(2)}) collective-permute-start(bf16[128,4096]{1,0:T(8,128)(2,1)} %get-tuple-element.41), channel_id=1, source_target_pairs={{193,192},{194,193},{195,194},{196,195},{197,196},{198,197},{199,1... | collective-permute-start | bytes 3145736 | tf_op jit(solution)/shard_map/ppermute | solution.py:368
  35.0 60.2 %collective-permute-start = (bf16[128,4096]{1,0:T(8,128)(2,1)}, bf16[128,4096]{1,0:T(8,128)(2,1)}, u32[]{:S(2)}, u32[]{:S(2)}) collective-permute-start(bf16[128,4096]{1,0:T(8,128)(2,1)} %forward_tile.1), channel_id=1, source_target_pairs={{64,128},{65,129},{66,130},{67,131},{68,132},{69,133},{70,134},{71... | collective-permute-start | bytes 3145736 | tf_op jit(solution)/shard_map/ppermute | solution.py:368
  68.1 21.8 %copy-start.1 = (bf16[1,384,4096]{2,1,0:T(8,128)(2,1)S(1)}, bf16[1,384,4096]{2,1,0:T(8,128)(2,1)}, u32[]{:S(2)}) copy-start(bf16[1,384,4096]{2,1,0:T(8,128)(2,1)} %param.11) | copy-start | bytes 9437188
  77.2 1.0 copy-start.12
  78.2 9.3 %collective-permute-start.6 = (bf16[128,128]{1,0:T(8,128)(2,1)S(1)}, bf16[128,128]{1,0:T(8,128)(2,1)S(1)}, u32[]{:S(2)}, u32[]{:S(2)}) collective-permute-start(bf16[128,128]{1,0:T(8,128)(2,1)S(1)} %get-tuple-element.47), channel_id=1, source_target_pairs={{0,1},{1,2},{2,3},{3,4},{4,5},{5,6},{6,7},{7,8},{8,9},{9,10},{10,1... | collective-permute-start | bytes 98312 | tf_op jit(solution)/shard_map/ppermute | solution.py:368
  78.9 11.1 %collective-permute-start.7 = (bf16[128,128]{1,0:T(8,128)(2,1)S(1)}, bf16[128,128]{1,0:T(8,128)(2,1)S(1)}, u32[]{:S(2)}, u32[]{:S(2)}) collective-permute-start(bf16[128,128]{1,0:T(8,128)(2,1)S(1)} %get-tuple-element.49), channel_id=1, source_target_pairs={{1,0},{2,1},{3,2},{4,3},{5,4},{6,5},{7,6},{8,7},{9,8},{10,9},{11,1... | collective-permute-start | bytes 98312 | tf_op jit(solution)/shard_map/ppermute | solution.py:368
  79.6 37.9 %collective-permute-start.10 = (bf16[128,4096]{1,0:T(8,128)(2,1)}, bf16[128,4096]{1,0:T(8,128)(2,1)}, u32[]{:S(2)}, u32[]{:S(2)}) collective-permute-start(bf16[128,4096]{1,0:T(8,128)(2,1)} %copy-done.14), channel_id=1, source_target_pairs={{65,64},{66,65},{67,66},{68,67},{69,68},{70,69},{71,70},{72,71},{7... | collective-permute-start | bytes 3145736 | tf_op jit(solution)/shard_map/ppermute | solution.py:368
  83.7 38.9 %collective-permute-start.9 = (bf16[128,4096]{1,0:T(8,128)(2,1)}, bf16[128,4096]{1,0:T(8,128)(2,1)}, u32[]{:S(2)}, u32[]{:S(2)}) collective-permute-start(bf16[128,4096]{1,0:T(8,128)(2,1)} %copy-done.14), channel_id=1, source_target_pairs={{64,65},{65,66},{66,67},{67,68},{68,69},{69,70},{70,71},{71,72},{7... | collective-permute-start | bytes 3145736 | tf_op jit(solution)/shard_map/ppermute | solution.py:368
  87.6 35.0 %collective-permute-start.8 = (bf16[128,5120]{1,0:T(8,128)(2,1)}, bf16[128,5120]{1,0:T(8,128)(2,1)}, u32[]{:S(2)}, u32[]{:S(2)}) collective-permute-start(bf16[128,5120]{1,0:T(8,128)(2,1)} %get-tuple-element.54), channel_id=1, source_target_pairs={{64,0},{65,1},{66,2},{67,3},{68,4},{69,5},{70,6},{71,7},{72,8},{73... | collective-permute-start | bytes 3932168 | tf_op jit(solution)/shard_map/ppermute | solution.py:368
  90.0 1.2 copy-start.11
  91.2 1.2 copy-start.13
  94.1 1.0 copy-start.7
  95.2 22.3 %all-to-all-start = ((bf16[16,256,128]{2,1,0:T(8,128)(2,1)}), bf16[16,256,128]{2,1,0:T(8,128)(2,1)}, u32[]{:S(2)}, u32[]{:S(2)}) async-start(bf16[16,256,128]{2,1,0:T(8,128)(2,1)} %bitcast.29), calls=%async_computation | async-start | bytes 2097152 | tf_op jit(solution)/shard_map/all_to_all | solution.py:392
  104.0 26.9 %copy-start.15 = (bf16[128,4096]{1,0:T(8,128)(2,1)S(1)}, bf16[128,4096]{1,0:T(8,128)(2,1)}, u32[]{:S(2)}) copy-start(bf16[128,4096]{1,0:T(8,128)(2,1)} %copy-done.14) | copy-start | bytes 3145732
  106.4 24.5 %collective-permute-start.11 = (bf16[128,4096]{1,0:T(8,128)(2,1)}, bf16[128,4096]{1,0:T(8,128)(2,1)S(1)}, u32[]{:S(2)}, u32[]{:S(2)}) collective-permute-start(bf16[128,4096]{1,0:T(8,128)(2,1)} %broadcast_select_fusion), channel_id=1, source_target_pairs={{67,132},{71,136},{75,140},{79,144},{83,148},{87,152},{91,156},{95... | collective-permute-start | bytes 3145736 | tf_op jit(solution)/shard_map/ppermute | solution.py:368
  107.1 23.8 %collective-permute-start.12 = (bf16[128,4096]{1,0:T(8,128)(2,1)}, bf16[128,4096]{1,0:T(8,128)(2,1)S(1)}, u32[]{:S(2)}, u32[]{:S(2)}) collective-permute-start(bf16[128,4096]{1,0:T(8,128)(2,1)} %broadcast_select_fusion), channel_id=1, source_target_pairs={{68,131},{72,135},{76,139},{80,143},{84,147},{88,151},{92,155},{96... | collective-permute-start | bytes 3145736 | tf_op jit(solution)/shard_map/ppermute | solution.py:368
  124.7 10.7 %all-to-all-start.1 = ((f32[4,64,128]{2,1,0:T(8,128)}), f32[4,64,128]{2,1,0:T(8,128)S(1)}, u32[]{:S(2)}, u32[]{:S(2)}) async-start(f32[4,64,128]{2,1,0:T(8,128)} %bitcast.14), calls=%async_computation.1 | async-start | bytes 262144 | tf_op jit(solution)/shard_map/all_to_all | solution.py:392
